TPU v7x, 32 devices: a whole 2x2x4 slice. The times are simulated.
32 devices in a mesh: ctx: 8 (over z, x), fsdp: 4 (over y, core).
Axes of the slice: x: 2, y: 2, z: 4, core: 2. Of those that a mesh axis runs over, the one named last changes fastest.
Arguments:
- tokens: bfloat16 [4, 1024, 1024], P('fsdp', 'ctx'), may hold values from -6 to 6
- cotangent: bfloat16 [4, 1024, 1024], P('fsdp', 'ctx'), may hold values from -6 to 6
- segments: int32 [4, 1024], P('fsdp'), may hold values from 0 to 1, as said below
- decay_index: int32 [4, 16, 8], P('fsdp'), may hold values from 0 to 8
- step_index: int32 [4, 16, 8], P('fsdp'), may hold values from 0 to 3
- w_qkv: bfloat16 [1024, 3072], P('fsdp'), may hold values from -0.1875 to 0.1875
- w_gate: bfloat16 [1024, 1024], P('fsdp'), may hold values from -0.1875 to 0.1875
- w_out: bfloat16 [1024, 1024], P('fsdp'), may hold values from -0.5 to 0.5
- w_gu: bfloat16 [1024, 5632], P('fsdp'), may hold values from -0.1875 to 0.1875
- w_down: bfloat16 [2816, 1024], P('fsdp'), may hold values from -0.109375 to 0.109375
- persist_keys: bfloat16 [16, 1024], P('fsdp'), may hold values from -5 to 5
- persist_values: bfloat16 [16, 1024], P('fsdp'), may hold values from -5 to 5
- norm_gain: bfloat16 [1024], P('fsdp'), may hold values from 0.5 to 1.5
- ffn_gain: bfloat16 [1024], P('fsdp'), may hold values from 0.5 to 1.5
Outputs:
- output: bfloat16 [4, 1024, 1024], P('fsdp', 'ctx')
- grad_tokens: float32 [4, 1024, 1024], P('fsdp', 'ctx')
- grad_w_qkv: float32 [1024, 3072], P('fsdp')
- grad_w_gate: float32 [1024, 1024], P('fsdp')
- grad_w_out: float32 [1024, 1024], P('fsdp')
- grad_w_gu: float32 [1024, 5632], P('fsdp')
- grad_w_down: float32 [2816, 1024], P('fsdp')
- grad_persist_keys: float32 [16, 1024], P('fsdp')
- grad_persist_values: float32 [16, 1024], P('fsdp')
- grad_norm_gain: float32 [1024], P('fsdp')
- grad_ffn_gain: float32 [1024], P('fsdp')
Inputs may be any that keep to these rules, and one draw needn't show every extreme that they name: `segments`: segment numbers start at 0 and never fall along positions; segment 0 covers at least positions 0 to 511; the last position of every sequence has the largest number, and the last document may be longer than 2000.
All inputs are finite; a program needn't handle non-finite values.
Results may differ from a plain program's by a relative error of at most 0.02.
Values may be sent and summed in bfloat16 or wider, within the bound.
No kernel may reach another device: no remote copies, remote signals or barrier semaphores. Data moves between devices by JAX's collectives and lax.ppermute only.
A program may use at most 384 MiB of HBM per device.

v0:
```python
import jax
import jax.numpy as jnp
from jax import lax
from jax.sharding import PartitionSpec as P

HEADS = 8
HEAD_WIDTH_SIZE = 128
FF = 2816
GROUP = 64


epsilon = 1e-06
momentum = 0.9
masked_score = -1e30
highest_precision = lax.Precision.HIGHEST


def rms_scale(values):
    return lax.rsqrt(jnp.mean(values * values, axis=-1, keepdims=True) + epsilon)


def norm_back(values, inv_rms, gain_vec, grad_normed):
    scaled_grad = grad_normed * gain_vec
    grad_gain = jnp.sum(grad_normed * values * inv_rms, axis=0)
    grad_values = inv_rms * scaled_grad - values * inv_rms * inv_rms * inv_rms * jnp.mean(
        scaled_grad * values, axis=-1, keepdims=True
    )
    return (grad_values, grad_gain)


def place_rows(row_index, shard_rows, dev_count):
    half_rows = shard_rows // 2
    owner_dev = row_index // shard_rows
    inner_row = row_index % shard_rows
    block_id = jnp.where(inner_row < half_rows, owner_dev, 2 * dev_count - 1 - owner_dev)
    return block_id * half_rows + inner_row % half_rows


def position_order(stored, dev_count):
    rows = stored.shape[0]
    rest = stored.shape[1:]
    split = stored.reshape((dev_count, 2, rows // (2 * dev_count)) + rest)
    early = split[:, 0].reshape((-1,) + rest)
    late = split[::-1, 1].reshape((-1,) + rest)
    return jnp.concatenate([early, late], axis=0)


def key_mask(query_pos, query_seg, key_pos, key_seg):
    return (key_seg[None, :] == query_seg[:, None]) & (key_pos[None, :] <= query_pos[:, None])


def head_scores(queries, key_block):
    return jnp.einsum(
        "qhd,khd->hqk", queries, key_block, preferred_element_type=jnp.float32
    ) * HEAD_WIDTH_SIZE ** (-0.5)


def online_step(running, scores, value_block):
    run_max, run_total, accumulated = running
    new_max = jnp.maximum(run_max, jnp.max(scores, axis=-1))
    rescale = jnp.exp(run_max - new_max)
    weights = jnp.exp(scores - new_max[:, :, None])
    run_total = run_total * rescale + jnp.sum(weights, axis=-1)
    update = jnp.einsum(
        "hqk,khd->qhd",
        weights.astype(jnp.bfloat16),
        value_block,
        preferred_element_type=jnp.float32,
    )
    accumulated = accumulated * jnp.transpose(rescale)[:, :, None] + update
    return (new_max, run_total, accumulated)


def fold_keys(running, all_keys, all_values, context):
    queries, query_pos, query_seg, segment_all, shard_rows, dev_count = context
    total_rows = all_keys.shape[0]
    block_rows = min(512, total_rows)

    def fold_one_block(carried, block_index):
        offset_row = block_index * block_rows
        key_block = lax.dynamic_slice_in_dim(all_keys, offset_row, block_rows, 0).reshape(
            block_rows, HEADS, HEAD_WIDTH_SIZE
        )
        value_block = lax.dynamic_slice_in_dim(all_values, offset_row, block_rows, 0).reshape(
            block_rows, HEADS, HEAD_WIDTH_SIZE
        )
        key_pos = place_rows(
            offset_row + jnp.arange(block_rows, dtype=jnp.int32), shard_rows, dev_count
        )
        key_seg = jnp.take(segment_all, key_pos)
        allowed = key_mask(query_pos, query_seg, key_pos, key_seg)
        scores = jnp.where(allowed[None], head_scores(queries, key_block), masked_score)
        carried = online_step(carried, scores, value_block)
        return (carried, None)

    running, _ = lax.scan(
        fold_one_block, running, jnp.arange(total_rows // block_rows, dtype=jnp.int32)
    )
    return running


def back_every_key(grad_query, all_keys, all_values, context, grad_heads, log_total, row_delta):
    queries, query_pos, query_seg, segment_all, shard_rows, dev_count = context
    total_rows = all_keys.shape[0]
    block_rows = min(512, total_rows)
    scale_factor = HEAD_WIDTH_SIZE ** (-0.5)

    def back_one_block(carried, block_index):
        offset_row = block_index * block_rows
        key_block = lax.dynamic_slice_in_dim(all_keys, offset_row, block_rows, 0).reshape(
            block_rows, HEADS, HEAD_WIDTH_SIZE
        )
        value_block = lax.dynamic_slice_in_dim(all_values, offset_row, block_rows, 0).reshape(
            block_rows, HEADS, HEAD_WIDTH_SIZE
        )
        key_pos = place_rows(
            offset_row + jnp.arange(block_rows, dtype=jnp.int32), shard_rows, dev_count
        )
        key_seg = jnp.take(segment_all, key_pos)
        allowed = key_mask(query_pos, query_seg, key_pos, key_seg)
        scores = jnp.where(allowed[None], head_scores(queries, key_block), masked_score)
        prob_block = jnp.exp(scores - log_total[:, :, None])
        grad_prob = jnp.einsum(
            "qhd,khd->hqk", grad_heads, value_block, preferred_element_type=jnp.float32
        )
        grad_scores = (prob_block * (grad_prob - row_delta[:, :, None])).astype(jnp.bfloat16)
        query_grad = (
            carried
            + jnp.einsum("hqk,khd->qhd", grad_scores, key_block, preferred_element_type=jnp.float32)
            * scale_factor
        )
        key_grad = (
            jnp.einsum("hqk,qhd->khd", grad_scores, queries, preferred_element_type=jnp.float32)
            * scale_factor
        )
        value_grad = jnp.einsum(
            "hqk,qhd->khd",
            prob_block.astype(jnp.bfloat16),
            grad_heads,
            preferred_element_type=jnp.float32,
        )
        return (query_grad, (key_grad, value_grad))

    grad_query, (key_grads, value_grads) = lax.scan(
        back_one_block, grad_query, jnp.arange(total_rows // block_rows, dtype=jnp.int32)
    )
    return (
        grad_query,
        key_grads.reshape(total_rows, HEADS, HEAD_WIDTH_SIZE),
        value_grads.reshape(total_rows, HEADS, HEAD_WIDTH_SIZE),
    )


def group_step(stacked_rows, group_key_rows, group_value_rows, alpha_row, learning_rate_row):
    current_memory = stacked_rows[:, :HEAD_WIDTH_SIZE]
    moment_now = stacked_rows[:, HEAD_WIDTH_SIZE:]
    gram_matrix = (
        jnp.einsum("thk,thj->hkj", group_key_rows, group_key_rows, precision=highest_precision)
        * learning_rate_row[:, None, None]
    )
    mixed_product = (
        jnp.einsum("qgw,qgc->gwc", group_key_rows, group_value_rows, precision=highest_precision)
        * learning_rate_row[:, None, None]
    )
    memory_gradient = (
        jnp.einsum("fld,fdi->fli", gram_matrix, current_memory, precision=highest_precision)
        - mixed_product
    )
    moment_next = momentum * moment_now - memory_gradient
    memory_next = (1.0 - alpha_row)[:, None, None] * current_memory + moment_next
    return jnp.concatenate([memory_next, moment_next], axis=1)


def run_block(stacked_rows, query_part, key_part, value_part, alphas, thetas):
    scale_factor = HEAD_WIDTH_SIZE ** (-0.5)
    group_query_rows = query_part * scale_factor
    recalled_rows = [
        jnp.einsum(
            "ipb,pbx->ipx",
            group_query_rows,
            stacked_rows[:, :HEAD_WIDTH_SIZE],
            precision=highest_precision,
        )
    ]
    stacked_rows = group_step(
        stacked_rows, key_part * scale_factor, value_part, alphas[0], thetas[0]
    )
    return (jnp.concatenate(recalled_rows, axis=0), stacked_rows)


def states_before(key_order, value_order, alpha_all, theta_all, early_index, late_index):
    groups = alpha_all.shape[0]
    scale_factor = HEAD_WIDTH_SIZE ** (-0.5)
    key_groups = key_order.reshape(groups, GROUP, HEADS, HEAD_WIDTH_SIZE)
    value_groups = value_order.reshape(groups, GROUP, HEADS, HEAD_WIDTH_SIZE)
    zero_state = jnp.zeros((HEADS, 2 * HEAD_WIDTH_SIZE, HEAD_WIDTH_SIZE), jnp.float32)

    def states_one_group(carried, inputs):
        stacked_rows, into_early, into_late = carried
        group_key_rows, group_value_rows, alpha_row, learning_rate_row, group_index = inputs
        into_early = jnp.where(group_index == early_index, stacked_rows, into_early)
        into_late = jnp.where(group_index == late_index, stacked_rows, into_late)
        current_memory = stacked_rows[:, :HEAD_WIDTH_SIZE]
        moment_now = stacked_rows[:, HEAD_WIDTH_SIZE:]
        gram_matrix = (
            jnp.einsum(
                "thk,thj->hkj", group_key_rows, group_key_rows, preferred_element_type=jnp.float32
            )
            * (learning_rate_row / HEAD_WIDTH_SIZE)[:, None, None]
        )
        mixed_product = (
            jnp.einsum(
                "qgw,qgc->gwc", group_key_rows, group_value_rows, preferred_element_type=jnp.float32
            )
            * (learning_rate_row * scale_factor)[:, None, None]
        )
        memory_gradient = (
            jnp.einsum("fld,fdi->fli", gram_matrix, current_memory, precision=highest_precision)
            - mixed_product
        )
        moment_next = momentum * moment_now - memory_gradient
        memory_next = (1.0 - alpha_row)[:, None, None] * current_memory + moment_next
        stacked_rows = jnp.concatenate([memory_next, moment_next], axis=1)
        return ((stacked_rows, into_early, into_late), None)

    (_, into_early, into_late), _ = lax.scan(
        states_one_group,
        (zero_state, zero_state, zero_state),
        (key_groups, value_groups, alpha_all, theta_all, jnp.arange(groups, dtype=jnp.int32)),
    )
    return (into_early, into_late)


def adjoints_after(
    query_order, key_order, recall_grad_order, alpha_all, theta_all, early_end, late_end
):
    groups = alpha_all.shape[0]
    scale_factor = HEAD_WIDTH_SIZE ** (-0.5)
    query_groups = query_order.reshape(groups, GROUP, HEADS, HEAD_WIDTH_SIZE)
    key_groups = key_order.reshape(groups, GROUP, HEADS, HEAD_WIDTH_SIZE)
    grad_groups = recall_grad_order.reshape(groups, GROUP, HEADS, HEAD_WIDTH_SIZE)
    zero_state = jnp.zeros((HEADS, 2 * HEAD_WIDTH_SIZE, HEAD_WIDTH_SIZE), jnp.float32)

    def adjoints_one_group(carried, inputs):
        adjoint, out_early, out_late = carried
        (
            group_query_rows,
            group_key_rows,
            gradient_group_rows,
            alpha_row,
            learning_rate_row,
            group_index,
        ) = inputs
        out_early = jnp.where(group_index + 1 == early_end, adjoint, out_early)
        out_late = jnp.where(group_index + 1 == late_end, adjoint, out_late)
        gram_matrix = (
            jnp.einsum(
                "thk,thj->hkj", group_key_rows, group_key_rows, preferred_element_type=jnp.float32
            )
            * (learning_rate_row / HEAD_WIDTH_SIZE)[:, None, None]
        )
        query_term = (
            jnp.einsum(
                "qgw,qgc->gwc",
                group_query_rows,
                gradient_group_rows,
                preferred_element_type=jnp.float32,
            )
            * scale_factor
        )
        grad_m = adjoint[:, :HEAD_WIDTH_SIZE]
        summed_rows = grad_m + adjoint[:, HEAD_WIDTH_SIZE:]
        new_m = (
            (1.0 - alpha_row)[:, None, None] * grad_m
            + query_term
            - jnp.einsum("fld,fdi->fli", gram_matrix, summed_rows, precision=highest_precision)
        )
        adjoint = jnp.concatenate([new_m, momentum * summed_rows], axis=1)
        return ((adjoint, out_early, out_late), None)

    (_, out_early, out_late), _ = lax.scan(
        adjoints_one_group,
        (zero_state, zero_state, zero_state),
        (
            query_groups,
            key_groups,
            grad_groups,
            alpha_all,
            theta_all,
            jnp.arange(groups, dtype=jnp.int32),
        ),
        reverse=True,
    )
    return (out_early, out_late)


def on_device(
    tokens,
    cotangent,
    segments,
    decay_index,
    step_index,
    w_qkv,
    w_gate,
    w_out,
    w_gu,
    w_down,
    persist_keys,
    persist_values,
    norm_gain,
    ffn_gain,
):
    shard_rows = tokens.shape[1]
    model_width = tokens.shape[2]
    half_rows = shard_rows // 2
    dev_count = lax.axis_size("ctx")
    device = lax.axis_index("ctx")
    scale_factor = HEAD_WIDTH_SIZE ** (-0.5)
    full_weights = (
        lax.all_gather(w_qkv, "fsdp", axis=0, tiled=True),
        lax.all_gather(w_gate, "fsdp", axis=0, tiled=True),
        lax.all_gather(w_out, "fsdp", axis=0, tiled=True),
        lax.all_gather(w_gu, "fsdp", axis=0, tiled=True),
        lax.all_gather(w_down, "fsdp", axis=0, tiled=True),
        lax.all_gather(persist_keys, "fsdp", axis=0, tiled=True),
        lax.all_gather(persist_values, "fsdp", axis=0, tiled=True),
        lax.all_gather(norm_gain, "fsdp", axis=0, tiled=True),
        lax.all_gather(ffn_gain, "fsdp", axis=0, tiled=True),
    )
    wq_full, wg_full, wo_full, wgu_full, wd_full, pkeys_full, pvalues_full, gain_attn, gain_ffn = (
        full_weights
    )
    gain_attn32 = gain_attn.astype(jnp.float32)
    gain_ffn32 = gain_ffn.astype(jnp.float32)
    pkeys_heads = pkeys_full.reshape(-1, HEADS, HEAD_WIDTH_SIZE)
    pvalues_heads = pvalues_full.reshape(-1, HEADS, HEAD_WIDTH_SIZE)
    inputs32 = tokens[0].astype(jnp.float32)
    inv_rms_one = rms_scale(inputs32)
    normed_low = (inputs32 * inv_rms_one * gain_attn32).astype(jnp.bfloat16)
    projected = jnp.dot(normed_low, wq_full, preferred_element_type=jnp.float32)
    query_flat = projected[:, :model_width].astype(jnp.bfloat16)
    key_flat = projected[:, model_width : 2 * model_width].astype(jnp.bfloat16)
    value_flat = projected[:, 2 * model_width :].astype(jnp.bfloat16)
    query_heads = query_flat.reshape(shard_rows, HEADS, HEAD_WIDTH_SIZE)
    gate_open = jax.nn.sigmoid(jnp.dot(normed_low, wg_full, preferred_element_type=jnp.float32))
    local_rows = jnp.arange(shard_rows, dtype=jnp.int32)
    query_pos = place_rows(device * shard_rows + local_rows, shard_rows, dev_count)
    segment_all = segments[0]
    query_seg = jnp.take(segment_all, query_pos)
    context = (query_heads, query_pos, query_seg, segment_all, shard_rows, dev_count)
    all_keys, all_values = (
        lax.all_gather(key_flat, "ctx", axis=0, tiled=True),
        lax.all_gather(value_flat, "ctx", axis=0, tiled=True),
    )
    persist_scores = head_scores(query_heads, pkeys_heads)
    start_state = (
        jnp.full((HEADS, shard_rows), masked_score, jnp.float32),
        jnp.zeros((HEADS, shard_rows), jnp.float32),
        jnp.zeros((shard_rows, HEADS, HEAD_WIDTH_SIZE), jnp.float32),
    )
    running = online_step(start_state, persist_scores, pvalues_heads)
    running = fold_keys(running, all_keys, all_values, context)
    run_max, run_total, accumulated = running
    attended = accumulated / jnp.transpose(run_total)[:, :, None]
    log_total = run_max + jnp.log(run_total)
    group_count = half_rows // GROUP
    alpha_all = 0.6 * jnp.exp2(-decay_index[0].astype(jnp.float32))
    theta_all = 0.1 * jnp.exp2(-step_index[0].astype(jnp.float32))
    early_first = device * group_count
    late_first = (2 * dev_count - 1 - device) * group_count
    alpha_early = lax.dynamic_slice_in_dim(alpha_all, early_first, group_count, 0)
    theta_early = lax.dynamic_slice_in_dim(theta_all, early_first, group_count, 0)
    alpha_late = lax.dynamic_slice_in_dim(alpha_all, late_first, group_count, 0)
    theta_late = lax.dynamic_slice_in_dim(theta_all, late_first, group_count, 0)
    query_f = query_heads.astype(jnp.float32)
    key_f = key_flat.astype(jnp.float32).reshape(shard_rows, HEADS, HEAD_WIDTH_SIZE)
    value_f = value_flat.astype(jnp.float32).reshape(shard_rows, HEADS, HEAD_WIDTH_SIZE)
    early_parts = (query_f[:half_rows], key_f[:half_rows], value_f[:half_rows])
    late_parts = (query_f[half_rows:], key_f[half_rows:], value_f[half_rows:])

    def early_run(stacked_rows, query_part, key_part, value_part):
        return run_block(stacked_rows, query_part, key_part, value_part, alpha_early, theta_early)

    def late_run(stacked_rows, query_part, key_part, value_part):
        return run_block(stacked_rows, query_part, key_part, value_part, alpha_late, theta_late)

    into_early, into_late = states_before(
        position_order(all_keys, dev_count),
        position_order(all_values, dev_count),
        alpha_all,
        theta_all,
        early_first,
        late_first,
    )
    recall_early, _ = early_run(into_early, early_parts[0], early_parts[1], early_parts[2])
    recall_late, _ = late_run(into_late, late_parts[0], late_parts[1], late_parts[2])
    recall = jnp.concatenate([recall_early, recall_late], axis=0).reshape(shard_rows, model_width)
    mixed_low = (attended.reshape(shard_rows, model_width) + gate_open * recall).astype(
        jnp.bfloat16
    )
    residual = inputs32 + jnp.dot(mixed_low, wo_full, preferred_element_type=jnp.float32)
    inv_rms_two = rms_scale(residual)
    normed_two = (residual * inv_rms_two * gain_ffn32).astype(jnp.bfloat16)
    gate_up = jnp.dot(normed_two, wgu_full, preferred_element_type=jnp.float32)
    gate_part = gate_up[:, :FF]
    up_part = gate_up[:, FF:]
    active = (jax.nn.silu(gate_part) * up_part).astype(jnp.bfloat16)
    result = residual + jnp.dot(active, wd_full, preferred_element_type=jnp.float32)
    cot_low = cotangent[0]
    grad_w_down = jnp.einsum("tf,td->fd", active, cot_low, preferred_element_type=jnp.float32)
    grad_active = jnp.einsum("td,fd->tf", cot_low, wd_full, preferred_element_type=jnp.float32)
    sigma_gate = jax.nn.sigmoid(gate_part)
    grad_gate_part = grad_active * up_part * sigma_gate * (1.0 + gate_part * (1.0 - sigma_gate))
    grad_up_part = grad_active * gate_part * sigma_gate
    grad_gu_low = jnp.concatenate([grad_gate_part, grad_up_part], axis=1).astype(jnp.bfloat16)
    grad_w_gu = jnp.einsum("td,tf->df", normed_two, grad_gu_low, preferred_element_type=jnp.float32)
    grad_normed_two = jnp.einsum(
        "tf,df->td", grad_gu_low, wgu_full, preferred_element_type=jnp.float32
    )
    grad_res_norm, grad_ffn_gain = norm_back(residual, inv_rms_two, gain_ffn32, grad_normed_two)
    grad_residual = cot_low.astype(jnp.float32) + grad_res_norm
    grad_branch = grad_residual.astype(jnp.bfloat16)
    grad_w_out = jnp.einsum("td,te->de", mixed_low, grad_branch, preferred_element_type=jnp.float32)
    grad_mixed_low = jnp.einsum(
        "te,de->td", grad_branch, wo_full, preferred_element_type=jnp.float32
    ).astype(jnp.bfloat16)
    grad_mixed32 = grad_mixed_low.astype(jnp.float32)
    grad_gate_low = (grad_mixed32 * recall * gate_open * (1.0 - gate_open)).astype(jnp.bfloat16)
    grad_w_gate = jnp.einsum(
        "td,tf->df", normed_low, grad_gate_low, preferred_element_type=jnp.float32
    )
    recall_grad_low = (grad_mixed32 * gate_open).astype(jnp.bfloat16)
    grad_recall = recall_grad_low.astype(jnp.float32).reshape(shard_rows, HEADS, HEAD_WIDTH_SIZE)
    grad_heads = grad_mixed_low.reshape(shard_rows, HEADS, HEAD_WIDTH_SIZE)
    row_delta = jnp.transpose(jnp.sum(grad_heads.astype(jnp.float32) * attended, axis=-1))
    memory_queries, all_recall_grads = (
        lax.all_gather(query_flat, "ctx", axis=0, tiled=True),
        lax.all_gather(recall_grad_low, "ctx", axis=0, tiled=True),
    )
    out_early, out_late = adjoints_after(
        position_order(memory_queries, dev_count),
        position_order(all_keys, dev_count),
        position_order(all_recall_grads, dev_count),
        alpha_all,
        theta_all,
        early_first + group_count,
        late_first + group_count,
    )
    _, pull_early = jax.vjp(early_run, into_early, early_parts[0], early_parts[1], early_parts[2])
    _, grad_qe, grad_ke, grad_ve = pull_early((grad_recall[:half_rows], out_early))
    _, pull_late = jax.vjp(late_run, into_late, late_parts[0], late_parts[1], late_parts[2])
    _, grad_ql, grad_kl, grad_vl = pull_late((grad_recall[half_rows:], out_late))
    grad_q_mem = jnp.concatenate([grad_qe, grad_ql], axis=0).reshape(shard_rows, model_width)
    grad_k_mem = jnp.concatenate([grad_ke, grad_kl], axis=0).reshape(shard_rows, model_width)
    grad_v_mem = jnp.concatenate([grad_ve, grad_vl], axis=0).reshape(shard_rows, model_width)
    persist_probs = jnp.exp(persist_scores - log_total[:, :, None])
    persist_grad_prob = jnp.einsum(
        "qhd,phd->hqp", grad_heads, pvalues_heads, preferred_element_type=jnp.float32
    )
    persist_ds = (persist_probs * (persist_grad_prob - row_delta[:, :, None])).astype(jnp.bfloat16)
    grad_query_att = (
        jnp.einsum("hqp,phd->qhd", persist_ds, pkeys_heads, preferred_element_type=jnp.float32)
        * scale_factor
    )
    grad_pkeys = (
        jnp.einsum("hqp,qhd->phd", persist_ds, query_heads, preferred_element_type=jnp.float32)
        * scale_factor
    )
    grad_pvalues = jnp.einsum(
        "hqp,qhd->phd",
        persist_probs.astype(jnp.bfloat16),
        grad_heads,
        preferred_element_type=jnp.float32,
    )
    grad_query_att, key_grads_all, value_grads_all = back_every_key(
        grad_query_att, all_keys, all_values, context, grad_heads, log_total, row_delta
    )
    key_grad_att, value_grad_att = (
        lax.psum_scatter(key_grads_all, "ctx", scatter_dimension=0, tiled=True),
        lax.psum_scatter(value_grads_all, "ctx", scatter_dimension=0, tiled=True),
    )
    grad_query = grad_query_att.reshape(shard_rows, model_width) + grad_q_mem
    grad_key = key_grad_att.reshape(shard_rows, model_width) + grad_k_mem
    grad_value = value_grad_att.reshape(shard_rows, model_width) + grad_v_mem
    grad_qkv_low = jnp.concatenate([grad_query, grad_key, grad_value], axis=1).astype(jnp.bfloat16)
    grad_w_qkv = jnp.einsum(
        "td,tf->df", normed_low, grad_qkv_low, preferred_element_type=jnp.float32
    )
    grad_normed = jnp.einsum(
        "tf,df->td", grad_qkv_low, wq_full, preferred_element_type=jnp.float32
    ) + jnp.einsum("tf,df->td", grad_gate_low, wg_full, preferred_element_type=jnp.float32)
    grad_in_norm, grad_norm_gain = norm_back(inputs32, inv_rms_one, gain_attn32, grad_normed)
    grad_inputs = grad_residual + grad_in_norm
    local_grads = (
        grad_w_qkv,
        grad_w_gate,
        grad_w_out,
        grad_w_gu,
        grad_w_down,
        grad_pkeys.reshape(-1, model_width),
        grad_pvalues.reshape(-1, model_width),
        grad_norm_gain,
        grad_ffn_gain,
    )
    shares = (
        lax.psum_scatter(
            local_grads[0].astype(jnp.bfloat16), "fsdp", scatter_dimension=0, tiled=True
        ).astype(jnp.float32),
        lax.psum_scatter(
            local_grads[1].astype(jnp.bfloat16), "fsdp", scatter_dimension=0, tiled=True
        ).astype(jnp.float32),
        lax.psum_scatter(
            local_grads[2].astype(jnp.bfloat16), "fsdp", scatter_dimension=0, tiled=True
        ).astype(jnp.float32),
        lax.psum_scatter(
            local_grads[3].astype(jnp.bfloat16), "fsdp", scatter_dimension=0, tiled=True
        ).astype(jnp.float32),
        lax.psum_scatter(
            local_grads[4].astype(jnp.bfloat16), "fsdp", scatter_dimension=0, tiled=True
        ).astype(jnp.float32),
        lax.psum_scatter(
            local_grads[5].astype(jnp.bfloat16), "fsdp", scatter_dimension=0, tiled=True
        ).astype(jnp.float32),
        lax.psum_scatter(
            local_grads[6].astype(jnp.bfloat16), "fsdp", scatter_dimension=0, tiled=True
        ).astype(jnp.float32),
        lax.psum_scatter(
            local_grads[7].astype(jnp.bfloat16), "fsdp", scatter_dimension=0, tiled=True
        ).astype(jnp.float32),
        lax.psum_scatter(
            local_grads[8].astype(jnp.bfloat16), "fsdp", scatter_dimension=0, tiled=True
        ).astype(jnp.float32),
    )
    totals = lax.psum(
        (
            shares[0],
            shares[1],
            shares[2],
            shares[3],
            shares[4],
            shares[5],
            shares[6],
            shares[7],
            shares[8],
        ),
        "ctx",
    )
    return (
        result.astype(jnp.bfloat16)[None],
        grad_inputs[None],
        totals[0],
        totals[1],
        totals[2],
        totals[3],
        totals[4],
        totals[5],
        totals[6],
        totals[7],
        totals[8],
    )


def solution(mesh):
    in_specs = (
        P("fsdp", "ctx", None),
        P("fsdp", "ctx", None),
        P("fsdp", None),
        P("fsdp", None, None),
        P("fsdp", None, None),
        P("fsdp", None),
        P("fsdp", None),
        P("fsdp", None),
        P("fsdp", None),
        P("fsdp", None),
        P("fsdp", None),
        P("fsdp", None),
        P("fsdp"),
        P("fsdp"),
    )
    out_specs = (
        P("fsdp", "ctx", None),
        P("fsdp", "ctx", None),
        P("fsdp", None),
        P("fsdp", None),
        P("fsdp", None),
        P("fsdp", None),
        P("fsdp", None),
        P("fsdp", None),
        P("fsdp", None),
        P("fsdp"),
        P("fsdp"),
    )
    return jax.shard_map(
        on_device, mesh=mesh, in_specs=in_specs, out_specs=out_specs, check_vma=False
    )
```

profile of v0, /device:TPU:0, one launch (start us, length us, event | category | flops | bytes accessed | tf_op | source)
XLA Modules:
  0.0 1477.2 jit_solution(12127265793419634208)
XLA Ops:
  8.6 6.0 all-gather
  15.7 43.0 %all-gather.14.cloned.1.call-done = bf16[1024,3072]{1,0:T(8,128)(2,1)} async-done(((bf16[256,3072]{1,0:T(8,128)(2,1)}), bf16[1024,3072]{1,0:T(8,128)(2,1)}) %all-gather.14.cloned.1.call-update) | async-done | bytes 6291472 | tf_op jit(solution)/shard_map/all_gather | solution.py:320
  58.7 3.8 convolution_convert_fusion.3
  67.3 5.2 all-gather.1
  72.5 5.2 all-gather.2
  78.6 5.1 all-gather.3
  87.3 26.0 %all-gather.16.cloned.1.call-done = bf16[1024,1024]{1,0:T(8,128)(2,1)} async-done(((bf16[128,1024]{1,0:T(8,128)(2,1)}), bf16[1024,1024]{1,0:T(8,128)(2,1)}) %all-gather.16.cloned.1.call-update) | async-done | bytes 2097168 | tf_op jit(solution)/shard_map/all_gather | solution.py:352
  113.3 3.9 copy.172
  117.3 46.6 %all-gather.18.cloned.1.call-done = bf16[1024,1024]{1,0:T(8,128)(2,1)} async-done(((bf16[128,1024]{1,0:T(8,128)(2,1)}), bf16[1024,1024]{1,0:T(8,128)(2,1)}) %all-gather.18.cloned.1.call-update) | async-done | bytes 2097168 | tf_op jit(solution)/shard_map/all_gather | solution.py:353
  163.8 4.0 copy.174
  167.8 16.0 %while.70 = (s32[]{:T(128)}, f32[8,128]{1,0:T(8,128)S(1)}, f32[8,128]{1,0:T(8,128)S(1)}, f32[128,8,128]{0,2,1:T(8,128)}, s32[2]{0:T(128)S(1)}, /*index=5*/s32[10...) while((s32[]{:T(128)}, f32[8,128]{1,0:T(8,128)S(1)}, ...), condition=%wide.region_6.8_spmd.clone, body=%wide.region_3.7_spmd.clone.sunk | while | flops 272614912 | bytes 18310936 | solution.py:96
  198.8 110.4 %while.72 = (s32[]{:T(128)}, f32[8,256,128]{2,1,0:T(8,128)S(1)}, f32[8,256,128]{2,1,0:T(8,128)S(1)}, f32[8,256,128]{2,1,0:T(8,128)S(1)}, f32[16,8]{1,0:T(8,128)S...) while((s32[]{:T(128)}, f32[8,256,128]{2,1,0:T(8,128)S(1)}, ...), condition=%wide.region_8.10_spmd.clone, body=%wide.region_7.9_spmd.clone.sunk | while | flops 237109280 | bytes 12714911 | solution.py:226
  313.0 3.1 fusion.84
  319.1 7.7 fusion.159
  326.8 6.2 all-gather.26.cloned.1.call-done
  333.0 6.8 multiply_convert_fusion.1
  339.8 4.4 multiply_reduce_fusion
  350.2 28.8 %while.71 = (s32[]{:T(128)}, f32[128,8,128]{0,2,1:T(8,128)}, f32[2,512,8,128]{3,1,0,2:T(8,128)}, f32[2,512,8,128]{3,1,0,2:T(8,128)}, s32[2]{0:T(128)S(1)}, /*ind...) while((s32[]{:T(128)}, f32[128,8,128]{0,2,1:T(8,128)}, ...), condition=%wide.region_13.15_spmd.clone, body=%wide.region_12.14_spmd.clone.sunk | while | flops 675789312 | bytes 95602664 | solution.py:144
  398.5 3.0 convolution_convert_fusion.4
  401.5 33.6 %all-gather.30.cloned.1.call-done = bf16[1024,1024]{1,0:T(8,128)(2,1)} async-done(((bf16[128,1024]{1,0:T(8,128)(2,1)}), bf16[1024,1024]{1,0:T(8,128)(2,1)}) %all-gather.30.cloned.1.call-update) | async-done | bytes 2097168 | tf_op jit(solution)/shard_map/all_gather | solution.py:438
  442.7 133.7 %while.73 = (s32[]{:T(128)}, f32[8,256,128]{2,1,0:T(8,128)S(1)}, f32[8,256,128]{2,1,0:T(8,128)}, f32[8,256,128]{2,1,0:T(8,128)}, f32[16,8]{1,0:T(8,128)}, /*inde...) while((s32[]{:T(128)}, f32[8,256,128]{2,1,0:T(8,128)S(1)}, ...), condition=%wide.region_16.18_spmd.clone, body=%wide.region_15.17_spmd.clone.sunk | while | flops 237240336 | bytes 14025699 | solution.py:281
  451.1 3.1 select_select_fusion.7
  459.5 3.0 select_select_fusion.7
  467.9 3.1 select_select_fusion.7
  476.4 3.0 select_select_fusion.7
  484.8 3.0 select_select_fusion.7
  493.2 3.0 select_select_fusion.7
  501.7 3.0 select_select_fusion.7
  510.1 3.0 select_select_fusion.7
  518.5 3.1 select_select_fusion.7
  526.9 3.0 select_select_fusion.7
  535.3 3.2 select_select_fusion.7
  543.9 3.0 select_select_fusion.7
  552.3 3.1 select_select_fusion.7
  560.8 3.0 select_select_fusion.7
  569.2 3.1 select_select_fusion.7
  591.8 25.6 %reduce-scatter.8.cloned.1.call-done = f32[128,8,128]{2,0,1:T(8,128)} async-done(((f32[1024,8,128]{2,0,1:T(8,128)}), f32[128,8,128]{2,0,1:T(8,128)}) %reduce-scatter.8.cloned.1.call-update) | async-done | bytes 524304 | tf_op jit(solution)/shard_map/reduce_scatter | solution.py:479
  618.8 5.2 fusion.102
  625.6 4.2 convolution_convert_fusion.1
  630.1 4.5 convolution_convert_fusion.2
  635.9 7.4 convolution_convert_fusion
  645.8 4.3 fusion.54
  651.1 34.1 %reduce-scatter.16.cloned.1.call-done = bf16[256,1024]{1,0:T(8,128)(2,1)} async-done(((bf16[1024,1024]{1,0:T(8,128)(2,1)}), bf16[256,1024]{1,0:T(8,128)(2,1)}) %reduce-scatter.16.cloned.1.call-update) | async-done | bytes 524304 | tf_op jit(solution)/shard_map/reduce_scatter | solution.py:512
  686.2 31.6 %all-reduce.9.cloned.1.call-done = (bf16[16,1024]{1,0:T(8,128)(2,1)}, bf16[16,1024]{1,0:T(8,128)(2,1)}, bf16[1024]{0:T(1024)(128)(2,1)}, bf16[1024]{0:T(1024)(128)(2,1)}) async-done(((bf16[16,1024]{1,0:T(8,128)(2,1)}, bf16[16,1024]{1,0:T(8,128)(2,1)}, bf16[1024]{0:T(1024)(128)(2,1)}, bf16[1024]{0:T(1024)(128)(2,1)}), (bf16[16,1024]{1,0:T(8,128)(2,1)}, bf16[16,1024]{1,0:T(8,128)(2,1)}, ...) | async-done | bytes 69648
  719.3 58.4 %reduce-scatter.20.cloned.1.call-done = bf16[704,1024]{1,0:T(8,128)(2,1)} async-done(((bf16[2816,1024]{1,0:T(8,128)(2,1)}), bf16[704,1024]{1,0:T(8,128)(2,1)}) %reduce-scatter.20.cloned.1.call-update) | async-done | bytes 1441808 | tf_op jit(solution)/shard_map/reduce_scatter | solution.py:518
  777.7 60.8 %reduce-scatter.12.cloned.1.call-done = bf16[256,3072]{1,0:T(8,128)(2,1)} async-done(((bf16[1024,3072]{1,0:T(8,128)(2,1)}), bf16[256,3072]{1,0:T(8,128)(2,1)}) %reduce-scatter.12.cloned.1.call-update) | async-done | bytes 1572880 | tf_op jit(solution)/shard_map/reduce_scatter | solution.py:506
  838.5 94.8 %reduce-scatter.18.cloned.1.call-done = bf16[256,5632]{1,0:T(8,128)(2,1)} async-done(((bf16[1024,5632]{1,0:T(8,128)(2,1)}), bf16[256,5632]{1,0:T(8,128)(2,1)}) %reduce-scatter.18.cloned.1.call-update) | async-done | bytes 2883600 | tf_op jit(solution)/shard_map/reduce_scatter | solution.py:515
  933.3 537.2 %all-reduce.10 = (f32[256,3072]{1,0:T(8,128)}, f32[256,1024]{1,0:T(8,128)}, f32[256,1024]{1,0:T(8,128)}, f32[256,5632]{1,0:T(8,128)}, f32[704,1024]{1,0:T(8,128)...) all-reduce(bf16[256,3072]{1,0:T(8,128)(2,1)} %reduce-scatter.12.clo, ...), channel_id=1, replica_groups=mesh['ctx'=8,'fsdp'=4] {'ctx'}, use_global_device_ids=true, to_apply=%region_20.22 | all-reduce | flops 3482112 | bytes 20910080 | tf_op jit(solution)/shard_map/psum | solution.py:534
  (723 shorter events, 295.6 us)
Async XLA Ops:
  7.2 51.5 %copy-start.17 = (bf16[1,128,1024]{2,1,0:T(8,128)(2,1)S(1)}, bf16[1,128,1024]{2,1,0:T(8,128)(2,1)}, u32[]{:S(2)}) copy-start(bf16[1,128,1024]{2,1,0:T(8,128)(2,1)} %param.24) | copy-start | bytes 786436
  7.2 51.5 %all-gather.14.cloned.1.call-start = ((), (), s32[]{:S(2)}) async-start(), calls=%async_computation.7 | async-start | bytes 7864320 | tf_op jit(solution)/shard_map/all_gather | solution.py:320
  7.9 105.4 %all-gather.16.cloned.1.call-start = ((), (), s32[]{:S(2)}) async-start(), calls=%async_computation.8 | async-start | bytes 2359296 | tf_op jit(solution)/shard_map/all_gather | solution.py:352
  15.7 46.8 %copy-start.72 = (f32[128]{0:T(128)}, f32[128]{0:T(128)S(1)}, u32[]{:S(2)}) copy-start(f32[128]{0:T(128)S(1)} %add_rsqrt_fusion.1) | copy-start | bytes 1540
  63.9 22.5 %copy-start.42 = (bf16[16,8,8,128]{3,2,1,0:T(8,128)(2,1)}, bf16[16,8,8,128]{3,2,1,0:T(8,128)(2,1)S(1)}, u32[]{:S(2)}) copy-start(bf16[16,8,8,128]{3,2,1,0:T(8,128)(2,1)S(1)} %get-tuple-element.1196) | copy-start | bytes 786436
  63.9 100.0 %all-gather.18.cloned.1.call-start = ((), (), s32[]{:S(2)}) async-start(), calls=%async_computation.9 | async-start | bytes 2359296 | tf_op jit(solution)/shard_map/all_gather | solution.py:353
  64.6 248.3 %all-gather.20.cloned.1.call-start = ((), (), s32[]{:S(2)}) async-start(), calls=%async_computation.10 | async-start | bytes 2621440 | tf_op jit(solution)/shard_map/all_gather | solution.py:321
  65.2 250.9 %all-gather.22.cloned.1.call-start = ((), (), s32[]{:S(2)}) async-start(), calls=%async_computation.11 | async-start | bytes 2621440 | tf_op jit(solution)/shard_map/all_gather | solution.py:322
  65.8 6.7 copy-start.87
  65.8 11.9 copy-start.89
  65.8 12.0 copy-start.88
  65.8 12.7 copy-start.90
  65.9 17.8 %copy-start = (s32[1,1024]{1,0:T(1,128)S(1)}, s32[1,1024]{1,0:T(1,128)}, u32[]{:S(2)}) copy-start(s32[1,1024]{1,0:T(1,128)} %param.26) | copy-start | bytes 12292
  65.9 253.2 %all-gather.24.cloned.1.call-start = ((), (), s32[]{:S(2)}) async-start(), calls=%async_computation.12 | async-start | bytes 14417920 | tf_op jit(solution)/shard_map/all_gather | solution.py:323
  66.5 266.6 %all-gather.26.cloned.1.call-start = ((), (), s32[]{:S(2)}) async-start(), calls=%async_computation.13 | async-start | bytes 7208960 | tf_op jit(solution)/shard_map/all_gather | solution.py:324
  67.2 318.6 %all-gather.28.cloned.1.call-start = ((), (), s32[]{:S(2)}) async-start(), calls=%async_computation.15 | async-start | bytes 2359296 | tf_op jit(solution)/shard_map/all_gather | solution.py:437
  72.5 12.5 copy-start.65
  77.8 39.5 %copy-start.67 = (bf16[16,8,128]{2,1,0:T(8,128)(2,1)}, bf16[16,8,128]{2,1,0:T(8,128)(2,1)S(1)}, u32[]{:S(2)}) copy-start(bf16[16,8,128]{2,1,0:T(8,128)(2,1)S(1)} %reshape.557) | copy-start | bytes 98308
  84.9 32.3 %copy-start.55 = (f32[8,128,16]{1,2,0:T(8,128)}, f32[8,128,16]{1,2,0:T(8,128)S(1)}, u32[]{:S(2)}) copy-start(f32[8,128,16]{1,2,0:T(8,128)S(1)} %get-tuple-element.1211) | copy-start | bytes 196612
  87.2 347.9 %all-gather.30.cloned.1.call-start = ((), (), s32[]{:S(2)}) async-start(), calls=%async_computation.16 | async-start | bytes 2359296 | tf_op jit(solution)/shard_map/all_gather | solution.py:438
  183.8 5.7 copy-start.62
  183.8 5.7 copy-start.69
  309.2 6.8 copy-start.3
  316.1 10.7 copy-start.54
  318.4 25.8 %copy-start.15 = (f32[128,1024]{1,0:T(8,128)}, f32[128,1024]{1,0:T(8,128)S(1)}, u32[]{:S(2)}) copy-start(f32[128,1024]{1,0:T(8,128)S(1)} %get-tuple-element.1215) | copy-start | bytes 1572868
  318.4 8.4 copy-start.78
  319.1 13.9 copy-start.48
  333.0 6.8 copy-start.1
  333.0 6.8 copy-start.79
  350.1 240.3 %reduce-scatter.10.cloned.1.call-start = ((), (), s32[]{:S(2)}) async-start(), calls=%async_computation.17 | async-start | bytes 4718592 | tf_op jit(solution)/shard_map/reduce_scatter | solution.py:480
  379.0 238.4 %reduce-scatter.8.cloned.1.call-start = ((), (), s32[]{:S(2)}) async-start(), calls=%async_computation.14 | async-start | bytes 4718592 | tf_op jit(solution)/shard_map/reduce_scatter | solution.py:479
  379.8 271.3 %reduce-scatter.14.cloned.1.call-start = ((), (), s32[]{:S(2)}) async-start(), calls=%async_computation.19 | async-start | bytes 2621440 | tf_op jit(solution)/shard_map/reduce_scatter | solution.py:509
  382.4 302.9 %reduce-scatter.16.cloned.1.call-start = ((), (), s32[]{:S(2)}) async-start(), calls=%async_computation.20 | async-start | bytes 2621440 | tf_op jit(solution)/shard_map/reduce_scatter | solution.py:512
  401.5 316.3 %all-reduce.9.cloned.1.call-start = ((), (), s32[]{:S(2)}) async-start(), calls=%async_computation.23 | async-start | bytes 139264
  442.7 135.8 %copy-start.61 = (bf16[8,8,8,128]{3,2,1,0:T(8,128)(2,1)S(1)}, bf16[8,8,8,128]{3,2,1,0:T(8,128)(2,1)}, u32[]{:S(2)}) copy-start(bf16[8,8,8,128]{3,2,1,0:T(8,128)(2,1)} %get-tuple-element.1193) | copy-start | bytes 393220
  576.4 6.8 copy-start.5
  576.4 6.8 copy-start.34
  576.4 6.8 copy-start.84
  576.4 8.1 copy-start.6
  576.4 8.1 copy-start.85
  578.5 7.3 copy-start.35
  590.4 28.3 %copy-start.50 = (bf16[128,8,128]{0,2,1:T(8,128)(2,1)S(1)}, bf16[128,8,128]{0,2,1:T(8,128)(2,1)}, u32[]{:S(2)}) copy-start(bf16[128,8,128]{0,2,1:T(8,128)(2,1)} %copy.194) | copy-start | bytes 786436
  625.5 152.1 %reduce-scatter.20.cloned.1.call-start = ((), (), s32[]{:S(2)}) async-start(), calls=%async_computation.22 | async-start | bytes 7208960 | tf_op jit(solution)/shard_map/reduce_scatter | solution.py:518
  629.8 208.6 %reduce-scatter.12.cloned.1.call-start = ((), (), s32[]{:S(2)}) async-start(), calls=%async_computation.18 | async-start | bytes 7864320 | tf_op jit(solution)/shard_map/reduce_scatter | solution.py:506
  634.6 298.6 %reduce-scatter.18.cloned.1.call-start = ((), (), s32[]{:S(2)}) async-start(), calls=%async_computation.21 | async-start | bytes 14417920 | tf_op jit(solution)/shard_map/reduce_scatter | solution.py:515
  645.8 39.4 %copy-start.22 = (f32[128,1024]{1,0:T(8,128)S(1)}, f32[128,1024]{1,0:T(8,128)}, u32[]{:S(2)}) copy-start(f32[128,1024]{1,0:T(8,128)} %copy-done.20) | copy-start | bytes 1572868
  651.1 282.2 %copy-start.58 = (bf16[256,1024]{1,0:T(8,128)(2,1)S(1)}, bf16[256,1024]{1,0:T(8,128)(2,1)}, u32[]{:S(2)}) copy-start(bf16[256,1024]{1,0:T(8,128)(2,1)} %reduce-scatter.14.cloned.1.call-done) | copy-start | bytes 1572868
  685.2 248.0 %copy-start.59 = (bf16[256,1024]{1,0:T(8,128)(2,1)S(1)}, bf16[256,1024]{1,0:T(8,128)(2,1)}, u32[]{:S(2)}) copy-start(bf16[256,1024]{1,0:T(8,128)(2,1)} %reduce-scatter.16.cloned.1.call-done) | copy-start | bytes 1572868
  (103 other events, 264.2 us)
Sparse Core Ops, SparseCore 0:
  9.6 49.0 all-gather.13
  64.0 49.2 all-gather.15
  116.0 47.7 all-gather.17
  165.3 21.0 all-gather.19
  187.8 22.5 all-gather.21
  211.8 76.1 all-gather.23
  289.6 43.3 all-gather.25
  335.7 49.4 all-gather.27
  387.3 47.7 all-gather.29
  438.6 86.4 reduce-scatter.9
  529.7 87.6 reduce-scatter.7
  619.8 31.2 reduce-scatter.13
  653.8 31.3 reduce-scatter.15
  688.2 29.5 all-reduce.8
  720.9 56.7 reduce-scatter.19
  780.1 58.3 reduce-scatter.11
  841.1 92.1 reduce-scatter.17
where the time goes:
time: 1490 us; the launch traced here: 1480 us
  blocking collectives  559 us (38%)
  waiting for transfers between devices  466 us (31%)
  matrix products  179 us (12%)
  local copies, waits for them, and re-layouts  125 us (8%)
  other arithmetic  93.6 us (6%)
  loops' own time  37.5 us (3%)
  between operations  16.7 us (1%)
    psum x1, blocking collectives, on_device(): lax.psum((shares[0], shares[1], shares[2], shares[3], shares[4], shares[5...  537 us
    reduce_scatter x1, waiting for transfers between devices, on_device(): lax.psum_scatter(local_grads[3].astype(jnp.bfloat16), 'fsdp', scatter_dim...  94.8 us
    reduce_scatter x1, waiting for transfers between devices, on_device(): lax.psum_scatter(local_grads[0].astype(jnp.bfloat16), 'fsdp', scatter_dim...  60.8 us
    reduce_scatter x1, waiting for transfers between devices, on_device(): lax.psum_scatter(local_grads[4].astype(jnp.bfloat16), 'fsdp', scatter_dim...  58.4 us
    dynamic_slice x64, local copies, waits for them, and re-layouts, states_before(): lax.scan(states_one_group, (zero_state, zero_state, zero_state), (key_gro...  49.5 us
    select_n x16, other arithmetic, adjoints_one_group(): out_late = jnp.where(group_index + 1 == late_end, adjoint, out_late)  47.5 us
    all_gather x1, waiting for transfers between devices, on_device(): lax.all_gather(value_flat, 'ctx', axis=0, tiled=True)  46.6 us
    all_gather x1, waiting for transfers between devices, on_device(): lax.all_gather(w_qkv, 'fsdp', axis=0, tiled=True)  43 us
  transfers between devices with their start and end apart: 17, of which 12 were waited for; matrix products, arithmetic and copies ran while one was open for 25% of the time, Pallas kernels for 0%

commit v1 on v0

--- a/solution.py
+++ b/solution.py
@@ -1,6 +1,9 @@
 import jax
 import jax.numpy as jnp
+import numpy as np
 from jax import lax
+from jax.experimental import pallas as pl
+from jax.experimental.pallas import tpu as pltpu
 from jax.sharding import PartitionSpec as P
 
 HEADS = 8
@@ -560,6 +563,790 @@
     )
 
 
+PERSIST = 16
+PLANES = 4
+HIDDEN_PAD = 384
+Z_HIDDEN = HIDDEN_PAD // PLANES
+VMEM_BYTES = 56 * 1024 * 1024
+
+
+def head_of(x, f, k):
+    return 2 * (f ^ (k & 3)) + (x ^ (k >> 2))
+
+
+def linear(z, x, f):
+    return (2 * z + x) * 4 + f
+
+
+def shift(value, move):
+    pairs = []
+    for z in range(4):
+        for x in range(2):
+            for f in range(4):
+                pairs.append((linear(z, x, f), linear(*move(z, x, f))))
+    return lax.ppermute(value, ("ctx", "fsdp"), pairs)
+
+
+def to_plane(value):
+    return shift(value, lambda z, x, f: (f, x, z))
+
+
+def flip(value, dx, df):
+    return shift(value, lambda z, x, f: (z, x ^ dx, f ^ df))
+
+
+def flip_z(value, dz):
+    return shift(value, lambda z, x, f: (z ^ dz, x, f))
+
+
+def gather_plane(block):
+    near = [block, flip(block, 0, 2), flip(block, 1, 0), flip(block, 1, 2)]
+    far = [flip(b, 0, 1) for b in near]
+    return [near[0], far[0], near[1], far[1], near[2], far[2], near[3], far[3]]
+
+
+def dot_nn(a, b):
+    return lax.dot_general(a, b, (((1,), (0,)), ((), ())), preferred_element_type=jnp.float32)
+
+
+def dot_nt(a, b):
+    return lax.dot_general(a, b, (((1,), (1,)), ((), ())), preferred_element_type=jnp.float32)
+
+
+def dot_tn(a, b):
+    return lax.dot_general(a, b, (((0,), (0,)), ((), ())), preferred_element_type=jnp.float32)
+
+
+def split_two(value):
+    high = value.astype(jnp.bfloat16)
+    return high, (value - high.astype(jnp.float32)).astype(jnp.bfloat16)
+
+
+def product_three(a, b_high, b_low):
+    a_high, a_low = split_two(a)
+    return dot_nn(a_high, b_high) + dot_nn(a_low, b_high) + dot_nn(a_high, b_low)
+
+
+def vspec():
+    return pl.BlockSpec(memory_space=pltpu.VMEM)
+
+
+def sspec():
+    return pl.BlockSpec(memory_space=pltpu.SMEM)
+
+
+def call(kernel, smem, operands, outs, scratch=(), flops=0, name=None):
+    moved = sum(o.size * o.dtype.itemsize for o in operands) + sum(
+        int(np.prod(s)) * jnp.dtype(d).itemsize for s, d in outs
+    )
+    return pl.pallas_call(
+        kernel,
+        out_shape=[jax.ShapeDtypeStruct(s, d) for s, d in outs],
+        in_specs=[sspec()] * len(smem) + [vspec()] * len(operands),
+        out_specs=[vspec()] * len(outs),
+        scratch_shapes=[pltpu.VMEM(s, d) for s, d in scratch],
+        compiler_params=pltpu.CompilerParams(vmem_limit_bytes=VMEM_BYTES),
+        cost_estimate=pl.CostEstimate(flops=flops, bytes_accessed=moved, transcendentals=0),
+        name=name,
+    )(*smem, *operands)
+
+
+def pack_qkvg_kernel(idx, wq, wg, o0, o1, o2, o3):
+    x, f = idx[1], idx[2]
+    for j, out in enumerate((o0, o1, o2, o3)):
+        head = 2 * (f ^ j) + x
+        start = pl.multiple_of(head * 128, 128)
+        for part in range(3):
+            out[:, part * 128 : part * 128 + 128] = wq[
+                :, pl.ds(pl.multiple_of(part * 1024 + start, 128), 128)
+            ]
+        out[:, 384:512] = wg[:, pl.ds(start, 128)]
+
+
+def pack_gu_kernel(idx, wgu, o0, o1, o2, o3):
+    x, f = idx[1], idx[2]
+    width = FF // 8
+    pad = jnp.zeros((wgu.shape[0], HIDDEN_PAD - width), jnp.bfloat16)
+    for j, out in enumerate((o0, o1, o2, o3)):
+        head = 2 * (f ^ j) + x
+        for h in range(8):
+
+            @pl.when(head == h)
+            def _():
+                for part in range(2):
+                    first = part * FF + h * width
+                    at = part * HIDDEN_PAD
+                    out[:, at : at + HIDDEN_PAD] = jnp.concatenate(
+                        [wgu[:, first : first + width], pad], axis=1
+                    )
+
+
+def mixer_forward_kernel(idx, rates, ints, *refs):
+    blocks = refs[0:8]
+    parts = refs[8:12]
+    gain, wo, pk, pv = refs[12:16]
+    send, keep, normed, w_full, qkv, gate, att, rec, probs, pprobs, states, mixed = refs[16:28]
+    x, f = idx[1], idx[2]
+    head = 2 * f + x
+    scale = HEAD_WIDTH_SIZE ** (-0.5)
+    gain_row = gain[...]
+    for j in range(4):
+        w_full[pl.ds(pl.multiple_of((f ^ j) * 256, 256), 256), :] = parts[j][...]
+    for k in range(8):
+        values = blocks[k][...].astype(jnp.float32)
+        normed_block = (values * rms_scale(values) * gain_row).astype(jnp.bfloat16)
+        hk = head_of(x, f, k)
+        normed[pl.ds(pl.multiple_of(hk * 64, 64), 64), :] = normed_block[:64]
+        normed[pl.ds(pl.multiple_of((15 - hk) * 64, 64), 64), :] = normed_block[64:]
+    for t in range(4):
+        rows = slice(t * 256, t * 256 + 256)
+        product = dot_nn(normed[rows, :], w_full[...])
+        qkv[rows, :] = product[:, :384].astype(jnp.bfloat16)
+        gate[rows, :] = jax.nn.sigmoid(product[:, 384:])
+    state = jnp.zeros((128, 128), jnp.float32)
+    moment = jnp.zeros((128, 128), jnp.float32)
+    for t in range(8):
+        rows = slice(t * 128, t * 128 + 128)
+        width = (t + 1) * 128
+        query = qkv[rows, 0:128]
+        scores = dot_nt(query, qkv[0:width, 128:256]) * scale
+        row_seg = jnp.transpose(jnp.broadcast_to(ints[t : t + 1, :], (128, 128)))[:, 0:1]
+        col_seg = jnp.concatenate([ints[u : u + 1, :] for u in range(t + 1)], axis=1)
+        row_pos = lax.broadcasted_iota(jnp.int32, (128, width), 0) + t * 128
+        col_pos = lax.broadcasted_iota(jnp.int32, (128, width), 1)
+        allowed = (row_seg == col_seg) & (col_pos <= row_pos)
+        scores = jnp.where(allowed, scores, masked_score)
+        pscores = dot_nt(query, pk[...]) * scale
+        top = jnp.maximum(
+            jnp.max(scores, axis=-1, keepdims=True), jnp.max(pscores, axis=-1, keepdims=True)
+        )
+        weights = jnp.exp(scores - top)
+        pweights = jnp.exp(pscores - top)
+        inverse = 1.0 / (
+            jnp.sum(weights, axis=-1, keepdims=True) + jnp.sum(pweights, axis=-1, keepdims=True)
+        )
+        weights = (weights * inverse).astype(jnp.bfloat16)
+        pweights = (pweights * inverse).astype(jnp.bfloat16)
+        probs[rows, 0:width] = weights
+        pprobs[rows, :] = pweights
+        att[rows, :] = dot_nn(weights, qkv[0:width, 256:384]) + dot_nn(pweights, pv[...])
+        for c in (2 * t, 2 * t + 1):
+            grows = slice(c * 64, c * 64 + 64)
+            alpha = rates[0, c * 8 + head]
+            theta = rates[1, c * 8 + head]
+            high, low = split_two(state)
+            states[c] = high
+            recalled = dot_nt(qkv[grows, 0:128], high) + dot_nt(qkv[grows, 0:128], low)
+            rec[grows, :] = recalled * scale
+            both = dot_tn(qkv[grows, 128:384], qkv[grows, 128:256])
+            gram_high, gram_low = split_two(both[:128] * (theta / HEAD_WIDTH_SIZE))
+            change = (
+                dot_nn(high, gram_high) + dot_nn(low, gram_high) + dot_nn(high, gram_low)
+            ) - both[128:] * (theta * scale)
+            moment = momentum * moment - change
+            state = (1.0 - alpha) * state + moment
+        mixed[rows, :] = (att[rows, :] + gate[rows, :] * rec[rows, :]).astype(jnp.bfloat16)
+    for k in range(8):
+        hk = head_of(x, f, k)
+        piece = jnp.concatenate(
+            [
+                mixed[pl.ds(pl.multiple_of(hk * 64, 64), 64), :],
+                mixed[pl.ds(pl.multiple_of((15 - hk) * 64, 64), 64), :],
+            ],
+            axis=0,
+        )
+        out = send if k & 1 else keep
+        out[k >> 1] = dot_nn(piece, wo[...]).astype(jnp.bfloat16)
+
+
+def mixer_backward_kernel(idx, rates, *refs):
+    blocks = refs[0:8]
+    wo, w_full, qkv, gate, att, rec, probs, pprobs, states, pk, pv = refs[8:19]
+    send, keep, dqkvg, branch, gpk, gpv = refs[19:25]
+    gm, dy, delta, ds, dk, dv, dsp = refs[25:32]
+    x, f = idx[1], idx[2]
+    head = 2 * f + x
+    scale = HEAD_WIDTH_SIZE ** (-0.5)
+    for k in range(8):
+        hk = head_of(x, f, k)
+        early = pl.ds(pl.multiple_of(hk * 64, 64), 64)
+        late = pl.ds(pl.multiple_of((15 - hk) * 64, 64), 64)
+        block = blocks[k][...]
+        grad = dot_nt(block, wo[...]).astype(jnp.bfloat16)
+        gm[early, :] = grad[:64]
+        gm[late, :] = grad[64:]
+        branch[early, :] = block[:64]
+        branch[late, :] = block[64:]
+    for t in range(8):
+        rows = slice(t * 128, t * 128 + 128)
+        width = (t + 1) * 128
+        grad_low = gm[rows, :]
+        grad = grad_low.astype(jnp.float32)
+        opened = gate[rows, :]
+        dqkvg[rows, 384:512] = (grad * rec[rows, :] * opened * (1.0 - opened)).astype(jnp.bfloat16)
+        dy[rows, :] = (grad * opened).astype(jnp.bfloat16)
+        row_delta = jnp.sum(grad * att[rows, :], axis=-1, keepdims=True)
+        grad_probs = dot_nt(grad_low, qkv[0:width, 256:384])
+        ds_tile = (probs[rows, 0:width].astype(jnp.float32) * (grad_probs - row_delta)).astype(
+            jnp.bfloat16
+        )
+        ds[rows, 0:width] = ds_tile
+        grad_pprobs = dot_nt(grad_low, pv[...])
+        dsp_tile = (pprobs[rows, :].astype(jnp.float32) * (grad_pprobs - row_delta)).astype(
+            jnp.bfloat16
+        )
+        dsp[rows, :] = dsp_tile
+        delta[rows, :] = (
+            dot_nn(ds_tile, qkv[0:width, 128:256]) + dot_nn(dsp_tile, pk[...])
+        ) * scale
+    gpk[...] = dot_tn(dsp[...], qkv[:, 0:128]) * scale
+    gpv[...] = dot_tn(pprobs[...], gm[...])
+    grad_state = jnp.zeros((128, 128), jnp.float32)
+    grad_moment = jnp.zeros((128, 128), jnp.float32)
+    for t in range(7, -1, -1):
+        rows = slice(t * 128, t * 128 + 128)
+        rest = slice(t * 128, 1024)
+        dk[rows, :] = dot_tn(ds[rest, rows], qkv[rest, 0:128]) * scale
+        dv[rows, :] = dot_tn(probs[rest, rows], gm[rest, :])
+        for c in (2 * t + 1, 2 * t):
+            grows = slice(c * 64, c * 64 + 64)
+            alpha = rates[0, c * 8 + head]
+            theta = rates[1, c * 8 + head]
+            query, key, value = qkv[grows, 0:128], qkv[grows, 128:256], qkv[grows, 256:384]
+            dy_rows = dy[grows, :]
+            state = states[c]
+            summed = grad_state + grad_moment
+            high, low = split_two(summed)
+            key_summed = dot_nt(key, high) * scale
+            error = value.astype(jnp.float32) - dot_nt(key, state) * scale
+            grad_value = dv[grows, :] + theta * key_summed
+            grad_key = dk[grows, :] + (theta * scale) * (
+                dot_nn(error.astype(jnp.bfloat16), high)
+                - dot_nn(key_summed.astype(jnp.bfloat16), state)
+            )
+            grad_query = delta[grows, :] + dot_nn(dy_rows, state) * scale
+            dqkvg[grows, 0:128] = grad_query.astype(jnp.bfloat16)
+            dqkvg[grows, 128:256] = grad_key.astype(jnp.bfloat16)
+            dqkvg[grows, 256:384] = grad_value.astype(jnp.bfloat16)
+            gram_high, gram_low = split_two(dot_tn(key, key) * (theta / HEAD_WIDTH_SIZE))
+            product = dot_nn(high, gram_high) + dot_nn(low, gram_high) + dot_nn(high, gram_low)
+            grad_state = (
+                dot_tn(dy_rows, query) * scale + (1.0 - alpha) * grad_state - product
+            )
+            grad_moment = momentum * summed
+    for k in range(8):
+        hk = head_of(x, f, k)
+        piece = jnp.concatenate(
+            [
+                dqkvg[pl.ds(pl.multiple_of(hk * 64, 64), 64), :],
+                dqkvg[pl.ds(pl.multiple_of((15 - hk) * 64, 64), 64), :],
+            ],
+            axis=0,
+        )
+        out = send if k & 1 else keep
+        out[k >> 1] = dot_nt(piece, w_full[...]).astype(jnp.bfloat16)
+
+
+def mixer_weights_kernel(idx, normed, dqkvg, mixed, branch, *refs):
+    outs, outs_o = refs[0:4], refs[4:8]
+    total, total_o = refs[8:10]
+    z, f = idx[0], idx[2]
+    for t in range(4):
+        total[...] = dot_tn(normed[:, t * 256 : t * 256 + 256], dqkvg[...])
+        for j in range(4):
+            outs[j][t ^ f] = total[pl.ds(pl.multiple_of((z ^ j) * 64, 64), 64), :].astype(
+                jnp.bfloat16
+            )
+    total_o[...] = dot_tn(mixed[...], branch[...])
+    for j in range(4):
+        outs_o[j][...] = total_o[pl.ds(pl.multiple_of((z ^ j) * 32, 32), 32), :].astype(
+            jnp.bfloat16
+        )
+
+
+def feed_kernel(idx, *refs):
+    blocks, cots, parts = refs[0:8], refs[8:16], refs[16:20]
+    wd = refs[20]
+    send_g, keep_g, send_d, keep_d, active, dgu, feeds, cot_all = refs[21:29]
+    w_full = refs[29]
+    f = idx[2]
+    for j in range(4):
+        w_full[pl.ds(pl.multiple_of((f ^ j) * 256, 256), 256), :] = parts[j][...]
+    for k in range(4):
+        rows = slice(k * 256, k * 256 + 256)
+        feed = jnp.concatenate([blocks[2 * k][...], blocks[2 * k + 1][...]], axis=0)
+        cot = jnp.concatenate([cots[2 * k][...], cots[2 * k + 1][...]], axis=0)
+        feeds[rows, :] = feed
+        cot_all[rows, :] = cot
+        gate_up = dot_nn(feed, w_full[...])
+        g, u = gate_up[:, :HIDDEN_PAD], gate_up[:, HIDDEN_PAD:]
+        sigma = jax.nn.sigmoid(g)
+        active_low = (g * sigma * u).astype(jnp.bfloat16)
+        active[rows, :] = active_low
+        grad_active = dot_nt(cot, wd[...])
+        grad_g = (grad_active * u * sigma * (1.0 + g * (1.0 - sigma))).astype(jnp.bfloat16)
+        grad_u = (grad_active * g * sigma).astype(jnp.bfloat16)
+        grad_low = jnp.concatenate([grad_g, grad_u], axis=1)
+        dgu[rows, :] = grad_low
+        grad_feed = dot_nt(grad_low, w_full[...]).astype(jnp.bfloat16)
+        keep_g[k] = grad_feed[:128]
+        send_g[k] = grad_feed[128:]
+        down = dot_nn(active_low, wd[...]).astype(jnp.bfloat16)
+        keep_d[k] = down[:128]
+        send_d[k] = down[128:]
+
+
+def feed_weights_kernel(idx, feeds, dgu, active, cots, *refs):
+    outs, outs_d = refs[0:4], refs[4:8]
+    total, total_d = refs[8:10]
+    z, f = idx[0], idx[2]
+    for t in range(4):
+        total[...] = dot_tn(feeds[:, t * 256 : t * 256 + 256], dgu[...])
+        for j in range(4):
+            outs[j][t ^ f] = total[pl.ds(pl.multiple_of((z ^ j) * 64, 64), 64), :].astype(
+                jnp.bfloat16
+            )
+    total_d[...] = dot_tn(active[...], cots[...])
+    for j in range(4):
+        first = pl.multiple_of((z ^ j) * Z_HIDDEN, 32)
+        outs_d[j][...] = total_d[pl.ds(first, Z_HIDDEN), :].astype(jnp.bfloat16)
+
+
+def add_kernel(keep, received, s0, s1, s2, s3):
+    s0[...] = keep[0].astype(jnp.float32) + received[0].astype(jnp.float32)
+    for k, out in ((1, s1), (2, s2), (3, s3)):
+        out[...] = (keep[k].astype(jnp.float32) + received[k].astype(jnp.float32)).astype(
+            jnp.bfloat16
+        )
+
+
+def total_of(refs):
+    return (
+        refs[0][...]
+        + refs[1][...].astype(jnp.float32)
+        + refs[2][...].astype(jnp.float32)
+        + refs[3][...].astype(jnp.float32)
+    )
+
+
+def residual_kernel(x, gain, s0, r1, r2, r3, residual, feed):
+    values = x[...].astype(jnp.float32) + total_of((s0, r1, r2, r3))
+    residual[...] = values
+    feed[...] = (values * rms_scale(values) * gain[...]).astype(jnp.bfloat16)
+
+
+def norm_grad(values, gain, grad):
+    inv = rms_scale(values)
+    scaled = grad * gain
+    return inv * scaled - values * (inv * inv * inv) * jnp.mean(
+        scaled * values, axis=-1, keepdims=True
+    )
+
+
+def branch_kernel(residual, gain, cot, s0, r1, r2, r3, grad_residual, branch):
+    grad = total_of((s0, r1, r2, r3))
+    total = cot[...].astype(jnp.float32) + norm_grad(residual[...], gain[...], grad)
+    grad_residual[...] = total
+    branch[...] = total.astype(jnp.bfloat16)
+
+
+def tokens_kernel(x, gain, grad_residual, s0, r1, r2, r3, out):
+    grad = total_of((s0, r1, r2, r3))
+    values = x[...].astype(jnp.float32)
+    out[...] = (grad_residual[...] + norm_grad(values, gain[...], grad)).astype(jnp.bfloat16)
+
+
+def output_kernel(residual, s0, r1, r2, r3, out):
+    out[...] = (residual[...] + total_of((s0, r1, r2, r3))).astype(jnp.bfloat16)
+
+
+def sum_parts_kernel(*refs):
+    wide, rows, outs, out_rows = refs[0:4], refs[4:8], refs[8:12], refs[12]
+    total = wide[0][...].astype(jnp.float32)
+    for part in wide[1:]:
+        total = total + part[...].astype(jnp.float32)
+    for j in range(4):
+        outs[j][...] = total[j].astype(jnp.bfloat16)
+    total = rows[0][...].astype(jnp.float32)
+    for part in rows[1:]:
+        total = total + part[...].astype(jnp.float32)
+    out_rows[...] = total.astype(jnp.bfloat16)
+
+
+def join_kernel(*refs):
+    parts, rows, out = refs[0:4], refs[4], refs[5]
+    width = out.shape[1]
+    for j in range(4):
+        out[j * 64 : j * 64 + 64, :] = parts[j][...]
+    count = rows.shape[0]
+    out[256 : 256 + count, :] = rows[:, 0:width]
+    left = 1024 - width
+    if left == width:
+        out[256 + count : 256 + 2 * count, :] = rows[:, width:1024]
+    else:
+        third = count * left // width
+        for i in range(count // third):
+            out[256 + count : 256 + count + third, i * left : (i + 1) * left] = rows[
+                i * third : (i + 1) * third, width:1024
+            ]
+
+
+def row_sums(products, out):
+    out[...] = jnp.sum(jnp.transpose(products), axis=0, keepdims=True)
+
+
+def feed_unpack_kernel(idx, *refs):
+    parts = refs[0:8]
+    wgu, gain = refs[8:10]
+    out_gu, out_down, out_gain = refs[10:13]
+    z, x, f = idx[0], idx[1], idx[2]
+    width = FF // 8
+    for j in range(4):
+        for dx in range(2):
+            part = parts[2 * j + dx]
+            zj, xj = z ^ j, x ^ dx
+            rows = pl.ds(pl.multiple_of(zj * 64, 64), 64)
+            for jf in range(4):
+                head = 2 * (f ^ jf) + xj
+                for h in range(8):
+
+                    @pl.when(head == h)
+                    def _():
+                        for side in range(2):
+                            first = side * FF + h * width
+                            out_gu[rows, first : first + width] = part[
+                                jf * 64 : jf * 64 + 64, side * HIDDEN_PAD : side * HIDDEN_PAD + width
+                            ].astype(jnp.float32)
+
+            lower = part[256:352, :].astype(jnp.float32)
+            upper = part[352:384, :].astype(jnp.float32)
+            valid = 64
+            base = pl.multiple_of(xj * 352 + zj * Z_HIDDEN, 32)
+
+            def put(first, count):
+                at = pl.ds(pl.multiple_of(base + first, 32), count)
+                out_down[at, 0:768] = lower[first : first + count]
+                for i in range(first // 32, (first + count) // 32):
+                    spot = pl.ds(pl.multiple_of(base + 32 * i, 32), 32)
+                    out_down[spot, 768:1024] = upper[:, i * 256 : (i + 1) * 256]
+
+            put(0, valid)
+
+            @pl.when(zj < 3)
+            def _():
+                put(64, 32)
+
+    sums = jnp.zeros((256, 128), jnp.float32)
+    for t in range(2 * FF // 128):
+        cols = slice(t * 128, t * 128 + 128)
+        sums = sums + out_gu[:, cols] * wgu[:, cols].astype(jnp.float32)
+    row_sums(sums, out_gain)
+    out_gain[...] = out_gain[...] / gain[...].astype(jnp.float32)
+
+
+def mixer_unpack_kernel(idx, *refs):
+    parts = refs[0:8]
+    wq, wg, gain = refs[8:11]
+    out_qkv, out_gate, out_out, out_gain = refs[11:15]
+    z, x, f = idx[0], idx[1], idx[2]
+    for j in range(4):
+        for dx in range(2):
+            part = parts[2 * j + dx]
+            zj, xj = z ^ j, x ^ dx
+            rows = pl.ds(pl.multiple_of(zj * 64, 64), 64)
+            for jf in range(4):
+                head = 2 * (f ^ jf) + xj
+                start = pl.multiple_of(head * 128, 128)
+                for side in range(3):
+                    out_qkv[rows, pl.ds(pl.multiple_of(side * 1024 + start, 128), 128)] = part[
+                        jf * 64 : jf * 64 + 64, side * 128 : side * 128 + 128
+                    ].astype(jnp.float32)
+                out_gate[rows, pl.ds(start, 128)] = part[jf * 64 : jf * 64 + 64, 384:512].astype(
+                    jnp.float32
+                )
+            spot = pl.ds(pl.multiple_of(xj * 128 + zj * 32, 32), 32)
+            out_out[spot, 0:512] = part[256:288, :].astype(jnp.float32)
+            out_out[spot, 512:1024] = part[288:320, :].astype(jnp.float32)
+    sums = jnp.zeros((256, 128), jnp.float32)
+    for t in range(24):
+        cols = slice(t * 128, t * 128 + 128)
+        sums = sums + out_qkv[:, cols] * wq[:, cols].astype(jnp.float32)
+    for t in range(8):
+        cols = slice(t * 128, t * 128 + 128)
+        sums = sums + out_gate[:, cols] * wg[:, cols].astype(jnp.float32)
+    row_sums(sums, out_gain)
+    out_gain[...] = out_gain[...] / gain[...].astype(jnp.float32)
+
+
+def scatter_plane(keep, send):
+    received = flip(send, 0, 1)
+    block = (128, 1024)
+    s0, s1, s2, s3 = call(
+        add_kernel,
+        (),
+        (keep, received),
+        [(block, jnp.float32)] + [(block, jnp.bfloat16)] * 3,
+        name="core_sum",
+    )
+    return s0, flip(s1, 0, 2), flip(s2, 1, 0), flip(s3, 1, 2)
+
+
+def reduce_parts(wide, rows, width, name):
+    wide = [wide[0]] + [flip_z(wide[j], j) for j in range(1, 4)]
+    rows = [rows[0]] + [flip_z(rows[j], j) for j in range(1, 4)]
+    count = rows[0].shape[0]
+    *parts, row_total = call(
+        sum_parts_kernel,
+        (),
+        (*wide, *rows),
+        [((64, width), jnp.bfloat16)] * 4 + [((count, 1024), jnp.bfloat16)],
+        name=name + "_sum",
+    )
+    parts = [parts[0]] + [flip(parts[j], 0, j) for j in range(1, 4)]
+    extra = count * 1024 // width
+    (joined,) = call(
+        join_kernel,
+        (),
+        (*parts, row_total),
+        [((256 + extra, width), jnp.bfloat16)],
+        name=name + "_join",
+    )
+    near = [joined] + [flip_z(joined, j) for j in range(1, 4)]
+    result = []
+    for piece in near:
+        result += [piece, flip(piece, 1, 0)]
+    return result
+
+
+def in_planes(
+    tokens,
+    cotangent,
+    segments,
+    decay_index,
+    step_index,
+    w_qkv,
+    w_gate,
+    w_out,
+    w_gu,
+    w_down,
+    persist_keys,
+    persist_values,
+    norm_gain,
+    ffn_gain,
+):
+    bf16, f32 = jnp.bfloat16, jnp.float32
+    ctx = lax.axis_index("ctx")
+    f = lax.axis_index("fsdp")
+    z, x = ctx // 2, ctx % 2
+    head = 2 * f + x
+    idx = jnp.stack([z, x, f, head]).astype(jnp.int32)
+
+    own = to_plane(tokens[0])
+    ints = to_plane(
+        jnp.concatenate([segments[0], decay_index[0].reshape(-1), step_index[0].reshape(-1)]).reshape(
+            10, 128
+        )
+    )
+    small = jnp.concatenate(
+        [
+            persist_keys,
+            persist_values,
+            jnp.concatenate([norm_gain, ffn_gain, norm_gain, ffn_gain]).reshape(1, 1024),
+            jnp.zeros((7, 1024), bf16),
+        ],
+        axis=0,
+    )
+    wq_parts = call(
+        pack_qkvg_kernel, (idx,), (w_qkv, w_gate), [((256, 512), bf16)] * 4, name="pack_qkvg"
+    )
+    wq_parts = [wq_parts[0]] + [flip(wq_parts[j], 0, j) for j in range(1, 4)]
+    smalls = jnp.stack([small] + [flip(small, 0, j) for j in range(1, 4)])
+    blocks = gather_plane(own)
+    own_cot = to_plane(cotangent[0])
+    gu_parts = call(pack_gu_kernel, (idx,), (w_gu,), [((256, 768), bf16)] * 4, name="pack_gu")
+    gu_parts = [gu_parts[0]] + [flip(gu_parts[j], 0, j) for j in range(1, 4)]
+    cots = gather_plane(own_cot)
+
+    smalls = jnp.stack(
+        [lax.dynamic_index_in_dim(smalls, f ^ j, 0, keepdims=False) for j in range(4)]
+    )
+    gain_one = smalls[:, 8, 0:256].reshape(1, 1024).astype(f32)
+    gain_two = smalls[:, 8, 256:512].reshape(1, 1024).astype(f32)
+    pk = lax.dynamic_slice_in_dim(smalls[:, 0:4].reshape(16, 1024), head * 128, 128, 1)
+    pv = lax.dynamic_slice_in_dim(smalls[:, 4:8].reshape(16, 1024), head * 128, 128, 1)
+    rates = jnp.stack(
+        [0.6 * jnp.exp2(-ints[8].astype(f32)), 0.1 * jnp.exp2(-ints[9].astype(f32))]
+    )
+    wo = lax.dynamic_slice_in_dim(w_out, x * 128, 128, 0)
+    wd = jnp.pad(
+        lax.dynamic_slice_in_dim(w_down, x * 352, 352, 0), ((0, HIDDEN_PAD - 352), (0, 0))
+    )
+
+    quad = ((4, 128, 1024), bf16)
+    (
+        send,
+        keep,
+        normed,
+        w_full,
+        qkv,
+        gate,
+        att,
+        rec,
+        probs,
+        pprobs,
+        states,
+        mixed,
+    ) = call(
+        mixer_forward_kernel,
+        (idx, rates),
+        (ints, *blocks, *wq_parts, gain_one, wo, pk, pv),
+        [
+            quad,
+            quad,
+            ((1024, 1024), bf16),
+            ((1024, 512), bf16),
+            ((1024, 384), bf16),
+            ((1024, 128), f32),
+            ((1024, 128), f32),
+            ((1024, 128), f32),
+            ((1024, 1024), bf16),
+            ((1024, 16), bf16),
+            ((16, 128, 128), bf16),
+            ((1024, 128), bf16),
+        ],
+        flops=3 * 10**9,
+        name="mixer_forward",
+    )
+    shares = scatter_plane(keep, send)
+    block = (128, 1024)
+    residual, feed = call(
+        residual_kernel,
+        (),
+        (own, gain_two, *shares),
+        [(block, f32), (block, bf16)],
+        name="residual",
+    )
+    feeds = gather_plane(feed)
+    send_g, keep_g, send_d, keep_d, active, dgu, feed_all, cot_all = call(
+        feed_kernel,
+        (idx,),
+        (*feeds, *cots, *gu_parts, wd),
+        [
+            quad,
+            quad,
+            quad,
+            quad,
+            ((1024, HIDDEN_PAD), bf16),
+            ((1024, 2 * HIDDEN_PAD), bf16),
+            ((1024, 1024), bf16),
+            ((1024, 1024), bf16),
+        ],
+        scratch=[((1024, 2 * HIDDEN_PAD), bf16)],
+        flops=5 * 10**9,
+        name="feed",
+    )
+    shares = scatter_plane(keep_g, send_g)
+    grad_residual, branch = call(
+        branch_kernel,
+        (),
+        (residual, gain_two, own_cot, *shares),
+        [(block, f32), (block, bf16)],
+        name="branch",
+    )
+    branches = gather_plane(branch)
+
+    feed_parts = call(
+        feed_weights_kernel,
+        (idx,),
+        (feed_all, dgu, active, cot_all),
+        [((4, 64, 768), bf16)] * 4 + [((Z_HIDDEN, 1024), bf16)] * 4,
+        scratch=[((256, 768), f32), ((HIDDEN_PAD, 1024), f32)],
+        flops=3 * 10**9,
+        name="feed_weights",
+    )
+    feed_pieces = reduce_parts(feed_parts[0:4], feed_parts[4:8], 768, "feed")
+
+    shares = scatter_plane(keep_d, send_d)
+    (result,) = call(output_kernel, (), (residual, *shares), [(block, bf16)], name="output")
+    result = to_plane(result)
+
+    send, keep, dqkvg, branch_all, gpk, gpv = call(
+        mixer_backward_kernel,
+        (idx, rates),
+        (*branches, wo, w_full, qkv, gate, att, rec, probs, pprobs, states, pk, pv),
+        [
+            quad,
+            quad,
+            ((1024, 512), bf16),
+            ((1024, 1024), bf16),
+            ((16, 128), f32),
+            ((16, 128), f32),
+        ],
+        scratch=[
+            ((1024, 128), bf16),
+            ((1024, 128), bf16),
+            ((1024, 128), f32),
+            ((1024, 1024), bf16),
+            ((1024, 128), f32),
+            ((1024, 128), f32),
+            ((1024, 16), bf16),
+        ],
+        flops=4 * 10**9,
+        name="mixer_backward",
+    )
+    mixer_parts = call(
+        mixer_weights_kernel,
+        (idx,),
+        (normed, dqkvg, mixed, branch_all),
+        [((4, 64, 512), bf16)] * 4 + [((32, 1024), bf16)] * 4,
+        scratch=[((256, 512), f32), ((128, 1024), f32)],
+        flops=2 * 10**9,
+        name="mixer_weights",
+    )
+    shares = scatter_plane(keep, send)
+    mixer_pieces = reduce_parts(mixer_parts[0:4], mixer_parts[4:8], 512, "mixer")
+    (grad_tokens,) = call(
+        tokens_kernel, (), (own, gain_one, grad_residual, *shares), [(block, bf16)], name="tokens"
+    )
+    grad_tokens = to_plane(grad_tokens)
+
+    persist = jnp.concatenate([gpk, gpv], axis=0)
+    persist = lax.dynamic_update_slice_in_dim(
+        jnp.zeros((32, 1024), f32), persist, head * 128, 1
+    )
+    persist = lax.psum(persist, ("ctx", "fsdp"))
+    grad_pk = lax.dynamic_slice_in_dim(persist, f * 4, 4, 0)
+    grad_pv = lax.dynamic_slice_in_dim(persist, 16 + f * 4, 4, 0)
+
+    grad_gu, grad_down, grad_ffn = call(
+        feed_unpack_kernel,
+        (idx,),
+        (*feed_pieces, w_gu, ffn_gain.reshape(1, 256)),
+        [((256, 2 * FF), f32), ((FF // 4, 1024), f32), ((1, 256), f32)],
+        name="feed_unpack",
+    )
+    grad_qkv, grad_gate, grad_out, grad_norm = call(
+        mixer_unpack_kernel,
+        (idx,),
+        (*mixer_pieces, w_qkv, w_gate, norm_gain.reshape(1, 256)),
+        [((256, 3072), f32), ((256, 1024), f32), ((256, 1024), f32), ((1, 256), f32)],
+        name="mixer_unpack",
+    )
+    return (
+        result[None],
+        grad_tokens.astype(f32)[None],
+        grad_qkv,
+        grad_gate,
+        grad_out,
+        grad_gu,
+        grad_down,
+        grad_pk,
+        grad_pv,
+        grad_norm.reshape(256),
+        grad_ffn.reshape(256),
+    )
+
+
 def solution(mesh):
     in_specs = (
         P("fsdp", "ctx", None),
@@ -590,6 +1377,7 @@
         P("fsdp"),
         P("fsdp"),
     )
+    planes = dict(mesh.shape) == {"ctx": HEADS, "fsdp": PLANES}
     return jax.shard_map(
-        on_device, mesh=mesh, in_specs=in_specs, out_specs=out_specs, check_vma=False
-    )
+        in_planes if planes else on_device, mesh=mesh, in_specs=in_specs, out_specs=out_specs, check_vma=False
+    )

time: 1490 us -> 547 us (0.37)
  blocking collectives: 559 us -> 0 us
  waiting for transfers between devices: 466 us -> 265 us
  matrix products: 179 us -> 0 us
  starting transfers between devices: 0.89 us -> 129 us
  local copies, waits for them, and re-layouts: 125 us -> 13.6 us
  Pallas kernels: 0 us -> 108 us
  other arithmetic: 93.6 us -> 6.62 us
  loops' own time: 37.5 us -> 0 us
    psum x1 -> x0, blocking collectives: 537 us -> none  [on_device(): lax.psum((shares[0], shares[1], shares[2], shares[3], shares[4], shares[5...]
    reduce_scatter x7 -> x0, waiting for transfers between devices: 275 us -> none  [the longest x1 94.8 us: on_device(): lax.psum_scatter(local_grads[3].astype(jnp.bfloat16), 'fsdp', scatter_dim...]
    dot_general x145 -> x0, matrix products: 179 us -> none  [the longest x16 20.3 us: states_one_group(): jnp.einsum('thk,thj->hkj', group_key_rows, group_key_rows, preferred_elem...]
    all_gather x9 -> x0, waiting for transfers between devices: 155 us -> none  [the longest x1 46.6 us: on_device(): lax.all_gather(value_flat, 'ctx', axis=0, tiled=True)]
    ppermute x0 -> x90, waiting for transfers between devices: none -> 153 us  [shift(): return lax.ppermute(value, ('ctx', 'fsdp'), pairs)]
    ppermute x0 -> x90, starting transfers between devices: none -> 128 us  [shift(): return lax.ppermute(value, ('ctx', 'fsdp'), pairs)]
    psum x0 -> x1, waiting for transfers between devices: none -> 111 us  [in_planes(): persist = lax.psum(persist, ('ctx', 'fsdp'))]
    pallas_call x0 -> x21, Pallas kernels: none -> 108 us  [call(): pl.pallas_call(kernel, out_shape=[jax.ShapeDtypeStruct(s, d) for s, d in...]
  transfers between devices with their start and end apart: 17 -> 91, of which waited for: 12 -> 26; matrix products, arithmetic and copies ran while one was open for 25% -> 2% of each run, Pallas kernels for 0% -> 15%
where the time goes in v1:
time: 547 us; the launch traced here: 537 us
  waiting for transfers between devices  265 us (48%)
  starting transfers between devices  129 us (24%)
  Pallas kernels  108 us (20%)
  between operations  15.3 us (3%)
  local copies, waits for them, and re-layouts  13.6 us (2%)
  other arithmetic  6.62 us (1%)
    ppermute x90, waiting for transfers between devices, shift(): return lax.ppermute(value, ('ctx', 'fsdp'), pairs)  153 us
    ppermute x90, starting transfers between devices, shift(): return lax.ppermute(value, ('ctx', 'fsdp'), pairs)  128 us
    psum x1, waiting for transfers between devices, in_planes(): persist = lax.psum(persist, ('ctx', 'fsdp'))  111 us
    pallas_call x21, Pallas kernels, call(): pl.pallas_call(kernel, out_shape=[jax.ShapeDtypeStruct(s, d) for s, d in...  108 us
  transfers between devices with their start and end apart: 91, of which 26 were waited for; matrix products, arithmetic and copies ran while one was open for 2% of the time, Pallas kernels for 15%

profile of v1, /device:TPU:0, one launch (start us, length us, event | category | flops | bytes accessed | tf_op | source)
XLA Modules:
  0.0 536.8 jit_solution(7461887050921026938)
XLA Ops:
  19.1 2.8 pack_qkvg.1
  21.8 3.8 collective-permute-start.12
  25.7 6.8 %collective-permute-start.13 = (bf16[256,512]{1,0:T(8,128)(2,1)}, bf16[256,512]{1,0:T(8,128)(2,1)S(1)}, u32[]{:S(2)}, u32[]{:S(2)}) collective-permute-start(bf16[256,512]{1,0:T(8,128)(2,1)} %get-tuple-element.100), channel_id=1, source_target_pairs={{0,2},{1,3},{2,0},{3,1},{4,6},{5,7},{6,4},{7,5},{8,10},{9,11},{10,... | collective-permute-start | bytes 786440 | tf_op jit(solution)/shard_map/ppermute | solution.py:587
  36.7 3.1 collective-permute-done.13.refs_10_
  39.8 11.2 %collective-permute-done.6.refs_2_ = bf16[128,1024]{1,0:T(8,128)(2,1)S(1)} collective-permute-done((bf16[128,1024]{1,0:T(8,128)(2,1)S(1)}, bf16[128,1024]{1,0:T(8,128)(2,1)S(1)}, u32[]{:S(2)}, u32[]{:S(2)}) %collective-permute-start.6) | collective-permute-done | bytes 262176 | tf_op jit(solution)/shard_map/ppermute | solution.py:587
  53.0 3.4 collective-permute-done.14.refs_11_
  56.5 15.0 %mixer_forward.1 = (bf16[4,128,1024]{2,1,0:T(8,128)(2,1)}, bf16[4,128,1024]{2,1,0:T(8,128)(2,1)}, bf16[1024,1024]{1,0:T(8,128)(2,1)}, bf16[1024,512]{1,0:T(8,128...) custom-call(s32[4]{0:T(128)} %pad_add_fusion.idx, ...), custom_call_target="tpu_custom_call" | custom-call | flops 3000000000 | bytes 13943808 | tf_op jit(solution)/shard_map/mixer_forward/pallas_call | solution.py:642
  71.7 3.7 pack_gu.1
  76.9 3.6 collective-permute-start.35
  81.4 2.7 core_sum.4
  85.9 9.4 %collective-permute-start.18 = (bf16[128,1024]{1,0:T(8,128)(2,1)}, bf16[128,1024]{1,0:T(8,128)(2,1)S(1)}, u32[]{:S(2)}, u32[]{:S(2)}) collective-permute-start(bf16[128,1024]{1,0:T(8,128)(2,1)} %get-tuple-element.107), channel_id=1, source_target_pairs={{0,6},{1,7},{2,4},{3,5},{4,2},{5,3},{6,0},{7,1},{8,14},{9,15},{10,... | collective-permute-start | bytes 786440 | tf_op jit(solution)/shard_map/ppermute | solution.py:587
  95.4 5.8 %collective-permute-done.35.refs_18_ = bf16[256,768]{1,0:T(8,128)(2,1)S(1)} collective-permute-done((bf16[256,768]{1,0:T(8,128)(2,1)}, bf16[256,768]{1,0:T(8,128)(2,1)S(1)}, u32[]{:S(2)}, u32[]{:S(2)}) %collective-permute-start.35) | collective-permute-done | bytes 393248 | tf_op jit(solution)/shard_map/ppermute | solution.py:587
  103.6 3.2 collective-permute-done.16.r1
  114.0 12.4 %collective-permute-done.28.refs_10_ = bf16[128,1024]{1,0:T(8,128)(2,1)S(1)} collective-permute-done((bf16[128,1024]{1,0:T(8,128)(2,1)S(1)}, bf16[128,1024]{1,0:T(8,128)(2,1)S(1)}, u32[]{:S(2)}, u32[]{:S(2)}) %collective-permute-start.28) | collective-permute-done | bytes 262176 | tf_op jit(solution)/shard_map/ppermute | solution.py:587
  131.9 4.4 collective-permute-done.20.refs_2_
  136.3 2.6 collective-permute-done.22.refs_4_
  138.9 4.3 collective-permute-done.24.refs_6_
  145.1 12.4 %feed.1 = (bf16[4,128,1024]{2,1,0:T(8,128)(2,1)}, bf16[4,128,1024]{2,1,0:T(8,128)(2,1)}, bf16[4,128,1024]{2,1,0:T(8,128)(2,1)}, bf16[4,128,1024]{2,1,0:T(8,128)(...) custom-call(s32[4]{0:T(128)} %pad_add_fusion.idx, ...), custom_call_target="tpu_custom_call" | custom-call | flops 5000000000 | bytes 17301504 | tf_op jit(solution)/shard_map/feed/pallas_call | solution.py:642
  157.7 6.7 %feed_weights.1 = (bf16[4,64,768]{2,1,0:T(8,128)(2,1)}, bf16[4,64,768]{2,1,0:T(8,128)(2,1)}, bf16[4,64,768]{2,1,0:T(8,128)(2,1)}, bf16[4,64,768]{2,1,0:T(8,128)(...) custom-call(s32[4]{0:T(128)} %pad_add_fusion.idx, ...), custom_call_target="tpu_custom_call" | custom-call | flops 3000000000 | bytes 8912896 | tf_op jit(solution)/shard_map/feed_weights/pallas_call | solution.py:642
  164.4 2.7 collective-permute-start.78
  169.3 6.7 %collective-permute-done.77.refs_5_ = bf16[96,1024]{1,0:T(8,128)(2,1)S(1)} collective-permute-done((bf16[96,1024]{1,0:T(8,128)(2,1)}, bf16[96,1024]{1,0:T(8,128)(2,1)S(1)}, u32[]{:S(2)}, u32[]{:S(2)}) %collective-permute-start.77) | collective-permute-done | bytes 196640 | tf_op jit(solution)/shard_map/ppermute | solution.py:587
  181.5 2.7 core_sum.6
  184.1 13.8 %collective-permute-done.79.refs_7_ = bf16[96,1024]{1,0:T(8,128)(2,1)S(1)} collective-permute-done((bf16[96,1024]{1,0:T(8,128)(2,1)}, bf16[96,1024]{1,0:T(8,128)(2,1)S(1)}, u32[]{:S(2)}, u32[]{:S(2)}) %collective-permute-start.79) | collective-permute-done | bytes 196640 | tf_op jit(solution)/shard_map/ppermute | solution.py:587
  200.0 7.0 %collective-permute-done.75.refs_2_ = bf16[4,64,768]{2,1,0:T(8,128)(2,1)S(1)} collective-permute-done((bf16[4,64,768]{2,1,0:T(8,128)(2,1)}, bf16[4,64,768]{2,1,0:T(8,128)(2,1)S(1)}, u32[]{:S(2)}, u32[]{:S(2)}) %collective-permute-start.75) | collective-permute-done | bytes 393248 | tf_op jit(solution)/shard_map/ppermute | solution.py:587
  207.1 2.8 collective-permute-start.45
  216.3 2.9 branch.1
  224.2 9.4 %collective-permute-done.81.refs_2_ = bf16[64,768]{1,0:T(8,128)(2,1)S(1)} collective-permute-done((bf16[64,768]{1,0:T(8,128)(2,1)S(1)}, bf16[64,768]{1,0:T(8,128)(2,1)S(1)}, u32[]{:S(2)}, u32[]{:S(2)}) %collective-permute-start.81) | collective-permute-done | bytes 98336 | tf_op jit(solution)/shard_map/ppermute | solution.py:587
  233.7 4.9 collective-permute-done.82.refs_3_
  242.9 10.6 %collective-permute-start.84 = (bf16[384,768]{1,0:T(8,128)(2,1)}, bf16[384,768]{1,0:T(8,128)(2,1)S(1)}, u32[]{:S(2)}, u32[]{:S(2)}) collective-permute-start(bf16[384,768]{1,0:T(8,128)(2,1)} %feed_join.1.refs_0_), channel_id=1, source_target_pairs={{0,8},{1,9},{2,10},{3,11},{4,12},{5,13},{6,14},{7,15},{8,0},{9,1},... | collective-permute-start | bytes 1769480 | tf_op jit(solution)/shard_map/ppermute | solution.py:587
  253.4 2.7 core_sum.5
  258.3 17.2 %mixer_backward.1 = (bf16[4,128,1024]{2,1,0:T(8,128)(2,1)}, bf16[4,128,1024]{2,1,0:T(8,128)(2,1)}, bf16[1024,512]{1,0:T(8,128)(2,1)}, bf16[1024,1024]{1,0:T(8,12...) custom-call(s32[4]{0:T(128)} %pad_add_fusion.idx, f32[2,128]{1,0:T(2,128)} %pad_maximum_fusion.8.rates, ...), custom_call_target="tpu_custom_call" | custom-call | flops 4000000000 | bytes 13688832 | tf_op jit(solution)/shard_map/mixer_backward/pallas_call | solution.py:642
  275.6 5.2 mixer_weights.1
  287.0 10.6 %collective-permute-done.61.refs_5_ = bf16[32,1024]{1,0:T(8,128)(2,1)S(1)} collective-permute-done((bf16[32,1024]{1,0:T(8,128)(2,1)}, bf16[32,1024]{1,0:T(8,128)(2,1)S(1)}, u32[]{:S(2)}, u32[]{:S(2)}) %collective-permute-start.61) | collective-permute-done | bytes 65568 | tf_op jit(solution)/shard_map/ppermute | solution.py:587
  297.7 13.5 %collective-permute-done.62.refs_6_ = bf16[32,1024]{1,0:T(8,128)(2,1)S(1)} collective-permute-done((bf16[32,1024]{1,0:T(8,128)(2,1)}, bf16[32,1024]{1,0:T(8,128)(2,1)S(1)}, u32[]{:S(2)}, u32[]{:S(2)}) %collective-permute-start.62) | collective-permute-done | bytes 65568 | tf_op jit(solution)/shard_map/ppermute | solution.py:587
  312.9 4.6 collective-permute-done.63.refs_7_
  326.8 6.0 %collective-permute-done.40.r3 = bf16[128,1024]{1,0:T(8,128)(2,1)S(1)} collective-permute-done((bf16[128,1024]{1,0:T(8,128)(2,1)S(1)}, bf16[128,1024]{1,0:T(8,128)(2,1)S(1)}, u32[]{:S(2)}, u32[]{:S(2)}) %collective-permute-start.40) | collective-permute-done | bytes 262176 | tf_op jit(solution)/shard_map/ppermute | solution.py:587
  333.9 3.6 collective-permute-done.65.refs_2_
  344.2 10.1 %collective-permute-start.70 = (bf16[320,512]{1,0:T(8,128)(2,1)}, bf16[320,512]{1,0:T(8,128)(2,1)}, u32[]{:S(2)}, u32[]{:S(2)}) collective-permute-start(bf16[320,512]{1,0:T(8,128)(2,1)} %mixer_join.1.refs_0_), channel_id=1, source_target_pairs={{0,16},{1,17},{2,18},{3,19},{4,20},{5,21},{6,22},{7,23},{8,24},{9,... | collective-permute-start | bytes 983048 | tf_op jit(solution)/shard_map/ppermute | solution.py:587
  358.1 2.7 core_sum.7
  360.9 4.3 collective-permute-start.54
  366.5 10.7 %collective-permute-done.70.refs_4_ = bf16[320,512]{1,0:T(8,128)(2,1)} collective-permute-done((bf16[320,512]{1,0:T(8,128)(2,1)}, bf16[320,512]{1,0:T(8,128)(2,1)}, u32[]{:S(2)}, u32[]{:S(2)}) %collective-permute-start.70) | collective-permute-done | bytes 327712 | tf_op jit(solution)/shard_map/ppermute | solution.py:587
  377.2 3.2 collective-permute-start.56
  382.6 5.3 collective-permute-done.56.r3
  389.1 2.5 tokens.1
  391.7 3.6 collective-permute-start.57
  397.2 10.9 %feed_unpack.1 = (f32[256,5632]{1,0:T(8,128)}, f32[704,1024]{1,0:T(8,128)}, f32[1,256]{1,0:T(1,128)}) custom-call(s32[4]{0:T(128)} %pad_add_fusion.idx, bf16[384,768]{1,0:T(8,128)(2,1)} %feed_join.1.refs_0_, bf16[384,768]{1,0:T(8,128)(2,1)} %copy-done.9, bf16[384,768]{1,0:T(8,128)(2,1)} %copy-done.10, bf16[384,768]{1,0:T(8,128)(2,1)} %copy-done.13, ...), custom_call_target="tpu_custom_call" | custom-call | bytes 16254464 | tf_op jit(solution)/shard_map/feed_unpack/pallas_call | solution.py:642
  408.1 111.2 %all-reduce.3.cloned.1.call-done = f32[32,1024]{1,0:T(8,128)} async-done(((f32[32,1024]{1,0:T(8,128)}), f32[32,1024]{1,0:T(8,128)}) %all-reduce.3.cloned.1.call-update) | async-done | bytes 131088 | tf_op jit(solution)/shard_map/psum | solution.py:1317
  521.7 5.2 mixer_unpack.1
  (360 shorter events, 107.3 us)
Async XLA Ops:
  7.2 512.1 %all-reduce.3.cloned.1.call-start = ((), (), s32[]{:S(2)}) async-start(), calls=%async_computation | async-start | bytes 262144 | tf_op jit(solution)/shard_map/psum | solution.py:1317
  11.4 21.2 %collective-permute-start.2 = (bf16[16,1024]{1,0:T(8,128)(2,1)S(1)}, bf16[16,1024]{1,0:T(8,128)(2,1)S(1)}, u32[]{:S(2)}, u32[]{:S(2)}) collective-permute-start(bf16[16,1024]{1,0:T(8,128)(2,1)S(1)} %get-tuple-element.196), channel_id=1, source_target_pairs={{0,2},{1,3},{2,0},{3,1},{4,6},{5,7},{6,4},{7,5},{8,10},{9,11},{10,... | collective-permute-start | bytes 98312 | tf_op jit(solution)/shard_map/ppermute | solution.py:587
  12.0 22.1 %collective-permute-start.1 = (bf16[16,1024]{1,0:T(8,128)(2,1)S(1)}, bf16[16,1024]{1,0:T(8,128)(2,1)S(1)}, u32[]{:S(2)}, u32[]{:S(2)}) collective-permute-start(bf16[16,1024]{1,0:T(8,128)(2,1)S(1)} %get-tuple-element.196), channel_id=1, source_target_pairs={{0,1},{1,0},{2,3},{3,2},{4,5},{5,4},{6,7},{7,6},{8,9},{9,8},{10,11... | collective-permute-start | bytes 98312 | tf_op jit(solution)/shard_map/ppermute | solution.py:587
  12.1 20.4 %collective-permute-start = (bf16[128,1024]{1,0:T(8,128)(2,1)}, bf16[128,1024]{1,0:T(8,128)(2,1)S(1)}, u32[]{:S(2)}, u32[]{:S(2)}) collective-permute-start(bf16[128,1024]{1,0:T(8,128)(2,1)} %bitcast.31), channel_id=1, source_target_pairs={{0,0},{1,8},{2,16},{3,24},{4,4},{5,12},{6,20},{7,28},{8,1},{9,9},{... | collective-permute-start | bytes 786440 | tf_op jit(solution)/shard_map/ppermute | solution.py:587
  32.5 18.6 %collective-permute-start.6 = (bf16[128,1024]{1,0:T(8,128)(2,1)S(1)}, bf16[128,1024]{1,0:T(8,128)(2,1)S(1)}, u32[]{:S(2)}, u32[]{:S(2)}) collective-permute-start(bf16[128,1024]{1,0:T(8,128)(2,1)S(1)} %collective-permute-done.refs_0_.x), channel_id=1, source_target_pairs={{0,2},{1,3},{2,0},{3,1},{4,6},{5,7},{6,4},{7,5},{8,10},{9,11},{10,... | collective-permute-start | bytes 786440 | tf_op jit(solution)/shard_map/ppermute | solution.py:587
  32.6 18.5 %collective-permute-start.8 = (bf16[128,1024]{1,0:T(8,128)(2,1)S(1)}, bf16[128,1024]{1,0:T(8,128)(2,1)S(1)}, u32[]{:S(2)}, u32[]{:S(2)}) collective-permute-start(bf16[128,1024]{1,0:T(8,128)(2,1)S(1)} %collective-permute-done.refs_0_.x), channel_id=1, source_target_pairs={{0,4},{1,5},{2,6},{3,7},{4,0},{5,1},{6,2},{7,3},{8,12},{9,13},{10,... | collective-permute-start | bytes 786440 | tf_op jit(solution)/shard_map/ppermute | solution.py:587
  36.6 19.8 %collective-permute-start.14 = (bf16[256,512]{1,0:T(8,128)(2,1)}, bf16[256,512]{1,0:T(8,128)(2,1)}, u32[]{:S(2)}, u32[]{:S(2)}) collective-permute-start(bf16[256,512]{1,0:T(8,128)(2,1)} %get-tuple-element.101), channel_id=1, source_target_pairs={{0,3},{1,2},{2,1},{3,0},{4,7},{5,6},{6,5},{7,4},{8,11},{9,10},{10,... | collective-permute-start | bytes 786440 | tf_op jit(solution)/shard_map/ppermute | solution.py:587
  75.5 19.8 %collective-permute-start.34 = (bf16[256,768]{1,0:T(8,128)(2,1)}, bf16[256,768]{1,0:T(8,128)(2,1)S(1)}, u32[]{:S(2)}, u32[]{:S(2)}) collective-permute-start(bf16[256,768]{1,0:T(8,128)(2,1)} %get-tuple-element.111), channel_id=1, source_target_pairs={{0,1},{1,0},{2,3},{3,2},{4,5},{5,4},{6,7},{7,6},{8,9},{9,8},{10,11... | collective-permute-start | bytes 1179656 | tf_op jit(solution)/shard_map/ppermute | solution.py:587
  76.9 24.3 %collective-permute-start.35 = (bf16[256,768]{1,0:T(8,128)(2,1)}, bf16[256,768]{1,0:T(8,128)(2,1)S(1)}, u32[]{:S(2)}, u32[]{:S(2)}) collective-permute-start(bf16[256,768]{1,0:T(8,128)(2,1)} %get-tuple-element.112), channel_id=1, source_target_pairs={{0,2},{1,3},{2,0},{3,1},{4,6},{5,7},{6,4},{7,5},{8,10},{9,11},{10,... | collective-permute-start | bytes 1179656 | tf_op jit(solution)/shard_map/ppermute | solution.py:587
  84.1 22.7 %collective-permute-start.16 = (bf16[128,1024]{1,0:T(8,128)(2,1)}, bf16[128,1024]{1,0:T(8,128)(2,1)S(1)}, u32[]{:S(2)}, u32[]{:S(2)}) collective-permute-start(bf16[128,1024]{1,0:T(8,128)(2,1)} %get-tuple-element.105), channel_id=1, source_target_pairs={{0,2},{1,3},{2,0},{3,1},{4,6},{5,7},{6,4},{7,5},{8,10},{9,11},{10,... | collective-permute-start | bytes 786440 | tf_op jit(solution)/shard_map/ppermute | solution.py:587
  84.1 24.5 %collective-permute-start.17 = (bf16[128,1024]{1,0:T(8,128)(2,1)}, bf16[128,1024]{1,0:T(8,128)(2,1)S(1)}, u32[]{:S(2)}, u32[]{:S(2)}) collective-permute-start(bf16[128,1024]{1,0:T(8,128)(2,1)} %get-tuple-element.106), channel_id=1, source_target_pairs={{0,4},{1,5},{2,6},{3,7},{4,0},{5,1},{6,2},{7,3},{8,12},{9,13},{10,... | collective-permute-start | bytes 786440 | tf_op jit(solution)/shard_map/ppermute | solution.py:587
  85.9 23.2 %collective-permute-start.18 = (bf16[128,1024]{1,0:T(8,128)(2,1)}, bf16[128,1024]{1,0:T(8,128)(2,1)S(1)}, u32[]{:S(2)}, u32[]{:S(2)}) collective-permute-start(bf16[128,1024]{1,0:T(8,128)(2,1)} %get-tuple-element.107), channel_id=1, source_target_pairs={{0,6},{1,7},{2,4},{3,5},{4,2},{5,3},{6,0},{7,1},{8,14},{9,15},{10,... | collective-permute-start | bytes 786440 | tf_op jit(solution)/shard_map/ppermute | solution.py:587
  95.3 31.6 %collective-permute-start.36 = (bf16[256,768]{1,0:T(8,128)(2,1)S(1)}, bf16[256,768]{1,0:T(8,128)(2,1)S(1)}, u32[]{:S(2)}, u32[]{:S(2)}) collective-permute-start(bf16[256,768]{1,0:T(8,128)(2,1)S(1)} %copy-done.63), channel_id=1, source_target_pairs={{0,3},{1,2},{2,1},{3,0},{4,7},{5,6},{6,5},{7,4},{8,11},{9,10},{10,... | collective-permute-start | bytes 1179656 | tf_op jit(solution)/shard_map/ppermute | solution.py:587
  101.2 25.2 %collective-permute-start.28 = (bf16[128,1024]{1,0:T(8,128)(2,1)S(1)}, bf16[128,1024]{1,0:T(8,128)(2,1)S(1)}, u32[]{:S(2)}, u32[]{:S(2)}) collective-permute-start(bf16[128,1024]{1,0:T(8,128)(2,1)S(1)} %collective-permute-done.26.refs_8_.cot), channel_id=1, source_target_pairs={{0,2},{1,3},{2,0},{3,1},{4,6},{5,7},{6,4},{7,5},{8,10},{9,11},{10,... | collective-permute-start | bytes 786440 | tf_op jit(solution)/shard_map/ppermute | solution.py:587
  106.8 20.0 %collective-permute-start.30 = (bf16[128,1024]{1,0:T(8,128)(2,1)S(1)}, bf16[128,1024]{1,0:T(8,128)(2,1)S(1)}, u32[]{:S(2)}, u32[]{:S(2)}) collective-permute-start(bf16[128,1024]{1,0:T(8,128)(2,1)S(1)} %collective-permute-done.26.refs_8_.cot), channel_id=1, source_target_pairs={{0,4},{1,5},{2,6},{3,7},{4,0},{5,1},{6,2},{7,3},{8,12},{9,13},{10,... | collective-permute-start | bytes 786440 | tf_op jit(solution)/shard_map/ppermute | solution.py:587
  108.6 20.8 %collective-permute-start.27 = (bf16[128,1024]{1,0:T(8,128)(2,1)S(1)}, bf16[128,1024]{1,0:T(8,128)(2,1)S(1)}, u32[]{:S(2)}, u32[]{:S(2)}) collective-permute-start(bf16[128,1024]{1,0:T(8,128)(2,1)S(1)} %collective-permute-done.26.refs_8_.cot), channel_id=1, source_target_pairs={{0,1},{1,0},{2,3},{3,2},{4,5},{5,4},{6,7},{7,6},{8,9},{9,8},{10,11... | collective-permute-start | bytes 786440 | tf_op jit(solution)/shard_map/ppermute | solution.py:587
  109.1 22.1 %collective-permute-start.32 = (bf16[128,1024]{1,0:T(8,128)(2,1)S(1)}, bf16[128,1024]{1,0:T(8,128)(2,1)}, u32[]{:S(2)}, u32[]{:S(2)}) collective-permute-start(bf16[128,1024]{1,0:T(8,128)(2,1)S(1)} %collective-permute-done.26.refs_8_.cot), channel_id=1, source_target_pairs={{0,6},{1,7},{2,4},{3,5},{4,2},{5,3},{6,0},{7,1},{8,14},{9,15},{10,... | collective-permute-start | bytes 786440 | tf_op jit(solution)/shard_map/ppermute | solution.py:587
  157.5 22.3 %collective-permute-start.42 = (bf16[4,128,1024]{2,1,0:T(8,128)(2,1)}, bf16[4,128,1024]{2,1,0:T(8,128)(2,1)S(1)}, u32[]{:S(2)}, u32[]{:S(2)}) collective-permute-start(bf16[4,128,1024]{2,1,0:T(8,128)(2,1)} %get-tuple-element.121), channel_id=1, source_target_pairs={{0,1},{1,0},{2,3},{3,2},{4,5},{5,4},{6,7},{7,6},{8,9},{9,8},{10,11... | collective-permute-start | bytes 3145736 | tf_op jit(solution)/shard_map/ppermute | solution.py:587
  167.1 31.2 %collective-permute-start.74 = (bf16[4,64,768]{2,1,0:T(8,128)(2,1)}, bf16[4,64,768]{2,1,0:T(8,128)(2,1)S(1)}, u32[]{:S(2)}, u32[]{:S(2)}) collective-permute-start(bf16[4,64,768]{2,1,0:T(8,128)(2,1)} %get-tuple-element.167), channel_id=1, source_target_pairs={{0,8},{1,9},{2,10},{3,11},{4,12},{5,13},{6,14},{7,15},{8,0},{9,1},... | collective-permute-start | bytes 1179656 | tf_op jit(solution)/shard_map/ppermute | solution.py:587
  167.2 39.9 %collective-permute-start.75 = (bf16[4,64,768]{2,1,0:T(8,128)(2,1)}, bf16[4,64,768]{2,1,0:T(8,128)(2,1)S(1)}, u32[]{:S(2)}, u32[]{:S(2)}) collective-permute-start(bf16[4,64,768]{2,1,0:T(8,128)(2,1)} %get-tuple-element.168), channel_id=1, source_target_pairs={{0,16},{1,17},{2,18},{3,19},{4,20},{5,21},{6,22},{7,23},{8,24},{9,... | collective-permute-start | bytes 1179656 | tf_op jit(solution)/shard_map/ppermute | solution.py:587
  176.0 65.6 %collective-permute-start.37 = (bf16[4,128,1024]{2,1,0:T(8,128)(2,1)S(1)}, bf16[4,128,1024]{2,1,0:T(8,128)(2,1)S(1)}, u32[]{:S(2)}, u32[]{:S(2)}) collective-permute-start(bf16[4,128,1024]{2,1,0:T(8,128)(2,1)S(1)} %copy-done.58), channel_id=1, source_target_pairs={{0,1},{1,0},{2,3},{3,2},{4,5},{5,4},{6,7},{7,6},{8,9},{9,8},{10,11... | collective-permute-start | bytes 3145736 | tf_op jit(solution)/shard_map/ppermute | solution.py:587
  177.6 20.3 %collective-permute-start.79 = (bf16[96,1024]{1,0:T(8,128)(2,1)}, bf16[96,1024]{1,0:T(8,128)(2,1)S(1)}, u32[]{:S(2)}, u32[]{:S(2)}) collective-permute-start(bf16[96,1024]{1,0:T(8,128)(2,1)} %get-tuple-element.173), channel_id=1, source_target_pairs={{0,24},{1,25},{2,26},{3,27},{4,28},{5,29},{6,30},{7,31},{8,16},{9,... | collective-permute-start | bytes 589832 | tf_op jit(solution)/shard_map/ppermute | solution.py:587
  179.8 30.1 %collective-permute-start.76 = (bf16[4,64,768]{2,1,0:T(8,128)(2,1)}, bf16[4,64,768]{2,1,0:T(8,128)(2,1)S(1)}, u32[]{:S(2)}, u32[]{:S(2)}) collective-permute-start(bf16[4,64,768]{2,1,0:T(8,128)(2,1)} %get-tuple-element.169), channel_id=1, source_target_pairs={{0,24},{1,25},{2,26},{3,27},{4,28},{5,29},{6,30},{7,31},{8,16},{9,... | collective-permute-start | bytes 1179656 | tf_op jit(solution)/shard_map/ppermute | solution.py:587
  219.2 19.4 %collective-permute-start.47 = (bf16[128,1024]{1,0:T(8,128)(2,1)}, bf16[128,1024]{1,0:T(8,128)(2,1)S(1)}, u32[]{:S(2)}, u32[]{:S(2)}) collective-permute-start(bf16[128,1024]{1,0:T(8,128)(2,1)} %get-tuple-element.127.refs_0_), channel_id=1, source_target_pairs={{0,2},{1,3},{2,0},{3,1},{4,6},{5,7},{6,4},{7,5},{8,10},{9,11},{10,... | collective-permute-start | bytes 786440 | tf_op jit(solution)/shard_map/ppermute | solution.py:587
  220.7 18.4 %collective-permute-start.49 = (bf16[128,1024]{1,0:T(8,128)(2,1)}, bf16[128,1024]{1,0:T(8,128)(2,1)S(1)}, u32[]{:S(2)}, u32[]{:S(2)}) collective-permute-start(bf16[128,1024]{1,0:T(8,128)(2,1)} %get-tuple-element.127.refs_0_), channel_id=1, source_target_pairs={{0,4},{1,5},{2,6},{3,7},{4,0},{5,1},{6,2},{7,3},{8,12},{9,13},{10,... | collective-permute-start | bytes 786440 | tf_op jit(solution)/shard_map/ppermute | solution.py:587
  239.2 18.4 %collective-permute-start.52 = (bf16[128,1024]{1,0:T(8,128)(2,1)S(1)}, bf16[128,1024]{1,0:T(8,128)(2,1)S(1)}, u32[]{:S(2)}, u32[]{:S(2)}) collective-permute-start(bf16[128,1024]{1,0:T(8,128)(2,1)S(1)} %collective-permute-done.51.refs_6_), channel_id=1, source_target_pairs={{0,1},{1,0},{2,3},{3,2},{4,5},{5,4},{6,7},{7,6},{8,9},{9,8},{10,11... | collective-permute-start | bytes 786440 | tf_op jit(solution)/shard_map/ppermute | solution.py:587
  241.7 41.0 %collective-permute-start.83 = (bf16[384,768]{1,0:T(8,128)(2,1)}, bf16[384,768]{1,0:T(8,128)(2,1)S(1)}, u32[]{:S(2)}, u32[]{:S(2)}) collective-permute-start(bf16[384,768]{1,0:T(8,128)(2,1)} %feed_join.1.refs_0_), channel_id=1, source_target_pairs={{0,4},{1,5},{2,6},{3,7},{4,0},{5,1},{6,2},{7,3},{8,12},{9,13},{10,... | collective-permute-start | bytes 1769480 | tf_op jit(solution)/shard_map/ppermute | solution.py:587
  242.9 39.9 %collective-permute-start.84 = (bf16[384,768]{1,0:T(8,128)(2,1)}, bf16[384,768]{1,0:T(8,128)(2,1)S(1)}, u32[]{:S(2)}, u32[]{:S(2)}) collective-permute-start(bf16[384,768]{1,0:T(8,128)(2,1)} %feed_join.1.refs_0_), channel_id=1, source_target_pairs={{0,8},{1,9},{2,10},{3,11},{4,12},{5,13},{6,14},{7,15},{8,0},{9,1},... | collective-permute-start | bytes 1769480 | tf_op jit(solution)/shard_map/ppermute | solution.py:587
  256.1 29.0 %collective-permute-start.86 = (bf16[384,768]{1,0:T(8,128)(2,1)S(1)}, bf16[384,768]{1,0:T(8,128)(2,1)S(1)}, u32[]{:S(2)}, u32[]{:S(2)}) collective-permute-start(bf16[384,768]{1,0:T(8,128)(2,1)S(1)} %copy-done.2), channel_id=1, source_target_pairs={{0,16},{1,17},{2,18},{3,19},{4,20},{5,21},{6,22},{7,23},{8,24},{9,... | collective-permute-start | bytes 1769480 | tf_op jit(solution)/shard_map/ppermute | solution.py:587
  256.6 30.4 %collective-permute-start.38 = (bf16[128,1024]{1,0:T(8,128)(2,1)}, bf16[128,1024]{1,0:T(8,128)(2,1)S(1)}, u32[]{:S(2)}, u32[]{:S(2)}) collective-permute-start(bf16[128,1024]{1,0:T(8,128)(2,1)} %get-tuple-element.117), channel_id=1, source_target_pairs={{0,2},{1,3},{2,0},{3,1},{4,6},{5,7},{6,4},{7,5},{8,10},{9,11},{10,... | collective-permute-start | bytes 786440 | tf_op jit(solution)/shard_map/ppermute | solution.py:587
  280.7 37.6 %collective-permute-start.58 = (bf16[4,64,512]{2,1,0:T(8,128)(2,1)}, bf16[4,64,512]{2,1,0:T(8,128)(2,1)S(1)}, u32[]{:S(2)}, u32[]{:S(2)}) collective-permute-start(bf16[4,64,512]{2,1,0:T(8,128)(2,1)} %get-tuple-element.147), channel_id=1, source_target_pairs={{0,8},{1,9},{2,10},{3,11},{4,12},{5,13},{6,14},{7,15},{8,0},{9,1},... | collective-permute-start | bytes 786440 | tf_op jit(solution)/shard_map/ppermute | solution.py:587
  282.8 37.3 %collective-permute-start.59 = (bf16[4,64,512]{2,1,0:T(8,128)(2,1)}, bf16[4,64,512]{2,1,0:T(8,128)(2,1)S(1)}, u32[]{:S(2)}, u32[]{:S(2)}) collective-permute-start(bf16[4,64,512]{2,1,0:T(8,128)(2,1)} %get-tuple-element.148), channel_id=1, source_target_pairs={{0,16},{1,17},{2,18},{3,19},{4,20},{5,21},{6,22},{7,23},{8,24},{9,... | collective-permute-start | bytes 786440 | tf_op jit(solution)/shard_map/ppermute | solution.py:587
  285.1 37.1 %collective-permute-start.60 = (bf16[4,64,512]{2,1,0:T(8,128)(2,1)}, bf16[4,64,512]{2,1,0:T(8,128)(2,1)S(1)}, u32[]{:S(2)}, u32[]{:S(2)}) collective-permute-start(bf16[4,64,512]{2,1,0:T(8,128)(2,1)} %get-tuple-element.149), channel_id=1, source_target_pairs={{0,24},{1,25},{2,26},{3,27},{4,28},{5,29},{6,30},{7,31},{8,16},{9,... | collective-permute-start | bytes 786440 | tf_op jit(solution)/shard_map/ppermute | solution.py:587
  287.0 24.1 %collective-permute-start.62 = (bf16[32,1024]{1,0:T(8,128)(2,1)}, bf16[32,1024]{1,0:T(8,128)(2,1)S(1)}, u32[]{:S(2)}, u32[]{:S(2)}) collective-permute-start(bf16[32,1024]{1,0:T(8,128)(2,1)} %get-tuple-element.152), channel_id=1, source_target_pairs={{0,16},{1,17},{2,18},{3,19},{4,20},{5,21},{6,22},{7,23},{8,24},{9,... | collective-permute-start | bytes 196616 | tf_op jit(solution)/shard_map/ppermute | solution.py:587
  297.7 59.0 %collective-permute-start.53 = (bf16[4,128,1024]{2,1,0:T(8,128)(2,1)S(1)}, bf16[4,128,1024]{2,1,0:T(8,128)(2,1)S(1)}, u32[]{:S(2)}, u32[]{:S(2)}) collective-permute-start(bf16[4,128,1024]{2,1,0:T(8,128)(2,1)S(1)} %copy-done.59), channel_id=1, source_target_pairs={{0,1},{1,0},{2,3},{3,2},{4,5},{5,4},{6,7},{7,6},{8,9},{9,8},{10,11... | collective-permute-start | bytes 3145736 | tf_op jit(solution)/shard_map/ppermute | solution.py:587
  320.0 24.0 %collective-permute-start.88 = (bf16[384,768]{1,0:T(8,128)(2,1)S(1)}, bf16[384,768]{1,0:T(8,128)(2,1)S(1)}, u32[]{:S(2)}, u32[]{:S(2)}) collective-permute-start(bf16[384,768]{1,0:T(8,128)(2,1)S(1)} %copy-done.2), channel_id=1, source_target_pairs={{0,24},{1,25},{2,26},{3,27},{4,28},{5,29},{6,30},{7,31},{8,16},{9,... | collective-permute-start | bytes 1769480 | tf_op jit(solution)/shard_map/ppermute | solution.py:587
  322.2 32.1 %collective-permute-start.85 = (bf16[384,768]{1,0:T(8,128)(2,1)S(1)}, bf16[384,768]{1,0:T(8,128)(2,1)S(1)}, u32[]{:S(2)}, u32[]{:S(2)}) collective-permute-start(bf16[384,768]{1,0:T(8,128)(2,1)S(1)} %collective-permute-done.84.refs_2_), channel_id=1, source_target_pairs={{0,4},{1,5},{2,6},{3,7},{4,0},{5,1},{6,2},{7,3},{8,12},{9,13},{10,... | collective-permute-start | bytes 1769480 | tf_op jit(solution)/shard_map/ppermute | solution.py:587
  337.5 23.3 %collective-permute-start.87 = (bf16[384,768]{1,0:T(8,128)(2,1)S(1)}, bf16[384,768]{1,0:T(8,128)(2,1)S(1)}, u32[]{:S(2)}, u32[]{:S(2)}) collective-permute-start(bf16[384,768]{1,0:T(8,128)(2,1)S(1)} %collective-permute-done.86.refs_4_), channel_id=1, source_target_pairs={{0,4},{1,5},{2,6},{3,7},{4,0},{5,1},{6,2},{7,3},{8,12},{9,13},{10,... | collective-permute-start | bytes 1769480 | tf_op jit(solution)/shard_map/ppermute | solution.py:587
  344.1 21.1 %collective-permute-start.68 = (bf16[320,512]{1,0:T(8,128)(2,1)}, bf16[320,512]{1,0:T(8,128)(2,1)}, u32[]{:S(2)}, u32[]{:S(2)}) collective-permute-start(bf16[320,512]{1,0:T(8,128)(2,1)} %mixer_join.1.refs_0_), channel_id=1, source_target_pairs={{0,8},{1,9},{2,10},{3,11},{4,12},{5,13},{6,14},{7,15},{8,0},{9,1},... | collective-permute-start | bytes 983048 | tf_op jit(solution)/shard_map/ppermute | solution.py:587
  344.2 33.0 %collective-permute-start.70 = (bf16[320,512]{1,0:T(8,128)(2,1)}, bf16[320,512]{1,0:T(8,128)(2,1)}, u32[]{:S(2)}, u32[]{:S(2)}) collective-permute-start(bf16[320,512]{1,0:T(8,128)(2,1)} %mixer_join.1.refs_0_), channel_id=1, source_target_pairs={{0,16},{1,17},{2,18},{3,19},{4,20},{5,21},{6,22},{7,23},{8,24},{9,... | collective-permute-start | bytes 983048 | tf_op jit(solution)/shard_map/ppermute | solution.py:587
  354.3 37.4 %collective-permute-start.89 = (bf16[384,768]{1,0:T(8,128)(2,1)S(1)}, bf16[384,768]{1,0:T(8,128)(2,1)S(1)}, u32[]{:S(2)}, u32[]{:S(2)}) collective-permute-start(bf16[384,768]{1,0:T(8,128)(2,1)S(1)} %collective-permute-done.88.refs_6_), channel_id=1, source_target_pairs={{0,4},{1,5},{2,6},{3,7},{4,0},{5,1},{6,2},{7,3},{8,12},{9,13},{10,... | collective-permute-start | bytes 1769480 | tf_op jit(solution)/shard_map/ppermute | solution.py:587
  356.7 23.8 %collective-permute-start.72 = (bf16[320,512]{1,0:T(8,128)(2,1)}, bf16[320,512]{1,0:T(8,128)(2,1)}, u32[]{:S(2)}, u32[]{:S(2)}) collective-permute-start(bf16[320,512]{1,0:T(8,128)(2,1)} %mixer_join.1.refs_0_), channel_id=1, source_target_pairs={{0,24},{1,25},{2,26},{3,27},{4,28},{5,29},{6,30},{7,31},{8,16},{9,... | collective-permute-start | bytes 983048 | tf_op jit(solution)/shard_map/ppermute | solution.py:587
  360.9 19.6 %collective-permute-start.54 = (bf16[128,1024]{1,0:T(8,128)(2,1)}, bf16[128,1024]{1,0:T(8,128)(2,1)S(1)}, u32[]{:S(2)}, u32[]{:S(2)}) collective-permute-start(bf16[128,1024]{1,0:T(8,128)(2,1)} %get-tuple-element.139), channel_id=1, source_target_pairs={{0,2},{1,3},{2,0},{3,1},{4,6},{5,7},{6,4},{7,5},{8,10},{9,11},{10,... | collective-permute-start | bytes 786440 | tf_op jit(solution)/shard_map/ppermute | solution.py:587
  380.4 140.4 %collective-permute-start.67 = (bf16[320,512]{1,0:T(8,128)(2,1)S(1)}, bf16[320,512]{1,0:T(8,128)(2,1)S(1)}, u32[]{:S(2)}, u32[]{:S(2)}) collective-permute-start(bf16[320,512]{1,0:T(8,128)(2,1)S(1)} %copy-done.3), channel_id=1, source_target_pairs={{0,4},{1,5},{2,6},{3,7},{4,0},{5,1},{6,2},{7,3},{8,12},{9,13},{10,... | collective-permute-start | bytes 983048 | tf_op jit(solution)/shard_map/ppermute | solution.py:587
  380.5 140.3 %collective-permute-start.69 = (bf16[320,512]{1,0:T(8,128)(2,1)}, bf16[320,512]{1,0:T(8,128)(2,1)S(1)}, u32[]{:S(2)}, u32[]{:S(2)}) collective-permute-start(bf16[320,512]{1,0:T(8,128)(2,1)} %collective-permute-done.68.refs_2_), channel_id=1, source_target_pairs={{0,4},{1,5},{2,6},{3,7},{4,0},{5,1},{6,2},{7,3},{8,12},{9,13},{10,... | collective-permute-start | bytes 983048 | tf_op jit(solution)/shard_map/ppermute | solution.py:587
  382.5 138.3 %collective-permute-start.71 = (bf16[320,512]{1,0:T(8,128)(2,1)}, bf16[320,512]{1,0:T(8,128)(2,1)S(1)}, u32[]{:S(2)}, u32[]{:S(2)}) collective-permute-start(bf16[320,512]{1,0:T(8,128)(2,1)} %collective-permute-done.70.refs_4_), channel_id=1, source_target_pairs={{0,4},{1,5},{2,6},{3,7},{4,0},{5,1},{6,2},{7,3},{8,12},{9,13},{10,... | collective-permute-start | bytes 983048 | tf_op jit(solution)/shard_map/ppermute | solution.py:587
  387.9 133.0 %collective-permute-start.73 = (bf16[320,512]{1,0:T(8,128)(2,1)}, bf16[320,512]{1,0:T(8,128)(2,1)}, u32[]{:S(2)}, u32[]{:S(2)}) collective-permute-start(bf16[320,512]{1,0:T(8,128)(2,1)} %collective-permute-done.72.refs_6_), channel_id=1, source_target_pairs={{0,4},{1,5},{2,6},{3,7},{4,0},{5,1},{6,2},{7,3},{8,12},{9,13},{10,... | collective-permute-start | bytes 983048 | tf_op jit(solution)/shard_map/ppermute | solution.py:587
  391.7 135.3 %collective-permute-start.57 = (bf16[128,1024]{1,0:T(8,128)(2,1)}, bf16[128,1024]{1,0:T(8,128)(2,1)}, u32[]{:S(2)}, u32[]{:S(2)}) collective-permute-start(bf16[128,1024]{1,0:T(8,128)(2,1)} %tokens.1), channel_id=1, source_target_pairs={{0,0},{1,8},{2,16},{3,24},{4,4},{5,12},{6,20},{7,28},{8,1},{9,9},{... | collective-permute-start | bytes 786440 | tf_op jit(solution)/shard_map/ppermute | solution.py:587
  (129 other events, 2076.4 us)
Sparse Core Ops, SparseCore 0:
  396.1 123.1 all-reduce.2

commit v2 on v1

--- a/solution.py
+++ b/solution.py
@@ -1,3 +1,5 @@
+import functools
+
 import jax
 import jax.numpy as jnp
 import numpy as np
@@ -567,7 +569,7 @@
 PLANES = 4
 HIDDEN_PAD = 384
 Z_HIDDEN = HIDDEN_PAD // PLANES
-VMEM_BYTES = 56 * 1024 * 1024
+EXTRA = 16
 
 
 def head_of(x, f, k):
@@ -599,8 +601,12 @@
     return shift(value, lambda z, x, f: (z ^ dz, x, f))
 
 
-def gather_plane(block):
-    near = [block, flip(block, 0, 2), flip(block, 1, 0), flip(block, 1, 2)]
+def gather_chips(block, last=None):
+    last = block if last is None else last
+    return [block, flip(block, 0, 2), flip(block, 1, 0), flip(last, 1, 2)]
+
+
+def gather_cores(near):
     far = [flip(b, 0, 1) for b in near]
     return [near[0], far[0], near[1], far[1], near[2], far[2], near[3], far[3]]
 
@@ -635,40 +641,74 @@
     return pl.BlockSpec(memory_space=pltpu.SMEM)
 
 
-def call(kernel, smem, operands, outs, scratch=(), flops=0, name=None):
-    moved = sum(o.size * o.dtype.itemsize for o in operands) + sum(
-        int(np.prod(s)) * jnp.dtype(d).itemsize for s, d in outs
-    )
+def padded_bytes(shape, dtype):
+    size = jnp.dtype(dtype).itemsize
+    lanes = -(-shape[-1] // 128) * 128
+    rows = -(-shape[-2] // (32 // size)) * (32 // size)
+    return int(np.prod(shape[:-2])) * rows * lanes * size
+
+
+def call(kernel, smem, operands, outs, scratch=(), name=None, spare=6, us=0.5):
+    held = [(o.shape, o.dtype) for o in operands] + list(outs) + list(scratch)
+    limit = sum(padded_bytes(shape, dtype) for shape, dtype in held) + spare * 1024 * 1024
     return pl.pallas_call(
         kernel,
-        out_shape=[jax.ShapeDtypeStruct(s, d) for s, d in outs],
+        out_shape=[jax.ShapeDtypeStruct(shape, dtype) for shape, dtype in outs],
         in_specs=[sspec()] * len(smem) + [vspec()] * len(operands),
         out_specs=[vspec()] * len(outs),
-        scratch_shapes=[pltpu.VMEM(s, d) for s, d in scratch],
-        compiler_params=pltpu.CompilerParams(vmem_limit_bytes=VMEM_BYTES),
-        cost_estimate=pl.CostEstimate(flops=flops, bytes_accessed=moved, transcendentals=0),
+        scratch_shapes=[pltpu.VMEM(shape, dtype) for shape, dtype in scratch],
+        compiler_params=pltpu.CompilerParams(vmem_limit_bytes=limit),
+        cost_estimate=pl.CostEstimate(
+            flops=int(us * 1.1e9), bytes_accessed=1000, transcendentals=0
+        ),
         name=name,
     )(*smem, *operands)
 
 
-def pack_qkvg_kernel(idx, wq, wg, o0, o1, o2, o3):
+def after(value, *others):
+    return lax.optimization_barrier((value, *others))[0]
+
+
+def pack_qkvg_kernel(idx, wq, wg, pk, pv, gain_one, gain_two, o0, o1, o2, o3, sems):
     x, f = idx[1], idx[2]
+    copies = []
+    for j, out in enumerate((o0, o1, o2, o3)):
+        start = pl.multiple_of((2 * (f ^ j) + x) * 128, 128)
+        for part in range(4):
+            first = start if part == 3 else pl.multiple_of(part * 1024 + start, 128)
+            source = wg if part == 3 else wq
+            copies.append(
+                pltpu.make_async_copy(
+                    source.at[:, pl.ds(first, 128)],
+                    out.at[pl.ds(0, 256), pl.ds(part * 128, 128)],
+                    sems.at[4 * j + part],
+                )
+            )
+    for copy in copies:
+        copy.start()
+    for j, out in enumerate((o0, o1, o2, o3)):
+        start = pl.multiple_of((2 * (f ^ j) + x) * 128, 128)
+        tail = [
+            jnp.concatenate([pk[:, pl.ds(start, 128)], pv[:, pl.ds(start, 128)]], axis=1),
+            gain_one[...],
+            gain_two[...],
+            jnp.zeros((EXTRA - 6, 256), jnp.bfloat16),
+        ]
+        tail = jnp.concatenate([t.astype(jnp.float32) for t in tail], axis=0)
+        tail = jnp.concatenate([tail, jnp.zeros((EXTRA, 256), jnp.float32)], axis=1)
+        out[256 : 256 + EXTRA, :] = tail.astype(jnp.bfloat16)
+    for copy in copies:
+        copy.wait()
+
+
+def pack_gu_kernel(idx, wgu, o0, o1, o2, o3):
+    z, x, f = idx[0], idx[1], idx[2]
+    width = FF // 8
     for j, out in enumerate((o0, o1, o2, o3)):
         head = 2 * (f ^ j) + x
-        start = pl.multiple_of(head * 128, 128)
-        for part in range(3):
-            out[:, part * 128 : part * 128 + 128] = wq[
-                :, pl.ds(pl.multiple_of(part * 1024 + start, 128), 128)
-            ]
-        out[:, 384:512] = wg[:, pl.ds(start, 128)]
-
-
-def pack_gu_kernel(idx, wgu, o0, o1, o2, o3):
-    x, f = idx[1], idx[2]
-    width = FF // 8
-    pad = jnp.zeros((wgu.shape[0], HIDDEN_PAD - width), jnp.bfloat16)
-    for j, out in enumerate((o0, o1, o2, o3)):
-        head = 2 * (f ^ j) + x
+        count = 256 if j < 2 else 128
+        rows = pl.ds(0 if j < 2 else pl.multiple_of((z & 1) * 128, 128), count)
+        pad = jnp.zeros((count, HIDDEN_PAD - width), jnp.bfloat16)
         for h in range(8):
 
             @pl.when(head == h)
@@ -677,21 +717,41 @@
                     first = part * FF + h * width
                     at = part * HIDDEN_PAD
                     out[:, at : at + HIDDEN_PAD] = jnp.concatenate(
-                        [wgu[:, first : first + width], pad], axis=1
+                        [wgu[rows, first : first + width], pad], axis=1
                     )
+
+
+def lay_weights(z, f, parts, w_full):
+    for j in range(2):
+        w_full[pl.ds(pl.multiple_of((f ^ j) * 256, 256), 256), :] = parts[j][0:256, :]
+    for j in (2, 3):
+        for side in range(2):
+            rows = pl.multiple_of((f ^ j) * 256 + ((z ^ side) & 1) * 128, 128)
+            w_full[pl.ds(rows, 128), :] = parts[j + 2 * side][0:128, :]
 
 
 def mixer_forward_kernel(idx, rates, ints, *refs):
     blocks = refs[0:8]
     parts = refs[8:12]
-    gain, wo, pk, pv = refs[12:16]
-    send, keep, normed, w_full, qkv, gate, att, rec, probs, pprobs, states, mixed = refs[16:28]
+    w_out = refs[12]
+    send, keep, normed, w_full, qkv, gate, att, rec, probs, pprobs, states, mixed = refs[13:25]
+    gain_one, gain_two, pk, pv = refs[25:29]
     x, f = idx[1], idx[2]
     head = 2 * f + x
     scale = HEAD_WIDTH_SIZE ** (-0.5)
-    gain_row = gain[...]
+    wo = w_out[pl.ds(pl.multiple_of(x * 128, 128), 128), :]
+    tails = []
     for j in range(4):
-        w_full[pl.ds(pl.multiple_of((f ^ j) * 256, 256), 256), :] = parts[j][...]
+        rows = pl.multiple_of((f ^ j) * 256, 256)
+        w_full[pl.ds(rows, 256), :] = parts[j][0:256, :]
+        tail = parts[j][256 : 256 + EXTRA, 0:256].astype(jnp.float32)
+        tails.append(tail)
+        gain_one[:, pl.ds(rows, 256)] = tail[4:5]
+        gain_two[:, pl.ds(rows, 256)] = tail[5:6]
+    tails = jnp.concatenate([tail[0:4] for tail in tails], axis=0).astype(jnp.bfloat16)
+    pk[...] = tails[:, 0:128]
+    pv[...] = tails[:, 128:256]
+    gain_row = gain_one[...]
     for k in range(8):
         values = blocks[k][...].astype(jnp.float32)
         normed_block = (values * rms_scale(values) * gain_row).astype(jnp.bfloat16)
@@ -756,23 +816,24 @@
             axis=0,
         )
         out = send if k & 1 else keep
-        out[k >> 1] = dot_nn(piece, wo[...]).astype(jnp.bfloat16)
+        out[k >> 1] = dot_nn(piece, wo).astype(jnp.bfloat16)
 
 
 def mixer_backward_kernel(idx, rates, *refs):
     blocks = refs[0:8]
-    wo, w_full, qkv, gate, att, rec, probs, pprobs, states, pk, pv = refs[8:19]
-    send, keep, dqkvg, branch, gpk, gpv = refs[19:25]
-    gm, dy, delta, ds, dk, dv, dsp = refs[25:32]
+    w_out, w_full, qkv, gate, att, rec, probs, pprobs, states, pk, pv = refs[8:19]
+    send, keep, dqkvg, branch = refs[19:23]
+    gm, dy, delta, ds, dk, dv, dsp = refs[23:30]
     x, f = idx[1], idx[2]
     head = 2 * f + x
     scale = HEAD_WIDTH_SIZE ** (-0.5)
+    wo = w_out[pl.ds(pl.multiple_of(x * 128, 128), 128), :]
     for k in range(8):
         hk = head_of(x, f, k)
         early = pl.ds(pl.multiple_of(hk * 64, 64), 64)
         late = pl.ds(pl.multiple_of((15 - hk) * 64, 64), 64)
         block = blocks[k][...]
-        grad = dot_nt(block, wo[...]).astype(jnp.bfloat16)
+        grad = dot_nt(block, wo).astype(jnp.bfloat16)
         gm[early, :] = grad[:64]
         gm[late, :] = grad[64:]
         branch[early, :] = block[:64]
@@ -799,8 +860,8 @@
         delta[rows, :] = (
             dot_nn(ds_tile, qkv[0:width, 128:256]) + dot_nn(dsp_tile, pk[...])
         ) * scale
-    gpk[...] = dot_tn(dsp[...], qkv[:, 0:128]) * scale
-    gpv[...] = dot_tn(pprobs[...], gm[...])
+    grad_pk = dot_tn(dsp[...], qkv[:, 0:128]) * scale
+    grad_pv = dot_tn(pprobs[...], gm[...])
     grad_state = jnp.zeros((128, 128), jnp.float32)
     grad_moment = jnp.zeros((128, 128), jnp.float32)
     for t in range(7, -1, -1):
@@ -844,40 +905,66 @@
             axis=0,
         )
         out = send if k & 1 else keep
-        out[k >> 1] = dot_nt(piece, w_full[...]).astype(jnp.bfloat16)
-
-
-def mixer_weights_kernel(idx, normed, dqkvg, mixed, branch, *refs):
-    outs, outs_o = refs[0:4], refs[4:8]
-    total, total_o = refs[8:10]
+        out[k >> 1, 0:128, :] = dot_nt(piece, w_full[...]).astype(jnp.bfloat16)
+        j = k & 3
+        extra = jnp.concatenate(
+            [
+                grad_pk[4 * j : 4 * j + 4],
+                grad_pv[4 * j : 4 * j + 4],
+                jnp.zeros((EXTRA - 8, 128), jnp.float32),
+            ],
+            axis=0,
+        )
+        out[k >> 1, 128 : 128 + EXTRA, :] = jnp.zeros((EXTRA, 1024), jnp.bfloat16)
+        out[k >> 1, 128 : 128 + EXTRA, pl.ds(pl.multiple_of(head * 128, 128), 128)] = extra.astype(
+            jnp.bfloat16
+        )
+
+
+def lay_chunk(out, rows, count, width):
+    out[256 : 256 + count, :] = rows[:, 0:width]
+    left = 1024 - width
+    part = count * left // width
+    for i in range(count // part):
+        out[256 + count : 256 + count + part, i * left : (i + 1) * left] = rows[
+            i * part : (i + 1) * part, width:1024
+        ]
+
+
+def lay_chunks(z, outs, total_rows, count, width):
+    for j in range(4):
+        first = pl.multiple_of((z ^ j) * count, 32)
+        rows = total_rows[pl.ds(first, count), :].astype(jnp.bfloat16)
+        lay_chunk(outs[j & 1].at[j >> 1], rows, count, width)
+
+
+def mixer_weights_kernel(idx, normed, dqkvg, mixed, branch, keep, send, total, total_o):
     z, f = idx[0], idx[2]
+    outs = (keep, send)
     for t in range(4):
         total[...] = dot_tn(normed[:, t * 256 : t * 256 + 256], dqkvg[...])
+        spot = pl.ds(pl.multiple_of((t ^ f) * 64, 64), 64)
         for j in range(4):
-            outs[j][t ^ f] = total[pl.ds(pl.multiple_of((z ^ j) * 64, 64), 64), :].astype(
-                jnp.bfloat16
-            )
+            outs[j & 1][j >> 1, spot, :] = total[
+                pl.ds(pl.multiple_of((z ^ j) * 64, 64), 64), :
+            ].astype(jnp.bfloat16)
     total_o[...] = dot_tn(mixed[...], branch[...])
-    for j in range(4):
-        outs_o[j][...] = total_o[pl.ds(pl.multiple_of((z ^ j) * 32, 32), 32), :].astype(
-            jnp.bfloat16
-        )
+    lay_chunks(z, outs, total_o, 32, 512)
 
 
 def feed_kernel(idx, *refs):
-    blocks, cots, parts = refs[0:8], refs[8:16], refs[16:20]
-    wd = refs[20]
-    send_g, keep_g, send_d, keep_d, active, dgu, feeds, cot_all = refs[21:29]
-    w_full = refs[29]
-    f = idx[2]
-    for j in range(4):
-        w_full[pl.ds(pl.multiple_of((f ^ j) * 256, 256), 256), :] = parts[j][...]
+    blocks, cots, parts = refs[0:8], refs[8:16], refs[16:22]
+    w_down = refs[22]
+    send_g, keep_g, send_d, keep_d, active, dgu = refs[23:29]
+    w_full, wd = refs[29:31]
+    z, x, f = idx[0], idx[1], idx[2]
+    lay_weights(z, f, parts, w_full)
+    wd[0:352, :] = w_down[pl.ds(pl.multiple_of(x * 352, 32), 352), :]
+    wd[352:HIDDEN_PAD, :] = jnp.zeros((HIDDEN_PAD - 352, 1024), jnp.bfloat16)
     for k in range(4):
         rows = slice(k * 256, k * 256 + 256)
         feed = jnp.concatenate([blocks[2 * k][...], blocks[2 * k + 1][...]], axis=0)
         cot = jnp.concatenate([cots[2 * k][...], cots[2 * k + 1][...]], axis=0)
-        feeds[rows, :] = feed
-        cot_all[rows, :] = cot
         gate_up = dot_nn(feed, w_full[...])
         g, u = gate_up[:, :HIDDEN_PAD], gate_up[:, HIDDEN_PAD:]
         sigma = jax.nn.sigmoid(g)
@@ -896,20 +983,30 @@
         send_d[k] = down[128:]
 
 
-def feed_weights_kernel(idx, feeds, dgu, active, cots, *refs):
-    outs, outs_d = refs[0:4], refs[4:8]
-    total, total_d = refs[8:10]
+def feed_weights_kernel(idx, dgu, active, *refs):
+    blocks, cot_blocks = refs[0:8], refs[8:16]
+    keeps, sends = refs[16:18], refs[18:20]
+    total, total_d, feeds, cots, laid = refs[20:25]
     z, f = idx[0], idx[2]
+    for k in range(8):
+        feeds[k * 128 : k * 128 + 128, :] = blocks[k][...]
+        cots[k * 128 : k * 128 + 128, :] = cot_blocks[k][...]
+    half = HIDDEN_PAD
     for t in range(4):
         total[...] = dot_tn(feeds[:, t * 256 : t * 256 + 256], dgu[...])
+        spot = pl.ds(pl.multiple_of((t ^ f) * 64, 64), 64)
         for j in range(4):
-            outs[j][t ^ f] = total[pl.ds(pl.multiple_of((z ^ j) * 64, 64), 64), :].astype(
-                jnp.bfloat16
-            )
+            rows = total[pl.ds(pl.multiple_of((z ^ j) * 64, 64), 64), :].astype(jnp.bfloat16)
+            outs = sends if j & 1 else keeps
+            outs[0][j >> 1, spot, :] = rows[:, 0:half]
+            outs[1][j >> 1, spot, :] = rows[:, half:]
     total_d[...] = dot_tn(active[...], cots[...])
     for j in range(4):
         first = pl.multiple_of((z ^ j) * Z_HIDDEN, 32)
-        outs_d[j][...] = total_d[pl.ds(first, Z_HIDDEN), :].astype(jnp.bfloat16)
+        lay_chunk(laid, total_d[pl.ds(first, Z_HIDDEN), :].astype(jnp.bfloat16), Z_HIDDEN, 768)
+        outs = sends if j & 1 else keeps
+        outs[0][j >> 1, 256:, :] = laid[256:, 0:half]
+        outs[1][j >> 1, 256:, :] = laid[256:, half:]
 
 
 def add_kernel(keep, received, s0, s1, s2, s3):
@@ -950,8 +1047,24 @@
     branch[...] = total.astype(jnp.bfloat16)
 
 
-def tokens_kernel(x, gain, grad_residual, s0, r1, r2, r3, out):
-    grad = total_of((s0, r1, r2, r3))
+def tokens_sum_kernel(keep, received, keep_far, keep_near, send_far):
+    keep_far[...] = keep[0].astype(jnp.float32) + received[0].astype(jnp.float32)
+    keep_near[...] = keep[1].astype(jnp.float32) + received[1].astype(jnp.float32)
+    for k in range(2):
+        send_far[k] = (keep[2 + k].astype(jnp.float32) + received[2 + k].astype(jnp.float32)).astype(
+            jnp.bfloat16
+        )
+
+
+def far_kernel(own, passed, received, out_own, out_passed):
+    out_own[...] = own[...] + received[0].astype(jnp.float32)
+    out_passed[...] = (passed[...] + received[1].astype(jnp.float32)).astype(jnp.bfloat16)
+
+
+def tokens_kernel(x, gain, grad_residual, own_sum, received, out, persist):
+    total = own_sum[...] + received[...].astype(jnp.float32)
+    grad = total[0:128]
+    persist[...] = total[128:136]
     values = x[...].astype(jnp.float32)
     out[...] = (grad_residual[...] + norm_grad(values, gain[...], grad)).astype(jnp.bfloat16)
 
@@ -960,35 +1073,29 @@
     out[...] = (residual[...] + total_of((s0, r1, r2, r3))).astype(jnp.bfloat16)
 
 
-def sum_parts_kernel(*refs):
-    wide, rows, outs, out_rows = refs[0:4], refs[4:8], refs[8:12], refs[12]
-    total = wide[0][...].astype(jnp.float32)
-    for part in wide[1:]:
-        total = total + part[...].astype(jnp.float32)
+def half_kernel(keep, received, own, passed):
+    own[...] = keep[0].astype(jnp.float32) + received[0].astype(jnp.float32)
+    passed[...] = (keep[1].astype(jnp.float32) + received[1].astype(jnp.float32)).astype(
+        jnp.bfloat16
+    )
+
+
+def whole_kernel(pieces, *refs):
+    own, received, outs = refs[:pieces], refs[pieces : 2 * pieces], refs[2 * pieces :]
+    total = [
+        (a[...] + b[...].astype(jnp.float32)).astype(jnp.bfloat16) for a, b in zip(own, received)
+    ]
+    total = jnp.concatenate(total, axis=1)
     for j in range(4):
-        outs[j][...] = total[j].astype(jnp.bfloat16)
-    total = rows[0][...].astype(jnp.float32)
-    for part in rows[1:]:
-        total = total + part[...].astype(jnp.float32)
-    out_rows[...] = total.astype(jnp.bfloat16)
+        outs[j][...] = total[j * 64 : j * 64 + 64]
+    outs[4][...] = total[256:]
 
 
 def join_kernel(*refs):
-    parts, rows, out = refs[0:4], refs[4], refs[5]
-    width = out.shape[1]
+    parts, rest, out = refs[0:4], refs[4], refs[5]
     for j in range(4):
         out[j * 64 : j * 64 + 64, :] = parts[j][...]
-    count = rows.shape[0]
-    out[256 : 256 + count, :] = rows[:, 0:width]
-    left = 1024 - width
-    if left == width:
-        out[256 + count : 256 + 2 * count, :] = rows[:, width:1024]
-    else:
-        third = count * left // width
-        for i in range(count // third):
-            out[256 + count : 256 + count + third, i * left : (i + 1) * left] = rows[
-                i * third : (i + 1) * third, width:1024
-            ]
+    out[256:, :] = rest[...]
 
 
 def row_sums(products, out):
@@ -999,24 +1106,16 @@
     parts = refs[0:8]
     wgu, gain = refs[8:10]
     out_gu, out_down, out_gain = refs[10:13]
+    laid = refs[13]
     z, x, f = idx[0], idx[1], idx[2]
     width = FF // 8
     for j in range(4):
         for dx in range(2):
             part = parts[2 * j + dx]
             zj, xj = z ^ j, x ^ dx
-            rows = pl.ds(pl.multiple_of(zj * 64, 64), 64)
             for jf in range(4):
                 head = 2 * (f ^ jf) + xj
-                for h in range(8):
-
-                    @pl.when(head == h)
-                    def _():
-                        for side in range(2):
-                            first = side * FF + h * width
-                            out_gu[rows, first : first + width] = part[
-                                jf * 64 : jf * 64 + 64, side * HIDDEN_PAD : side * HIDDEN_PAD + width
-                            ].astype(jnp.float32)
+                laid[zj, head] = part[jf * 64 : jf * 64 + 64, :]
 
             lower = part[256:352, :].astype(jnp.float32)
             upper = part[352:384, :].astype(jnp.float32)
@@ -1036,6 +1135,16 @@
             def _():
                 put(64, 32)
 
+    for zj in range(4):
+        for side in range(2):
+            rows = jnp.concatenate(
+                [
+                    laid[zj, head][:, side * HIDDEN_PAD : side * HIDDEN_PAD + width]
+                    for head in range(8)
+                ],
+                axis=1,
+            )
+            out_gu[zj * 64 : zj * 64 + 64, side * FF : side * FF + FF] = rows.astype(jnp.float32)
     sums = jnp.zeros((256, 128), jnp.float32)
     for t in range(2 * FF // 128):
         cols = slice(t * 128, t * 128 + 128)
@@ -1078,44 +1187,62 @@
     out_gain[...] = out_gain[...] / gain[...].astype(jnp.float32)
 
 
-def scatter_plane(keep, send):
-    received = flip(send, 0, 1)
-    block = (128, 1024)
-    s0, s1, s2, s3 = call(
+def sum_cores(keep, send):
+    block = keep.shape[1:]
+    return call(
         add_kernel,
         (),
-        (keep, received),
+        (keep, flip(send, 0, 1)),
         [(block, jnp.float32)] + [(block, jnp.bfloat16)] * 3,
         name="core_sum",
     )
+
+
+def cross_chips(s0, s1, s2, s3):
     return s0, flip(s1, 0, 2), flip(s2, 1, 0), flip(s3, 1, 2)
 
 
-def reduce_parts(wide, rows, width, name):
-    wide = [wide[0]] + [flip_z(wide[j], j) for j in range(1, 4)]
-    rows = [rows[0]] + [flip_z(rows[j], j) for j in range(1, 4)]
-    count = rows[0].shape[0]
-    *parts, row_total = call(
-        sum_parts_kernel,
+def half_sum(keep, received, name):
+    _, rows, width = keep.shape
+    return call(
+        half_kernel,
         (),
-        (*wide, *rows),
-        [((64, width), jnp.bfloat16)] * 4 + [((count, 1024), jnp.bfloat16)],
-        name=name + "_sum",
-    )
-    parts = [parts[0]] + [flip(parts[j], 0, j) for j in range(1, 4)]
-    extra = count * 1024 // width
+        (keep, received),
+        [((rows, width), jnp.float32), ((rows, width), jnp.bfloat16)],
+        name=name + "_half",
+    )
+
+
+def whole_sum(own, moved, name):
+    rows = own[0].shape[0]
+    width = sum(piece.shape[1] for piece in own)
+    return call(
+        functools.partial(whole_kernel, len(own)),
+        (),
+        (*own, *moved),
+        [((64, width), jnp.bfloat16)] * 4 + [((rows - 256, width), jnp.bfloat16)],
+        name=name + "_whole",
+    )
+
+
+def hand_rows(parts):
+    return [parts[0]] + [flip(parts[j], 0, j) for j in range(1, 4)]
+
+
+def join(parts, rest, name):
+    rows, width = 256 + rest.shape[0], rest.shape[1]
     (joined,) = call(
-        join_kernel,
-        (),
-        (*parts, row_total),
-        [((256 + extra, width), jnp.bfloat16)],
-        name=name + "_join",
-    )
-    near = [joined] + [flip_z(joined, j) for j in range(1, 4)]
-    result = []
-    for piece in near:
-        result += [piece, flip(piece, 1, 0)]
-    return result
+        join_kernel, (), (*parts, rest), [((rows, width), jnp.bfloat16)], name=name + "_join"
+    )
+    return joined
+
+
+def spread_far(joined):
+    return flip_z(joined, 2), flip_z(joined, 1)
+
+
+def halves_from_next_plane(parts):
+    return list(parts) + [flip_z(parts[2], 1), flip_z(parts[3], 1)]
 
 
 def in_planes(
@@ -1147,41 +1274,46 @@
             10, 128
         )
     )
-    small = jnp.concatenate(
-        [
-            persist_keys,
-            persist_values,
-            jnp.concatenate([norm_gain, ffn_gain, norm_gain, ffn_gain]).reshape(1, 1024),
-            jnp.zeros((7, 1024), bf16),
-        ],
-        axis=0,
-    )
-    wq_parts = call(
-        pack_qkvg_kernel, (idx,), (w_qkv, w_gate), [((256, 512), bf16)] * 4, name="pack_qkvg"
-    )
-    wq_parts = [wq_parts[0]] + [flip(wq_parts[j], 0, j) for j in range(1, 4)]
-    smalls = jnp.stack([small] + [flip(small, 0, j) for j in range(1, 4)])
-    blocks = gather_plane(own)
-    own_cot = to_plane(cotangent[0])
-    gu_parts = call(pack_gu_kernel, (idx,), (w_gu,), [((256, 768), bf16)] * 4, name="pack_gu")
-    gu_parts = [gu_parts[0]] + [flip(gu_parts[j], 0, j) for j in range(1, 4)]
-    cots = gather_plane(own_cot)
-
-    smalls = jnp.stack(
-        [lax.dynamic_index_in_dim(smalls, f ^ j, 0, keepdims=False) for j in range(4)]
-    )
-    gain_one = smalls[:, 8, 0:256].reshape(1, 1024).astype(f32)
-    gain_two = smalls[:, 8, 256:512].reshape(1, 1024).astype(f32)
-    pk = lax.dynamic_slice_in_dim(smalls[:, 0:4].reshape(16, 1024), head * 128, 128, 1)
-    pv = lax.dynamic_slice_in_dim(smalls[:, 4:8].reshape(16, 1024), head * 128, 128, 1)
+    anywhere = pl.BlockSpec(memory_space=pl.ANY)
+    wq_parts = pl.pallas_call(
+        pack_qkvg_kernel,
+        out_shape=[jax.ShapeDtypeStruct((256 + EXTRA, 512), bf16)] * 4,
+        in_specs=[sspec(), anywhere, anywhere] + [vspec()] * 4,
+        out_specs=[vspec()] * 4,
+        scratch_shapes=[pltpu.SemaphoreType.DMA((16,))],
+        compiler_params=pltpu.CompilerParams(vmem_limit_bytes=60 * 1024 * 1024),
+        cost_estimate=pl.CostEstimate(flops=1000, bytes_accessed=1000, transcendentals=0),
+        name="pack_qkvg",
+    )(
+        idx,
+        w_qkv,
+        w_gate,
+        persist_keys,
+        persist_values,
+        norm_gain.reshape(1, 256),
+        ffn_gain.reshape(1, 256),
+    )
+    gu_parts = call(
+        pack_gu_kernel,
+        (idx,),
+        (w_gu,),
+        [((256, 768), bf16)] * 2 + [((128, 768), bf16)] * 2,
+        name="pack_gu",
+    )
     rates = jnp.stack(
         [0.6 * jnp.exp2(-ints[8].astype(f32)), 0.1 * jnp.exp2(-ints[9].astype(f32))]
     )
-    wo = lax.dynamic_slice_in_dim(w_out, x * 128, 128, 0)
-    wd = jnp.pad(
-        lax.dynamic_slice_in_dim(w_down, x * 352, 352, 0), ((0, HIDDEN_PAD - 352), (0, 0))
-    )
-
+    wq_parts = hand_rows(wq_parts)
+    own = after(own, wq_parts[0], gu_parts[0], rates)
+    near = gather_chips(own)
+    own_cot = to_plane(after(cotangent[0], own))
+    gu_parts = [after(w, own) for w in gu_parts]
+    gu_parts = [gu_parts[0], gu_parts[1], flip(gu_parts[2], 0, 2), flip(gu_parts[3], 0, 3)]
+    blocks = gather_cores(near)
+    rates = after(rates, own_cot)
+    cot_near = gather_chips(after(own_cot, near[2]))
+
+    block = (128, 1024)
     quad = ((4, 128, 1024), bf16)
     (
         send,
@@ -1196,10 +1328,14 @@
         pprobs,
         states,
         mixed,
+        gain_one,
+        gain_two,
+        pk,
+        pv,
     ) = call(
         mixer_forward_kernel,
         (idx, rates),
-        (ints, *blocks, *wq_parts, gain_one, wo, pk, pv),
+        (ints, *blocks, *wq_parts, w_out),
         [
             quad,
             quad,
@@ -1213,24 +1349,33 @@
             ((1024, 16), bf16),
             ((16, 128, 128), bf16),
             ((1024, 128), bf16),
+            ((1, 1024), f32),
+            ((1, 1024), f32),
+            ((16, 128), bf16),
+            ((16, 128), bf16),
         ],
-        flops=3 * 10**9,
         name="mixer_forward",
-    )
-    shares = scatter_plane(keep, send)
-    block = (128, 1024)
+        spare=10,
+        us=10.0,
+    )
+    send = after(send, *cot_near[1:], gu_parts[2], gu_parts[3])
+    sums = sum_cores(keep, send)
+    shares = cross_chips(*sums)
+    gu_parts[1] = flip(gu_parts[1], 0, 1)
+    gu_parts = halves_from_next_plane(gu_parts)
+    cots = gather_cores(cot_near)
     residual, feed = call(
         residual_kernel,
         (),
-        (own, gain_two, *shares),
+        (after(own, *gu_parts), gain_two, *shares),
         [(block, f32), (block, bf16)],
         name="residual",
     )
-    feeds = gather_plane(feed)
-    send_g, keep_g, send_d, keep_d, active, dgu, feed_all, cot_all = call(
+    feeds = gather_cores(gather_chips(feed))
+    send_g, keep_g, send_d, keep_d, active, dgu = call(
         feed_kernel,
         (idx,),
-        (*feeds, *cots, *gu_parts, wd),
+        (*feeds, *cots, *gu_parts, w_down),
         [
             quad,
             quad,
@@ -1238,14 +1383,33 @@
             quad,
             ((1024, HIDDEN_PAD), bf16),
             ((1024, 2 * HIDDEN_PAD), bf16),
+        ],
+        scratch=[((1024, 2 * HIDDEN_PAD), bf16), ((HIDDEN_PAD, 1024), bf16)],
+        name="feed",
+        spare=10,
+        us=7.5,
+    )
+    feed_keep, feed_later_keep, feed_send, feed_later_send = call(
+        feed_weights_kernel,
+        (idx,),
+        (dgu, active, *feeds, *cots),
+        [((2, 256 + 4 * Z_HIDDEN // 3, HIDDEN_PAD), bf16)] * 4,
+        scratch=[
+            ((256, 768), f32),
+            ((HIDDEN_PAD, 1024), f32),
             ((1024, 1024), bf16),
             ((1024, 1024), bf16),
+            ((256 + 4 * Z_HIDDEN // 3, 768), bf16),
         ],
-        scratch=[((1024, 2 * HIDDEN_PAD), bf16)],
-        flops=5 * 10**9,
-        name="feed",
-    )
-    shares = scatter_plane(keep_g, send_g)
+        name="feed_weights",
+        spare=10,
+        us=3.5,
+    )
+    sums = sum_cores(after(keep_g, feed_send), send_g)
+    send_d = after(send_d, sums[0])
+    shares = cross_chips(*sums)
+    feed_received = flip_z(feed_send, 1)
+    feed_later_received = flip_z(after(feed_later_send, sums[0]), 1)
     grad_residual, branch = call(
         branch_kernel,
         (),
@@ -1253,34 +1417,29 @@
         [(block, f32), (block, bf16)],
         name="branch",
     )
-    branches = gather_plane(branch)
-
-    feed_parts = call(
-        feed_weights_kernel,
-        (idx,),
-        (feed_all, dgu, active, cot_all),
-        [((4, 64, 768), bf16)] * 4 + [((Z_HIDDEN, 1024), bf16)] * 4,
-        scratch=[((256, 768), f32), ((HIDDEN_PAD, 1024), f32)],
-        flops=3 * 10**9,
-        name="feed_weights",
-    )
-    feed_pieces = reduce_parts(feed_parts[0:4], feed_parts[4:8], 768, "feed")
-
-    shares = scatter_plane(keep_d, send_d)
-    (result,) = call(output_kernel, (), (residual, *shares), [(block, bf16)], name="output")
-    result = to_plane(result)
-
-    send, keep, dqkvg, branch_all, gpk, gpv = call(
+    feed_own, feed_passed = half_sum(after(feed_keep, branch), feed_received, "feed")
+    branch_near = gather_chips(branch, after(branch, feed_passed))
+    keep_d = after(keep_d, feed_passed)
+    out_sums = sum_cores(keep_d, send_d)
+    feed_moved = flip_z(feed_passed, 2)
+    branches = gather_cores([after(piece, feed_moved) for piece in branch_near])
+    feed_later, feed_later_passed = half_sum(
+        after(feed_later_keep, out_sums[0]), feed_later_received, "feed_later"
+    )
+    rates = after(rates, feed_later_passed)
+    feed_later_moved = flip_z(feed_later_passed, 2)
+    out_sums = lax.optimization_barrier((*out_sums, branches[6]))[:4]
+    out_shares = cross_chips(*out_sums)
+
+    send, keep, dqkvg, branch_all = call(
         mixer_backward_kernel,
         (idx, rates),
-        (*branches, wo, w_full, qkv, gate, att, rec, probs, pprobs, states, pk, pv),
+        (*branches, w_out, w_full, qkv, gate, att, rec, probs, pprobs, states, pk, pv),
         [
-            quad,
-            quad,
+            ((4, 128 + EXTRA, 1024), bf16),
+            ((4, 128 + EXTRA, 1024), bf16),
             ((1024, 512), bf16),
             ((1024, 1024), bf16),
-            ((16, 128), f32),
-            ((16, 128), f32),
         ],
         scratch=[
             ((1024, 128), bf16),
@@ -1291,45 +1450,128 @@
             ((1024, 128), f32),
             ((1024, 16), bf16),
         ],
-        flops=4 * 10**9,
         name="mixer_backward",
-    )
-    mixer_parts = call(
+        spare=10,
+        us=13.0,
+    )
+    send, dqkvg = lax.optimization_barrier(
+        (send, dqkvg, feed_later_moved, *out_shares[1:])
+    )[:2]
+    *feed_parts, feed_rest = whole_sum(
+        (after(feed_own, send), feed_later), (feed_moved, feed_later_moved), "feed"
+    )
+    feed_parts = hand_rows(feed_parts)
+    dqkvg = after(dqkvg, feed_rest)
+    mixer_keep, mixer_send = call(
         mixer_weights_kernel,
         (idx,),
         (normed, dqkvg, mixed, branch_all),
-        [((4, 64, 512), bf16)] * 4 + [((32, 1024), bf16)] * 4,
+        [((2, 320, 512), bf16)] * 2,
         scratch=[((256, 512), f32), ((128, 1024), f32)],
-        flops=2 * 10**9,
         name="mixer_weights",
-    )
-    shares = scatter_plane(keep, send)
-    mixer_pieces = reduce_parts(mixer_parts[0:4], mixer_parts[4:8], 512, "mixer")
-    (grad_tokens,) = call(
-        tokens_kernel, (), (own, gain_one, grad_residual, *shares), [(block, bf16)], name="tokens"
+        spare=10,
+        us=2.2,
+    )
+    (result,) = call(output_kernel, (), (residual, *out_shares), [(block, bf16)], name="output")
+    result = to_plane(after(result, mixer_send))
+    feed_joined = join(feed_parts, after(feed_rest, mixer_send), "feed")
+    feed_second, feed_first = spread_far(feed_joined)
+    feed_beside = flip(feed_joined, 1, 0)
+    rows = (128 + EXTRA, 1024)
+    keep_far, keep_near, send_far = call(
+        tokens_sum_kernel,
+        (),
+        (after(keep, feed_joined), flip(send, 0, 1)),
+        [(rows, f32), (rows, f32), ((2, *rows), bf16)],
+        name="tokens_sum",
+    )
+    mixer_own, mixer_passed = half_sum(
+        after(mixer_keep, keep_near, result), flip_z(mixer_send, 1), "mixer"
+    )
+    mixer_moved = flip_z(mixer_passed, 2)
+    tokens_far = flip(after(send_far, mixer_passed), 1, 0)
+    feed_first_beside = flip(after(feed_first, feed_beside), 1, 0)
+    mixer_own = after(mixer_own, feed_second, feed_first_beside, tokens_far)
+    *mixer_parts, mixer_rest = whole_sum((mixer_own,), (mixer_moved,), "mixer")
+    feed_third = flip_z(after(feed_second, mixer_rest), 1)
+    feed_second_beside = flip(after(feed_second, mixer_rest), 1, 0)
+    mixer_joined = join(hand_rows(mixer_parts), mixer_rest, "mixer")
+    mixer_second, mixer_first = spread_far(mixer_joined)
+    mixer_beside = flip(mixer_joined, 1, 0)
+    feed_third_beside = flip(after(feed_third, mixer_joined), 1, 0)
+    tokens_own, tokens_passed = call(
+        far_kernel,
+        (),
+        (after(keep_far, mixer_joined), keep_near, tokens_far),
+        [((128 + EXTRA, 1024), f32), ((128 + EXTRA, 1024), bf16)],
+        name="tokens_far",
+    )
+    tokens_near = flip(tokens_passed, 0, 2)
+    mixer_second = after(
+        mixer_second,
+        mixer_first,
+        mixer_beside,
+        feed_second_beside,
+        feed_third_beside,
+        tokens_near,
+    )
+    mixer_third = flip_z(mixer_second, 1)
+    mixer_first_beside = flip(after(mixer_first, mixer_second), 1, 0)
+    mixer_second_beside = flip(mixer_second, 1, 0)
+    grad_tokens, persist = call(
+        tokens_kernel,
+        (),
+        (after(own, mixer_second), gain_one, grad_residual, tokens_own, tokens_near),
+        [(block, bf16), ((8, 1024), f32)],
+        name="tokens",
     )
     grad_tokens = to_plane(grad_tokens)
-
-    persist = jnp.concatenate([gpk, gpv], axis=0)
-    persist = lax.dynamic_update_slice_in_dim(
-        jnp.zeros((32, 1024), f32), persist, head * 128, 1
-    )
-    persist = lax.psum(persist, ("ctx", "fsdp"))
-    grad_pk = lax.dynamic_slice_in_dim(persist, f * 4, 4, 0)
-    grad_pv = lax.dynamic_slice_in_dim(persist, 16 + f * 4, 4, 0)
+    persist = persist + flip_z(persist, 1)
+    feed_pieces = (
+        feed_joined,
+        feed_beside,
+        feed_first,
+        feed_first_beside,
+        feed_second,
+        feed_second_beside,
+        feed_third,
+        feed_third_beside,
+    )
 
     grad_gu, grad_down, grad_ffn = call(
         feed_unpack_kernel,
         (idx,),
-        (*feed_pieces, w_gu, ffn_gain.reshape(1, 256)),
+        (*feed_pieces, w_gu, after(ffn_gain.reshape(1, 256), mixer_second)),
         [((256, 2 * FF), f32), ((FF // 4, 1024), f32), ((1, 256), f32)],
+        scratch=[((4, 8, 64, 768), bf16)],
         name="feed_unpack",
+        spare=10,
+        us=5.5,
+    )
+    mixer_third_beside = flip(
+        after(mixer_third, grad_ffn, mixer_first_beside, mixer_second_beside, persist), 1, 0
+    )
+    persist = persist + flip_z(persist, 2)
+    mixer_pieces = (
+        mixer_joined,
+        mixer_beside,
+        mixer_first,
+        mixer_first_beside,
+        mixer_second,
+        mixer_second_beside,
+        mixer_third,
+        mixer_third_beside,
     )
     grad_qkv, grad_gate, grad_out, grad_norm = call(
         mixer_unpack_kernel,
         (idx,),
         (*mixer_pieces, w_qkv, w_gate, norm_gain.reshape(1, 256)),
-        [((256, 3072), f32), ((256, 1024), f32), ((256, 1024), f32), ((1, 256), f32)],
+        [
+            ((256, 3072), f32),
+            ((256, 1024), f32),
+            ((256, 1024), f32),
+            ((1, 256), f32),
+        ],
         name="mixer_unpack",
     )
     return (
@@ -1340,8 +1582,8 @@
         grad_out,
         grad_gu,
         grad_down,
-        grad_pk,
-        grad_pv,
+        persist[0:4],
+        persist[4:8],
         grad_norm.reshape(256),
         grad_ffn.reshape(256),
     )

time: 547 us -> 338 us (0.62); the launches traced: 537 us -> 335 us
  waiting for transfers between devices: 265 us -> 188 us
  Pallas kernels: 108 us -> 52.2 us
  starting transfers between devices: 129 us -> 83.9 us
  between operations: 15.3 us -> 1.57 us
  local copies, waits for them, and re-layouts: 13.6 us -> 7.32 us
    psum x1 -> x0, waiting for transfers between devices: 111 us -> none  [in_planes(): persist = lax.psum(persist, ('ctx', 'fsdp'))]
    pallas_call x21 -> x25, Pallas kernels: 108 us -> 52.2 us  [the longest x24 49 us: call(): pl.pallas_call(kernel, out_shape=[jax.ShapeDtypeStruct(shape, dtype) for...]
    ppermute x90 -> x84, starting transfers between devices: 128 us -> 83.9 us  [shift(): return lax.ppermute(value, ('ctx', 'fsdp'), pairs)]
    ppermute x90 -> x84, waiting for transfers between devices: 153 us -> 188 us  [shift(): return lax.ppermute(value, ('ctx', 'fsdp'), pairs)]
  transfers between devices with their start and end apart: 91 -> 84, of which waited for: 26 -> 34; matrix products, arithmetic and copies ran while one was open for 2% -> 1% of each run, Pallas kernels for 15% -> 12%
where the time goes in v2:
time: 338 us; the launch traced here: 335 us
  waiting for transfers between devices  188 us (56%)
  starting transfers between devices  83.9 us (25%)
  Pallas kernels  52.2 us (15%)
  local copies, waits for them, and re-layouts  7.32 us (2%)
    ppermute x84, waiting for transfers between devices, shift(): return lax.ppermute(value, ('ctx', 'fsdp'), pairs)  188 us
    ppermute x84, starting transfers between devices, shift(): return lax.ppermute(value, ('ctx', 'fsdp'), pairs)  83.9 us
    pallas_call x24, Pallas kernels, call(): pl.pallas_call(kernel, out_shape=[jax.ShapeDtypeStruct(shape, dtype) for...  49 us
  transfers between devices with their start and end apart: 84, of which 34 were waited for; matrix products, arithmetic and copies ran while one was open for 1% of the time, Pallas kernels for 12%

profile of v2, /device:TPU:0, one launch (start us, length us, event | category | flops | bytes accessed | tf_op | source)
XLA Modules:
  0.0 334.8 jit_solution(1095597286601376167)
XLA Ops:
  8.3 3.2 pack_qkvg.1
  11.6 4.8 %collective-permute-start.15 = (bf16[272,512]{1,0:T(8,128)(2,1)}, bf16[272,512]{1,0:T(8,128)(2,1)S(1)}, u32[]{:S(2)}, u32[]{:S(2)}) collective-permute-start(bf16[272,512]{1,0:T(8,128)(2,1)} %get-tuple-element.155), channel_id=1, source_target_pairs={{0,1},{1,0},{2,3},{3,2},{4,5},{5,4},{6,7},{7,6},{8,9},{9,8},{10,11... | collective-permute-start | bytes 835592 | tf_op jit(solution)/shard_map/ppermute | solution.py:589
  16.3 4.1 %collective-permute-start.16 = (bf16[272,512]{1,0:T(8,128)(2,1)}, bf16[272,512]{1,0:T(8,128)(2,1)S(1)}, u32[]{:S(2)}, u32[]{:S(2)}) collective-permute-start(bf16[272,512]{1,0:T(8,128)(2,1)} %get-tuple-element.156), channel_id=1, source_target_pairs={{0,2},{1,3},{2,0},{3,1},{4,6},{5,7},{6,4},{7,5},{8,10},{9,11},{10,... | collective-permute-start | bytes 835592 | tf_op jit(solution)/shard_map/ppermute | solution.py:589
  20.4 1.8 copy-done.1
  24.3 6.0 %collective-permute-start.13 = (bf16[128,1024]{1,0:T(8,128)(2,1)S(1)}, bf16[128,1024]{1,0:T(8,128)(2,1)S(1)}, u32[]{:S(2)}, u32[]{:S(2)}) collective-permute-start(bf16[128,1024]{1,0:T(8,128)(2,1)S(1)} %collective-permute-done.refs_0_.x), channel_id=1, source_target_pairs={{0,6},{1,7},{2,4},{3,5},{4,2},{5,3},{6,0},{7,1},{8,14},{9,15},{10,... | collective-permute-start | bytes 786440 | tf_op jit(solution)/shard_map/ppermute | solution.py:589
  30.9 10.3 %collective-permute-done.16.refs_10_ = bf16[272,512]{1,0:T(8,128)(2,1)S(1)} collective-permute-done((bf16[272,512]{1,0:T(8,128)(2,1)}, bf16[272,512]{1,0:T(8,128)(2,1)S(1)}, u32[]{:S(2)}, u32[]{:S(2)}) %collective-permute-start.16) | collective-permute-done | bytes 278560 | tf_op jit(solution)/shard_map/ppermute | solution.py:589
  44.5 2.4 collective-permute-done.9.refs_2_
  46.9 5.5 %collective-permute-done.17.refs_11_ = bf16[272,512]{1,0:T(8,128)(2,1)S(1)} collective-permute-done((bf16[272,512]{1,0:T(8,128)(2,1)S(1)}, bf16[272,512]{1,0:T(8,128)(2,1)S(1)}, u32[]{:S(2)}, u32[]{:S(2)}) %collective-permute-start.17) | collective-permute-done | bytes 278560 | tf_op jit(solution)/shard_map/ppermute | solution.py:589
  52.4 2.0 collective-permute-start.3
  54.5 2.8 collective-permute-start.20
  58.1 10.1 %mixer_forward.1 = (bf16[4,128,1024]{2,1,0:T(8,128)(2,1)S(1)}, bf16[4,128,1024]{2,1,0:T(8,128)(2,1)S(1)}, bf16[1024,1024]{1,0:T(8,128)(2,1)S(1)}, bf16[1024,512]...) custom-call(s32[4]{0:T(128)S(1)} %copy-done.4, ...), custom_call_target="tpu_custom_call" | custom-call | flops 11000000512 | bytes 1000 | tf_op jit(solution)/shard_map/mixer_forward/pallas_call | solution.py:654
  69.9 5.3 %collective-permute-done.18.refs_10_ = bf16[128,1024]{1,0:T(8,128)(2,1)S(1)} collective-permute-done((bf16[128,1024]{1,0:T(8,128)(2,1)S(1)}, bf16[128,1024]{1,0:T(8,128)(2,1)S(1)}, u32[]{:S(2)}, u32[]{:S(2)}) %collective-permute-start.18) | collective-permute-done | bytes 262176 | tf_op jit(solution)/shard_map/ppermute | solution.py:589
  75.2 2.3 collective-permute-start.5
  78.1 1.8 collective-permute-start.22
  79.9 1.8 collective-permute-start.23
  83.3 2.7 collective-permute-start.24
  89.1 4.4 %collective-permute-done.24.r3 = bf16[128,1024]{1,0:T(8,128)(2,1)S(1)} collective-permute-done((bf16[128,1024]{1,0:T(8,128)(2,1)S(1)}, bf16[128,1024]{1,0:T(8,128)(2,1)S(1)}, u32[]{:S(2)}, u32[]{:S(2)}) %collective-permute-start.24) | collective-permute-done | bytes 262176 | tf_op jit(solution)/shard_map/ppermute | solution.py:589
  93.8 2.8 collective-permute-start.30
  97.9 6.2 %collective-permute-done.30.refs_6_ = bf16[128,1024]{1,0:T(8,128)(2,1)S(1)} collective-permute-done((bf16[128,1024]{1,0:T(8,128)(2,1)S(1)}, bf16[128,1024]{1,0:T(8,128)(2,1)S(1)}, u32[]{:S(2)}, u32[]{:S(2)}) %collective-permute-start.30) | collective-permute-done | bytes 262176 | tf_op jit(solution)/shard_map/ppermute | solution.py:589
  104.1 3.9 %collective-permute-done.28.refs_4_ = bf16[128,1024]{1,0:T(8,128)(2,1)S(1)} collective-permute-done((bf16[128,1024]{1,0:T(8,128)(2,1)S(1)}, bf16[128,1024]{1,0:T(8,128)(2,1)S(1)}, u32[]{:S(2)}, u32[]{:S(2)}) %collective-permute-start.28) | collective-permute-done | bytes 262176 | tf_op jit(solution)/shard_map/ppermute | solution.py:589
  109.8 7.2 %feed.1 = (bf16[4,128,1024]{2,1,0:T(8,128)(2,1)S(1)}, bf16[4,128,1024]{2,1,0:T(8,128)(2,1)S(1)}, bf16[4,128,1024]{2,1,0:T(8,128)(2,1)S(1)}, bf16[4,128,1024]{2,1...) custom-call(s32[4]{0:T(128)S(1)} %copy-done.4, ...), custom_call_target="tpu_custom_call" | custom-call | flops 8249999872 | bytes 1000 | tf_op jit(solution)/shard_map/feed/pallas_call | solution.py:654
  117.3 3.5 %feed_weights.1 = (bf16[2,384,384]{2,1,0:T(8,128)(2,1)S(1)}, bf16[2,384,384]{2,1,0:T(8,128)(2,1)S(1)}, bf16[2,384,384]{2,1,0:T(8,128)(2,1)S(1)}, bf16[2,384,384]{2,1,0:T(8,128)(2,1)S(1)}) custom-call(s32[4]{0:T(128)S(1)} %copy-done.4, bf16[1024,768]{1,0:T(8,128)(2,1)S(1)} %get-tuple-element.170.dgu, bf16[1024,384]{1,0:T(8,128)(2,1)S(1)} %get-tuple-element.171.active, ...), custom_call_target="tpu_custom_call" | custom-call | flops 3849999872 | bytes 1000 | tf_op jit(solution)/shard_map/feed_weights/pallas_call | solution.py:654
  121.5 2.1 collective-permute-start.40
  127.1 4.8 %collective-permute-done.37.r1 = bf16[128,1024]{1,0:T(8,128)(2,1)S(1)} collective-permute-done((bf16[128,1024]{1,0:T(8,128)(2,1)S(1)}, bf16[128,1024]{1,0:T(8,128)(2,1)S(1)}, u32[]{:S(2)}, u32[]{:S(2)}) %collective-permute-start.37) | collective-permute-done | bytes 262176 | tf_op jit(solution)/shard_map/ppermute | solution.py:589
  131.9 2.0 collective-permute-done.38.r2
  133.9 4.6 %collective-permute-done.39.r3 = bf16[128,1024]{1,0:T(8,128)(2,1)S(1)} collective-permute-done((bf16[128,1024]{1,0:T(8,128)(2,1)S(1)}, bf16[128,1024]{1,0:T(8,128)(2,1)S(1)}, u32[]{:S(2)}, u32[]{:S(2)}) %collective-permute-start.39) | collective-permute-done | bytes 262176 | tf_op jit(solution)/shard_map/ppermute | solution.py:589
  140.8 1.7 collective-permute-start.43
  143.5 4.7 %collective-permute-done.51.refs_4_ = bf16[128,1024]{1,0:T(8,128)(2,1)S(1)} collective-permute-done((bf16[128,1024]{1,0:T(8,128)(2,1)S(1)}, bf16[128,1024]{1,0:T(8,128)(2,1)S(1)}, u32[]{:S(2)}, u32[]{:S(2)}) %collective-permute-start.51) | collective-permute-done | bytes 262176 | tf_op jit(solution)/shard_map/ppermute | solution.py:589
  149.2 9.3 %collective-permute-done.43.refs_2_ = bf16[384,384]{1,0:T(8,128)(2,1)S(1)} collective-permute-done((bf16[384,384]{1,0:T(8,128)(2,1)S(1)}, bf16[384,384]{1,0:T(8,128)(2,1)S(1)}, u32[]{:S(2)}, u32[]{:S(2)}) %collective-permute-start.43) | collective-permute-done | bytes 294944 | tf_op jit(solution)/shard_map/ppermute | solution.py:589
  160.5 2.8 collective-permute-start.54
  164.9 1.9 collective-permute-start.46
  166.8 13.2 %mixer_backward.1 = (bf16[4,144,1024]{2,1,0:T(8,128)(2,1)S(1)}, bf16[4,144,1024]{2,1,0:T(8,128)(2,1)S(1)}, bf16[1024,512]{1,0:T(8,128)(2,1)S(1)}, bf16[1024,1024]{1,0:T(8,128)(2,1)S(1)}) custom-call(s32[4]{0:T(128)S(1)} %copy-done.4, f32[2,128]{1,0:T(2,128)S(1)} %pad_maximum_fusion.rates, bf16[128,1024]{1,0:T(8,128)(2,1)S(1)} %get-tuple-element.204.refs_0_, ...), custom_call_target="tpu_custom_call" | custom-call | flops 14300000256 | bytes 1000 | tf_op jit(solution)/shard_map/mixer_backward/pallas_call | solution.py:654
  182.3 2.2 mixer_weights.1
  184.5 1.8 collective-permute-done.57.refs_2_
  188.5 14.4 %collective-permute-done.63.refs_1_ = bf16[384,768]{1,0:T(8,128)(2,1)S(1)} collective-permute-done((bf16[384,768]{1,0:T(8,128)(2,1)S(1)}, bf16[384,768]{1,0:T(8,128)(2,1)S(1)}, u32[]{:S(2)}, u32[]{:S(2)}) %collective-permute-start.63) | collective-permute-done | bytes 589856 | tf_op jit(solution)/shard_map/ppermute | solution.py:589
  203.0 25.2 %collective-permute-done.62.refs_2_ = bf16[384,768]{1,0:T(8,128)(2,1)S(1)} collective-permute-done((bf16[384,768]{1,0:T(8,128)(2,1)S(1)}, bf16[384,768]{1,0:T(8,128)(2,1)S(1)}, u32[]{:S(2)}, u32[]{:S(2)}) %collective-permute-start.62) | collective-permute-done | bytes 589856 | tf_op jit(solution)/shard_map/ppermute | solution.py:589
  230.7 14.6 %collective-permute-done.61.refs_4_ = bf16[384,768]{1,0:T(8,128)(2,1)S(1)} collective-permute-done((bf16[384,768]{1,0:T(8,128)(2,1)S(1)}, bf16[384,768]{1,0:T(8,128)(2,1)S(1)}, u32[]{:S(2)}, u32[]{:S(2)}) %collective-permute-start.61) | collective-permute-done | bytes 589856 | tf_op jit(solution)/shard_map/ppermute | solution.py:589
  245.3 10.6 %collective-permute-done.65.received = bf16[2,144,1024]{2,1,0:T(8,128)(2,1)S(1)} collective-permute-done((bf16[2,144,1024]{2,1,0:T(8,128)(2,1)S(1)}, bf16[2,144,1024]{2,1,0:T(8,128)(2,1)S(1)}, u32[]{:S(2)}, u32[]{:S(2)}) %collective-permute-start.65) | collective-permute-done | bytes 589856 | tf_op jit(solution)/shard_map/ppermute | solution.py:589
  256.2 1.8 collective-permute-start.69
  258.0 3.1 collective-permute-done.68.refs_2_
  263.1 7.2 %collective-permute-done.74.refs_6_ = bf16[384,768]{1,0:T(8,128)(2,1)S(1)} collective-permute-done((bf16[384,768]{1,0:T(8,128)(2,1)S(1)}, bf16[384,768]{1,0:T(8,128)(2,1)S(1)}, u32[]{:S(2)}, u32[]{:S(2)}) %collective-permute-start.74) | collective-permute-done | bytes 589856 | tf_op jit(solution)/shard_map/ppermute | solution.py:589
  273.7 23.9 %collective-permute-done.72.refs_1_ = bf16[320,512]{1,0:T(8,128)(2,1)S(1)} collective-permute-done((bf16[320,512]{1,0:T(8,128)(2,1)S(1)}, bf16[320,512]{1,0:T(8,128)(2,1)S(1)}, u32[]{:S(2)}, u32[]{:S(2)}) %collective-permute-start.72) | collective-permute-done | bytes 327712 | tf_op jit(solution)/shard_map/ppermute | solution.py:589
  297.9 1.9 collective-permute-start.81
  302.8 5.1 %collective-permute-start.83 = (f32[8,1024]{1,0:T(8,128)S(1)}, f32[8,1024]{1,0:T(8,128)S(1)}, u32[]{:S(2)}, u32[]{:S(2)}) collective-permute-start(f32[8,1024]{1,0:T(8,128)S(1)} %add.16), channel_id=1, source_target_pairs={{0,16},{1,17},{2,18},{3,19},{4,20},{5,21},{6,22},{7,23},{8,24},{9,... | collective-permute-start | bytes 98312 | tf_op jit(solution)/shard_map/ppermute | solution.py:589
  307.9 5.5 %feed_unpack.1 = (f32[256,5632]{1,0:T(8,128)}, f32[704,1024]{1,0:T(8,128)}, f32[1,256]{1,0:T(1,128)}) custom-call(s32[4]{0:T(128)S(1)} %copy-done.4, bf16[384,768]{1,0:T(8,128)(2,1)S(1)} %feed_join.1.refs_0_, bf16[384,768]{1,0:T(8,128)(2,1)S(1)} %collective-permute-done.63.refs_1_, bf16[384,768]{1,0:T(8,128)(2,1)S(1)} %collective-permute-done.62.refs_2_, ...), custom_call_target="tpu_custom_call" | custom-call | flops 6049999872 | bytes 1000 | tf_op jit(solution)/shard_map/feed_unpack/pallas_call | solution.py:654
  313.4 6.9 %collective-permute-done.83 = f32[8,1024]{1,0:T(8,128)S(1)} collective-permute-done((f32[8,1024]{1,0:T(8,128)S(1)}, f32[8,1024]{1,0:T(8,128)S(1)}, u32[]{:S(2)}, u32[]{:S(2)}) %collective-permute-start.83) | collective-permute-done | bytes 32800 | tf_op jit(solution)/shard_map/ppermute | solution.py:589
  323.4 6.7 %collective-permute-done.82.refs_7_ = bf16[320,512]{1,0:T(8,128)(2,1)S(1)} collective-permute-done((bf16[320,512]{1,0:T(8,128)(2,1)S(1)}, bf16[320,512]{1,0:T(8,128)(2,1)S(1)}, u32[]{:S(2)}, u32[]{:S(2)}) %collective-permute-start.82) | collective-permute-done | bytes 327712 | tf_op jit(solution)/shard_map/ppermute | solution.py:589
  330.0 3.6 %mixer_unpack.1 = (f32[256,3072]{1,0:T(8,128)}, f32[256,1024]{1,0:T(8,128)}, f32[256,1024]{1,0:T(8,128)}, f32[1,256]{1,0:T(1,128)}) custom-call(s32[4]{0:T(128)S(1)} %copy-done.4, bf16[320,512]{1,0:T(8,128)(2,1)S(1)} %mixer_join.1.refs_0_, bf16[320,512]{1,0:T(8,128)(2,1)S(1)} %collective-permute-done.72.refs_1_, ...), custom_call_target="tpu_custom_call" | custom-call | flops 550000000 | bytes 1000 | tf_op jit(solution)/shard_map/mixer_unpack/pallas_call | solution.py:654
  (184 shorter events, 56.6 us)
Async XLA Ops:
  3.0 20.3 %collective-permute-start.1 = (s32[10,128]{1,0:T(8,128)S(1)}, s32[10,128]{1,0:T(8,128)S(1)}, u32[]{:S(2)}, u32[]{:S(2)}) collective-permute-start(s32[10,128]{1,0:T(8,128)S(1)} %add_bitcast_fusion), channel_id=1, source_target_pairs={{0,0},{1,8},{2,16},{3,24},{4,4},{5,12},{6,20},{7,28},{8,1},{9,9},{... | collective-permute-start | bytes 15368 | tf_op jit(solution)/shard_map/ppermute | solution.py:589
  3.7 19.7 %collective-permute-start = (bf16[128,1024]{1,0:T(8,128)(2,1)}, bf16[128,1024]{1,0:T(8,128)(2,1)S(1)}, u32[]{:S(2)}, u32[]{:S(2)}) collective-permute-start(bf16[128,1024]{1,0:T(8,128)(2,1)} %bitcast.17), channel_id=1, source_target_pairs={{0,0},{1,8},{2,16},{3,24},{4,4},{5,12},{6,20},{7,28},{8,1},{9,9},{... | collective-permute-start | bytes 786440 | tf_op jit(solution)/shard_map/ppermute | solution.py:589
  11.6 19.3 %collective-permute-start.15 = (bf16[272,512]{1,0:T(8,128)(2,1)}, bf16[272,512]{1,0:T(8,128)(2,1)S(1)}, u32[]{:S(2)}, u32[]{:S(2)}) collective-permute-start(bf16[272,512]{1,0:T(8,128)(2,1)} %get-tuple-element.155), channel_id=1, source_target_pairs={{0,1},{1,0},{2,3},{3,2},{4,5},{5,4},{6,7},{7,6},{8,9},{9,8},{10,11... | collective-permute-start | bytes 835592 | tf_op jit(solution)/shard_map/ppermute | solution.py:589
  16.3 24.9 %collective-permute-start.16 = (bf16[272,512]{1,0:T(8,128)(2,1)}, bf16[272,512]{1,0:T(8,128)(2,1)S(1)}, u32[]{:S(2)}, u32[]{:S(2)}) collective-permute-start(bf16[272,512]{1,0:T(8,128)(2,1)} %get-tuple-element.156), channel_id=1, source_target_pairs={{0,2},{1,3},{2,0},{3,1},{4,6},{5,7},{6,4},{7,5},{8,10},{9,11},{10,... | collective-permute-start | bytes 835592 | tf_op jit(solution)/shard_map/ppermute | solution.py:589
  23.4 18.8 %collective-permute-start.7 = (bf16[128,1024]{1,0:T(8,128)(2,1)S(1)}, bf16[128,1024]{1,0:T(8,128)(2,1)S(1)}, u32[]{:S(2)}, u32[]{:S(2)}) collective-permute-start(bf16[128,1024]{1,0:T(8,128)(2,1)S(1)} %bitcast.18), channel_id=1, source_target_pairs={{0,0},{1,8},{2,16},{3,24},{4,4},{5,12},{6,20},{7,28},{8,1},{9,9},{... | collective-permute-start | bytes 786440 | tf_op jit(solution)/shard_map/ppermute | solution.py:589
  24.3 19.6 %collective-permute-start.13 = (bf16[128,1024]{1,0:T(8,128)(2,1)S(1)}, bf16[128,1024]{1,0:T(8,128)(2,1)S(1)}, u32[]{:S(2)}, u32[]{:S(2)}) collective-permute-start(bf16[128,1024]{1,0:T(8,128)(2,1)S(1)} %collective-permute-done.refs_0_.x), channel_id=1, source_target_pairs={{0,6},{1,7},{2,4},{3,5},{4,2},{5,3},{6,0},{7,1},{8,14},{9,15},{10,... | collective-permute-start | bytes 786440 | tf_op jit(solution)/shard_map/ppermute | solution.py:589
  30.3 14.2 %collective-permute-start.11 = (bf16[128,1024]{1,0:T(8,128)(2,1)S(1)}, bf16[128,1024]{1,0:T(8,128)(2,1)S(1)}, u32[]{:S(2)}, u32[]{:S(2)}) collective-permute-start(bf16[128,1024]{1,0:T(8,128)(2,1)S(1)} %collective-permute-done.refs_0_.x), channel_id=1, source_target_pairs={{0,4},{1,5},{2,6},{3,7},{4,0},{5,1},{6,2},{7,3},{8,12},{9,13},{10,... | collective-permute-start | bytes 786440 | tf_op jit(solution)/shard_map/ppermute | solution.py:589
  30.8 16.0 %collective-permute-start.9 = (bf16[128,1024]{1,0:T(8,128)(2,1)S(1)}, bf16[128,1024]{1,0:T(8,128)(2,1)S(1)}, u32[]{:S(2)}, u32[]{:S(2)}) collective-permute-start(bf16[128,1024]{1,0:T(8,128)(2,1)S(1)} %collective-permute-done.refs_0_.x), channel_id=1, source_target_pairs={{0,2},{1,3},{2,0},{3,1},{4,6},{5,7},{6,4},{7,5},{8,10},{9,11},{10,... | collective-permute-start | bytes 786440 | tf_op jit(solution)/shard_map/ppermute | solution.py:589
  41.2 11.2 %collective-permute-start.17 = (bf16[272,512]{1,0:T(8,128)(2,1)S(1)}, bf16[272,512]{1,0:T(8,128)(2,1)S(1)}, u32[]{:S(2)}, u32[]{:S(2)}) collective-permute-start(bf16[272,512]{1,0:T(8,128)(2,1)S(1)} %copy-done.10), channel_id=1, source_target_pairs={{0,3},{1,2},{2,1},{3,0},{4,7},{5,6},{6,5},{7,4},{8,11},{9,10},{10,... | collective-permute-start | bytes 835592 | tf_op jit(solution)/shard_map/ppermute | solution.py:589
  42.2 12.3 %collective-permute-start.8 = (bf16[128,1024]{1,0:T(8,128)(2,1)S(1)}, bf16[128,1024]{1,0:T(8,128)(2,1)S(1)}, u32[]{:S(2)}, u32[]{:S(2)}) collective-permute-start(bf16[128,1024]{1,0:T(8,128)(2,1)S(1)} %collective-permute-done.refs_0_.x), channel_id=1, source_target_pairs={{0,1},{1,0},{2,3},{3,2},{4,5},{5,4},{6,7},{7,6},{8,9},{9,8},{10,11... | collective-permute-start | bytes 786440 | tf_op jit(solution)/shard_map/ppermute | solution.py:589
  44.5 12.8 %collective-permute-start.12 = (bf16[128,1024]{1,0:T(8,128)(2,1)S(1)}, bf16[128,1024]{1,0:T(8,128)(2,1)S(1)}, u32[]{:S(2)}, u32[]{:S(2)}) collective-permute-start(bf16[128,1024]{1,0:T(8,128)(2,1)S(1)} %collective-permute-done.11.refs_4_), channel_id=1, source_target_pairs={{0,1},{1,0},{2,3},{3,2},{4,5},{5,4},{6,7},{7,6},{8,9},{9,8},{10,11... | collective-permute-start | bytes 786440 | tf_op jit(solution)/shard_map/ppermute | solution.py:589
  52.4 15.7 %collective-permute-start.3 = (bf16[128,768]{1,0:T(8,128)(2,1)S(1)}, bf16[128,768]{1,0:T(8,128)(2,1)S(1)}, u32[]{:S(2)}, u32[]{:S(2)}) collective-permute-start(bf16[128,768]{1,0:T(8,128)(2,1)S(1)} %get-tuple-element.149), channel_id=1, source_target_pairs={{0,2},{1,3},{2,0},{3,1},{4,6},{5,7},{6,4},{7,5},{8,10},{9,11},{10,... | collective-permute-start | bytes 589832 | tf_op jit(solution)/shard_map/ppermute | solution.py:589
  54.5 15.1 %collective-permute-start.4 = (bf16[128,768]{1,0:T(8,128)(2,1)S(1)}, bf16[128,768]{1,0:T(8,128)(2,1)S(1)}, u32[]{:S(2)}, u32[]{:S(2)}) collective-permute-start(bf16[128,768]{1,0:T(8,128)(2,1)S(1)} %get-tuple-element.151), channel_id=1, source_target_pairs={{0,3},{1,2},{2,1},{3,0},{4,7},{5,6},{6,5},{7,4},{8,11},{9,10},{10,... | collective-permute-start | bytes 589832 | tf_op jit(solution)/shard_map/ppermute | solution.py:589
  54.5 15.1 %collective-permute-start.20 = (bf16[128,1024]{1,0:T(8,128)(2,1)S(1)}, bf16[128,1024]{1,0:T(8,128)(2,1)S(1)}, u32[]{:S(2)}, u32[]{:S(2)}) collective-permute-start(bf16[128,1024]{1,0:T(8,128)(2,1)S(1)} %collective-permute-done.7.refs_8_.cot), channel_id=1, source_target_pairs={{0,6},{1,7},{2,4},{3,5},{4,2},{5,3},{6,0},{7,1},{8,14},{9,15},{10,... | collective-permute-start | bytes 786440 | tf_op jit(solution)/shard_map/ppermute | solution.py:589
  57.3 12.7 %collective-permute-start.19 = (bf16[128,1024]{1,0:T(8,128)(2,1)S(1)}, bf16[128,1024]{1,0:T(8,128)(2,1)S(1)}, u32[]{:S(2)}, u32[]{:S(2)}) collective-permute-start(bf16[128,1024]{1,0:T(8,128)(2,1)S(1)} %collective-permute-done.7.refs_8_.cot), channel_id=1, source_target_pairs={{0,4},{1,5},{2,6},{3,7},{4,0},{5,1},{6,2},{7,3},{8,12},{9,13},{10,... | collective-permute-start | bytes 786440 | tf_op jit(solution)/shard_map/ppermute | solution.py:589
  57.6 17.7 %collective-permute-start.18 = (bf16[128,1024]{1,0:T(8,128)(2,1)S(1)}, bf16[128,1024]{1,0:T(8,128)(2,1)S(1)}, u32[]{:S(2)}, u32[]{:S(2)}) collective-permute-start(bf16[128,1024]{1,0:T(8,128)(2,1)S(1)} %collective-permute-done.7.refs_8_.cot), channel_id=1, source_target_pairs={{0,2},{1,3},{2,0},{3,1},{4,6},{5,7},{6,4},{7,5},{8,10},{9,11},{10,... | collective-permute-start | bytes 786440 | tf_op jit(solution)/shard_map/ppermute | solution.py:589
  96.6 11.3 %collective-permute-start.28 = (bf16[128,1024]{1,0:T(8,128)(2,1)S(1)}, bf16[128,1024]{1,0:T(8,128)(2,1)S(1)}, u32[]{:S(2)}, u32[]{:S(2)}) collective-permute-start(bf16[128,1024]{1,0:T(8,128)(2,1)S(1)} %get-tuple-element.168.refs_0_), channel_id=1, source_target_pairs={{0,4},{1,5},{2,6},{3,7},{4,0},{5,1},{6,2},{7,3},{8,12},{9,13},{10,... | collective-permute-start | bytes 786440 | tf_op jit(solution)/shard_map/ppermute | solution.py:589
  97.4 11.1 %collective-permute-start.33 = (bf16[128,1024]{1,0:T(8,128)(2,1)S(1)}, bf16[128,1024]{1,0:T(8,128)(2,1)S(1)}, u32[]{:S(2)}, u32[]{:S(2)}) collective-permute-start(bf16[128,1024]{1,0:T(8,128)(2,1)S(1)} %collective-permute-done.18.refs_10_), channel_id=1, source_target_pairs={{0,1},{1,0},{2,3},{3,2},{4,5},{5,4},{6,7},{7,6},{8,9},{9,8},{10,11... | collective-permute-start | bytes 786440 | tf_op jit(solution)/shard_map/ppermute | solution.py:589
  121.1 37.9 %collective-permute-start.41 = (bf16[4,128,1024]{2,1,0:T(8,128)(2,1)S(1)}, bf16[4,128,1024]{2,1,0:T(8,128)(2,1)S(1)}, u32[]{:S(2)}, u32[]{:S(2)}) collective-permute-start(bf16[4,128,1024]{2,1,0:T(8,128)(2,1)S(1)} %get-tuple-element.186), channel_id=1, source_target_pairs={{0,1},{1,0},{2,3},{3,2},{4,5},{5,4},{6,7},{7,6},{8,9},{9,8},{10,11... | collective-permute-start | bytes 3145736 | tf_op jit(solution)/shard_map/ppermute | solution.py:589
  121.5 19.2 %collective-permute-start.40 = (bf16[2,384,384]{2,1,0:T(8,128)(2,1)S(1)}, bf16[2,384,384]{2,1,0:T(8,128)(2,1)S(1)}, u32[]{:S(2)}, u32[]{:S(2)}) collective-permute-start(bf16[2,384,384]{2,1,0:T(8,128)(2,1)S(1)} %get-tuple-element.174), channel_id=1, source_target_pairs={{0,8},{1,9},{2,10},{3,11},{4,12},{5,13},{6,14},{7,15},{8,0},{9,1},... | collective-permute-start | bytes 1769480 | tf_op jit(solution)/shard_map/ppermute | solution.py:589
  126.1 12.4 %collective-permute-start.39 = (bf16[128,1024]{1,0:T(8,128)(2,1)S(1)}, bf16[128,1024]{1,0:T(8,128)(2,1)S(1)}, u32[]{:S(2)}, u32[]{:S(2)}) collective-permute-start(bf16[128,1024]{1,0:T(8,128)(2,1)S(1)} %get-tuple-element.180), channel_id=1, source_target_pairs={{0,6},{1,7},{2,4},{3,5},{4,2},{5,3},{6,0},{7,1},{8,14},{9,15},{10,... | collective-permute-start | bytes 786440 | tf_op jit(solution)/shard_map/ppermute | solution.py:589
  140.4 20.0 %collective-permute-start.47 = (bf16[2,384,384]{2,1,0:T(8,128)(2,1)S(1)}, bf16[2,384,384]{2,1,0:T(8,128)(2,1)S(1)}, u32[]{:S(2)}, u32[]{:S(2)}) collective-permute-start(bf16[2,384,384]{2,1,0:T(8,128)(2,1)S(1)} %get-tuple-element.201), channel_id=1, source_target_pairs={{0,8},{1,9},{2,10},{3,11},{4,12},{5,13},{6,14},{7,15},{8,0},{9,1},... | collective-permute-start | bytes 1769480 | tf_op jit(solution)/shard_map/ppermute | solution.py:589
  140.8 17.7 %collective-permute-start.43 = (bf16[384,384]{1,0:T(8,128)(2,1)S(1)}, bf16[384,384]{1,0:T(8,128)(2,1)S(1)}, u32[]{:S(2)}, u32[]{:S(2)}) collective-permute-start(bf16[384,384]{1,0:T(8,128)(2,1)S(1)} %get-tuple-element.183), channel_id=1, source_target_pairs={{0,16},{1,17},{2,18},{3,19},{4,20},{5,21},{6,22},{7,23},{8,24},{9,... | collective-permute-start | bytes 884744 | tf_op jit(solution)/shard_map/ppermute | solution.py:589
  142.5 16.0 %collective-permute-start.42 = (bf16[128,1024]{1,0:T(8,128)(2,1)S(1)}, bf16[128,1024]{1,0:T(8,128)(2,1)S(1)}, u32[]{:S(2)}, u32[]{:S(2)}) collective-permute-start(bf16[128,1024]{1,0:T(8,128)(2,1)S(1)} %get-tuple-element.204.refs_0_), channel_id=1, source_target_pairs={{0,6},{1,7},{2,4},{3,5},{4,2},{5,3},{6,0},{7,1},{8,14},{9,15},{10,... | collective-permute-start | bytes 786440 | tf_op jit(solution)/shard_map/ppermute | solution.py:589
  160.5 19.6 %collective-permute-start.54 = (bf16[384,384]{1,0:T(8,128)(2,1)S(1)}, bf16[384,384]{1,0:T(8,128)(2,1)S(1)}, u32[]{:S(2)}, u32[]{:S(2)}) collective-permute-start(bf16[384,384]{1,0:T(8,128)(2,1)S(1)} %get-tuple-element.202), channel_id=1, source_target_pairs={{0,16},{1,17},{2,18},{3,19},{4,20},{5,21},{6,22},{7,23},{8,24},{9,... | collective-permute-start | bytes 884744 | tf_op jit(solution)/shard_map/ppermute | solution.py:589
  163.3 16.7 %collective-permute-start.44 = (bf16[128,1024]{1,0:T(8,128)(2,1)S(1)}, bf16[128,1024]{1,0:T(8,128)(2,1)S(1)}, u32[]{:S(2)}, u32[]{:S(2)}) collective-permute-start(bf16[128,1024]{1,0:T(8,128)(2,1)S(1)} %get-tuple-element.194), channel_id=1, source_target_pairs={{0,2},{1,3},{2,0},{3,1},{4,6},{5,7},{6,4},{7,5},{8,10},{9,11},{10,... | collective-permute-start | bytes 786440 | tf_op jit(solution)/shard_map/ppermute | solution.py:589
  164.4 15.7 %collective-permute-start.45 = (bf16[128,1024]{1,0:T(8,128)(2,1)S(1)}, bf16[128,1024]{1,0:T(8,128)(2,1)S(1)}, u32[]{:S(2)}, u32[]{:S(2)}) collective-permute-start(bf16[128,1024]{1,0:T(8,128)(2,1)S(1)} %get-tuple-element.195), channel_id=1, source_target_pairs={{0,4},{1,5},{2,6},{3,7},{4,0},{5,1},{6,2},{7,3},{8,12},{9,13},{10,... | collective-permute-start | bytes 786440 | tf_op jit(solution)/shard_map/ppermute | solution.py:589
  164.9 15.1 %collective-permute-start.46 = (bf16[128,1024]{1,0:T(8,128)(2,1)S(1)}, bf16[128,1024]{1,0:T(8,128)(2,1)S(1)}, u32[]{:S(2)}, u32[]{:S(2)}) collective-permute-start(bf16[128,1024]{1,0:T(8,128)(2,1)S(1)} %get-tuple-element.196), channel_id=1, source_target_pairs={{0,6},{1,7},{2,4},{3,5},{4,2},{5,3},{6,0},{7,1},{8,14},{9,15},{10,... | collective-permute-start | bytes 786440 | tf_op jit(solution)/shard_map/ppermute | solution.py:589
  180.1 48.7 %collective-permute-start.59 = (bf16[4,144,1024]{2,1,0:T(8,128)(2,1)S(1)}, bf16[4,144,1024]{2,1,0:T(8,128)(2,1)S(1)}, u32[]{:S(2)}, u32[]{:S(2)}) collective-permute-start(bf16[4,144,1024]{2,1,0:T(8,128)(2,1)S(1)} %get-tuple-element.221), channel_id=1, source_target_pairs={{0,1},{1,0},{2,3},{3,2},{4,5},{5,4},{6,7},{7,6},{8,9},{9,8},{10,11... | collective-permute-start | bytes 3538952 | tf_op jit(solution)/shard_map/ppermute | solution.py:589
  184.4 44.6 %collective-permute-start.60 = (bf16[2,320,512]{2,1,0:T(8,128)(2,1)S(1)}, bf16[2,320,512]{2,1,0:T(8,128)(2,1)S(1)}, u32[]{:S(2)}, u32[]{:S(2)}) collective-permute-start(bf16[2,320,512]{2,1,0:T(8,128)(2,1)S(1)} %get-tuple-element.228), channel_id=1, source_target_pairs={{0,8},{1,9},{2,10},{3,11},{4,12},{5,13},{6,14},{7,15},{8,0},{9,1},... | collective-permute-start | bytes 1966088 | tf_op jit(solution)/shard_map/ppermute | solution.py:589
  187.0 15.9 %collective-permute-start.63 = (bf16[384,768]{1,0:T(8,128)(2,1)S(1)}, bf16[384,768]{1,0:T(8,128)(2,1)S(1)}, u32[]{:S(2)}, u32[]{:S(2)}) collective-permute-start(bf16[384,768]{1,0:T(8,128)(2,1)S(1)} %feed_join.1.refs_0_), channel_id=1, source_target_pairs={{0,4},{1,5},{2,6},{3,7},{4,0},{5,1},{6,2},{7,3},{8,12},{9,13},{10,... | collective-permute-start | bytes 1769480 | tf_op jit(solution)/shard_map/ppermute | solution.py:589
  187.6 40.6 %collective-permute-start.62 = (bf16[384,768]{1,0:T(8,128)(2,1)S(1)}, bf16[384,768]{1,0:T(8,128)(2,1)S(1)}, u32[]{:S(2)}, u32[]{:S(2)}) collective-permute-start(bf16[384,768]{1,0:T(8,128)(2,1)S(1)} %feed_join.1.refs_0_), channel_id=1, source_target_pairs={{0,8},{1,9},{2,10},{3,11},{4,12},{5,13},{6,14},{7,15},{8,0},{9,1},... | collective-permute-start | bytes 1769480 | tf_op jit(solution)/shard_map/ppermute | solution.py:589
  187.8 41.2 %collective-permute-start.55 = (bf16[128,1024]{1,0:T(8,128)(2,1)S(1)}, bf16[128,1024]{1,0:T(8,128)(2,1)S(1)}, u32[]{:S(2)}, u32[]{:S(2)}) collective-permute-start(bf16[128,1024]{1,0:T(8,128)(2,1)S(1)} %output.1), channel_id=1, source_target_pairs={{0,0},{1,8},{2,16},{3,24},{4,4},{5,12},{6,20},{7,28},{8,1},{9,9},{... | collective-permute-start | bytes 786440 | tf_op jit(solution)/shard_map/ppermute | solution.py:589
  202.9 42.4 %collective-permute-start.61 = (bf16[384,768]{1,0:T(8,128)(2,1)S(1)}, bf16[384,768]{1,0:T(8,128)(2,1)S(1)}, u32[]{:S(2)}, u32[]{:S(2)}) collective-permute-start(bf16[384,768]{1,0:T(8,128)(2,1)S(1)} %feed_join.1.refs_0_), channel_id=1, source_target_pairs={{0,16},{1,17},{2,18},{3,19},{4,20},{5,21},{6,22},{7,23},{8,24},{9,... | collective-permute-start | bytes 1769480 | tf_op jit(solution)/shard_map/ppermute | solution.py:589
  228.2 17.1 %collective-permute-start.64 = (bf16[384,768]{1,0:T(8,128)(2,1)S(1)}, bf16[384,768]{1,0:T(8,128)(2,1)S(1)}, u32[]{:S(2)}, u32[]{:S(2)}) collective-permute-start(bf16[384,768]{1,0:T(8,128)(2,1)S(1)} %collective-permute-done.62.refs_2_), channel_id=1, source_target_pairs={{0,4},{1,5},{2,6},{3,7},{4,0},{5,1},{6,2},{7,3},{8,12},{9,13},{10,... | collective-permute-start | bytes 1769480 | tf_op jit(solution)/shard_map/ppermute | solution.py:589
  229.2 26.8 %collective-permute-start.65 = (bf16[2,144,1024]{2,1,0:T(8,128)(2,1)S(1)}, bf16[2,144,1024]{2,1,0:T(8,128)(2,1)S(1)}, u32[]{:S(2)}, u32[]{:S(2)}) collective-permute-start(bf16[2,144,1024]{2,1,0:T(8,128)(2,1)S(1)} %get-tuple-element.244), channel_id=1, source_target_pairs={{0,4},{1,5},{2,6},{3,7},{4,0},{5,1},{6,2},{7,3},{8,12},{9,13},{10,... | collective-permute-start | bytes 1769480 | tf_op jit(solution)/shard_map/ppermute | solution.py:589
  230.7 25.2 %collective-permute-start.66 = (bf16[320,512]{1,0:T(8,128)(2,1)S(1)}, bf16[320,512]{1,0:T(8,128)(2,1)S(1)}, u32[]{:S(2)}, u32[]{:S(2)}) collective-permute-start(bf16[320,512]{1,0:T(8,128)(2,1)S(1)} %get-tuple-element.243), channel_id=1, source_target_pairs={{0,16},{1,17},{2,18},{3,19},{4,20},{5,21},{6,22},{7,23},{8,24},{9,... | collective-permute-start | bytes 983048 | tf_op jit(solution)/shard_map/ppermute | solution.py:589
  256.0 14.3 %collective-permute-start.74 = (bf16[384,768]{1,0:T(8,128)(2,1)S(1)}, bf16[384,768]{1,0:T(8,128)(2,1)S(1)}, u32[]{:S(2)}, u32[]{:S(2)}) collective-permute-start(bf16[384,768]{1,0:T(8,128)(2,1)S(1)} %collective-permute-done.61.refs_4_), channel_id=1, source_target_pairs={{0,8},{1,9},{2,10},{3,11},{4,12},{5,13},{6,14},{7,15},{8,0},{9,1},... | collective-permute-start | bytes 1769480 | tf_op jit(solution)/shard_map/ppermute | solution.py:589
  262.5 35.1 %collective-permute-start.73 = (bf16[384,768]{1,0:T(8,128)(2,1)S(1)}, bf16[384,768]{1,0:T(8,128)(2,1)S(1)}, u32[]{:S(2)}, u32[]{:S(2)}) collective-permute-start(bf16[384,768]{1,0:T(8,128)(2,1)S(1)} %collective-permute-done.61.refs_4_), channel_id=1, source_target_pairs={{0,4},{1,5},{2,6},{3,7},{4,0},{5,1},{6,2},{7,3},{8,12},{9,13},{10,... | collective-permute-start | bytes 1769480 | tf_op jit(solution)/shard_map/ppermute | solution.py:589
  270.3 27.3 %collective-permute-start.75 = (bf16[384,768]{1,0:T(8,128)(2,1)S(1)}, bf16[384,768]{1,0:T(8,128)(2,1)S(1)}, u32[]{:S(2)}, u32[]{:S(2)}) collective-permute-start(bf16[384,768]{1,0:T(8,128)(2,1)S(1)} %collective-permute-done.74.refs_6_), channel_id=1, source_target_pairs={{0,4},{1,5},{2,6},{3,7},{4,0},{5,1},{6,2},{7,3},{8,12},{9,13},{10,... | collective-permute-start | bytes 1769480 | tf_op jit(solution)/shard_map/ppermute | solution.py:589
  270.8 26.8 %collective-permute-start.72 = (bf16[320,512]{1,0:T(8,128)(2,1)S(1)}, bf16[320,512]{1,0:T(8,128)(2,1)S(1)}, u32[]{:S(2)}, u32[]{:S(2)}) collective-permute-start(bf16[320,512]{1,0:T(8,128)(2,1)S(1)} %mixer_join.1.refs_0_), channel_id=1, source_target_pairs={{0,4},{1,5},{2,6},{3,7},{4,0},{5,1},{6,2},{7,3},{8,12},{9,13},{10,... | collective-permute-start | bytes 983048 | tf_op jit(solution)/shard_map/ppermute | solution.py:589
  272.3 25.3 %collective-permute-start.71 = (bf16[320,512]{1,0:T(8,128)(2,1)S(1)}, bf16[320,512]{1,0:T(8,128)(2,1)S(1)}, u32[]{:S(2)}, u32[]{:S(2)}) collective-permute-start(bf16[320,512]{1,0:T(8,128)(2,1)S(1)} %mixer_join.1.refs_0_), channel_id=1, source_target_pairs={{0,8},{1,9},{2,10},{3,11},{4,12},{5,13},{6,14},{7,15},{8,0},{9,1},... | collective-permute-start | bytes 983048 | tf_op jit(solution)/shard_map/ppermute | solution.py:589
  272.6 25.0 %collective-permute-start.70 = (bf16[320,512]{1,0:T(8,128)(2,1)S(1)}, bf16[320,512]{1,0:T(8,128)(2,1)S(1)}, u32[]{:S(2)}, u32[]{:S(2)}) collective-permute-start(bf16[320,512]{1,0:T(8,128)(2,1)S(1)} %mixer_join.1.refs_0_), channel_id=1, source_target_pairs={{0,16},{1,17},{2,18},{3,19},{4,20},{5,21},{6,22},{7,23},{8,24},{9,... | collective-permute-start | bytes 983048 | tf_op jit(solution)/shard_map/ppermute | solution.py:589
  299.8 20.5 %collective-permute-start.80 = (bf16[320,512]{1,0:T(8,128)(2,1)S(1)}, bf16[320,512]{1,0:T(8,128)(2,1)S(1)}, u32[]{:S(2)}, u32[]{:S(2)}) collective-permute-start(bf16[320,512]{1,0:T(8,128)(2,1)S(1)} %collective-permute-done.70.refs_4_), channel_id=1, source_target_pairs={{0,8},{1,9},{2,10},{3,11},{4,12},{5,13},{6,14},{7,15},{8,0},{9,1},... | collective-permute-start | bytes 983048 | tf_op jit(solution)/shard_map/ppermute | solution.py:589
  300.0 20.3 %collective-permute-start.79 = (bf16[320,512]{1,0:T(8,128)(2,1)S(1)}, bf16[320,512]{1,0:T(8,128)(2,1)S(1)}, u32[]{:S(2)}, u32[]{:S(2)}) collective-permute-start(bf16[320,512]{1,0:T(8,128)(2,1)S(1)} %collective-permute-done.70.refs_4_), channel_id=1, source_target_pairs={{0,4},{1,5},{2,6},{3,7},{4,0},{5,1},{6,2},{7,3},{8,12},{9,13},{10,... | collective-permute-start | bytes 983048 | tf_op jit(solution)/shard_map/ppermute | solution.py:589
  300.5 22.0 %collective-permute-start.77 = (bf16[128,1024]{1,0:T(8,128)(2,1)S(1)}, bf16[128,1024]{1,0:T(8,128)(2,1)S(1)}, u32[]{:S(2)}, u32[]{:S(2)}) collective-permute-start(bf16[128,1024]{1,0:T(8,128)(2,1)S(1)} %get-tuple-element.261), channel_id=1, source_target_pairs={{0,0},{1,8},{2,16},{3,24},{4,4},{5,12},{6,20},{7,28},{8,1},{9,9},{... | collective-permute-start | bytes 786440 | tf_op jit(solution)/shard_map/ppermute | solution.py:589
  301.2 19.1 %collective-permute-start.78 = (bf16[320,512]{1,0:T(8,128)(2,1)S(1)}, bf16[320,512]{1,0:T(8,128)(2,1)S(1)}, u32[]{:S(2)}, u32[]{:S(2)}) collective-permute-start(bf16[320,512]{1,0:T(8,128)(2,1)S(1)} %collective-permute-done.71.refs_2_), channel_id=1, source_target_pairs={{0,4},{1,5},{2,6},{3,7},{4,0},{5,1},{6,2},{7,3},{8,12},{9,13},{10,... | collective-permute-start | bytes 983048 | tf_op jit(solution)/shard_map/ppermute | solution.py:589
  302.8 17.5 %collective-permute-start.83 = (f32[8,1024]{1,0:T(8,128)S(1)}, f32[8,1024]{1,0:T(8,128)S(1)}, u32[]{:S(2)}, u32[]{:S(2)}) collective-permute-start(f32[8,1024]{1,0:T(8,128)S(1)} %add.16), channel_id=1, source_target_pairs={{0,16},{1,17},{2,18},{3,19},{4,20},{5,21},{6,22},{7,23},{8,24},{9,... | collective-permute-start | bytes 98312 | tf_op jit(solution)/shard_map/ppermute | solution.py:589
  (48 other events, 617.9 us)

commit v3 on v2

--- a/solution.py
+++ b/solution.py
@@ -669,10 +669,10 @@
     return lax.optimization_barrier((value, *others))[0]
 
 
-def pack_qkvg_kernel(idx, wq, wg, pk, pv, gain_one, gain_two, o0, o1, o2, o3, sems):
+def pack_qkvg_kernel(idx, wq, wg, pk, pv, gains, o0, o1, o23, sems):
     x, f = idx[1], idx[2]
     copies = []
-    for j, out in enumerate((o0, o1, o2, o3)):
+    for j, out in enumerate((o0, o1, o23.at[0], o23.at[1])):
         start = pl.multiple_of((2 * (f ^ j) + x) * 128, 128)
         for part in range(4):
             first = start if part == 3 else pl.multiple_of(part * 1024 + start, 128)
@@ -686,12 +686,12 @@
             )
     for copy in copies:
         copy.start()
-    for j, out in enumerate((o0, o1, o2, o3)):
+    for j, out in enumerate((o0, o1, o23.at[0], o23.at[1])):
         start = pl.multiple_of((2 * (f ^ j) + x) * 128, 128)
         tail = [
             jnp.concatenate([pk[:, pl.ds(start, 128)], pv[:, pl.ds(start, 128)]], axis=1),
-            gain_one[...],
-            gain_two[...],
+            gains[:, 0:256],
+            gains[:, 256:512],
             jnp.zeros((EXTRA - 6, 256), jnp.bfloat16),
         ]
         tail = jnp.concatenate([t.astype(jnp.float32) for t in tail], axis=0)
@@ -701,10 +701,10 @@
         copy.wait()
 
 
-def pack_gu_kernel(idx, wgu, o0, o1, o2, o3):
+def pack_gu_kernel(idx, wgu, o0, o1, o23):
     z, x, f = idx[0], idx[1], idx[2]
     width = FF // 8
-    for j, out in enumerate((o0, o1, o2, o3)):
+    for j, out in enumerate((o0, o1, o23.at[0], o23.at[1])):
         head = 2 * (f ^ j) + x
         count = 256 if j < 2 else 128
         rows = pl.ds(0 if j < 2 else pl.multiple_of((z & 1) * 128, 128), count)
@@ -722,12 +722,13 @@
 
 
 def lay_weights(z, f, parts, w_full):
-    for j in range(2):
-        w_full[pl.ds(pl.multiple_of((f ^ j) * 256, 256), 256), :] = parts[j][0:256, :]
-    for j in (2, 3):
-        for side in range(2):
-            rows = pl.multiple_of((f ^ j) * 256 + ((z ^ side) & 1) * 128, 128)
-            w_full[pl.ds(rows, 128), :] = parts[j + 2 * side][0:128, :]
+    own, beside, far, far_beside, next_far, next_beside = parts
+    w_full[pl.ds(pl.multiple_of(f * 256, 256), 256), :] = own[...]
+    w_full[pl.ds(pl.multiple_of((f ^ 1) * 256, 256), 256), :] = beside[...]
+    halves = ((2, 0, far, 0), (3, 0, far_beside, 1), (2, 1, next_far, 0), (3, 1, next_beside, 1))
+    for j, side, part, which in halves:
+        rows = pl.multiple_of((f ^ j) * 256 + ((z ^ side) & 1) * 128, 128)
+        w_full[pl.ds(rows, 128), :] = part[which]
 
 
 def mixer_forward_kernel(idx, rates, ints, *refs):
@@ -741,10 +742,10 @@
     scale = HEAD_WIDTH_SIZE ** (-0.5)
     wo = w_out[pl.ds(pl.multiple_of(x * 128, 128), 128), :]
     tails = []
-    for j in range(4):
+    for j, part in enumerate((parts[0], parts[1], parts[2].at[0], parts[3].at[1])):
         rows = pl.multiple_of((f ^ j) * 256, 256)
-        w_full[pl.ds(rows, 256), :] = parts[j][0:256, :]
-        tail = parts[j][256 : 256 + EXTRA, 0:256].astype(jnp.float32)
+        w_full[pl.ds(rows, 256), :] = part[0:256, :]
+        tail = part[256 : 256 + EXTRA, 0:256].astype(jnp.float32)
         tails.append(tail)
         gain_one[:, pl.ds(rows, 256)] = tail[4:5]
         gain_two[:, pl.ds(rows, 256)] = tail[5:6]
@@ -1241,10 +1242,6 @@
     return flip_z(joined, 2), flip_z(joined, 1)
 
 
-def halves_from_next_plane(parts):
-    return list(parts) + [flip_z(parts[2], 1), flip_z(parts[3], 1)]
-
-
 def in_planes(
     tokens,
     cotangent,
@@ -1269,17 +1266,13 @@
     idx = jnp.stack([z, x, f, head]).astype(jnp.int32)
 
     own = to_plane(tokens[0])
-    ints = to_plane(
-        jnp.concatenate([segments[0], decay_index[0].reshape(-1), step_index[0].reshape(-1)]).reshape(
-            10, 128
-        )
-    )
     anywhere = pl.BlockSpec(memory_space=pl.ANY)
     wq_parts = pl.pallas_call(
         pack_qkvg_kernel,
-        out_shape=[jax.ShapeDtypeStruct((256 + EXTRA, 512), bf16)] * 4,
-        in_specs=[sspec(), anywhere, anywhere] + [vspec()] * 4,
-        out_specs=[vspec()] * 4,
+        out_shape=[jax.ShapeDtypeStruct((256 + EXTRA, 512), bf16)] * 2
+        + [jax.ShapeDtypeStruct((2, 256 + EXTRA, 512), bf16)],
+        in_specs=[sspec(), anywhere, anywhere] + [vspec()] * 3,
+        out_specs=[vspec()] * 3,
         scratch_shapes=[pltpu.SemaphoreType.DMA((16,))],
         compiler_params=pltpu.CompilerParams(vmem_limit_bytes=60 * 1024 * 1024),
         cost_estimate=pl.CostEstimate(flops=1000, bytes_accessed=1000, transcendentals=0),
@@ -1290,25 +1283,26 @@
         w_gate,
         persist_keys,
         persist_values,
-        norm_gain.reshape(1, 256),
-        ffn_gain.reshape(1, 256),
+        jnp.concatenate([norm_gain, ffn_gain]).reshape(1, 512),
     )
     gu_parts = call(
         pack_gu_kernel,
         (idx,),
         (w_gu,),
-        [((256, 768), bf16)] * 2 + [((128, 768), bf16)] * 2,
+        [((256, 768), bf16)] * 2 + [((2, 128, 768), bf16)],
         name="pack_gu",
     )
+    ints = jnp.concatenate([segments[0], decay_index[0].reshape(-1), step_index[0].reshape(-1)])
+    ints = to_plane(after(ints.reshape(10, 128), wq_parts[0]))
     rates = jnp.stack(
         [0.6 * jnp.exp2(-ints[8].astype(f32)), 0.1 * jnp.exp2(-ints[9].astype(f32))]
     )
-    wq_parts = hand_rows(wq_parts)
-    own = after(own, wq_parts[0], gu_parts[0], rates)
+    far = flip(wq_parts[2], 0, 2)
+    wq_parts = [wq_parts[0], flip(wq_parts[1], 0, 1), far, flip(far, 0, 1)]
+    own = after(own, wq_parts[0])
     near = gather_chips(own)
     own_cot = to_plane(after(cotangent[0], own))
-    gu_parts = [after(w, own) for w in gu_parts]
-    gu_parts = [gu_parts[0], gu_parts[1], flip(gu_parts[2], 0, 2), flip(gu_parts[3], 0, 3)]
+    gu_far = flip(after(gu_parts[2], own), 0, 2)
     blocks = gather_cores(near)
     rates = after(rates, own_cot)
     cot_near = gather_chips(after(own_cot, near[2]))
@@ -1358,16 +1352,17 @@
         spare=10,
         us=10.0,
     )
-    send = after(send, *cot_near[1:], gu_parts[2], gu_parts[3])
+    send = after(send, *cot_near[1:], gu_far)
     sums = sum_cores(keep, send)
     shares = cross_chips(*sums)
-    gu_parts[1] = flip(gu_parts[1], 0, 1)
-    gu_parts = halves_from_next_plane(gu_parts)
+    gu_next = flip_z(gu_far, 1)
+    gu_parts = [gu_parts[0], flip(gu_parts[1], 0, 1), gu_far, flip(gu_far, 0, 1)]
+    gu_parts += [gu_next, flip(after(gu_next, shares[3]), 0, 1)]
     cots = gather_cores(cot_near)
     residual, feed = call(
         residual_kernel,
         (),
-        (after(own, *gu_parts), gain_two, *shares),
+        (own, gain_two, *shares),
         [(block, f32), (block, bf16)],
         name="residual",
     )
@@ -1410,23 +1405,22 @@
     shares = cross_chips(*sums)
     feed_received = flip_z(feed_send, 1)
     feed_later_received = flip_z(after(feed_later_send, sums[0]), 1)
+    out_sums = sum_cores(keep_d, send_d)
     grad_residual, branch = call(
         branch_kernel,
         (),
-        (residual, gain_two, own_cot, *shares),
+        (residual, gain_two, after(own_cot, out_sums[0]), *shares),
         [(block, f32), (block, bf16)],
         name="branch",
     )
     feed_own, feed_passed = half_sum(after(feed_keep, branch), feed_received, "feed")
     branch_near = gather_chips(branch, after(branch, feed_passed))
-    keep_d = after(keep_d, feed_passed)
-    out_sums = sum_cores(keep_d, send_d)
     feed_moved = flip_z(feed_passed, 2)
-    branches = gather_cores([after(piece, feed_moved) for piece in branch_near])
+    branches = gather_cores(branch_near)
     feed_later, feed_later_passed = half_sum(
-        after(feed_later_keep, out_sums[0]), feed_later_received, "feed_later"
-    )
-    rates = after(rates, feed_later_passed)
+        after(feed_later_keep, branch_near[3]), feed_later_received, "feed_later"
+    )
+    rates = after(rates, feed_later_passed, feed_moved)
     feed_later_moved = flip_z(feed_later_passed, 2)
     out_sums = lax.optimization_barrier((*out_sums, branches[6]))[:4]
     out_shares = cross_chips(*out_sums)
@@ -1455,7 +1449,7 @@
         us=13.0,
     )
     send, dqkvg = lax.optimization_barrier(
-        (send, dqkvg, feed_later_moved, *out_shares[1:])
+        (send, dqkvg, feed_moved, feed_later_moved, *out_shares[1:])
     )[:2]
     *feed_parts, feed_rest = whole_sum(
         (after(feed_own, send), feed_later), (feed_moved, feed_later_moved), "feed"
@@ -1473,32 +1467,44 @@
         us=2.2,
     )
     (result,) = call(output_kernel, (), (residual, *out_shares), [(block, bf16)], name="output")
-    result = to_plane(after(result, mixer_send))
-    feed_joined = join(feed_parts, after(feed_rest, mixer_send), "feed")
-    feed_second, feed_first = spread_far(feed_joined)
-    feed_beside = flip(feed_joined, 1, 0)
     rows = (128 + EXTRA, 1024)
     keep_far, keep_near, send_far = call(
         tokens_sum_kernel,
         (),
-        (after(keep, feed_joined), flip(send, 0, 1)),
+        (after(keep, feed_rest), flip(send, 0, 1)),
         [(rows, f32), (rows, f32), ((2, *rows), bf16)],
         name="tokens_sum",
     )
+    feed_joined = join(feed_parts, after(feed_rest, mixer_send, keep_near), "feed")
+    feed_second = flip_z(feed_joined, 2)
+    feed_beside = flip(feed_joined, 1, 0)
     mixer_own, mixer_passed = half_sum(
-        after(mixer_keep, keep_near, result), flip_z(mixer_send, 1), "mixer"
+        after(mixer_keep, feed_joined), flip_z(mixer_send, 1), "mixer"
     )
     mixer_moved = flip_z(mixer_passed, 2)
+    feed_first = flip_z(feed_joined, 1)
     tokens_far = flip(after(send_far, mixer_passed), 1, 0)
-    feed_first_beside = flip(after(feed_first, feed_beside), 1, 0)
-    mixer_own = after(mixer_own, feed_second, feed_first_beside, tokens_far)
+    feed_first_beside = flip(after(feed_first, mixer_passed), 1, 0)
+    mixer_own = after(mixer_own, feed_beside)
     *mixer_parts, mixer_rest = whole_sum((mixer_own,), (mixer_moved,), "mixer")
+    result = to_plane(after(result, mixer_passed))
     feed_third = flip_z(after(feed_second, mixer_rest), 1)
     feed_second_beside = flip(after(feed_second, mixer_rest), 1, 0)
-    mixer_joined = join(hand_rows(mixer_parts), mixer_rest, "mixer")
+    mixer_joined = join(
+        hand_rows(mixer_parts), after(mixer_rest, tokens_far, feed_first_beside), "mixer"
+    )
     mixer_second, mixer_first = spread_far(mixer_joined)
     mixer_beside = flip(mixer_joined, 1, 0)
-    feed_third_beside = flip(after(feed_third, mixer_joined), 1, 0)
+    feed_third_beside = flip(
+        after(
+            feed_third,
+            mixer_joined,
+
+
+        ),
+        1,
+        0,
+    )
     tokens_own, tokens_passed = call(
         far_kernel,
         (),
@@ -1512,7 +1518,6 @@
         mixer_first,
         mixer_beside,
         feed_second_beside,
-        feed_third_beside,
         tokens_near,
     )
     mixer_third = flip_z(mixer_second, 1)
@@ -1526,7 +1531,7 @@
         name="tokens",
     )
     grad_tokens = to_plane(grad_tokens)
-    persist = persist + flip_z(persist, 1)
+    persist = persist + after(flip_z(persist, 1), mixer_third)
     feed_pieces = (
         feed_joined,
         feed_beside,
@@ -1549,7 +1554,7 @@
         us=5.5,
     )
     mixer_third_beside = flip(
-        after(mixer_third, grad_ffn, mixer_first_beside, mixer_second_beside, persist), 1, 0
+        after(mixer_third, grad_ffn, mixer_first_beside, mixer_second_beside), 1, 0
     )
     persist = persist + flip_z(persist, 2)
     mixer_pieces = (

time: 338 us -> 303 us (0.90)
  waiting for transfers between devices: 188 us -> 142 us
  starting transfers between devices: 83.9 us -> 96.9 us
    ppermute x84, waiting for transfers between devices: 188 us -> 142 us  [shift(): return lax.ppermute(value, ('ctx', 'fsdp'), pairs)]
    ppermute x84, starting transfers between devices: 83.9 us -> 96.9 us  [shift(): return lax.ppermute(value, ('ctx', 'fsdp'), pairs)]
  transfers between devices with their start and end apart: 84 -> 84, of which waited for: 34 -> 30; matrix products, arithmetic and copies ran while one was open for 1% -> 1% of each run, Pallas kernels for 12% -> 13%
where the time goes in v3:
time: 303 us; the launch traced here: 300 us
  waiting for transfers between devices  142 us (47%)
  starting transfers between devices  96.9 us (32%)
  Pallas kernels  52.4 us (17%)
  local copies, waits for them, and re-layouts  4.11 us (1%)
    ppermute x84, waiting for transfers between devices, shift(): return lax.ppermute(value, ('ctx', 'fsdp'), pairs)  142 us
    ppermute x84, starting transfers between devices, shift(): return lax.ppermute(value, ('ctx', 'fsdp'), pairs)  96.9 us
    pallas_call x24, Pallas kernels, call(): pl.pallas_call(kernel, out_shape=[jax.ShapeDtypeStruct(shape, dtype) for...  49.2 us
  transfers between devices with their start and end apart: 84, of which 30 were waited for; matrix products, arithmetic and copies ran while one was open for 1% of the time, Pallas kernels for 13%

profile of v3, /device:TPU:0, one launch (start us, length us, event | category | flops | bytes accessed | tf_op | source)
XLA Modules:
  0.0 299.5 jit_solution(3847536539675554584)
XLA Ops:
  2.6 3.2 %pack_qkvg.1 = (bf16[272,512]{1,0:T(8,128)(2,1)}, bf16[272,512]{1,0:T(8,128)(2,1)}, bf16[2,272,512]{2,1,0:T(8,128)(2,1)}) custom-call(s32[4]{0:T(128)} %pad_add_fusion.idx, bf16[256,3072]{1,0:T(8,128)(2,1)} %refs_8_.5, bf16[256,1024]{1,0:T(8,128)(2,1)} %refs_9_.1, bf16[4,1024]{1,0:T(4,128)(2,1)} %pk.1, bf16[4,1024]{1,0:T(4,128)(2,1)} %pv.1, ...), custom_call_target="tpu_custom_call" | custom-call | flops 1000 | bytes 1000 | tf_op jit(solution)/shard_map/pack_qkvg/pallas_call | solution.py:1270
  5.9 3.0 %collective-permute-start.11 = (bf16[2,272,512]{2,1,0:T(8,128)(2,1)}, bf16[2,272,512]{2,1,0:T(8,128)(2,1)S(1)}, u32[]{:S(2)}, u32[]{:S(2)}) collective-permute-start(bf16[2,272,512]{2,1,0:T(8,128)(2,1)} %get-tuple-element.142), channel_id=1, source_target_pairs={{0,2},{1,3},{2,0},{3,1},{4,6},{5,7},{6,4},{7,5},{8,10},{9,11},{10,... | collective-permute-start | bytes 1671176 | tf_op jit(solution)/shard_map/ppermute | solution.py:589
  11.3 18.5 %collective-permute-start.4 = (bf16[128,1024]{1,0:T(8,128)(2,1)S(1)}, bf16[128,1024]{1,0:T(8,128)(2,1)S(1)}, u32[]{:S(2)}, u32[]{:S(2)}) collective-permute-start(bf16[128,1024]{1,0:T(8,128)(2,1)S(1)} %collective-permute-done.refs_0_.x), channel_id=1, source_target_pairs={{0,2},{1,3},{2,0},{3,1},{4,6},{5,7},{6,4},{7,5},{8,10},{9,11},{10,... | collective-permute-start | bytes 786440 | tf_op jit(solution)/shard_map/ppermute | solution.py:589
  31.4 1.8 copy-done.1
  35.0 9.9 %collective-permute-done.4.refs_2_ = bf16[128,1024]{1,0:T(8,128)(2,1)S(1)} collective-permute-done((bf16[128,1024]{1,0:T(8,128)(2,1)S(1)}, bf16[128,1024]{1,0:T(8,128)(2,1)S(1)}, u32[]{:S(2)}, u32[]{:S(2)}) %collective-permute-start.4) | collective-permute-done | bytes 262176 | tf_op jit(solution)/shard_map/ppermute | solution.py:589
  45.6 2.5 collective-permute-start.16
  51.6 10.1 %mixer_forward.1 = (bf16[4,128,1024]{2,1,0:T(8,128)(2,1)S(1)}, bf16[4,128,1024]{2,1,0:T(8,128)(2,1)S(1)}, bf16[1024,1024]{1,0:T(8,128)(2,1)S(1)}, bf16[1024,512]...) custom-call(s32[4]{0:T(128)S(1)} %copy-done.4, ...), custom_call_target="tpu_custom_call" | custom-call | flops 11000000512 | bytes 1000 | tf_op jit(solution)/shard_map/mixer_forward/pallas_call | solution.py:654
  61.7 2.0 collective-permute-done.16.refs_18_
  63.7 5.4 %collective-permute-done.13.refs_10_ = bf16[128,1024]{1,0:T(8,128)(2,1)S(1)} collective-permute-done((bf16[128,1024]{1,0:T(8,128)(2,1)S(1)}, bf16[128,1024]{1,0:T(8,128)(2,1)S(1)}, u32[]{:S(2)}, u32[]{:S(2)}) %collective-permute-start.13) | collective-permute-done | bytes 262176 | tf_op jit(solution)/shard_map/ppermute | solution.py:589
  69.7 2.1 collective-permute-done.17.received
  72.0 1.8 collective-permute-start.18
  75.5 3.3 %collective-permute-start.34 = (bf16[2,128,768]{2,1,0:T(8,128)(2,1)S(1)}, bf16[2,128,768]{2,1,0:T(8,128)(2,1)S(1)}, u32[]{:S(2)}, u32[]{:S(2)}) collective-permute-start(bf16[2,128,768]{2,1,0:T(8,128)(2,1)S(1)} %collective-permute-done.16.refs_18_), channel_id=1, source_target_pairs={{0,8},{1,9},{2,10},{3,11},{4,12},{5,13},{6,14},{7,15},{8,0},{9,1},... | collective-permute-start | bytes 1179656 | tf_op jit(solution)/shard_map/ppermute | solution.py:589
  80.4 2.6 collective-permute-done.19.r2
  83.0 4.3 %collective-permute-done.20.r3 = bf16[128,1024]{1,0:T(8,128)(2,1)S(1)} collective-permute-done((bf16[128,1024]{1,0:T(8,128)(2,1)S(1)}, bf16[128,1024]{1,0:T(8,128)(2,1)S(1)}, u32[]{:S(2)}, u32[]{:S(2)}) %collective-permute-start.20) | collective-permute-done | bytes 262176 | tf_op jit(solution)/shard_map/ppermute | solution.py:589
  87.5 1.7 collective-permute-start.22
  91.6 4.7 %collective-permute-done.22.refs_2_ = bf16[128,1024]{1,0:T(8,128)(2,1)S(1)} collective-permute-done((bf16[128,1024]{1,0:T(8,128)(2,1)S(1)}, bf16[128,1024]{1,0:T(8,128)(2,1)S(1)}, u32[]{:S(2)}, u32[]{:S(2)}) %collective-permute-start.22) | collective-permute-done | bytes 262176 | tf_op jit(solution)/shard_map/ppermute | solution.py:589
  96.3 2.1 collective-permute-done.24.refs_4_
  98.4 4.7 %collective-permute-done.26.refs_6_ = bf16[128,1024]{1,0:T(8,128)(2,1)S(1)} collective-permute-done((bf16[128,1024]{1,0:T(8,128)(2,1)S(1)}, bf16[128,1024]{1,0:T(8,128)(2,1)S(1)}, u32[]{:S(2)}, u32[]{:S(2)}) %collective-permute-start.26) | collective-permute-done | bytes 262176 | tf_op jit(solution)/shard_map/ppermute | solution.py:589
  104.7 7.3 %feed.1 = (bf16[4,128,1024]{2,1,0:T(8,128)(2,1)S(1)}, bf16[4,128,1024]{2,1,0:T(8,128)(2,1)S(1)}, bf16[4,128,1024]{2,1,0:T(8,128)(2,1)S(1)}, bf16[4,128,1024]{2,1...) custom-call(s32[4]{0:T(128)S(1)} %copy-done.4, ...), custom_call_target="tpu_custom_call" | custom-call | flops 8249999872 | bytes 1000 | tf_op jit(solution)/shard_map/feed/pallas_call | solution.py:654
  112.1 3.5 %feed_weights.1 = (bf16[2,384,384]{2,1,0:T(8,128)(2,1)S(1)}, bf16[2,384,384]{2,1,0:T(8,128)(2,1)S(1)}, bf16[2,384,384]{2,1,0:T(8,128)(2,1)S(1)}, bf16[2,384,384]{2,1,0:T(8,128)(2,1)S(1)}) custom-call(s32[4]{0:T(128)S(1)} %copy-done.4, bf16[1024,768]{1,0:T(8,128)(2,1)S(1)} %get-tuple-element.162.dgu, bf16[1024,384]{1,0:T(8,128)(2,1)S(1)} %get-tuple-element.163.active, ...), custom_call_target="tpu_custom_call" | custom-call | flops 3849999872 | bytes 1000 | tf_op jit(solution)/shard_map/feed_weights/pallas_call | solution.py:654
  116.3 3.3 %collective-permute-start.41 = (bf16[2,384,384]{2,1,0:T(8,128)(2,1)S(1)}, bf16[2,384,384]{2,1,0:T(8,128)(2,1)S(1)}, u32[]{:S(2)}, u32[]{:S(2)}) collective-permute-start(bf16[2,384,384]{2,1,0:T(8,128)(2,1)S(1)} %get-tuple-element.164), channel_id=1, source_target_pairs={{0,8},{1,9},{2,10},{3,11},{4,12},{5,13},{6,14},{7,15},{8,0},{9,1},... | collective-permute-start | bytes 1769480 | tf_op jit(solution)/shard_map/ppermute | solution.py:589
  119.6 1.7 collective-permute-start.38
  123.4 4.6 %collective-permute-done.38.r1 = bf16[128,1024]{1,0:T(8,128)(2,1)S(1)} collective-permute-done((bf16[128,1024]{1,0:T(8,128)(2,1)S(1)}, bf16[128,1024]{1,0:T(8,128)(2,1)S(1)}, u32[]{:S(2)}, u32[]{:S(2)}) %collective-permute-start.38) | collective-permute-done | bytes 262176 | tf_op jit(solution)/shard_map/ppermute | solution.py:589
  128.0 2.6 collective-permute-done.39.r2
  130.5 4.0 %collective-permute-done.40.r3 = bf16[128,1024]{1,0:T(8,128)(2,1)S(1)} collective-permute-done((bf16[128,1024]{1,0:T(8,128)(2,1)S(1)}, bf16[128,1024]{1,0:T(8,128)(2,1)S(1)}, u32[]{:S(2)}, u32[]{:S(2)}) %collective-permute-start.40) | collective-permute-done | bytes 262176 | tf_op jit(solution)/shard_map/ppermute | solution.py:589
  134.9 1.7 collective-permute-start.49
  140.3 12.0 %collective-permute-done.46.received = bf16[2,384,384]{2,1,0:T(8,128)(2,1)S(1)} collective-permute-done((bf16[2,384,384]{2,1,0:T(8,128)(2,1)S(1)}, bf16[2,384,384]{2,1,0:T(8,128)(2,1)S(1)}, u32[]{:S(2)}, u32[]{:S(2)}) %collective-permute-start.46) | collective-permute-done | bytes 589856 | tf_op jit(solution)/shard_map/ppermute | solution.py:589
  154.9 1.7 collective-permute-start.43
  158.4 13.1 %mixer_backward.1 = (bf16[4,144,1024]{2,1,0:T(8,128)(2,1)S(1)}, bf16[4,144,1024]{2,1,0:T(8,128)(2,1)S(1)}, bf16[1024,512]{1,0:T(8,128)(2,1)S(1)}, bf16[1024,1024]{1,0:T(8,128)(2,1)S(1)}) custom-call(s32[4]{0:T(128)S(1)} %copy-done.4, f32[2,128]{1,0:T(2,128)S(1)} %pad_maximum_fusion.1.rates, bf16[128,1024]{1,0:T(8,128)(2,1)S(1)} %get-tuple-element.181.refs_0_, ...), custom_call_target="tpu_custom_call" | custom-call | flops 14300000256 | bytes 1000 | tf_op jit(solution)/shard_map/mixer_backward/pallas_call | solution.py:654
  171.8 2.2 mixer_weights.1
  174.0 2.1 collective-permute-start.59
  178.2 3.7 %collective-permute-done.56.refs_2_ = bf16[64,768]{1,0:T(8,128)(2,1)S(1)} collective-permute-done((bf16[64,768]{1,0:T(8,128)(2,1)S(1)}, bf16[64,768]{1,0:T(8,128)(2,1)S(1)}, u32[]{:S(2)}, u32[]{:S(2)}) %collective-permute-start.56) | collective-permute-done | bytes 98336 | tf_op jit(solution)/shard_map/ppermute | solution.py:589
  186.2 18.1 %collective-permute-done.59.received = bf16[2,320,512]{2,1,0:T(8,128)(2,1)S(1)} collective-permute-done((bf16[2,320,512]{2,1,0:T(8,128)(2,1)S(1)}, bf16[2,320,512]{2,1,0:T(8,128)(2,1)S(1)}, u32[]{:S(2)}, u32[]{:S(2)}) %collective-permute-start.59) | collective-permute-done | bytes 655392 | tf_op jit(solution)/shard_map/ppermute | solution.py:589
  206.7 10.1 %collective-permute-done.67.refs_2_ = bf16[384,768]{1,0:T(8,128)(2,1)S(1)} collective-permute-done((bf16[384,768]{1,0:T(8,128)(2,1)S(1)}, bf16[384,768]{1,0:T(8,128)(2,1)S(1)}, u32[]{:S(2)}, u32[]{:S(2)}) %collective-permute-start.67) | collective-permute-done | bytes 589856 | tf_op jit(solution)/shard_map/ppermute | solution.py:589
  218.1 13.4 %collective-permute-done.62.refs_1_ = bf16[320,512]{1,0:T(8,128)(2,1)S(1)} collective-permute-done((bf16[320,512]{1,0:T(8,128)(2,1)S(1)}, bf16[320,512]{1,0:T(8,128)(2,1)S(1)}, u32[]{:S(2)}, u32[]{:S(2)}) %collective-permute-start.62) | collective-permute-done | bytes 327712 | tf_op jit(solution)/shard_map/ppermute | solution.py:589
  233.2 1.7 collective-permute-start.64
  239.0 11.6 %collective-permute-done.79.refs_6_ = bf16[384,768]{1,0:T(8,128)(2,1)S(1)} collective-permute-done((bf16[384,768]{1,0:T(8,128)(2,1)S(1)}, bf16[384,768]{1,0:T(8,128)(2,1)S(1)}, u32[]{:S(2)}, u32[]{:S(2)}) %collective-permute-start.79) | collective-permute-done | bytes 589856 | tf_op jit(solution)/shard_map/ppermute | solution.py:589
  250.6 1.9 collective-permute-start.80
  252.8 7.9 %collective-permute-start.74 = (bf16[144,1024]{1,0:T(8,128)(2,1)S(1)}, bf16[144,1024]{1,0:T(8,128)(2,1)S(1)}, u32[]{:S(2)}, u32[]{:S(2)}) collective-permute-start(bf16[144,1024]{1,0:T(8,128)(2,1)S(1)} %get-tuple-element.241), channel_id=1, source_target_pairs={{0,2},{1,3},{2,0},{3,1},{4,6},{5,7},{6,4},{7,5},{8,10},{9,11},{10,... | collective-permute-start | bytes 884744 | tf_op jit(solution)/shard_map/ppermute | solution.py:589
  260.7 7.4 %collective-permute-done.74.received = bf16[144,1024]{1,0:T(8,128)(2,1)S(1)} collective-permute-done((bf16[144,1024]{1,0:T(8,128)(2,1)S(1)}, bf16[144,1024]{1,0:T(8,128)(2,1)S(1)}, u32[]{:S(2)}, u32[]{:S(2)}) %collective-permute-start.74) | collective-permute-done | bytes 294944 | tf_op jit(solution)/shard_map/ppermute | solution.py:589
  269.4 1.8 collective-permute-done.71.refs_1_
  271.2 1.8 collective-permute-start.77
  274.3 3.3 %collective-permute-start.82 = (f32[8,1024]{1,0:T(8,128)S(1)}, f32[8,1024]{1,0:T(8,128)S(1)}, u32[]{:S(2)}, u32[]{:S(2)}) collective-permute-start(f32[8,1024]{1,0:T(8,128)S(1)} %get-tuple-element.258), channel_id=1, source_target_pairs={{0,8},{1,9},{2,10},{3,11},{4,12},{5,13},{6,14},{7,15},{8,0},{9,1},... | collective-permute-start | bytes 98312 | tf_op jit(solution)/shard_map/ppermute | solution.py:589
  277.5 5.5 %feed_unpack.1 = (f32[256,5632]{1,0:T(8,128)}, f32[704,1024]{1,0:T(8,128)}, f32[1,256]{1,0:T(1,128)}) custom-call(s32[4]{0:T(128)S(1)} %copy-done.4, bf16[384,768]{1,0:T(8,128)(2,1)S(1)} %feed_join.1.refs_0_, bf16[384,768]{1,0:T(8,128)(2,1)S(1)} %collective-permute-done.61.refs_1_, bf16[384,768]{1,0:T(8,128)(2,1)S(1)} %collective-permute-done.67.refs_2_, ...), custom_call_target="tpu_custom_call" | custom-call | flops 6049999872 | bytes 1000 | tf_op jit(solution)/shard_map/feed_unpack/pallas_call | solution.py:654
  284.3 2.5 collective-permute-start.81
  286.8 2.4 collective-permute-done.82
  290.0 4.0 %collective-permute-done.83 = f32[8,1024]{1,0:T(8,128)S(1)} collective-permute-done((f32[8,1024]{1,0:T(8,128)S(1)}, f32[8,1024]{1,0:T(8,128)S(1)}, u32[]{:S(2)}, u32[]{:S(2)}) %collective-permute-start.83) | collective-permute-done | bytes 32800 | tf_op jit(solution)/shard_map/ppermute | solution.py:589
  294.8 3.6 %mixer_unpack.1 = (f32[256,3072]{1,0:T(8,128)}, f32[256,1024]{1,0:T(8,128)}, f32[256,1024]{1,0:T(8,128)}, f32[1,256]{1,0:T(1,128)}) custom-call(s32[4]{0:T(128)S(1)} %copy-done.4, bf16[320,512]{1,0:T(8,128)(2,1)S(1)} %mixer_join.1.refs_0_, bf16[320,512]{1,0:T(8,128)(2,1)S(1)} %collective-permute-done.71.refs_1_, ...), custom_call_target="tpu_custom_call" | custom-call | flops 550000000 | bytes 1000 | tf_op jit(solution)/shard_map/mixer_unpack/pallas_call | solution.py:654
  (192 shorter events, 54.0 us)
Async XLA Ops:
  5.9 25.5 %collective-permute-start.11 = (bf16[2,272,512]{2,1,0:T(8,128)(2,1)}, bf16[2,272,512]{2,1,0:T(8,128)(2,1)S(1)}, u32[]{:S(2)}, u32[]{:S(2)}) collective-permute-start(bf16[2,272,512]{2,1,0:T(8,128)(2,1)} %get-tuple-element.142), channel_id=1, source_target_pairs={{0,2},{1,3},{2,0},{3,1},{4,6},{5,7},{6,4},{7,5},{8,10},{9,11},{10,... | collective-permute-start | bytes 1671176 | tf_op jit(solution)/shard_map/ppermute | solution.py:589
  8.9 22.3 %collective-permute-start.10 = (bf16[272,512]{1,0:T(8,128)(2,1)}, bf16[272,512]{1,0:T(8,128)(2,1)S(1)}, u32[]{:S(2)}, u32[]{:S(2)}) collective-permute-start(bf16[272,512]{1,0:T(8,128)(2,1)} %get-tuple-element.141), channel_id=1, source_target_pairs={{0,1},{1,0},{2,3},{3,2},{4,5},{5,4},{6,7},{7,6},{8,9},{9,8},{10,11... | collective-permute-start | bytes 835592 | tf_op jit(solution)/shard_map/ppermute | solution.py:589
  9.9 19.9 %collective-permute-start.1 = (s32[10,128]{1,0:T(8,128)S(1)}, s32[10,128]{1,0:T(8,128)S(1)}, u32[]{:S(2)}, u32[]{:S(2)}) collective-permute-start(s32[10,128]{1,0:T(8,128)S(1)} %add_bitcast_fusion), channel_id=1, source_target_pairs={{0,0},{1,8},{2,16},{3,24},{4,4},{5,12},{6,20},{7,28},{8,1},{9,9},{... | collective-permute-start | bytes 15368 | tf_op jit(solution)/shard_map/ppermute | solution.py:589
  10.6 23.8 %collective-permute-start.2 = (bf16[128,1024]{1,0:T(8,128)(2,1)S(1)}, bf16[128,1024]{1,0:T(8,128)(2,1)S(1)}, u32[]{:S(2)}, u32[]{:S(2)}) collective-permute-start(bf16[128,1024]{1,0:T(8,128)(2,1)S(1)} %bitcast.18), channel_id=1, source_target_pairs={{0,0},{1,8},{2,16},{3,24},{4,4},{5,12},{6,20},{7,28},{8,1},{9,9},{... | collective-permute-start | bytes 786440 | tf_op jit(solution)/shard_map/ppermute | solution.py:589
  11.3 33.6 %collective-permute-start.4 = (bf16[128,1024]{1,0:T(8,128)(2,1)S(1)}, bf16[128,1024]{1,0:T(8,128)(2,1)S(1)}, u32[]{:S(2)}, u32[]{:S(2)}) collective-permute-start(bf16[128,1024]{1,0:T(8,128)(2,1)S(1)} %collective-permute-done.refs_0_.x), channel_id=1, source_target_pairs={{0,2},{1,3},{2,0},{3,1},{4,6},{5,7},{6,4},{7,5},{8,10},{9,11},{10,... | collective-permute-start | bytes 786440 | tf_op jit(solution)/shard_map/ppermute | solution.py:589
  29.8 15.2 %collective-permute-start.6 = (bf16[128,1024]{1,0:T(8,128)(2,1)S(1)}, bf16[128,1024]{1,0:T(8,128)(2,1)S(1)}, u32[]{:S(2)}, u32[]{:S(2)}) collective-permute-start(bf16[128,1024]{1,0:T(8,128)(2,1)S(1)} %collective-permute-done.refs_0_.x), channel_id=1, source_target_pairs={{0,4},{1,5},{2,6},{3,7},{4,0},{5,1},{6,2},{7,3},{8,12},{9,13},{10,... | collective-permute-start | bytes 786440 | tf_op jit(solution)/shard_map/ppermute | solution.py:589
  31.2 14.2 %collective-permute-start.8 = (bf16[128,1024]{1,0:T(8,128)(2,1)S(1)}, bf16[128,1024]{1,0:T(8,128)(2,1)S(1)}, u32[]{:S(2)}, u32[]{:S(2)}) collective-permute-start(bf16[128,1024]{1,0:T(8,128)(2,1)S(1)} %collective-permute-done.refs_0_.x), channel_id=1, source_target_pairs={{0,6},{1,7},{2,4},{3,5},{4,2},{5,3},{6,0},{7,1},{8,14},{9,15},{10,... | collective-permute-start | bytes 786440 | tf_op jit(solution)/shard_map/ppermute | solution.py:589
  31.3 20.3 %collective-permute-start.12 = (bf16[2,272,512]{2,1,0:T(8,128)(2,1)S(1)}, bf16[2,272,512]{2,1,0:T(8,128)(2,1)S(1)}, u32[]{:S(2)}, u32[]{:S(2)}) collective-permute-start(bf16[2,272,512]{2,1,0:T(8,128)(2,1)S(1)} %collective-permute-done.11.refs_10_), channel_id=1, source_target_pairs={{0,1},{1,0},{2,3},{3,2},{4,5},{5,4},{6,7},{7,6},{8,9},{9,8},{10,11... | collective-permute-start | bytes 1671176 | tf_op jit(solution)/shard_map/ppermute | solution.py:589
  34.4 11.1 %collective-permute-start.3 = (bf16[128,1024]{1,0:T(8,128)(2,1)S(1)}, bf16[128,1024]{1,0:T(8,128)(2,1)S(1)}, u32[]{:S(2)}, u32[]{:S(2)}) collective-permute-start(bf16[128,1024]{1,0:T(8,128)(2,1)S(1)} %collective-permute-done.refs_0_.x), channel_id=1, source_target_pairs={{0,1},{1,0},{2,3},{3,2},{4,5},{5,4},{6,7},{7,6},{8,9},{9,8},{10,11... | collective-permute-start | bytes 786440 | tf_op jit(solution)/shard_map/ppermute | solution.py:589
  45.6 18.1 %collective-permute-start.16 = (bf16[2,128,768]{2,1,0:T(8,128)(2,1)S(1)}, bf16[2,128,768]{2,1,0:T(8,128)(2,1)S(1)}, u32[]{:S(2)}, u32[]{:S(2)}) collective-permute-start(bf16[2,128,768]{2,1,0:T(8,128)(2,1)S(1)} %get-tuple-element.148), channel_id=1, source_target_pairs={{0,2},{1,3},{2,0},{3,1},{4,6},{5,7},{6,4},{7,5},{8,10},{9,11},{10,... | collective-permute-start | bytes 1179656 | tf_op jit(solution)/shard_map/ppermute | solution.py:589
  48.1 21.0 %collective-permute-start.13 = (bf16[128,1024]{1,0:T(8,128)(2,1)S(1)}, bf16[128,1024]{1,0:T(8,128)(2,1)S(1)}, u32[]{:S(2)}, u32[]{:S(2)}) collective-permute-start(bf16[128,1024]{1,0:T(8,128)(2,1)S(1)} %collective-permute-done.2.refs_8_.cot), channel_id=1, source_target_pairs={{0,2},{1,3},{2,0},{3,1},{4,6},{5,7},{6,4},{7,5},{8,10},{9,11},{10,... | collective-permute-start | bytes 786440 | tf_op jit(solution)/shard_map/ppermute | solution.py:589
  49.0 20.1 %collective-permute-start.14 = (bf16[128,1024]{1,0:T(8,128)(2,1)S(1)}, bf16[128,1024]{1,0:T(8,128)(2,1)S(1)}, u32[]{:S(2)}, u32[]{:S(2)}) collective-permute-start(bf16[128,1024]{1,0:T(8,128)(2,1)S(1)} %collective-permute-done.2.refs_8_.cot), channel_id=1, source_target_pairs={{0,4},{1,5},{2,6},{3,7},{4,0},{5,1},{6,2},{7,3},{8,12},{9,13},{10,... | collective-permute-start | bytes 786440 | tf_op jit(solution)/shard_map/ppermute | solution.py:589
  50.4 18.6 %collective-permute-start.15 = (bf16[128,1024]{1,0:T(8,128)(2,1)S(1)}, bf16[128,1024]{1,0:T(8,128)(2,1)S(1)}, u32[]{:S(2)}, u32[]{:S(2)}) collective-permute-start(bf16[128,1024]{1,0:T(8,128)(2,1)S(1)} %collective-permute-done.2.refs_8_.cot), channel_id=1, source_target_pairs={{0,6},{1,7},{2,4},{3,5},{4,2},{5,3},{6,0},{7,1},{8,14},{9,15},{10,... | collective-permute-start | bytes 786440 | tf_op jit(solution)/shard_map/ppermute | solution.py:589
  75.3 12.0 %collective-permute-start.20 = (bf16[128,1024]{1,0:T(8,128)(2,1)S(1)}, bf16[128,1024]{1,0:T(8,128)(2,1)S(1)}, u32[]{:S(2)}, u32[]{:S(2)}) collective-permute-start(bf16[128,1024]{1,0:T(8,128)(2,1)S(1)} %get-tuple-element.153), channel_id=1, source_target_pairs={{0,6},{1,7},{2,4},{3,5},{4,2},{5,3},{6,0},{7,1},{8,14},{9,15},{10,... | collective-permute-start | bytes 786440 | tf_op jit(solution)/shard_map/ppermute | solution.py:589
  75.5 15.2 %collective-permute-start.34 = (bf16[2,128,768]{2,1,0:T(8,128)(2,1)S(1)}, bf16[2,128,768]{2,1,0:T(8,128)(2,1)S(1)}, u32[]{:S(2)}, u32[]{:S(2)}) collective-permute-start(bf16[2,128,768]{2,1,0:T(8,128)(2,1)S(1)} %collective-permute-done.16.refs_18_), channel_id=1, source_target_pairs={{0,8},{1,9},{2,10},{3,11},{4,12},{5,13},{6,14},{7,15},{8,0},{9,1},... | collective-permute-start | bytes 1179656 | tf_op jit(solution)/shard_map/ppermute | solution.py:589
  90.8 12.4 %collective-permute-start.26 = (bf16[128,1024]{1,0:T(8,128)(2,1)S(1)}, bf16[128,1024]{1,0:T(8,128)(2,1)S(1)}, u32[]{:S(2)}, u32[]{:S(2)}) collective-permute-start(bf16[128,1024]{1,0:T(8,128)(2,1)S(1)} %get-tuple-element.155.refs_0_), channel_id=1, source_target_pairs={{0,6},{1,7},{2,4},{3,5},{4,2},{5,3},{6,0},{7,1},{8,14},{9,15},{10,... | collective-permute-start | bytes 786440 | tf_op jit(solution)/shard_map/ppermute | solution.py:589
  91.1 12.0 %collective-permute-start.35 = (bf16[2,128,768]{2,1,0:T(8,128)(2,1)S(1)}, bf16[2,128,768]{2,1,0:T(8,128)(2,1)S(1)}, u32[]{:S(2)}, u32[]{:S(2)}) collective-permute-start(bf16[2,128,768]{2,1,0:T(8,128)(2,1)S(1)} %collective-permute-done.34.refs_20_), channel_id=1, source_target_pairs={{0,1},{1,0},{2,3},{3,2},{4,5},{5,4},{6,7},{7,6},{8,9},{9,8},{10,11... | collective-permute-start | bytes 1179656 | tf_op jit(solution)/shard_map/ppermute | solution.py:589
  91.1 12.0 %collective-permute-start.21 = (bf16[128,1024]{1,0:T(8,128)(2,1)S(1)}, bf16[128,1024]{1,0:T(8,128)(2,1)S(1)}, u32[]{:S(2)}, u32[]{:S(2)}) collective-permute-start(bf16[128,1024]{1,0:T(8,128)(2,1)S(1)} %get-tuple-element.155.refs_0_), channel_id=1, source_target_pairs={{0,1},{1,0},{2,3},{3,2},{4,5},{5,4},{6,7},{7,6},{8,9},{9,8},{10,11... | collective-permute-start | bytes 786440 | tf_op jit(solution)/shard_map/ppermute | solution.py:589
  116.3 21.8 %collective-permute-start.41 = (bf16[2,384,384]{2,1,0:T(8,128)(2,1)S(1)}, bf16[2,384,384]{2,1,0:T(8,128)(2,1)S(1)}, u32[]{:S(2)}, u32[]{:S(2)}) collective-permute-start(bf16[2,384,384]{2,1,0:T(8,128)(2,1)S(1)} %get-tuple-element.164), channel_id=1, source_target_pairs={{0,8},{1,9},{2,10},{3,11},{4,12},{5,13},{6,14},{7,15},{8,0},{9,1},... | collective-permute-start | bytes 1769480 | tf_op jit(solution)/shard_map/ppermute | solution.py:589
  122.8 11.7 %collective-permute-start.40 = (bf16[128,1024]{1,0:T(8,128)(2,1)S(1)}, bf16[128,1024]{1,0:T(8,128)(2,1)S(1)}, u32[]{:S(2)}, u32[]{:S(2)}) collective-permute-start(bf16[128,1024]{1,0:T(8,128)(2,1)S(1)} %get-tuple-element.176), channel_id=1, source_target_pairs={{0,6},{1,7},{2,4},{3,5},{4,2},{5,3},{6,0},{7,1},{8,14},{9,15},{10,... | collective-permute-start | bytes 786440 | tf_op jit(solution)/shard_map/ppermute | solution.py:589
  123.1 29.1 %collective-permute-start.46 = (bf16[2,384,384]{2,1,0:T(8,128)(2,1)S(1)}, bf16[2,384,384]{2,1,0:T(8,128)(2,1)S(1)}, u32[]{:S(2)}, u32[]{:S(2)}) collective-permute-start(bf16[2,384,384]{2,1,0:T(8,128)(2,1)S(1)} %get-tuple-element.190), channel_id=1, source_target_pairs={{0,8},{1,9},{2,10},{3,11},{4,12},{5,13},{6,14},{7,15},{8,0},{9,1},... | collective-permute-start | bytes 1769480 | tf_op jit(solution)/shard_map/ppermute | solution.py:589
  134.9 17.4 %collective-permute-start.49 = (bf16[128,1024]{1,0:T(8,128)(2,1)S(1)}, bf16[128,1024]{1,0:T(8,128)(2,1)S(1)}, u32[]{:S(2)}, u32[]{:S(2)}) collective-permute-start(bf16[128,1024]{1,0:T(8,128)(2,1)S(1)} %get-tuple-element.181.refs_0_), channel_id=1, source_target_pairs={{0,2},{1,3},{2,0},{3,1},{4,6},{5,7},{6,4},{7,5},{8,10},{9,11},{10,... | collective-permute-start | bytes 786440 | tf_op jit(solution)/shard_map/ppermute | solution.py:589
  136.6 16.2 %collective-permute-start.51 = (bf16[128,1024]{1,0:T(8,128)(2,1)S(1)}, bf16[128,1024]{1,0:T(8,128)(2,1)S(1)}, u32[]{:S(2)}, u32[]{:S(2)}) collective-permute-start(bf16[128,1024]{1,0:T(8,128)(2,1)S(1)} %get-tuple-element.181.refs_0_), channel_id=1, source_target_pairs={{0,4},{1,5},{2,6},{3,7},{4,0},{5,1},{6,2},{7,3},{8,12},{9,13},{10,... | collective-permute-start | bytes 786440 | tf_op jit(solution)/shard_map/ppermute | solution.py:589
  138.2 14.6 %collective-permute-start.42 = (bf16[128,1024]{1,0:T(8,128)(2,1)S(1)}, bf16[128,1024]{1,0:T(8,128)(2,1)S(1)}, u32[]{:S(2)}, u32[]{:S(2)}) collective-permute-start(bf16[128,1024]{1,0:T(8,128)(2,1)S(1)} %get-tuple-element.181.refs_0_), channel_id=1, source_target_pairs={{0,6},{1,7},{2,4},{3,5},{4,2},{5,3},{6,0},{7,1},{8,14},{9,15},{10,... | collective-permute-start | bytes 786440 | tf_op jit(solution)/shard_map/ppermute | solution.py:589
  138.6 14.8 %collective-permute-start.47 = (bf16[384,384]{1,0:T(8,128)(2,1)S(1)}, bf16[384,384]{1,0:T(8,128)(2,1)S(1)}, u32[]{:S(2)}, u32[]{:S(2)}) collective-permute-start(bf16[384,384]{1,0:T(8,128)(2,1)S(1)} %get-tuple-element.180), channel_id=1, source_target_pairs={{0,16},{1,17},{2,18},{3,19},{4,20},{5,21},{6,22},{7,23},{8,24},{9,... | collective-permute-start | bytes 884744 | tf_op jit(solution)/shard_map/ppermute | solution.py:589
  153.4 18.1 %collective-permute-start.54 = (bf16[384,384]{1,0:T(8,128)(2,1)S(1)}, bf16[384,384]{1,0:T(8,128)(2,1)S(1)}, u32[]{:S(2)}, u32[]{:S(2)}) collective-permute-start(bf16[384,384]{1,0:T(8,128)(2,1)S(1)} %get-tuple-element.191), channel_id=1, source_target_pairs={{0,16},{1,17},{2,18},{3,19},{4,20},{5,21},{6,22},{7,23},{8,24},{9,... | collective-permute-start | bytes 884744 | tf_op jit(solution)/shard_map/ppermute | solution.py:589
  154.9 16.7 %collective-permute-start.43 = (bf16[128,1024]{1,0:T(8,128)(2,1)S(1)}, bf16[128,1024]{1,0:T(8,128)(2,1)S(1)}, u32[]{:S(2)}, u32[]{:S(2)}) collective-permute-start(bf16[128,1024]{1,0:T(8,128)(2,1)S(1)} %get-tuple-element.183), channel_id=1, source_target_pairs={{0,2},{1,3},{2,0},{3,1},{4,6},{5,7},{6,4},{7,5},{8,10},{9,11},{10,... | collective-permute-start | bytes 786440 | tf_op jit(solution)/shard_map/ppermute | solution.py:589
  156.6 15.0 %collective-permute-start.44 = (bf16[128,1024]{1,0:T(8,128)(2,1)S(1)}, bf16[128,1024]{1,0:T(8,128)(2,1)S(1)}, u32[]{:S(2)}, u32[]{:S(2)}) collective-permute-start(bf16[128,1024]{1,0:T(8,128)(2,1)S(1)} %get-tuple-element.184), channel_id=1, source_target_pairs={{0,4},{1,5},{2,6},{3,7},{4,0},{5,1},{6,2},{7,3},{8,12},{9,13},{10,... | collective-permute-start | bytes 786440 | tf_op jit(solution)/shard_map/ppermute | solution.py:589
  158.0 13.5 %collective-permute-start.45 = (bf16[128,1024]{1,0:T(8,128)(2,1)S(1)}, bf16[128,1024]{1,0:T(8,128)(2,1)S(1)}, u32[]{:S(2)}, u32[]{:S(2)}) collective-permute-start(bf16[128,1024]{1,0:T(8,128)(2,1)S(1)} %get-tuple-element.185), channel_id=1, source_target_pairs={{0,6},{1,7},{2,4},{3,5},{4,2},{5,3},{6,0},{7,1},{8,14},{9,15},{10,... | collective-permute-start | bytes 786440 | tf_op jit(solution)/shard_map/ppermute | solution.py:589
  174.0 30.3 %collective-permute-start.59 = (bf16[2,320,512]{2,1,0:T(8,128)(2,1)S(1)}, bf16[2,320,512]{2,1,0:T(8,128)(2,1)S(1)}, u32[]{:S(2)}, u32[]{:S(2)}) collective-permute-start(bf16[2,320,512]{2,1,0:T(8,128)(2,1)S(1)} %get-tuple-element.219), channel_id=1, source_target_pairs={{0,8},{1,9},{2,10},{3,11},{4,12},{5,13},{6,14},{7,15},{8,0},{9,1},... | collective-permute-start | bytes 1966088 | tf_op jit(solution)/shard_map/ppermute | solution.py:589
  182.7 34.1 %collective-permute-start.67 = (bf16[384,768]{1,0:T(8,128)(2,1)S(1)}, bf16[384,768]{1,0:T(8,128)(2,1)S(1)}, u32[]{:S(2)}, u32[]{:S(2)}) collective-permute-start(bf16[384,768]{1,0:T(8,128)(2,1)S(1)} %feed_join.1.refs_0_), channel_id=1, source_target_pairs={{0,8},{1,9},{2,10},{3,11},{4,12},{5,13},{6,14},{7,15},{8,0},{9,1},... | collective-permute-start | bytes 1769480 | tf_op jit(solution)/shard_map/ppermute | solution.py:589
  183.1 35.0 %collective-permute-start.61 = (bf16[384,768]{1,0:T(8,128)(2,1)S(1)}, bf16[384,768]{1,0:T(8,128)(2,1)S(1)}, u32[]{:S(2)}, u32[]{:S(2)}) collective-permute-start(bf16[384,768]{1,0:T(8,128)(2,1)S(1)} %feed_join.1.refs_0_), channel_id=1, source_target_pairs={{0,4},{1,5},{2,6},{3,7},{4,0},{5,1},{6,2},{7,3},{8,12},{9,13},{10,... | collective-permute-start | bytes 1769480 | tf_op jit(solution)/shard_map/ppermute | solution.py:589
  184.6 47.0 %collective-permute-start.72 = (bf16[384,768]{1,0:T(8,128)(2,1)S(1)}, bf16[384,768]{1,0:T(8,128)(2,1)S(1)}, u32[]{:S(2)}, u32[]{:S(2)}) collective-permute-start(bf16[384,768]{1,0:T(8,128)(2,1)S(1)} %feed_join.1.refs_0_), channel_id=1, source_target_pairs={{0,16},{1,17},{2,18},{3,19},{4,20},{5,21},{6,22},{7,23},{8,24},{9,... | collective-permute-start | bytes 1769480 | tf_op jit(solution)/shard_map/ppermute | solution.py:589
  204.4 27.1 %collective-permute-start.62 = (bf16[320,512]{1,0:T(8,128)(2,1)S(1)}, bf16[320,512]{1,0:T(8,128)(2,1)S(1)}, u32[]{:S(2)}, u32[]{:S(2)}) collective-permute-start(bf16[320,512]{1,0:T(8,128)(2,1)S(1)} %get-tuple-element.225), channel_id=1, source_target_pairs={{0,16},{1,17},{2,18},{3,19},{4,20},{5,21},{6,22},{7,23},{8,24},{9,... | collective-permute-start | bytes 983048 | tf_op jit(solution)/shard_map/ppermute | solution.py:589
  205.3 27.9 %collective-permute-start.66 = (bf16[2,144,1024]{2,1,0:T(8,128)(2,1)S(1)}, bf16[2,144,1024]{2,1,0:T(8,128)(2,1)S(1)}, u32[]{:S(2)}, u32[]{:S(2)}) collective-permute-start(bf16[2,144,1024]{2,1,0:T(8,128)(2,1)S(1)} %get-tuple-element.235), channel_id=1, source_target_pairs={{0,4},{1,5},{2,6},{3,7},{4,0},{5,1},{6,2},{7,3},{8,12},{9,13},{10,... | collective-permute-start | bytes 1769480 | tf_op jit(solution)/shard_map/ppermute | solution.py:589
  216.8 19.2 %collective-permute-start.68 = (bf16[384,768]{1,0:T(8,128)(2,1)S(1)}, bf16[384,768]{1,0:T(8,128)(2,1)S(1)}, u32[]{:S(2)}, u32[]{:S(2)}) collective-permute-start(bf16[384,768]{1,0:T(8,128)(2,1)S(1)} %collective-permute-done.67.refs_2_), channel_id=1, source_target_pairs={{0,4},{1,5},{2,6},{3,7},{4,0},{5,1},{6,2},{7,3},{8,12},{9,13},{10,... | collective-permute-start | bytes 1769480 | tf_op jit(solution)/shard_map/ppermute | solution.py:589
  231.6 18.9 %collective-permute-start.79 = (bf16[384,768]{1,0:T(8,128)(2,1)S(1)}, bf16[384,768]{1,0:T(8,128)(2,1)S(1)}, u32[]{:S(2)}, u32[]{:S(2)}) collective-permute-start(bf16[384,768]{1,0:T(8,128)(2,1)S(1)} %collective-permute-done.72.refs_4_), channel_id=1, source_target_pairs={{0,8},{1,9},{2,10},{3,11},{4,12},{5,13},{6,14},{7,15},{8,0},{9,1},... | collective-permute-start | bytes 1769480 | tf_op jit(solution)/shard_map/ppermute | solution.py:589
  231.7 21.1 %collective-permute-start.73 = (bf16[384,768]{1,0:T(8,128)(2,1)S(1)}, bf16[384,768]{1,0:T(8,128)(2,1)S(1)}, u32[]{:S(2)}, u32[]{:S(2)}) collective-permute-start(bf16[384,768]{1,0:T(8,128)(2,1)S(1)} %collective-permute-done.72.refs_4_), channel_id=1, source_target_pairs={{0,4},{1,5},{2,6},{3,7},{4,0},{5,1},{6,2},{7,3},{8,12},{9,13},{10,... | collective-permute-start | bytes 1769480 | tf_op jit(solution)/shard_map/ppermute | solution.py:589
  236.0 16.4 %collective-permute-start.60 = (bf16[128,1024]{1,0:T(8,128)(2,1)S(1)}, bf16[128,1024]{1,0:T(8,128)(2,1)S(1)}, u32[]{:S(2)}, u32[]{:S(2)}) collective-permute-start(bf16[128,1024]{1,0:T(8,128)(2,1)S(1)} %output.1), channel_id=1, source_target_pairs={{0,0},{1,8},{2,16},{3,24},{4,4},{5,12},{6,20},{7,28},{8,1},{9,9},{... | collective-permute-start | bytes 786440 | tf_op jit(solution)/shard_map/ppermute | solution.py:589
  250.6 23.7 %collective-permute-start.80 = (bf16[384,768]{1,0:T(8,128)(2,1)S(1)}, bf16[384,768]{1,0:T(8,128)(2,1)S(1)}, u32[]{:S(2)}, u32[]{:S(2)}) collective-permute-start(bf16[384,768]{1,0:T(8,128)(2,1)S(1)} %collective-permute-done.79.refs_6_), channel_id=1, source_target_pairs={{0,4},{1,5},{2,6},{3,7},{4,0},{5,1},{6,2},{7,3},{8,12},{9,13},{10,... | collective-permute-start | bytes 1769480 | tf_op jit(solution)/shard_map/ppermute | solution.py:589
  252.4 15.7 %collective-permute-start.69 = (bf16[320,512]{1,0:T(8,128)(2,1)S(1)}, bf16[320,512]{1,0:T(8,128)(2,1)S(1)}, u32[]{:S(2)}, u32[]{:S(2)}) collective-permute-start(bf16[320,512]{1,0:T(8,128)(2,1)S(1)} %mixer_join.1.refs_0_), channel_id=1, source_target_pairs={{0,16},{1,17},{2,18},{3,19},{4,20},{5,21},{6,22},{7,23},{8,24},{9,... | collective-permute-start | bytes 983048 | tf_op jit(solution)/shard_map/ppermute | solution.py:589
  252.5 17.0 %collective-permute-start.70 = (bf16[320,512]{1,0:T(8,128)(2,1)S(1)}, bf16[320,512]{1,0:T(8,128)(2,1)S(1)}, u32[]{:S(2)}, u32[]{:S(2)}) collective-permute-start(bf16[320,512]{1,0:T(8,128)(2,1)S(1)} %mixer_join.1.refs_0_), channel_id=1, source_target_pairs={{0,8},{1,9},{2,10},{3,11},{4,12},{5,13},{6,14},{7,15},{8,0},{9,1},... | collective-permute-start | bytes 983048 | tf_op jit(solution)/shard_map/ppermute | solution.py:589
  252.5 18.7 %collective-permute-start.71 = (bf16[320,512]{1,0:T(8,128)(2,1)S(1)}, bf16[320,512]{1,0:T(8,128)(2,1)S(1)}, u32[]{:S(2)}, u32[]{:S(2)}) collective-permute-start(bf16[320,512]{1,0:T(8,128)(2,1)S(1)} %mixer_join.1.refs_0_), channel_id=1, source_target_pairs={{0,4},{1,5},{2,6},{3,7},{4,0},{5,1},{6,2},{7,3},{8,12},{9,13},{10,... | collective-permute-start | bytes 983048 | tf_op jit(solution)/shard_map/ppermute | solution.py:589
  252.8 15.3 %collective-permute-start.74 = (bf16[144,1024]{1,0:T(8,128)(2,1)S(1)}, bf16[144,1024]{1,0:T(8,128)(2,1)S(1)}, u32[]{:S(2)}, u32[]{:S(2)}) collective-permute-start(bf16[144,1024]{1,0:T(8,128)(2,1)S(1)} %get-tuple-element.241), channel_id=1, source_target_pairs={{0,2},{1,3},{2,0},{3,1},{4,6},{5,7},{6,4},{7,5},{8,10},{9,11},{10,... | collective-permute-start | bytes 884744 | tf_op jit(solution)/shard_map/ppermute | solution.py:589
  271.2 13.1 %collective-permute-start.77 = (bf16[320,512]{1,0:T(8,128)(2,1)S(1)}, bf16[320,512]{1,0:T(8,128)(2,1)S(1)}, u32[]{:S(2)}, u32[]{:S(2)}) collective-permute-start(bf16[320,512]{1,0:T(8,128)(2,1)S(1)} %collective-permute-done.69.refs_4_), channel_id=1, source_target_pairs={{0,4},{1,5},{2,6},{3,7},{4,0},{5,1},{6,2},{7,3},{8,12},{9,13},{10,... | collective-permute-start | bytes 983048 | tf_op jit(solution)/shard_map/ppermute | solution.py:589
  273.0 11.3 %collective-permute-start.78 = (bf16[320,512]{1,0:T(8,128)(2,1)S(1)}, bf16[320,512]{1,0:T(8,128)(2,1)S(1)}, u32[]{:S(2)}, u32[]{:S(2)}) collective-permute-start(bf16[320,512]{1,0:T(8,128)(2,1)S(1)} %collective-permute-done.69.refs_4_), channel_id=1, source_target_pairs={{0,8},{1,9},{2,10},{3,11},{4,12},{5,13},{6,14},{7,15},{8,0},{9,1},... | collective-permute-start | bytes 983048 | tf_op jit(solution)/shard_map/ppermute | solution.py:589
  273.3 15.9 %collective-permute-start.75 = (bf16[128,1024]{1,0:T(8,128)(2,1)S(1)}, bf16[128,1024]{1,0:T(8,128)(2,1)S(1)}, u32[]{:S(2)}, u32[]{:S(2)}) collective-permute-start(bf16[128,1024]{1,0:T(8,128)(2,1)S(1)} %get-tuple-element.247), channel_id=1, source_target_pairs={{0,0},{1,8},{2,16},{3,24},{4,4},{5,12},{6,20},{7,28},{8,1},{9,9},{... | collective-permute-start | bytes 786440 | tf_op jit(solution)/shard_map/ppermute | solution.py:589
  274.3 14.9 %collective-permute-start.82 = (f32[8,1024]{1,0:T(8,128)S(1)}, f32[8,1024]{1,0:T(8,128)S(1)}, u32[]{:S(2)}, u32[]{:S(2)}) collective-permute-start(f32[8,1024]{1,0:T(8,128)S(1)} %get-tuple-element.258), channel_id=1, source_target_pairs={{0,8},{1,9},{2,10},{3,11},{4,12},{5,13},{6,14},{7,15},{8,0},{9,1},... | collective-permute-start | bytes 98312 | tf_op jit(solution)/shard_map/ppermute | solution.py:589
  (51 other events, 524.8 us)

commit v4 on v3

--- a/solution.py
+++ b/solution.py
@@ -759,14 +759,14 @@
         hk = head_of(x, f, k)
         normed[pl.ds(pl.multiple_of(hk * 64, 64), 64), :] = normed_block[:64]
         normed[pl.ds(pl.multiple_of((15 - hk) * 64, 64), 64), :] = normed_block[64:]
-    for t in range(4):
-        rows = slice(t * 256, t * 256 + 256)
-        product = dot_nn(normed[rows, :], w_full[...])
-        qkv[rows, :] = product[:, :384].astype(jnp.bfloat16)
-        gate[rows, :] = jax.nn.sigmoid(product[:, 384:])
     state = jnp.zeros((128, 128), jnp.float32)
     moment = jnp.zeros((128, 128), jnp.float32)
     for t in range(8):
+        if t % 2 == 0:
+            rows = slice(t * 128, t * 128 + 256)
+            product = dot_nn(normed[rows, :], w_full[...])
+            qkv[rows, :] = product[:, :384].astype(jnp.bfloat16)
+            gate[rows, :] = jax.nn.sigmoid(product[:, 384:])
         rows = slice(t * 128, t * 128 + 128)
         width = (t + 1) * 128
         query = qkv[rows, 0:128]
@@ -824,7 +824,7 @@
     blocks = refs[0:8]
     w_out, w_full, qkv, gate, att, rec, probs, pprobs, states, pk, pv = refs[8:19]
     send, keep, dqkvg, branch = refs[19:23]
-    gm, dy, delta, ds, dk, dv, dsp = refs[23:30]
+    gm, ds, dk, dv, dsp = refs[23:28]
     x, f = idx[1], idx[2]
     head = 2 * f + x
     scale = HEAD_WIDTH_SIZE ** (-0.5)
@@ -839,14 +839,16 @@
         gm[late, :] = grad[64:]
         branch[early, :] = block[:64]
         branch[late, :] = block[64:]
-    for t in range(8):
+    grad_state = jnp.zeros((128, 128), jnp.float32)
+    grad_moment = jnp.zeros((128, 128), jnp.float32)
+    for t in range(7, -1, -1):
         rows = slice(t * 128, t * 128 + 128)
         width = (t + 1) * 128
         grad_low = gm[rows, :]
         grad = grad_low.astype(jnp.float32)
         opened = gate[rows, :]
         dqkvg[rows, 384:512] = (grad * rec[rows, :] * opened * (1.0 - opened)).astype(jnp.bfloat16)
-        dy[rows, :] = (grad * opened).astype(jnp.bfloat16)
+        dy_tile = (grad * opened).astype(jnp.bfloat16)
         row_delta = jnp.sum(grad * att[rows, :], axis=-1, keepdims=True)
         grad_probs = dot_nt(grad_low, qkv[0:width, 256:384])
         ds_tile = (probs[rows, 0:width].astype(jnp.float32) * (grad_probs - row_delta)).astype(
@@ -858,44 +860,44 @@
             jnp.bfloat16
         )
         dsp[rows, :] = dsp_tile
-        delta[rows, :] = (
+        query_grad = (
             dot_nn(ds_tile, qkv[0:width, 128:256]) + dot_nn(dsp_tile, pk[...])
         ) * scale
-    grad_pk = dot_tn(dsp[...], qkv[:, 0:128]) * scale
-    grad_pv = dot_tn(pprobs[...], gm[...])
-    grad_state = jnp.zeros((128, 128), jnp.float32)
-    grad_moment = jnp.zeros((128, 128), jnp.float32)
-    for t in range(7, -1, -1):
-        rows = slice(t * 128, t * 128 + 128)
-        rest = slice(t * 128, 1024)
-        dk[rows, :] = dot_tn(ds[rest, rows], qkv[rest, 0:128]) * scale
-        dv[rows, :] = dot_tn(probs[rest, rows], gm[rest, :])
         for c in (2 * t + 1, 2 * t):
             grows = slice(c * 64, c * 64 + 64)
+            local = slice((c - 2 * t) * 64, (c - 2 * t) * 64 + 64)
             alpha = rates[0, c * 8 + head]
             theta = rates[1, c * 8 + head]
             query, key, value = qkv[grows, 0:128], qkv[grows, 128:256], qkv[grows, 256:384]
-            dy_rows = dy[grows, :]
+            dy_rows = dy_tile[local]
             state = states[c]
             summed = grad_state + grad_moment
             high, low = split_two(summed)
-            key_summed = dot_nt(key, high) * scale
-            error = value.astype(jnp.float32) - dot_nt(key, state) * scale
-            grad_value = dv[grows, :] + theta * key_summed
-            grad_key = dk[grows, :] + (theta * scale) * (
-                dot_nn(error.astype(jnp.bfloat16), high)
-                - dot_nn(key_summed.astype(jnp.bfloat16), state)
-            )
-            grad_query = delta[grows, :] + dot_nn(dy_rows, state) * scale
-            dqkvg[grows, 0:128] = grad_query.astype(jnp.bfloat16)
-            dqkvg[grows, 128:256] = grad_key.astype(jnp.bfloat16)
-            dqkvg[grows, 256:384] = grad_value.astype(jnp.bfloat16)
             gram_high, gram_low = split_two(dot_tn(key, key) * (theta / HEAD_WIDTH_SIZE))
             product = dot_nn(high, gram_high) + dot_nn(low, gram_high) + dot_nn(high, gram_low)
             grad_state = (
                 dot_tn(dy_rows, query) * scale + (1.0 - alpha) * grad_state - product
             )
             grad_moment = momentum * summed
+            key_summed = dot_nt(key, high) * scale
+            error = value.astype(jnp.float32) - dot_nt(key, state) * scale
+            dv[grows, :] = theta * key_summed
+            dk[grows, :] = (theta * scale) * (
+                dot_nn(error.astype(jnp.bfloat16), high)
+                - dot_nn(key_summed.astype(jnp.bfloat16), state)
+            )
+            dqkvg[grows, 0:128] = (
+                query_grad[local] + dot_nn(dy_rows, state) * scale
+            ).astype(jnp.bfloat16)
+    grad_pk = dot_tn(dsp[...], qkv[:, 0:128]) * scale
+    grad_pv = dot_tn(pprobs[...], gm[...])
+    for t in range(8):
+        rows = slice(t * 128, t * 128 + 128)
+        rest = slice(t * 128, 1024)
+        key_grad = dk[rows, :] + dot_tn(ds[rest, rows], qkv[rest, 0:128]) * scale
+        value_grad = dv[rows, :] + dot_tn(probs[rest, rows], gm[rest, :])
+        dqkvg[rows, 128:256] = key_grad.astype(jnp.bfloat16)
+        dqkvg[rows, 256:384] = value_grad.astype(jnp.bfloat16)
     for k in range(8):
         hk = head_of(x, f, k)
         piece = jnp.concatenate(
@@ -1048,13 +1050,14 @@
     branch[...] = total.astype(jnp.bfloat16)
 
 
-def tokens_sum_kernel(keep, received, keep_far, keep_near, send_far):
-    keep_far[...] = keep[0].astype(jnp.float32) + received[0].astype(jnp.float32)
-    keep_near[...] = keep[1].astype(jnp.float32) + received[1].astype(jnp.float32)
-    for k in range(2):
-        send_far[k] = (keep[2 + k].astype(jnp.float32) + received[2 + k].astype(jnp.float32)).astype(
-            jnp.bfloat16
-        )
+def split_kernel(order, keep, received, own, beside, crossing):
+    def total(k):
+        return keep[k].astype(jnp.float32) + received[k].astype(jnp.float32)
+
+    own[...] = total(order[0])
+    beside[...] = total(order[1])
+    for i in range(2):
+        crossing[i] = total(order[2 + i]).astype(jnp.bfloat16)
 
 
 def far_kernel(own, passed, received, out_own, out_passed):
@@ -1070,8 +1073,12 @@
     out[...] = (grad_residual[...] + norm_grad(values, gain[...], grad)).astype(jnp.bfloat16)
 
 
-def output_kernel(residual, s0, r1, r2, r3, out):
-    out[...] = (residual[...] + total_of((s0, r1, r2, r3))).astype(jnp.bfloat16)
+def output_kernel(residual, own_sum, *refs):
+    received, out = refs[:-1], refs[-1]
+    total = residual[...] + own_sum[...]
+    for piece in received:
+        total = total + piece[...].astype(jnp.float32)
+    out[...] = total.astype(jnp.bfloat16)
 
 
 def half_kernel(keep, received, own, passed):
@@ -1199,6 +1206,28 @@
     )
 
 
+def split_sums(keep, received, order, name):
+    rows = keep.shape[1:]
+    return call(
+        functools.partial(split_kernel, order),
+        (),
+        (keep, received),
+        [(rows, jnp.float32), (rows, jnp.float32), ((2, *rows), jnp.bfloat16)],
+        name=name,
+    )
+
+
+def second_stage(own, beside, received, name):
+    rows = own.shape
+    return call(
+        far_kernel,
+        (),
+        (own, beside, received),
+        [(rows, jnp.float32), (rows, jnp.bfloat16)],
+        name=name,
+    )
+
+
 def cross_chips(s0, s1, s2, s3):
     return s0, flip(s1, 0, 2), flip(s2, 1, 0), flip(s3, 1, 2)
 
@@ -1305,8 +1334,10 @@
     gu_far = flip(after(gu_parts[2], own), 0, 2)
     blocks = gather_cores(near)
     rates = after(rates, own_cot)
-    cot_near = gather_chips(after(own_cot, near[2]))
-
+    ready = after(own_cot, near[2])
+    cot_near = [own_cot, flip(ready, 0, 2), flip(ready, 1, 0)]
+    cot_near += [flip(cot_near[1], 1, 0)]
+    rates = rates
     block = (128, 1024)
     quad = ((4, 128, 1024), bf16)
     (
@@ -1405,7 +1436,7 @@
     shares = cross_chips(*sums)
     feed_received = flip_z(feed_send, 1)
     feed_later_received = flip_z(after(feed_later_send, sums[0]), 1)
-    out_sums = sum_cores(keep_d, send_d)
+    out_sums = split_sums(keep_d, flip(send_d, 0, 1), (0, 1, 2, 3), "output_cores")
     grad_residual, branch = call(
         branch_kernel,
         (),
@@ -1422,9 +1453,7 @@
     )
     rates = after(rates, feed_later_passed, feed_moved)
     feed_later_moved = flip_z(feed_later_passed, 2)
-    out_sums = lax.optimization_barrier((*out_sums, branches[6]))[:4]
-    out_shares = cross_chips(*out_sums)
-
+    out_shares = (out_sums[0], flip(after(out_sums[2], branches[6]), 1, 0))
     send, keep, dqkvg, branch_all = call(
         mixer_backward_kernel,
         (idx, rates),
@@ -1437,8 +1466,6 @@
         ],
         scratch=[
             ((1024, 128), bf16),
-            ((1024, 128), bf16),
-            ((1024, 128), f32),
             ((1024, 1024), bf16),
             ((1024, 128), f32),
             ((1024, 128), f32),
@@ -1466,28 +1493,29 @@
         spare=10,
         us=2.2,
     )
+    out_own, out_passed = second_stage(
+        after(out_sums[0], mixer_send), out_sums[1], out_shares[1], "output_far"
+    )
+    out_shares = (out_own, flip(out_passed, 0, 2))
     (result,) = call(output_kernel, (), (residual, *out_shares), [(block, bf16)], name="output")
-    rows = (128 + EXTRA, 1024)
-    keep_far, keep_near, send_far = call(
-        tokens_sum_kernel,
-        (),
-        (after(keep, feed_rest), flip(send, 0, 1)),
-        [(rows, f32), (rows, f32), ((2, *rows), bf16)],
-        name="tokens_sum",
-    )
-    feed_joined = join(feed_parts, after(feed_rest, mixer_send, keep_near), "feed")
+    tokens_sums = split_sums(
+        after(keep, feed_rest),
+        flip(send, 0, 1),
+        (0, 1, 2, 3),
+        "tokens_cores",
+    )
+    feed_joined = join(feed_parts, after(feed_rest, mixer_send, tokens_sums[0]), "feed")
     feed_second = flip_z(feed_joined, 2)
     feed_beside = flip(feed_joined, 1, 0)
     mixer_own, mixer_passed = half_sum(
-        after(mixer_keep, feed_joined), flip_z(mixer_send, 1), "mixer"
+        after(mixer_keep, feed_joined, result), flip_z(mixer_send, 1), "mixer"
     )
     mixer_moved = flip_z(mixer_passed, 2)
     feed_first = flip_z(feed_joined, 1)
-    tokens_far = flip(after(send_far, mixer_passed), 1, 0)
+    tokens_far = flip(after(tokens_sums[2], mixer_passed), 1, 0)
     feed_first_beside = flip(after(feed_first, mixer_passed), 1, 0)
     mixer_own = after(mixer_own, feed_beside)
     *mixer_parts, mixer_rest = whole_sum((mixer_own,), (mixer_moved,), "mixer")
-    result = to_plane(after(result, mixer_passed))
     feed_third = flip_z(after(feed_second, mixer_rest), 1)
     feed_second_beside = flip(after(feed_second, mixer_rest), 1, 0)
     mixer_joined = join(
@@ -1495,6 +1523,7 @@
     )
     mixer_second, mixer_first = spread_far(mixer_joined)
     mixer_beside = flip(mixer_joined, 1, 0)
+    result = to_plane(after(result,   mixer_first))
     feed_third_beside = flip(
         after(
             feed_third,
@@ -1505,12 +1534,16 @@
         1,
         0,
     )
-    tokens_own, tokens_passed = call(
-        far_kernel,
-        (),
-        (after(keep_far, mixer_joined), keep_near, tokens_far),
-        [((128 + EXTRA, 1024), f32), ((128 + EXTRA, 1024), bf16)],
-        name="tokens_far",
+    tokens_own, tokens_passed = second_stage(
+        after(
+            tokens_sums[0],
+            mixer_joined,
+
+
+        ),
+        tokens_sums[1],
+        tokens_far,
+        "tokens_far",
     )
     tokens_near = flip(tokens_passed, 0, 2)
     mixer_second = after(
@@ -1554,7 +1587,14 @@
         us=5.5,
     )
     mixer_third_beside = flip(
-        after(mixer_third, grad_ffn, mixer_first_beside, mixer_second_beside), 1, 0
+        after(
+            mixer_third,
+            grad_ffn,
+            mixer_first_beside, mixer_second_beside,
+
+        ),
+        1,
+        0,
     )
     persist = persist + flip_z(persist, 2)
     mixer_pieces = (
@@ -1570,7 +1610,7 @@
     grad_qkv, grad_gate, grad_out, grad_norm = call(
         mixer_unpack_kernel,
         (idx,),
-        (*mixer_pieces, w_qkv, w_gate, norm_gain.reshape(1, 256)),
+        (*mixer_pieces, w_qkv, w_gate, after(norm_gain.reshape(1, 256))),
         [
             ((256, 3072), f32),
             ((256, 1024), f32),

time: 303 us -> 296 us (0.977)
  starting transfers between devices: 96.9 us -> 87.5 us
  waiting for transfers between devices: 142 us -> 147 us
    ppermute x84 -> x83, starting transfers between devices: 96.9 us -> 87.5 us  [shift(): return lax.ppermute(value, ('ctx', 'fsdp'), pairs)]
    ppermute x84 -> x83, waiting for transfers between devices: 142 us -> 147 us  [shift(): return lax.ppermute(value, ('ctx', 'fsdp'), pairs)]
    pallas_call x24 -> x25, Pallas kernels: 49.2 us -> 47.1 us  [call(): pl.pallas_call(kernel, out_shape=[jax.ShapeDtypeStruct(shape, dtype) for...]
  transfers between devices with their start and end apart: 84 -> 83, of which waited for: 30 -> 29; matrix products, arithmetic and copies ran while one was open for 1% -> 1% of each run, Pallas kernels for 13% -> 13%
where the time goes in v4:
time: 296 us; the launch traced here: 293 us
  waiting for transfers between devices  147 us (50%)
  starting transfers between devices  87.5 us (30%)
  Pallas kernels  50.3 us (17%)
  local copies, waits for them, and re-layouts  4.11 us (1%)
    ppermute x83, waiting for transfers between devices, shift(): return lax.ppermute(value, ('ctx', 'fsdp'), pairs)  147 us
    ppermute x83, starting transfers between devices, shift(): return lax.ppermute(value, ('ctx', 'fsdp'), pairs)  87.5 us
    pallas_call x25, Pallas kernels, call(): pl.pallas_call(kernel, out_shape=[jax.ShapeDtypeStruct(shape, dtype) for...  47.1 us
  transfers between devices with their start and end apart: 83, of which 29 were waited for; matrix products, arithmetic and copies ran while one was open for 1% of the time, Pallas kernels for 13%

profile of v4, /device:TPU:0, one launch (start us, length us, event | category | flops | bytes accessed | tf_op | source)
XLA Modules:
  0.0 292.7 jit_solution(8428996472466270738)
XLA Ops:
  0.7 1.7 collective-permute-start
  4.3 3.2 %pack_qkvg.1 = (bf16[272,512]{1,0:T(8,128)(2,1)}, bf16[272,512]{1,0:T(8,128)(2,1)}, bf16[2,272,512]{2,1,0:T(8,128)(2,1)}) custom-call(s32[4]{0:T(128)} %pad_add_fusion.idx, bf16[256,3072]{1,0:T(8,128)(2,1)} %refs_8_.5, bf16[256,1024]{1,0:T(8,128)(2,1)} %refs_9_.1, bf16[4,1024]{1,0:T(4,128)(2,1)} %pk.1, bf16[4,1024]{1,0:T(4,128)(2,1)} %pv.1, ...), custom_call_target="tpu_custom_call" | custom-call | flops 1000 | bytes 1000 | tf_op jit(solution)/shard_map/pack_qkvg/pallas_call | solution.py:1299
  7.5 5.9 %collective-permute-start.11 = (bf16[2,272,512]{2,1,0:T(8,128)(2,1)}, bf16[2,272,512]{2,1,0:T(8,128)(2,1)S(1)}, u32[]{:S(2)}, u32[]{:S(2)}) collective-permute-start(bf16[2,272,512]{2,1,0:T(8,128)(2,1)} %get-tuple-element.141), channel_id=1, source_target_pairs={{0,2},{1,3},{2,0},{3,1},{4,6},{5,7},{6,4},{7,5},{8,10},{9,11},{10,... | collective-permute-start | bytes 1671176 | tf_op jit(solution)/shard_map/ppermute | solution.py:589
  15.6 1.8 collective-permute-start.10
  18.5 5.7 %collective-permute-start.3 = (bf16[128,1024]{1,0:T(8,128)(2,1)S(1)}, bf16[128,1024]{1,0:T(8,128)(2,1)S(1)}, u32[]{:S(2)}, u32[]{:S(2)}) collective-permute-start(bf16[128,1024]{1,0:T(8,128)(2,1)S(1)} %collective-permute-done.refs_0_.x), channel_id=1, source_target_pairs={{0,1},{1,0},{2,3},{3,2},{4,5},{5,4},{6,7},{7,6},{8,9},{9,8},{10,11... | collective-permute-start | bytes 786440 | tf_op jit(solution)/shard_map/ppermute | solution.py:589
  24.1 12.0 %collective-permute-start.4 = (bf16[128,1024]{1,0:T(8,128)(2,1)S(1)}, bf16[128,1024]{1,0:T(8,128)(2,1)S(1)}, u32[]{:S(2)}, u32[]{:S(2)}) collective-permute-start(bf16[128,1024]{1,0:T(8,128)(2,1)S(1)} %collective-permute-done.refs_0_.x), channel_id=1, source_target_pairs={{0,2},{1,3},{2,0},{3,1},{4,6},{5,7},{6,4},{7,5},{8,10},{9,11},{10,... | collective-permute-start | bytes 786440 | tf_op jit(solution)/shard_map/ppermute | solution.py:589
  37.3 1.8 copy-done.1
  40.4 1.8 collective-permute-start.13
  42.4 6.5 %collective-permute-done.4.refs_2_ = bf16[128,1024]{1,0:T(8,128)(2,1)S(1)} collective-permute-done((bf16[128,1024]{1,0:T(8,128)(2,1)S(1)}, bf16[128,1024]{1,0:T(8,128)(2,1)S(1)}, u32[]{:S(2)}, u32[]{:S(2)}) %collective-permute-start.4) | collective-permute-done | bytes 262176 | tf_op jit(solution)/shard_map/ppermute | solution.py:589
  50.4 1.9 collective-permute-start.16
  56.0 10.1 %mixer_forward.1 = (bf16[4,128,1024]{2,1,0:T(8,128)(2,1)S(1)}, bf16[4,128,1024]{2,1,0:T(8,128)(2,1)S(1)}, bf16[1024,1024]{1,0:T(8,128)(2,1)S(1)}, bf16[1024,512]...) custom-call(s32[4]{0:T(128)S(1)} %copy-done.4, ...), custom_call_target="tpu_custom_call" | custom-call | flops 11000000512 | bytes 1000 | tf_op jit(solution)/shard_map/mixer_forward/pallas_call | solution.py:654
  66.7 2.1 collective-permute-done.17.received
  69.1 2.0 collective-permute-start.18
  73.1 4.6 %collective-permute-done.18.r1 = bf16[128,1024]{1,0:T(8,128)(2,1)S(1)} collective-permute-done((bf16[128,1024]{1,0:T(8,128)(2,1)S(1)}, bf16[128,1024]{1,0:T(8,128)(2,1)S(1)}, u32[]{:S(2)}, u32[]{:S(2)}) %collective-permute-start.18) | collective-permute-done | bytes 262176 | tf_op jit(solution)/shard_map/ppermute | solution.py:589
  77.7 2.6 collective-permute-done.19.r2
  80.3 4.3 %collective-permute-done.20.r3 = bf16[128,1024]{1,0:T(8,128)(2,1)S(1)} collective-permute-done((bf16[128,1024]{1,0:T(8,128)(2,1)S(1)}, bf16[128,1024]{1,0:T(8,128)(2,1)S(1)}, u32[]{:S(2)}, u32[]{:S(2)}) %collective-permute-start.20) | collective-permute-done | bytes 262176 | tf_op jit(solution)/shard_map/ppermute | solution.py:589
  85.5 1.7 collective-permute-start.22
  89.8 4.0 %collective-permute-done.22.refs_2_ = bf16[128,1024]{1,0:T(8,128)(2,1)S(1)} collective-permute-done((bf16[128,1024]{1,0:T(8,128)(2,1)S(1)}, bf16[128,1024]{1,0:T(8,128)(2,1)S(1)}, u32[]{:S(2)}, u32[]{:S(2)}) %collective-permute-start.22) | collective-permute-done | bytes 262176 | tf_op jit(solution)/shard_map/ppermute | solution.py:589
  93.8 2.6 collective-permute-done.24.refs_4_
  96.3 4.9 %collective-permute-done.26.refs_6_ = bf16[128,1024]{1,0:T(8,128)(2,1)S(1)} collective-permute-done((bf16[128,1024]{1,0:T(8,128)(2,1)S(1)}, bf16[128,1024]{1,0:T(8,128)(2,1)S(1)}, u32[]{:S(2)}, u32[]{:S(2)}) %collective-permute-start.26) | collective-permute-done | bytes 262176 | tf_op jit(solution)/shard_map/ppermute | solution.py:589
  102.7 7.3 %feed.1 = (bf16[4,128,1024]{2,1,0:T(8,128)(2,1)S(1)}, bf16[4,128,1024]{2,1,0:T(8,128)(2,1)S(1)}, bf16[4,128,1024]{2,1,0:T(8,128)(2,1)S(1)}, bf16[4,128,1024]{2,1...) custom-call(s32[4]{0:T(128)S(1)} %copy-done.4, ...), custom_call_target="tpu_custom_call" | custom-call | flops 8249999872 | bytes 1000 | tf_op jit(solution)/shard_map/feed/pallas_call | solution.py:654
  110.2 3.5 %feed_weights.1 = (bf16[2,384,384]{2,1,0:T(8,128)(2,1)S(1)}, bf16[2,384,384]{2,1,0:T(8,128)(2,1)S(1)}, bf16[2,384,384]{2,1,0:T(8,128)(2,1)S(1)}, bf16[2,384,384]{2,1,0:T(8,128)(2,1)S(1)}) custom-call(s32[4]{0:T(128)S(1)} %copy-done.4, bf16[1024,768]{1,0:T(8,128)(2,1)S(1)} %get-tuple-element.161.dgu, bf16[1024,384]{1,0:T(8,128)(2,1)S(1)} %get-tuple-element.162.active, ...), custom_call_target="tpu_custom_call" | custom-call | flops 3849999872 | bytes 1000 | tf_op jit(solution)/shard_map/feed_weights/pallas_call | solution.py:654
  116.5 1.9 collective-permute-start.40
  118.4 1.6 collective-permute-start.43
  120.2 3.0 %collective-permute-done.38.r1 = bf16[128,1024]{1,0:T(8,128)(2,1)S(1)} collective-permute-done((bf16[128,1024]{1,0:T(8,128)(2,1)S(1)}, bf16[128,1024]{1,0:T(8,128)(2,1)S(1)}, u32[]{:S(2)}, u32[]{:S(2)}) %collective-permute-start.38) | collective-permute-done | bytes 262176 | tf_op jit(solution)/shard_map/ppermute | solution.py:589
  123.2 1.9 collective-permute-done.39.r2
  125.1 4.6 %collective-permute-done.40.r3 = bf16[128,1024]{1,0:T(8,128)(2,1)S(1)} collective-permute-done((bf16[128,1024]{1,0:T(8,128)(2,1)S(1)}, bf16[128,1024]{1,0:T(8,128)(2,1)S(1)}, u32[]{:S(2)}, u32[]{:S(2)}) %collective-permute-start.40) | collective-permute-done | bytes 262176 | tf_op jit(solution)/shard_map/ppermute | solution.py:589
  131.9 2.0 collective-permute-start.42
  133.9 2.5 collective-permute-start.44
  136.4 12.4 %collective-permute-done.43.received = bf16[2,384,384]{2,1,0:T(8,128)(2,1)S(1)} collective-permute-done((bf16[2,384,384]{2,1,0:T(8,128)(2,1)S(1)}, bf16[2,384,384]{2,1,0:T(8,128)(2,1)S(1)}, u32[]{:S(2)}, u32[]{:S(2)}) %collective-permute-start.43) | collective-permute-done | bytes 589856 | tf_op jit(solution)/shard_map/ppermute | solution.py:589
  151.5 10.8 %mixer_backward.1 = (bf16[4,144,1024]{2,1,0:T(8,128)(2,1)S(1)}, bf16[4,144,1024]{2,1,0:T(8,128)(2,1)S(1)}, bf16[1024,512]{1,0:T(8,128)(2,1)S(1)}, bf16[1024,1024]{1,0:T(8,128)(2,1)S(1)}) custom-call(s32[4]{0:T(128)S(1)} %copy-done.4, f32[2,128]{1,0:T(2,128)S(1)} %pad_maximum_fusion.1.rates, bf16[128,1024]{1,0:T(8,128)(2,1)S(1)} %get-tuple-element.179.refs_0_, ...), custom_call_target="tpu_custom_call" | custom-call | flops 14300000256 | bytes 1000 | tf_op jit(solution)/shard_map/mixer_backward/pallas_call | solution.py:654
  162.4 3.6 %collective-permute-done.51.refs_3_ = bf16[384,384]{1,0:T(8,128)(2,1)S(1)} collective-permute-done((bf16[384,384]{1,0:T(8,128)(2,1)S(1)}, bf16[384,384]{1,0:T(8,128)(2,1)S(1)}, u32[]{:S(2)}, u32[]{:S(2)}) %collective-permute-start.51) | collective-permute-done | bytes 294944 | tf_op jit(solution)/shard_map/ppermute | solution.py:589
  166.1 2.2 mixer_weights.1
  171.1 3.7 %collective-permute-done.55.refs_2_ = bf16[64,768]{1,0:T(8,128)(2,1)S(1)} collective-permute-done((bf16[64,768]{1,0:T(8,128)(2,1)S(1)}, bf16[64,768]{1,0:T(8,128)(2,1)S(1)}, u32[]{:S(2)}, u32[]{:S(2)}) %collective-permute-start.55) | collective-permute-done | bytes 98336 | tf_op jit(solution)/shard_map/ppermute | solution.py:589
  179.6 6.5 %collective-permute-done.53.refs_0_ = bf16[128,1024]{1,0:T(8,128)(2,1)S(1)} collective-permute-done((bf16[128,1024]{1,0:T(8,128)(2,1)S(1)}, bf16[128,1024]{1,0:T(8,128)(2,1)S(1)}, u32[]{:S(2)}, u32[]{:S(2)}) %collective-permute-start.53) | collective-permute-done | bytes 262176 | tf_op jit(solution)/shard_map/ppermute | solution.py:589
  186.2 12.4 %collective-permute-done.58.received = bf16[2,320,512]{2,1,0:T(8,128)(2,1)S(1)} collective-permute-done((bf16[2,320,512]{2,1,0:T(8,128)(2,1)S(1)}, bf16[2,320,512]{2,1,0:T(8,128)(2,1)S(1)}, u32[]{:S(2)}, u32[]{:S(2)}) %collective-permute-start.58) | collective-permute-done | bytes 655392 | tf_op jit(solution)/shard_map/ppermute | solution.py:589
  199.6 11.3 %collective-permute-done.65.refs_2_ = bf16[384,768]{1,0:T(8,128)(2,1)S(1)} collective-permute-done((bf16[384,768]{1,0:T(8,128)(2,1)S(1)}, bf16[384,768]{1,0:T(8,128)(2,1)S(1)}, u32[]{:S(2)}, u32[]{:S(2)}) %collective-permute-start.65) | collective-permute-done | bytes 589856 | tf_op jit(solution)/shard_map/ppermute | solution.py:589
  211.7 13.2 %collective-permute-done.60.refs_1_ = bf16[320,512]{1,0:T(8,128)(2,1)S(1)} collective-permute-done((bf16[320,512]{1,0:T(8,128)(2,1)S(1)}, bf16[320,512]{1,0:T(8,128)(2,1)S(1)}, u32[]{:S(2)}, u32[]{:S(2)}) %collective-permute-start.60) | collective-permute-done | bytes 327712 | tf_op jit(solution)/shard_map/ppermute | solution.py:589
  227.9 3.0 %collective-permute-done.62.refs_2_ = bf16[64,512]{1,0:T(8,128)(2,1)S(1)} collective-permute-done((bf16[64,512]{1,0:T(8,128)(2,1)S(1)}, bf16[64,512]{1,0:T(8,128)(2,1)S(1)}, u32[]{:S(2)}, u32[]{:S(2)}) %collective-permute-start.62) | collective-permute-done | bytes 65568 | tf_op jit(solution)/shard_map/ppermute | solution.py:589
  231.6 2.0 collective-permute-start.67
  235.9 12.3 %collective-permute-done.78.refs_6_ = bf16[384,768]{1,0:T(8,128)(2,1)S(1)} collective-permute-done((bf16[384,768]{1,0:T(8,128)(2,1)S(1)}, bf16[384,768]{1,0:T(8,128)(2,1)S(1)}, u32[]{:S(2)}, u32[]{:S(2)}) %collective-permute-start.78) | collective-permute-done | bytes 589856 | tf_op jit(solution)/shard_map/ppermute | solution.py:589
  250.2 5.2 %collective-permute-done.73.received = bf16[144,1024]{1,0:T(8,128)(2,1)S(1)} collective-permute-done((bf16[144,1024]{1,0:T(8,128)(2,1)S(1)}, bf16[144,1024]{1,0:T(8,128)(2,1)S(1)}, u32[]{:S(2)}, u32[]{:S(2)}) %collective-permute-start.73) | collective-permute-done | bytes 294944 | tf_op jit(solution)/shard_map/ppermute | solution.py:589
  258.7 6.9 %collective-permute-done.79.refs_7_ = bf16[384,768]{1,0:T(8,128)(2,1)S(1)} collective-permute-done((bf16[384,768]{1,0:T(8,128)(2,1)S(1)}, bf16[384,768]{1,0:T(8,128)(2,1)S(1)}, u32[]{:S(2)}, u32[]{:S(2)}) %collective-permute-start.79) | collective-permute-done | bytes 589856 | tf_op jit(solution)/shard_map/ppermute | solution.py:589
  266.2 6.3 %collective-permute-done.75.refs_3_ = bf16[320,512]{1,0:T(8,128)(2,1)S(1)} collective-permute-done((bf16[320,512]{1,0:T(8,128)(2,1)S(1)}, bf16[320,512]{1,0:T(8,128)(2,1)S(1)}, u32[]{:S(2)}, u32[]{:S(2)}) %collective-permute-start.75) | collective-permute-done | bytes 327712 | tf_op jit(solution)/shard_map/ppermute | solution.py:589
  272.6 5.5 %feed_unpack.1 = (f32[256,5632]{1,0:T(8,128)}, f32[704,1024]{1,0:T(8,128)}, f32[1,256]{1,0:T(1,128)}) custom-call(s32[4]{0:T(128)S(1)} %copy-done.4, bf16[384,768]{1,0:T(8,128)(2,1)S(1)} %feed_join.1.refs_0_, bf16[384,768]{1,0:T(8,128)(2,1)S(1)} %collective-permute-done.59.refs_1_, bf16[384,768]{1,0:T(8,128)(2,1)S(1)} %collective-permute-done.65.refs_2_, ...), custom_call_target="tpu_custom_call" | custom-call | flops 6049999872 | bytes 1000 | tf_op jit(solution)/shard_map/feed_unpack/pallas_call | solution.py:654
  279.0 3.1 %collective-permute-start.82 = (f32[8,1024]{1,0:T(8,128)S(1)}, f32[8,1024]{1,0:T(8,128)S(1)}, u32[]{:S(2)}, u32[]{:S(2)}) collective-permute-start(f32[8,1024]{1,0:T(8,128)S(1)} %add.16), channel_id=1, source_target_pairs={{0,16},{1,17},{2,18},{3,19},{4,20},{5,21},{6,22},{7,23},{8,24},{9,... | collective-permute-start | bytes 98312 | tf_op jit(solution)/shard_map/ppermute | solution.py:589
  283.0 4.4 %collective-permute-done.82 = f32[8,1024]{1,0:T(8,128)S(1)} collective-permute-done((f32[8,1024]{1,0:T(8,128)S(1)}, f32[8,1024]{1,0:T(8,128)S(1)}, u32[]{:S(2)}, u32[]{:S(2)}) %collective-permute-start.82) | collective-permute-done | bytes 32800 | tf_op jit(solution)/shard_map/ppermute | solution.py:589
  288.0 3.6 %mixer_unpack.1 = (f32[256,3072]{1,0:T(8,128)}, f32[256,1024]{1,0:T(8,128)}, f32[256,1024]{1,0:T(8,128)}, f32[1,256]{1,0:T(1,128)}) custom-call(s32[4]{0:T(128)S(1)} %copy-done.4, bf16[320,512]{1,0:T(8,128)(2,1)S(1)} %mixer_join.1.refs_0_, bf16[320,512]{1,0:T(8,128)(2,1)S(1)} %collective-permute-done.70.refs_1_, ...), custom_call_target="tpu_custom_call" | custom-call | flops 550000000 | bytes 1000 | tf_op jit(solution)/shard_map/mixer_unpack/pallas_call | solution.py:654
  (189 shorter events, 53.1 us)
Async XLA Ops:
  0.7 12.7 %collective-permute-start = (bf16[128,1024]{1,0:T(8,128)(2,1)}, bf16[128,1024]{1,0:T(8,128)(2,1)S(1)}, u32[]{:S(2)}, u32[]{:S(2)}) collective-permute-start(bf16[128,1024]{1,0:T(8,128)(2,1)} %bitcast.17), channel_id=1, source_target_pairs={{0,0},{1,8},{2,16},{3,24},{4,4},{5,12},{6,20},{7,28},{8,1},{9,9},{... | collective-permute-start | bytes 786440 | tf_op jit(solution)/shard_map/ppermute | solution.py:589
  7.5 29.6 %collective-permute-start.11 = (bf16[2,272,512]{2,1,0:T(8,128)(2,1)}, bf16[2,272,512]{2,1,0:T(8,128)(2,1)S(1)}, u32[]{:S(2)}, u32[]{:S(2)}) collective-permute-start(bf16[2,272,512]{2,1,0:T(8,128)(2,1)} %get-tuple-element.141), channel_id=1, source_target_pairs={{0,2},{1,3},{2,0},{3,1},{4,6},{5,7},{6,4},{7,5},{8,10},{9,11},{10,... | collective-permute-start | bytes 1671176 | tf_op jit(solution)/shard_map/ppermute | solution.py:589
  13.4 10.8 %collective-permute-start.2 = (bf16[128,1024]{1,0:T(8,128)(2,1)S(1)}, bf16[128,1024]{1,0:T(8,128)(2,1)S(1)}, u32[]{:S(2)}, u32[]{:S(2)}) collective-permute-start(bf16[128,1024]{1,0:T(8,128)(2,1)S(1)} %bitcast.18), channel_id=1, source_target_pairs={{0,0},{1,8},{2,16},{3,24},{4,4},{5,12},{6,20},{7,28},{8,1},{9,9},{... | collective-permute-start | bytes 786440 | tf_op jit(solution)/shard_map/ppermute | solution.py:589
  14.1 22.0 %collective-permute-start.6 = (bf16[128,1024]{1,0:T(8,128)(2,1)S(1)}, bf16[128,1024]{1,0:T(8,128)(2,1)S(1)}, u32[]{:S(2)}, u32[]{:S(2)}) collective-permute-start(bf16[128,1024]{1,0:T(8,128)(2,1)S(1)} %collective-permute-done.refs_0_.x), channel_id=1, source_target_pairs={{0,4},{1,5},{2,6},{3,7},{4,0},{5,1},{6,2},{7,3},{8,12},{9,13},{10,... | collective-permute-start | bytes 786440 | tf_op jit(solution)/shard_map/ppermute | solution.py:589
  15.6 24.8 %collective-permute-start.10 = (bf16[272,512]{1,0:T(8,128)(2,1)}, bf16[272,512]{1,0:T(8,128)(2,1)S(1)}, u32[]{:S(2)}, u32[]{:S(2)}) collective-permute-start(bf16[272,512]{1,0:T(8,128)(2,1)} %get-tuple-element.140), channel_id=1, source_target_pairs={{0,1},{1,0},{2,3},{3,2},{4,5},{5,4},{6,7},{7,6},{8,9},{9,8},{10,11... | collective-permute-start | bytes 835592 | tf_op jit(solution)/shard_map/ppermute | solution.py:589
  18.5 23.7 %collective-permute-start.3 = (bf16[128,1024]{1,0:T(8,128)(2,1)S(1)}, bf16[128,1024]{1,0:T(8,128)(2,1)S(1)}, u32[]{:S(2)}, u32[]{:S(2)}) collective-permute-start(bf16[128,1024]{1,0:T(8,128)(2,1)S(1)} %collective-permute-done.refs_0_.x), channel_id=1, source_target_pairs={{0,1},{1,0},{2,3},{3,2},{4,5},{5,4},{6,7},{7,6},{8,9},{9,8},{10,11... | collective-permute-start | bytes 786440 | tf_op jit(solution)/shard_map/ppermute | solution.py:589
  24.1 24.7 %collective-permute-start.4 = (bf16[128,1024]{1,0:T(8,128)(2,1)S(1)}, bf16[128,1024]{1,0:T(8,128)(2,1)S(1)}, u32[]{:S(2)}, u32[]{:S(2)}) collective-permute-start(bf16[128,1024]{1,0:T(8,128)(2,1)S(1)} %collective-permute-done.refs_0_.x), channel_id=1, source_target_pairs={{0,2},{1,3},{2,0},{3,1},{4,6},{5,7},{6,4},{7,5},{8,10},{9,11},{10,... | collective-permute-start | bytes 786440 | tf_op jit(solution)/shard_map/ppermute | solution.py:589
  36.1 12.8 %collective-permute-start.8 = (bf16[128,1024]{1,0:T(8,128)(2,1)S(1)}, bf16[128,1024]{1,0:T(8,128)(2,1)S(1)}, u32[]{:S(2)}, u32[]{:S(2)}) collective-permute-start(bf16[128,1024]{1,0:T(8,128)(2,1)S(1)} %collective-permute-done.refs_0_.x), channel_id=1, source_target_pairs={{0,6},{1,7},{2,4},{3,5},{4,2},{5,3},{6,0},{7,1},{8,14},{9,15},{10,... | collective-permute-start | bytes 786440 | tf_op jit(solution)/shard_map/ppermute | solution.py:589
  37.1 18.9 %collective-permute-start.12 = (bf16[2,272,512]{2,1,0:T(8,128)(2,1)S(1)}, bf16[2,272,512]{2,1,0:T(8,128)(2,1)S(1)}, u32[]{:S(2)}, u32[]{:S(2)}) collective-permute-start(bf16[2,272,512]{2,1,0:T(8,128)(2,1)S(1)} %collective-permute-done.11.refs_10_), channel_id=1, source_target_pairs={{0,1},{1,0},{2,3},{3,2},{4,5},{5,4},{6,7},{7,6},{8,9},{9,8},{10,11... | collective-permute-start | bytes 1671176 | tf_op jit(solution)/shard_map/ppermute | solution.py:589
  40.4 14.1 %collective-permute-start.13 = (bf16[128,1024]{1,0:T(8,128)(2,1)S(1)}, bf16[128,1024]{1,0:T(8,128)(2,1)S(1)}, u32[]{:S(2)}, u32[]{:S(2)}) collective-permute-start(bf16[128,1024]{1,0:T(8,128)(2,1)S(1)} %collective-permute-done.2.refs_8_.cot), channel_id=1, source_target_pairs={{0,2},{1,3},{2,0},{3,1},{4,6},{5,7},{6,4},{7,5},{8,10},{9,11},{10,... | collective-permute-start | bytes 786440 | tf_op jit(solution)/shard_map/ppermute | solution.py:589
  42.2 10.2 %collective-permute-start.7 = (bf16[128,1024]{1,0:T(8,128)(2,1)S(1)}, bf16[128,1024]{1,0:T(8,128)(2,1)S(1)}, u32[]{:S(2)}, u32[]{:S(2)}) collective-permute-start(bf16[128,1024]{1,0:T(8,128)(2,1)S(1)} %collective-permute-done.6.refs_4_), channel_id=1, source_target_pairs={{0,1},{1,0},{2,3},{3,2},{4,5},{5,4},{6,7},{7,6},{8,9},{9,8},{10,11... | collective-permute-start | bytes 786440 | tf_op jit(solution)/shard_map/ppermute | solution.py:589
  50.4 15.7 %collective-permute-start.16 = (bf16[2,128,768]{2,1,0:T(8,128)(2,1)S(1)}, bf16[2,128,768]{2,1,0:T(8,128)(2,1)S(1)}, u32[]{:S(2)}, u32[]{:S(2)}) collective-permute-start(bf16[2,128,768]{2,1,0:T(8,128)(2,1)S(1)} %get-tuple-element.147), channel_id=1, source_target_pairs={{0,2},{1,3},{2,0},{3,1},{4,6},{5,7},{6,4},{7,5},{8,10},{9,11},{10,... | collective-permute-start | bytes 1179656 | tf_op jit(solution)/shard_map/ppermute | solution.py:589
  52.4 13.8 %collective-permute-start.14 = (bf16[128,1024]{1,0:T(8,128)(2,1)S(1)}, bf16[128,1024]{1,0:T(8,128)(2,1)S(1)}, u32[]{:S(2)}, u32[]{:S(2)}) collective-permute-start(bf16[128,1024]{1,0:T(8,128)(2,1)S(1)} %collective-permute-done.2.refs_8_.cot), channel_id=1, source_target_pairs={{0,4},{1,5},{2,6},{3,7},{4,0},{5,1},{6,2},{7,3},{8,12},{9,13},{10,... | collective-permute-start | bytes 786440 | tf_op jit(solution)/shard_map/ppermute | solution.py:589
  54.5 11.6 %collective-permute-start.15 = (bf16[128,1024]{1,0:T(8,128)(2,1)S(1)}, bf16[128,1024]{1,0:T(8,128)(2,1)S(1)}, u32[]{:S(2)}, u32[]{:S(2)}) collective-permute-start(bf16[128,1024]{1,0:T(8,128)(2,1)S(1)} %collective-permute-done.13.refs_10_), channel_id=1, source_target_pairs={{0,4},{1,5},{2,6},{3,7},{4,0},{5,1},{6,2},{7,3},{8,12},{9,13},{10,... | collective-permute-start | bytes 786440 | tf_op jit(solution)/shard_map/ppermute | solution.py:589
  71.7 12.9 %collective-permute-start.20 = (bf16[128,1024]{1,0:T(8,128)(2,1)S(1)}, bf16[128,1024]{1,0:T(8,128)(2,1)S(1)}, u32[]{:S(2)}, u32[]{:S(2)}) collective-permute-start(bf16[128,1024]{1,0:T(8,128)(2,1)S(1)} %get-tuple-element.152), channel_id=1, source_target_pairs={{0,6},{1,7},{2,4},{3,5},{4,2},{5,3},{6,0},{7,1},{8,14},{9,15},{10,... | collective-permute-start | bytes 786440 | tf_op jit(solution)/shard_map/ppermute | solution.py:589
  72.6 15.0 %collective-permute-start.34 = (bf16[2,128,768]{2,1,0:T(8,128)(2,1)S(1)}, bf16[2,128,768]{2,1,0:T(8,128)(2,1)S(1)}, u32[]{:S(2)}, u32[]{:S(2)}) collective-permute-start(bf16[2,128,768]{2,1,0:T(8,128)(2,1)S(1)} %collective-permute-done.16.refs_18_), channel_id=1, source_target_pairs={{0,8},{1,9},{2,10},{3,11},{4,12},{5,13},{6,14},{7,15},{8,0},{9,1},... | collective-permute-start | bytes 1179656 | tf_op jit(solution)/shard_map/ppermute | solution.py:589
  73.1 11.8 %collective-permute-start.28 = (bf16[128,1024]{1,0:T(8,128)(2,1)S(1)}, bf16[128,1024]{1,0:T(8,128)(2,1)S(1)}, u32[]{:S(2)}, u32[]{:S(2)}) collective-permute-start(bf16[128,1024]{1,0:T(8,128)(2,1)S(1)} %collective-permute-done.2.refs_8_.cot), channel_id=1, source_target_pairs={{0,1},{1,0},{2,3},{3,2},{4,5},{5,4},{6,7},{7,6},{8,9},{9,8},{10,11... | collective-permute-start | bytes 786440 | tf_op jit(solution)/shard_map/ppermute | solution.py:589
  87.7 13.5 %collective-permute-start.26 = (bf16[128,1024]{1,0:T(8,128)(2,1)S(1)}, bf16[128,1024]{1,0:T(8,128)(2,1)S(1)}, u32[]{:S(2)}, u32[]{:S(2)}) collective-permute-start(bf16[128,1024]{1,0:T(8,128)(2,1)S(1)} %get-tuple-element.154.refs_0_), channel_id=1, source_target_pairs={{0,6},{1,7},{2,4},{3,5},{4,2},{5,3},{6,0},{7,1},{8,14},{9,15},{10,... | collective-permute-start | bytes 786440 | tf_op jit(solution)/shard_map/ppermute | solution.py:589
  89.3 11.9 %collective-permute-start.35 = (bf16[2,128,768]{2,1,0:T(8,128)(2,1)S(1)}, bf16[2,128,768]{2,1,0:T(8,128)(2,1)S(1)}, u32[]{:S(2)}, u32[]{:S(2)}) collective-permute-start(bf16[2,128,768]{2,1,0:T(8,128)(2,1)S(1)} %collective-permute-done.34.refs_20_), channel_id=1, source_target_pairs={{0,1},{1,0},{2,3},{3,2},{4,5},{5,4},{6,7},{7,6},{8,9},{9,8},{10,11... | collective-permute-start | bytes 1179656 | tf_op jit(solution)/shard_map/ppermute | solution.py:589
  89.3 11.9 %collective-permute-start.21 = (bf16[128,1024]{1,0:T(8,128)(2,1)S(1)}, bf16[128,1024]{1,0:T(8,128)(2,1)S(1)}, u32[]{:S(2)}, u32[]{:S(2)}) collective-permute-start(bf16[128,1024]{1,0:T(8,128)(2,1)S(1)} %get-tuple-element.154.refs_0_), channel_id=1, source_target_pairs={{0,1},{1,0},{2,3},{3,2},{4,5},{5,4},{6,7},{7,6},{8,9},{9,8},{10,11... | collective-permute-start | bytes 786440 | tf_op jit(solution)/shard_map/ppermute | solution.py:589
  114.4 17.3 %collective-permute-start.41 = (bf16[2,384,384]{2,1,0:T(8,128)(2,1)S(1)}, bf16[2,384,384]{2,1,0:T(8,128)(2,1)S(1)}, u32[]{:S(2)}, u32[]{:S(2)}) collective-permute-start(bf16[2,384,384]{2,1,0:T(8,128)(2,1)S(1)} %get-tuple-element.163), channel_id=1, source_target_pairs={{0,8},{1,9},{2,10},{3,11},{4,12},{5,13},{6,14},{7,15},{8,0},{9,1},... | collective-permute-start | bytes 1769480 | tf_op jit(solution)/shard_map/ppermute | solution.py:589
  116.5 13.3 %collective-permute-start.40 = (bf16[128,1024]{1,0:T(8,128)(2,1)S(1)}, bf16[128,1024]{1,0:T(8,128)(2,1)S(1)}, u32[]{:S(2)}, u32[]{:S(2)}) collective-permute-start(bf16[128,1024]{1,0:T(8,128)(2,1)S(1)} %get-tuple-element.174), channel_id=1, source_target_pairs={{0,6},{1,7},{2,4},{3,5},{4,2},{5,3},{6,0},{7,1},{8,14},{9,15},{10,... | collective-permute-start | bytes 786440 | tf_op jit(solution)/shard_map/ppermute | solution.py:589
  118.4 30.4 %collective-permute-start.43 = (bf16[2,384,384]{2,1,0:T(8,128)(2,1)S(1)}, bf16[2,384,384]{2,1,0:T(8,128)(2,1)S(1)}, u32[]{:S(2)}, u32[]{:S(2)}) collective-permute-start(bf16[2,384,384]{2,1,0:T(8,128)(2,1)S(1)} %get-tuple-element.182), channel_id=1, source_target_pairs={{0,8},{1,9},{2,10},{3,11},{4,12},{5,13},{6,14},{7,15},{8,0},{9,1},... | collective-permute-start | bytes 1769480 | tf_op jit(solution)/shard_map/ppermute | solution.py:589
  130.1 18.7 %collective-permute-start.46 = (bf16[128,1024]{1,0:T(8,128)(2,1)S(1)}, bf16[128,1024]{1,0:T(8,128)(2,1)S(1)}, u32[]{:S(2)}, u32[]{:S(2)}) collective-permute-start(bf16[128,1024]{1,0:T(8,128)(2,1)S(1)} %get-tuple-element.179.refs_0_), channel_id=1, source_target_pairs={{0,2},{1,3},{2,0},{3,1},{4,6},{5,7},{6,4},{7,5},{8,10},{9,11},{10,... | collective-permute-start | bytes 786440 | tf_op jit(solution)/shard_map/ppermute | solution.py:589
  131.2 18.1 %collective-permute-start.48 = (bf16[128,1024]{1,0:T(8,128)(2,1)S(1)}, bf16[128,1024]{1,0:T(8,128)(2,1)S(1)}, u32[]{:S(2)}, u32[]{:S(2)}) collective-permute-start(bf16[128,1024]{1,0:T(8,128)(2,1)S(1)} %get-tuple-element.179.refs_0_), channel_id=1, source_target_pairs={{0,4},{1,5},{2,6},{3,7},{4,0},{5,1},{6,2},{7,3},{8,12},{9,13},{10,... | collective-permute-start | bytes 786440 | tf_op jit(solution)/shard_map/ppermute | solution.py:589
  131.9 17.5 %collective-permute-start.42 = (bf16[128,1024]{1,0:T(8,128)(2,1)S(1)}, bf16[128,1024]{1,0:T(8,128)(2,1)S(1)}, u32[]{:S(2)}, u32[]{:S(2)}) collective-permute-start(bf16[128,1024]{1,0:T(8,128)(2,1)S(1)} %get-tuple-element.179.refs_0_), channel_id=1, source_target_pairs={{0,6},{1,7},{2,4},{3,5},{4,2},{5,3},{6,0},{7,1},{8,14},{9,15},{10,... | collective-permute-start | bytes 786440 | tf_op jit(solution)/shard_map/ppermute | solution.py:589
  133.9 16.1 %collective-permute-start.44 = (bf16[384,384]{1,0:T(8,128)(2,1)S(1)}, bf16[384,384]{1,0:T(8,128)(2,1)S(1)}, u32[]{:S(2)}, u32[]{:S(2)}) collective-permute-start(bf16[384,384]{1,0:T(8,128)(2,1)S(1)} %get-tuple-element.178), channel_id=1, source_target_pairs={{0,16},{1,17},{2,18},{3,19},{4,20},{5,21},{6,22},{7,23},{8,24},{9,... | collective-permute-start | bytes 884744 | tf_op jit(solution)/shard_map/ppermute | solution.py:589
  150.0 16.1 %collective-permute-start.51 = (bf16[384,384]{1,0:T(8,128)(2,1)S(1)}, bf16[384,384]{1,0:T(8,128)(2,1)S(1)}, u32[]{:S(2)}, u32[]{:S(2)}) collective-permute-start(bf16[384,384]{1,0:T(8,128)(2,1)S(1)} %get-tuple-element.183), channel_id=1, source_target_pairs={{0,16},{1,17},{2,18},{3,19},{4,20},{5,21},{6,22},{7,23},{8,24},{9,... | collective-permute-start | bytes 884744 | tf_op jit(solution)/shard_map/ppermute | solution.py:589
  150.5 15.5 %collective-permute-start.52 = (bf16[2,128,1024]{2,1,0:T(8,128)(2,1)S(1)}, bf16[2,128,1024]{2,1,0:T(8,128)(2,1)S(1)}, u32[]{:S(2)}, u32[]{:S(2)}) collective-permute-start(bf16[2,128,1024]{2,1,0:T(8,128)(2,1)S(1)} %get-tuple-element.198), channel_id=1, source_target_pairs={{0,4},{1,5},{2,6},{3,7},{4,0},{5,1},{6,2},{7,3},{8,12},{9,13},{10,... | collective-permute-start | bytes 1572872 | tf_op jit(solution)/shard_map/ppermute | solution.py:589
  168.4 30.2 %collective-permute-start.58 = (bf16[2,320,512]{2,1,0:T(8,128)(2,1)S(1)}, bf16[2,320,512]{2,1,0:T(8,128)(2,1)S(1)}, u32[]{:S(2)}, u32[]{:S(2)}) collective-permute-start(bf16[2,320,512]{2,1,0:T(8,128)(2,1)S(1)} %get-tuple-element.208), channel_id=1, source_target_pairs={{0,8},{1,9},{2,10},{3,11},{4,12},{5,13},{6,14},{7,15},{8,0},{9,1},... | collective-permute-start | bytes 1966088 | tf_op jit(solution)/shard_map/ppermute | solution.py:589
  175.7 35.2 %collective-permute-start.65 = (bf16[384,768]{1,0:T(8,128)(2,1)S(1)}, bf16[384,768]{1,0:T(8,128)(2,1)S(1)}, u32[]{:S(2)}, u32[]{:S(2)}) collective-permute-start(bf16[384,768]{1,0:T(8,128)(2,1)S(1)} %feed_join.1.refs_0_), channel_id=1, source_target_pairs={{0,8},{1,9},{2,10},{3,11},{4,12},{5,13},{6,14},{7,15},{8,0},{9,1},... | collective-permute-start | bytes 1769480 | tf_op jit(solution)/shard_map/ppermute | solution.py:589
  178.4 33.3 %collective-permute-start.59 = (bf16[384,768]{1,0:T(8,128)(2,1)S(1)}, bf16[384,768]{1,0:T(8,128)(2,1)S(1)}, u32[]{:S(2)}, u32[]{:S(2)}) collective-permute-start(bf16[384,768]{1,0:T(8,128)(2,1)S(1)} %feed_join.1.refs_0_), channel_id=1, source_target_pairs={{0,4},{1,5},{2,6},{3,7},{4,0},{5,1},{6,2},{7,3},{8,12},{9,13},{10,... | collective-permute-start | bytes 1769480 | tf_op jit(solution)/shard_map/ppermute | solution.py:589
  179.2 45.8 %collective-permute-start.71 = (bf16[384,768]{1,0:T(8,128)(2,1)S(1)}, bf16[384,768]{1,0:T(8,128)(2,1)S(1)}, u32[]{:S(2)}, u32[]{:S(2)}) collective-permute-start(bf16[384,768]{1,0:T(8,128)(2,1)S(1)} %feed_join.1.refs_0_), channel_id=1, source_target_pairs={{0,16},{1,17},{2,18},{3,19},{4,20},{5,21},{6,22},{7,23},{8,24},{9,... | collective-permute-start | bytes 1769480 | tf_op jit(solution)/shard_map/ppermute | solution.py:589
  198.7 26.1 %collective-permute-start.60 = (bf16[320,512]{1,0:T(8,128)(2,1)S(1)}, bf16[320,512]{1,0:T(8,128)(2,1)S(1)}, u32[]{:S(2)}, u32[]{:S(2)}) collective-permute-start(bf16[320,512]{1,0:T(8,128)(2,1)S(1)} %get-tuple-element.225), channel_id=1, source_target_pairs={{0,16},{1,17},{2,18},{3,19},{4,20},{5,21},{6,22},{7,23},{8,24},{9,... | collective-permute-start | bytes 983048 | tf_op jit(solution)/shard_map/ppermute | solution.py:589
  198.8 27.2 %collective-permute-start.64 = (bf16[2,144,1024]{2,1,0:T(8,128)(2,1)S(1)}, bf16[2,144,1024]{2,1,0:T(8,128)(2,1)S(1)}, u32[]{:S(2)}, u32[]{:S(2)}) collective-permute-start(bf16[2,144,1024]{2,1,0:T(8,128)(2,1)S(1)} %get-tuple-element.232), channel_id=1, source_target_pairs={{0,4},{1,5},{2,6},{3,7},{4,0},{5,1},{6,2},{7,3},{8,12},{9,13},{10,... | collective-permute-start | bytes 1769480 | tf_op jit(solution)/shard_map/ppermute | solution.py:589
  210.9 16.1 %collective-permute-start.66 = (bf16[384,768]{1,0:T(8,128)(2,1)S(1)}, bf16[384,768]{1,0:T(8,128)(2,1)S(1)}, u32[]{:S(2)}, u32[]{:S(2)}) collective-permute-start(bf16[384,768]{1,0:T(8,128)(2,1)S(1)} %collective-permute-done.65.refs_2_), channel_id=1, source_target_pairs={{0,4},{1,5},{2,6},{3,7},{4,0},{5,1},{6,2},{7,3},{8,12},{9,13},{10,... | collective-permute-start | bytes 1769480 | tf_op jit(solution)/shard_map/ppermute | solution.py:589
  225.0 23.3 %collective-permute-start.78 = (bf16[384,768]{1,0:T(8,128)(2,1)S(1)}, bf16[384,768]{1,0:T(8,128)(2,1)S(1)}, u32[]{:S(2)}, u32[]{:S(2)}) collective-permute-start(bf16[384,768]{1,0:T(8,128)(2,1)S(1)} %collective-permute-done.71.refs_4_), channel_id=1, source_target_pairs={{0,8},{1,9},{2,10},{3,11},{4,12},{5,13},{6,14},{7,15},{8,0},{9,1},... | collective-permute-start | bytes 1769480 | tf_op jit(solution)/shard_map/ppermute | solution.py:589
  225.1 24.2 %collective-permute-start.72 = (bf16[384,768]{1,0:T(8,128)(2,1)S(1)}, bf16[384,768]{1,0:T(8,128)(2,1)S(1)}, u32[]{:S(2)}, u32[]{:S(2)}) collective-permute-start(bf16[384,768]{1,0:T(8,128)(2,1)S(1)} %collective-permute-done.71.refs_4_), channel_id=1, source_target_pairs={{0,4},{1,5},{2,6},{3,7},{4,0},{5,1},{6,2},{7,3},{8,12},{9,13},{10,... | collective-permute-start | bytes 1769480 | tf_op jit(solution)/shard_map/ppermute | solution.py:589
  231.6 23.8 %collective-permute-start.67 = (bf16[320,512]{1,0:T(8,128)(2,1)S(1)}, bf16[320,512]{1,0:T(8,128)(2,1)S(1)}, u32[]{:S(2)}, u32[]{:S(2)}) collective-permute-start(bf16[320,512]{1,0:T(8,128)(2,1)S(1)} %mixer_join.1.refs_0_), channel_id=1, source_target_pairs={{0,8},{1,9},{2,10},{3,11},{4,12},{5,13},{6,14},{7,15},{8,0},{9,1},... | collective-permute-start | bytes 983048 | tf_op jit(solution)/shard_map/ppermute | solution.py:589
  233.6 21.8 %collective-permute-start.69 = (bf16[320,512]{1,0:T(8,128)(2,1)S(1)}, bf16[320,512]{1,0:T(8,128)(2,1)S(1)}, u32[]{:S(2)}, u32[]{:S(2)}) collective-permute-start(bf16[320,512]{1,0:T(8,128)(2,1)S(1)} %mixer_join.1.refs_0_), channel_id=1, source_target_pairs={{0,16},{1,17},{2,18},{3,19},{4,20},{5,21},{6,22},{7,23},{8,24},{9,... | collective-permute-start | bytes 983048 | tf_op jit(solution)/shard_map/ppermute | solution.py:589
  234.7 20.7 %collective-permute-start.70 = (bf16[320,512]{1,0:T(8,128)(2,1)S(1)}, bf16[320,512]{1,0:T(8,128)(2,1)S(1)}, u32[]{:S(2)}, u32[]{:S(2)}) collective-permute-start(bf16[320,512]{1,0:T(8,128)(2,1)S(1)} %mixer_join.1.refs_0_), channel_id=1, source_target_pairs={{0,4},{1,5},{2,6},{3,7},{4,0},{5,1},{6,2},{7,3},{8,12},{9,13},{10,... | collective-permute-start | bytes 983048 | tf_op jit(solution)/shard_map/ppermute | solution.py:589
  249.3 16.3 %collective-permute-start.79 = (bf16[384,768]{1,0:T(8,128)(2,1)S(1)}, bf16[384,768]{1,0:T(8,128)(2,1)S(1)}, u32[]{:S(2)}, u32[]{:S(2)}) collective-permute-start(bf16[384,768]{1,0:T(8,128)(2,1)S(1)} %collective-permute-done.78.refs_6_), channel_id=1, source_target_pairs={{0,4},{1,5},{2,6},{3,7},{4,0},{5,1},{6,2},{7,3},{8,12},{9,13},{10,... | collective-permute-start | bytes 1769480 | tf_op jit(solution)/shard_map/ppermute | solution.py:589
  255.4 17.2 %collective-permute-start.75 = (bf16[320,512]{1,0:T(8,128)(2,1)S(1)}, bf16[320,512]{1,0:T(8,128)(2,1)S(1)}, u32[]{:S(2)}, u32[]{:S(2)}) collective-permute-start(bf16[320,512]{1,0:T(8,128)(2,1)S(1)} %collective-permute-done.67.refs_2_), channel_id=1, source_target_pairs={{0,4},{1,5},{2,6},{3,7},{4,0},{5,1},{6,2},{7,3},{8,12},{9,13},{10,... | collective-permute-start | bytes 983048 | tf_op jit(solution)/shard_map/ppermute | solution.py:589
  256.4 21.7 %collective-permute-start.76 = (bf16[320,512]{1,0:T(8,128)(2,1)S(1)}, bf16[320,512]{1,0:T(8,128)(2,1)S(1)}, u32[]{:S(2)}, u32[]{:S(2)}) collective-permute-start(bf16[320,512]{1,0:T(8,128)(2,1)S(1)} %collective-permute-done.69.refs_4_), channel_id=1, source_target_pairs={{0,4},{1,5},{2,6},{3,7},{4,0},{5,1},{6,2},{7,3},{8,12},{9,13},{10,... | collective-permute-start | bytes 983048 | tf_op jit(solution)/shard_map/ppermute | solution.py:589
  257.6 20.5 %collective-permute-start.77 = (bf16[320,512]{1,0:T(8,128)(2,1)S(1)}, bf16[320,512]{1,0:T(8,128)(2,1)S(1)}, u32[]{:S(2)}, u32[]{:S(2)}) collective-permute-start(bf16[320,512]{1,0:T(8,128)(2,1)S(1)} %collective-permute-done.69.refs_4_), channel_id=1, source_target_pairs={{0,8},{1,9},{2,10},{3,11},{4,12},{5,13},{6,14},{7,15},{8,0},{9,1},... | collective-permute-start | bytes 983048 | tf_op jit(solution)/shard_map/ppermute | solution.py:589
  257.7 25.3 %collective-permute-start.68 = (bf16[128,1024]{1,0:T(8,128)(2,1)S(1)}, bf16[128,1024]{1,0:T(8,128)(2,1)S(1)}, u32[]{:S(2)}, u32[]{:S(2)}) collective-permute-start(bf16[128,1024]{1,0:T(8,128)(2,1)S(1)} %output.1), channel_id=1, source_target_pairs={{0,0},{1,8},{2,16},{3,24},{4,4},{5,12},{6,20},{7,28},{8,1},{9,9},{... | collective-permute-start | bytes 786440 | tf_op jit(solution)/shard_map/ppermute | solution.py:589
  265.5 16.6 %collective-permute-start.74 = (bf16[128,1024]{1,0:T(8,128)(2,1)S(1)}, bf16[128,1024]{1,0:T(8,128)(2,1)S(1)}, u32[]{:S(2)}, u32[]{:S(2)}) collective-permute-start(bf16[128,1024]{1,0:T(8,128)(2,1)S(1)} %get-tuple-element.245), channel_id=1, source_target_pairs={{0,0},{1,8},{2,16},{3,24},{4,4},{5,12},{6,20},{7,28},{8,1},{9,9},{... | collective-permute-start | bytes 786440 | tf_op jit(solution)/shard_map/ppermute | solution.py:589
  278.1 9.9 %collective-permute-start.80 = (bf16[320,512]{1,0:T(8,128)(2,1)S(1)}, bf16[320,512]{1,0:T(8,128)(2,1)S(1)}, u32[]{:S(2)}, u32[]{:S(2)}) collective-permute-start(bf16[320,512]{1,0:T(8,128)(2,1)S(1)} %collective-permute-done.77.refs_6_), channel_id=1, source_target_pairs={{0,4},{1,5},{2,6},{3,7},{4,0},{5,1},{6,2},{7,3},{8,12},{9,13},{10,... | collective-permute-start | bytes 983048 | tf_op jit(solution)/shard_map/ppermute | solution.py:589
  (49 other events, 525.2 us)

commit v5 on v4

--- a/solution.py
+++ b/solution.py
@@ -569,6 +569,7 @@
 PLANES = 4
 HIDDEN_PAD = 384
 Z_HIDDEN = HIDDEN_PAD // PLANES
+FIRST_LANES = 384
 EXTRA = 16
 
 
@@ -994,7 +995,7 @@
     for k in range(8):
         feeds[k * 128 : k * 128 + 128, :] = blocks[k][...]
         cots[k * 128 : k * 128 + 128, :] = cot_blocks[k][...]
-    half = HIDDEN_PAD
+    half = FIRST_LANES
     for t in range(4):
         total[...] = dot_tn(feeds[:, t * 256 : t * 256 + 256], dgu[...])
         spot = pl.ds(pl.multiple_of((t ^ f) * 64, 64), 64)
@@ -1327,12 +1328,13 @@
         [0.6 * jnp.exp2(-ints[8].astype(f32)), 0.1 * jnp.exp2(-ints[9].astype(f32))]
     )
     far = flip(wq_parts[2], 0, 2)
-    wq_parts = [wq_parts[0], flip(wq_parts[1], 0, 1), far, flip(far, 0, 1)]
     own = after(own, wq_parts[0])
     near = gather_chips(own)
+    wq_beside = flip(wq_parts[1], 0, 1)
+    wq_parts = [wq_parts[0], wq_beside, far, flip(far, 0, 1)]
     own_cot = to_plane(after(cotangent[0], own))
     gu_far = flip(after(gu_parts[2], own), 0, 2)
-    blocks = gather_cores(near)
+    blocks = gather_cores([near[0], *near[1:]])
     rates = after(rates, own_cot)
     ready = after(own_cot, near[2])
     cot_near = [own_cot, flip(ready, 0, 2), flip(ready, 1, 0)]
@@ -1397,7 +1399,8 @@
         [(block, f32), (block, bf16)],
         name="residual",
     )
-    feeds = gather_cores(gather_chips(feed))
+    feed_near = gather_chips(feed)
+    feeds = gather_cores(feed_near)
     send_g, keep_g, send_d, keep_d, active, dgu = call(
         feed_kernel,
         (idx,),
@@ -1419,7 +1422,10 @@
         feed_weights_kernel,
         (idx,),
         (dgu, active, *feeds, *cots),
-        [((2, 256 + 4 * Z_HIDDEN // 3, HIDDEN_PAD), bf16)] * 4,
+        [
+            ((2, 256 + 4 * Z_HIDDEN // 3, lanes), bf16)
+            for lanes in (FIRST_LANES, 768 - FIRST_LANES) * 2
+        ],
         scratch=[
             ((256, 768), f32),
             ((HIDDEN_PAD, 1024), f32),
@@ -1516,7 +1522,7 @@
     feed_first_beside = flip(after(feed_first, mixer_passed), 1, 0)
     mixer_own = after(mixer_own, feed_beside)
     *mixer_parts, mixer_rest = whole_sum((mixer_own,), (mixer_moved,), "mixer")
-    feed_third = flip_z(after(feed_second, mixer_rest), 1)
+    feed_third = flip_z(feed_second, 1)
     feed_second_beside = flip(after(feed_second, mixer_rest), 1, 0)
     mixer_joined = join(
         hand_rows(mixer_parts), after(mixer_rest, tokens_far, feed_first_beside), "mixer"

time: 296 us -> 291 us (0.983)
  waiting for transfers between devices: 147 us -> 142 us
    ppermute x83, waiting for transfers between devices: 147 us -> 142 us  [shift(): return lax.ppermute(value, ('ctx', 'fsdp'), pairs)]
  transfers between devices with their start and end apart: 83 -> 83, of which waited for: 29 -> 33; matrix products, arithmetic and copies ran while one was open for 1% -> 1% of each run, Pallas kernels for 13% -> 14%
where the time goes in v5:
time: 291 us; the launch traced here: 287 us
  waiting for transfers between devices  142 us (49%)
  starting transfers between devices  87.3 us (30%)
  Pallas kernels  50.3 us (17%)
  local copies, waits for them, and re-layouts  4.11 us (1%)
    ppermute x83, waiting for transfers between devices, shift(): return lax.ppermute(value, ('ctx', 'fsdp'), pairs)  142 us
    ppermute x83, starting transfers between devices, shift(): return lax.ppermute(value, ('ctx', 'fsdp'), pairs)  87.3 us
    pallas_call x25, Pallas kernels, call(): pl.pallas_call(kernel, out_shape=[jax.ShapeDtypeStruct(shape, dtype) for...  47.1 us
  transfers between devices with their start and end apart: 83, of which 33 were waited for; matrix products, arithmetic and copies ran while one was open for 1% of the time, Pallas kernels for 14%

profile of v5, /device:TPU:0, one launch (start us, length us, event | category | flops | bytes accessed | tf_op | source)
XLA Modules:
  0.0 287.5 jit_solution(1690812870925559717)
XLA Ops:
  0.7 1.7 collective-permute-start
  4.3 3.2 %pack_qkvg.1 = (bf16[272,512]{1,0:T(8,128)(2,1)}, bf16[272,512]{1,0:T(8,128)(2,1)}, bf16[2,272,512]{2,1,0:T(8,128)(2,1)}) custom-call(s32[4]{0:T(128)} %pad_add_fusion.idx, bf16[256,3072]{1,0:T(8,128)(2,1)} %refs_8_.5, bf16[256,1024]{1,0:T(8,128)(2,1)} %refs_9_.1, bf16[4,1024]{1,0:T(4,128)(2,1)} %pk.1, bf16[4,1024]{1,0:T(4,128)(2,1)} %pv.1, ...), custom_call_target="tpu_custom_call" | custom-call | flops 1000 | bytes 1000 | tf_op jit(solution)/shard_map/pack_qkvg/pallas_call | solution.py:1300
  7.5 5.9 %collective-permute-start.11 = (bf16[2,272,512]{2,1,0:T(8,128)(2,1)}, bf16[2,272,512]{2,1,0:T(8,128)(2,1)S(1)}, u32[]{:S(2)}, u32[]{:S(2)}) collective-permute-start(bf16[2,272,512]{2,1,0:T(8,128)(2,1)} %get-tuple-element.141), channel_id=1, source_target_pairs={{0,2},{1,3},{2,0},{3,1},{4,6},{5,7},{6,4},{7,5},{8,10},{9,11},{10,... | collective-permute-start | bytes 1671176 | tf_op jit(solution)/shard_map/ppermute | solution.py:590
  15.6 1.8 collective-permute-start.10
  18.5 5.7 %collective-permute-start.3 = (bf16[128,1024]{1,0:T(8,128)(2,1)S(1)}, bf16[128,1024]{1,0:T(8,128)(2,1)S(1)}, u32[]{:S(2)}, u32[]{:S(2)}) collective-permute-start(bf16[128,1024]{1,0:T(8,128)(2,1)S(1)} %collective-permute-done.refs_0_.x), channel_id=1, source_target_pairs={{0,1},{1,0},{2,3},{3,2},{4,5},{5,4},{6,7},{7,6},{8,9},{9,8},{10,11... | collective-permute-start | bytes 786440 | tf_op jit(solution)/shard_map/ppermute | solution.py:590
  24.1 12.0 %collective-permute-start.4 = (bf16[128,1024]{1,0:T(8,128)(2,1)S(1)}, bf16[128,1024]{1,0:T(8,128)(2,1)S(1)}, u32[]{:S(2)}, u32[]{:S(2)}) collective-permute-start(bf16[128,1024]{1,0:T(8,128)(2,1)S(1)} %collective-permute-done.refs_0_.x), channel_id=1, source_target_pairs={{0,2},{1,3},{2,0},{3,1},{4,6},{5,7},{6,4},{7,5},{8,10},{9,11},{10,... | collective-permute-start | bytes 786440 | tf_op jit(solution)/shard_map/ppermute | solution.py:590
  37.3 1.8 copy-done.1
  40.4 1.8 collective-permute-start.13
  42.4 6.5 %collective-permute-done.4.refs_2_ = bf16[128,1024]{1,0:T(8,128)(2,1)S(1)} collective-permute-done((bf16[128,1024]{1,0:T(8,128)(2,1)S(1)}, bf16[128,1024]{1,0:T(8,128)(2,1)S(1)}, u32[]{:S(2)}, u32[]{:S(2)}) %collective-permute-start.4) | collective-permute-done | bytes 262176 | tf_op jit(solution)/shard_map/ppermute | solution.py:590
  50.4 1.9 collective-permute-start.16
  56.0 10.1 %mixer_forward.1 = (bf16[4,128,1024]{2,1,0:T(8,128)(2,1)S(1)}, bf16[4,128,1024]{2,1,0:T(8,128)(2,1)S(1)}, bf16[1024,1024]{1,0:T(8,128)(2,1)S(1)}, bf16[1024,512]...) custom-call(s32[4]{0:T(128)S(1)} %copy-done.4, ...), custom_call_target="tpu_custom_call" | custom-call | flops 11000000512 | bytes 1000 | tf_op jit(solution)/shard_map/mixer_forward/pallas_call | solution.py:655
  66.7 2.1 collective-permute-done.17.received
  69.1 2.0 collective-permute-start.18
  73.1 4.6 %collective-permute-done.18.r1 = bf16[128,1024]{1,0:T(8,128)(2,1)S(1)} collective-permute-done((bf16[128,1024]{1,0:T(8,128)(2,1)S(1)}, bf16[128,1024]{1,0:T(8,128)(2,1)S(1)}, u32[]{:S(2)}, u32[]{:S(2)}) %collective-permute-start.18) | collective-permute-done | bytes 262176 | tf_op jit(solution)/shard_map/ppermute | solution.py:590
  77.7 2.6 collective-permute-done.19.r2
  80.3 4.3 %collective-permute-done.20.r3 = bf16[128,1024]{1,0:T(8,128)(2,1)S(1)} collective-permute-done((bf16[128,1024]{1,0:T(8,128)(2,1)S(1)}, bf16[128,1024]{1,0:T(8,128)(2,1)S(1)}, u32[]{:S(2)}, u32[]{:S(2)}) %collective-permute-start.20) | collective-permute-done | bytes 262176 | tf_op jit(solution)/shard_map/ppermute | solution.py:590
  85.5 1.7 collective-permute-start.22
  89.8 4.0 %collective-permute-done.22.refs_2_ = bf16[128,1024]{1,0:T(8,128)(2,1)S(1)} collective-permute-done((bf16[128,1024]{1,0:T(8,128)(2,1)S(1)}, bf16[128,1024]{1,0:T(8,128)(2,1)S(1)}, u32[]{:S(2)}, u32[]{:S(2)}) %collective-permute-start.22) | collective-permute-done | bytes 262176 | tf_op jit(solution)/shard_map/ppermute | solution.py:590
  93.8 2.6 collective-permute-done.24.refs_4_
  96.3 4.9 %collective-permute-done.26.refs_6_ = bf16[128,1024]{1,0:T(8,128)(2,1)S(1)} collective-permute-done((bf16[128,1024]{1,0:T(8,128)(2,1)S(1)}, bf16[128,1024]{1,0:T(8,128)(2,1)S(1)}, u32[]{:S(2)}, u32[]{:S(2)}) %collective-permute-start.26) | collective-permute-done | bytes 262176 | tf_op jit(solution)/shard_map/ppermute | solution.py:590
  102.7 7.3 %feed.1 = (bf16[4,128,1024]{2,1,0:T(8,128)(2,1)S(1)}, bf16[4,128,1024]{2,1,0:T(8,128)(2,1)S(1)}, bf16[4,128,1024]{2,1,0:T(8,128)(2,1)S(1)}, bf16[4,128,1024]{2,1...) custom-call(s32[4]{0:T(128)S(1)} %copy-done.4, ...), custom_call_target="tpu_custom_call" | custom-call | flops 8249999872 | bytes 1000 | tf_op jit(solution)/shard_map/feed/pallas_call | solution.py:655
  110.2 3.5 %feed_weights.1 = (bf16[2,384,384]{2,1,0:T(8,128)(2,1)S(1)}, bf16[2,384,384]{2,1,0:T(8,128)(2,1)S(1)}, bf16[2,384,384]{2,1,0:T(8,128)(2,1)S(1)}, bf16[2,384,384]{2,1,0:T(8,128)(2,1)S(1)}) custom-call(s32[4]{0:T(128)S(1)} %copy-done.4, bf16[1024,768]{1,0:T(8,128)(2,1)S(1)} %get-tuple-element.161.dgu, bf16[1024,384]{1,0:T(8,128)(2,1)S(1)} %get-tuple-element.162.active, ...), custom_call_target="tpu_custom_call" | custom-call | flops 3849999872 | bytes 1000 | tf_op jit(solution)/shard_map/feed_weights/pallas_call | solution.py:655
  116.5 1.9 collective-permute-start.40
  120.2 3.0 %collective-permute-done.38.r1 = bf16[128,1024]{1,0:T(8,128)(2,1)S(1)} collective-permute-done((bf16[128,1024]{1,0:T(8,128)(2,1)S(1)}, bf16[128,1024]{1,0:T(8,128)(2,1)S(1)}, u32[]{:S(2)}, u32[]{:S(2)}) %collective-permute-start.38) | collective-permute-done | bytes 262176 | tf_op jit(solution)/shard_map/ppermute | solution.py:590
  123.2 1.9 collective-permute-done.39.r2
  125.1 4.6 %collective-permute-done.40.r3 = bf16[128,1024]{1,0:T(8,128)(2,1)S(1)} collective-permute-done((bf16[128,1024]{1,0:T(8,128)(2,1)S(1)}, bf16[128,1024]{1,0:T(8,128)(2,1)S(1)}, u32[]{:S(2)}, u32[]{:S(2)}) %collective-permute-start.40) | collective-permute-done | bytes 262176 | tf_op jit(solution)/shard_map/ppermute | solution.py:590
  131.9 2.0 collective-permute-start.42
  133.9 2.5 collective-permute-start.44
  136.4 12.4 %collective-permute-done.43.received = bf16[2,384,384]{2,1,0:T(8,128)(2,1)S(1)} collective-permute-done((bf16[2,384,384]{2,1,0:T(8,128)(2,1)S(1)}, bf16[2,384,384]{2,1,0:T(8,128)(2,1)S(1)}, u32[]{:S(2)}, u32[]{:S(2)}) %collective-permute-start.43) | collective-permute-done | bytes 589856 | tf_op jit(solution)/shard_map/ppermute | solution.py:590
  151.5 10.8 %mixer_backward.1 = (bf16[4,144,1024]{2,1,0:T(8,128)(2,1)S(1)}, bf16[4,144,1024]{2,1,0:T(8,128)(2,1)S(1)}, bf16[1024,512]{1,0:T(8,128)(2,1)S(1)}, bf16[1024,1024]{1,0:T(8,128)(2,1)S(1)}) custom-call(s32[4]{0:T(128)S(1)} %copy-done.4, f32[2,128]{1,0:T(2,128)S(1)} %pad_maximum_fusion.1.rates, bf16[128,1024]{1,0:T(8,128)(2,1)S(1)} %get-tuple-element.179.refs_0_, ...), custom_call_target="tpu_custom_call" | custom-call | flops 14300000256 | bytes 1000 | tf_op jit(solution)/shard_map/mixer_backward/pallas_call | solution.py:655
  162.4 3.6 %collective-permute-done.51.refs_3_ = bf16[384,384]{1,0:T(8,128)(2,1)S(1)} collective-permute-done((bf16[384,384]{1,0:T(8,128)(2,1)S(1)}, bf16[384,384]{1,0:T(8,128)(2,1)S(1)}, u32[]{:S(2)}, u32[]{:S(2)}) %collective-permute-start.51) | collective-permute-done | bytes 294944 | tf_op jit(solution)/shard_map/ppermute | solution.py:590
  166.1 2.2 mixer_weights.1
  171.1 3.7 %collective-permute-done.55.refs_2_ = bf16[64,768]{1,0:T(8,128)(2,1)S(1)} collective-permute-done((bf16[64,768]{1,0:T(8,128)(2,1)S(1)}, bf16[64,768]{1,0:T(8,128)(2,1)S(1)}, u32[]{:S(2)}, u32[]{:S(2)}) %collective-permute-start.55) | collective-permute-done | bytes 98336 | tf_op jit(solution)/shard_map/ppermute | solution.py:590
  179.6 6.5 %collective-permute-done.53.refs_0_ = bf16[128,1024]{1,0:T(8,128)(2,1)S(1)} collective-permute-done((bf16[128,1024]{1,0:T(8,128)(2,1)S(1)}, bf16[128,1024]{1,0:T(8,128)(2,1)S(1)}, u32[]{:S(2)}, u32[]{:S(2)}) %collective-permute-start.53) | collective-permute-done | bytes 262176 | tf_op jit(solution)/shard_map/ppermute | solution.py:590
  186.2 12.4 %collective-permute-done.58.received = bf16[2,320,512]{2,1,0:T(8,128)(2,1)S(1)} collective-permute-done((bf16[2,320,512]{2,1,0:T(8,128)(2,1)S(1)}, bf16[2,320,512]{2,1,0:T(8,128)(2,1)S(1)}, u32[]{:S(2)}, u32[]{:S(2)}) %collective-permute-start.58) | collective-permute-done | bytes 655392 | tf_op jit(solution)/shard_map/ppermute | solution.py:590
  199.6 11.3 %collective-permute-done.65.refs_2_ = bf16[384,768]{1,0:T(8,128)(2,1)S(1)} collective-permute-done((bf16[384,768]{1,0:T(8,128)(2,1)S(1)}, bf16[384,768]{1,0:T(8,128)(2,1)S(1)}, u32[]{:S(2)}, u32[]{:S(2)}) %collective-permute-start.65) | collective-permute-done | bytes 589856 | tf_op jit(solution)/shard_map/ppermute | solution.py:590
  211.9 13.1 %collective-permute-done.60.refs_1_ = bf16[320,512]{1,0:T(8,128)(2,1)S(1)} collective-permute-done((bf16[320,512]{1,0:T(8,128)(2,1)S(1)}, bf16[320,512]{1,0:T(8,128)(2,1)S(1)}, u32[]{:S(2)}, u32[]{:S(2)}) %collective-permute-start.60) | collective-permute-done | bytes 327712 | tf_op jit(solution)/shard_map/ppermute | solution.py:590
  227.9 3.0 %collective-permute-done.62.refs_2_ = bf16[64,512]{1,0:T(8,128)(2,1)S(1)} collective-permute-done((bf16[64,512]{1,0:T(8,128)(2,1)S(1)}, bf16[64,512]{1,0:T(8,128)(2,1)S(1)}, u32[]{:S(2)}, u32[]{:S(2)}) %collective-permute-start.62) | collective-permute-done | bytes 65568 | tf_op jit(solution)/shard_map/ppermute | solution.py:590
  232.4 2.4 collective-permute-start.69
  237.0 4.3 %collective-permute-done.72.refs_5_ = bf16[384,768]{1,0:T(8,128)(2,1)S(1)} collective-permute-done((bf16[384,768]{1,0:T(8,128)(2,1)S(1)}, bf16[384,768]{1,0:T(8,128)(2,1)S(1)}, u32[]{:S(2)}, u32[]{:S(2)}) %collective-permute-start.72) | collective-permute-done | bytes 589856 | tf_op jit(solution)/shard_map/ppermute | solution.py:590
  242.2 2.4 collective-permute-done.73.received
  244.6 4.1 %collective-permute-done.67.refs_2_ = bf16[320,512]{1,0:T(8,128)(2,1)S(1)} collective-permute-done((bf16[320,512]{1,0:T(8,128)(2,1)S(1)}, bf16[320,512]{1,0:T(8,128)(2,1)S(1)}, u32[]{:S(2)}, u32[]{:S(2)}) %collective-permute-start.67) | collective-permute-done | bytes 327712 | tf_op jit(solution)/shard_map/ppermute | solution.py:590
  253.4 7.6 %collective-permute-done.79.refs_7_ = bf16[384,768]{1,0:T(8,128)(2,1)S(1)} collective-permute-done((bf16[384,768]{1,0:T(8,128)(2,1)S(1)}, bf16[384,768]{1,0:T(8,128)(2,1)S(1)}, u32[]{:S(2)}, u32[]{:S(2)}) %collective-permute-start.79) | collective-permute-done | bytes 589856 | tf_op jit(solution)/shard_map/ppermute | solution.py:590
  261.7 6.3 %collective-permute-done.75.refs_3_ = bf16[320,512]{1,0:T(8,128)(2,1)S(1)} collective-permute-done((bf16[320,512]{1,0:T(8,128)(2,1)S(1)}, bf16[320,512]{1,0:T(8,128)(2,1)S(1)}, u32[]{:S(2)}, u32[]{:S(2)}) %collective-permute-start.75) | collective-permute-done | bytes 327712 | tf_op jit(solution)/shard_map/ppermute | solution.py:590
  268.0 5.5 %feed_unpack.1 = (f32[256,5632]{1,0:T(8,128)}, f32[704,1024]{1,0:T(8,128)}, f32[1,256]{1,0:T(1,128)}) custom-call(s32[4]{0:T(128)S(1)} %copy-done.4, bf16[384,768]{1,0:T(8,128)(2,1)S(1)} %feed_join.1.refs_0_, bf16[384,768]{1,0:T(8,128)(2,1)S(1)} %collective-permute-done.59.refs_1_, bf16[384,768]{1,0:T(8,128)(2,1)S(1)} %collective-permute-done.65.refs_2_, ...), custom_call_target="tpu_custom_call" | custom-call | flops 6049999872 | bytes 1000 | tf_op jit(solution)/shard_map/feed_unpack/pallas_call | solution.py:655
  274.9 2.6 collective-permute-start.82
  278.4 3.0 %collective-permute-done.82 = f32[8,1024]{1,0:T(8,128)S(1)} collective-permute-done((f32[8,1024]{1,0:T(8,128)S(1)}, f32[8,1024]{1,0:T(8,128)S(1)}, u32[]{:S(2)}, u32[]{:S(2)}) %collective-permute-start.82) | collective-permute-done | bytes 32800 | tf_op jit(solution)/shard_map/ppermute | solution.py:590
  282.8 3.6 %mixer_unpack.1 = (f32[256,3072]{1,0:T(8,128)}, f32[256,1024]{1,0:T(8,128)}, f32[256,1024]{1,0:T(8,128)}, f32[1,256]{1,0:T(1,128)}) custom-call(s32[4]{0:T(128)S(1)} %copy-done.4, bf16[320,512]{1,0:T(8,128)(2,1)S(1)} %mixer_join.1.refs_0_, bf16[320,512]{1,0:T(8,128)(2,1)S(1)} %collective-permute-done.70.refs_1_, ...), custom_call_target="tpu_custom_call" | custom-call | flops 550000000 | bytes 1000 | tf_op jit(solution)/shard_map/mixer_unpack/pallas_call | solution.py:655
  (189 shorter events, 57.2 us)
Async XLA Ops:
  0.7 12.7 %collective-permute-start = (bf16[128,1024]{1,0:T(8,128)(2,1)}, bf16[128,1024]{1,0:T(8,128)(2,1)S(1)}, u32[]{:S(2)}, u32[]{:S(2)}) collective-permute-start(bf16[128,1024]{1,0:T(8,128)(2,1)} %bitcast.17), channel_id=1, source_target_pairs={{0,0},{1,8},{2,16},{3,24},{4,4},{5,12},{6,20},{7,28},{8,1},{9,9},{... | collective-permute-start | bytes 786440 | tf_op jit(solution)/shard_map/ppermute | solution.py:590
  7.5 29.6 %collective-permute-start.11 = (bf16[2,272,512]{2,1,0:T(8,128)(2,1)}, bf16[2,272,512]{2,1,0:T(8,128)(2,1)S(1)}, u32[]{:S(2)}, u32[]{:S(2)}) collective-permute-start(bf16[2,272,512]{2,1,0:T(8,128)(2,1)} %get-tuple-element.141), channel_id=1, source_target_pairs={{0,2},{1,3},{2,0},{3,1},{4,6},{5,7},{6,4},{7,5},{8,10},{9,11},{10,... | collective-permute-start | bytes 1671176 | tf_op jit(solution)/shard_map/ppermute | solution.py:590
  13.4 10.8 %collective-permute-start.2 = (bf16[128,1024]{1,0:T(8,128)(2,1)S(1)}, bf16[128,1024]{1,0:T(8,128)(2,1)S(1)}, u32[]{:S(2)}, u32[]{:S(2)}) collective-permute-start(bf16[128,1024]{1,0:T(8,128)(2,1)S(1)} %bitcast.18), channel_id=1, source_target_pairs={{0,0},{1,8},{2,16},{3,24},{4,4},{5,12},{6,20},{7,28},{8,1},{9,9},{... | collective-permute-start | bytes 786440 | tf_op jit(solution)/shard_map/ppermute | solution.py:590
  14.1 22.0 %collective-permute-start.6 = (bf16[128,1024]{1,0:T(8,128)(2,1)S(1)}, bf16[128,1024]{1,0:T(8,128)(2,1)S(1)}, u32[]{:S(2)}, u32[]{:S(2)}) collective-permute-start(bf16[128,1024]{1,0:T(8,128)(2,1)S(1)} %collective-permute-done.refs_0_.x), channel_id=1, source_target_pairs={{0,4},{1,5},{2,6},{3,7},{4,0},{5,1},{6,2},{7,3},{8,12},{9,13},{10,... | collective-permute-start | bytes 786440 | tf_op jit(solution)/shard_map/ppermute | solution.py:590
  15.6 24.8 %collective-permute-start.10 = (bf16[272,512]{1,0:T(8,128)(2,1)}, bf16[272,512]{1,0:T(8,128)(2,1)S(1)}, u32[]{:S(2)}, u32[]{:S(2)}) collective-permute-start(bf16[272,512]{1,0:T(8,128)(2,1)} %get-tuple-element.140), channel_id=1, source_target_pairs={{0,1},{1,0},{2,3},{3,2},{4,5},{5,4},{6,7},{7,6},{8,9},{9,8},{10,11... | collective-permute-start | bytes 835592 | tf_op jit(solution)/shard_map/ppermute | solution.py:590
  18.5 23.7 %collective-permute-start.3 = (bf16[128,1024]{1,0:T(8,128)(2,1)S(1)}, bf16[128,1024]{1,0:T(8,128)(2,1)S(1)}, u32[]{:S(2)}, u32[]{:S(2)}) collective-permute-start(bf16[128,1024]{1,0:T(8,128)(2,1)S(1)} %collective-permute-done.refs_0_.x), channel_id=1, source_target_pairs={{0,1},{1,0},{2,3},{3,2},{4,5},{5,4},{6,7},{7,6},{8,9},{9,8},{10,11... | collective-permute-start | bytes 786440 | tf_op jit(solution)/shard_map/ppermute | solution.py:590
  24.1 24.7 %collective-permute-start.4 = (bf16[128,1024]{1,0:T(8,128)(2,1)S(1)}, bf16[128,1024]{1,0:T(8,128)(2,1)S(1)}, u32[]{:S(2)}, u32[]{:S(2)}) collective-permute-start(bf16[128,1024]{1,0:T(8,128)(2,1)S(1)} %collective-permute-done.refs_0_.x), channel_id=1, source_target_pairs={{0,2},{1,3},{2,0},{3,1},{4,6},{5,7},{6,4},{7,5},{8,10},{9,11},{10,... | collective-permute-start | bytes 786440 | tf_op jit(solution)/shard_map/ppermute | solution.py:590
  36.1 12.8 %collective-permute-start.8 = (bf16[128,1024]{1,0:T(8,128)(2,1)S(1)}, bf16[128,1024]{1,0:T(8,128)(2,1)S(1)}, u32[]{:S(2)}, u32[]{:S(2)}) collective-permute-start(bf16[128,1024]{1,0:T(8,128)(2,1)S(1)} %collective-permute-done.refs_0_.x), channel_id=1, source_target_pairs={{0,6},{1,7},{2,4},{3,5},{4,2},{5,3},{6,0},{7,1},{8,14},{9,15},{10,... | collective-permute-start | bytes 786440 | tf_op jit(solution)/shard_map/ppermute | solution.py:590
  37.1 18.9 %collective-permute-start.12 = (bf16[2,272,512]{2,1,0:T(8,128)(2,1)S(1)}, bf16[2,272,512]{2,1,0:T(8,128)(2,1)S(1)}, u32[]{:S(2)}, u32[]{:S(2)}) collective-permute-start(bf16[2,272,512]{2,1,0:T(8,128)(2,1)S(1)} %collective-permute-done.11.refs_10_), channel_id=1, source_target_pairs={{0,1},{1,0},{2,3},{3,2},{4,5},{5,4},{6,7},{7,6},{8,9},{9,8},{10,11... | collective-permute-start | bytes 1671176 | tf_op jit(solution)/shard_map/ppermute | solution.py:590
  40.4 14.1 %collective-permute-start.13 = (bf16[128,1024]{1,0:T(8,128)(2,1)S(1)}, bf16[128,1024]{1,0:T(8,128)(2,1)S(1)}, u32[]{:S(2)}, u32[]{:S(2)}) collective-permute-start(bf16[128,1024]{1,0:T(8,128)(2,1)S(1)} %collective-permute-done.2.refs_8_.cot), channel_id=1, source_target_pairs={{0,2},{1,3},{2,0},{3,1},{4,6},{5,7},{6,4},{7,5},{8,10},{9,11},{10,... | collective-permute-start | bytes 786440 | tf_op jit(solution)/shard_map/ppermute | solution.py:590
  42.2 10.2 %collective-permute-start.7 = (bf16[128,1024]{1,0:T(8,128)(2,1)S(1)}, bf16[128,1024]{1,0:T(8,128)(2,1)S(1)}, u32[]{:S(2)}, u32[]{:S(2)}) collective-permute-start(bf16[128,1024]{1,0:T(8,128)(2,1)S(1)} %collective-permute-done.6.refs_4_), channel_id=1, source_target_pairs={{0,1},{1,0},{2,3},{3,2},{4,5},{5,4},{6,7},{7,6},{8,9},{9,8},{10,11... | collective-permute-start | bytes 786440 | tf_op jit(solution)/shard_map/ppermute | solution.py:590
  50.4 15.7 %collective-permute-start.16 = (bf16[2,128,768]{2,1,0:T(8,128)(2,1)S(1)}, bf16[2,128,768]{2,1,0:T(8,128)(2,1)S(1)}, u32[]{:S(2)}, u32[]{:S(2)}) collective-permute-start(bf16[2,128,768]{2,1,0:T(8,128)(2,1)S(1)} %get-tuple-element.147), channel_id=1, source_target_pairs={{0,2},{1,3},{2,0},{3,1},{4,6},{5,7},{6,4},{7,5},{8,10},{9,11},{10,... | collective-permute-start | bytes 1179656 | tf_op jit(solution)/shard_map/ppermute | solution.py:590
  52.4 13.8 %collective-permute-start.14 = (bf16[128,1024]{1,0:T(8,128)(2,1)S(1)}, bf16[128,1024]{1,0:T(8,128)(2,1)S(1)}, u32[]{:S(2)}, u32[]{:S(2)}) collective-permute-start(bf16[128,1024]{1,0:T(8,128)(2,1)S(1)} %collective-permute-done.2.refs_8_.cot), channel_id=1, source_target_pairs={{0,4},{1,5},{2,6},{3,7},{4,0},{5,1},{6,2},{7,3},{8,12},{9,13},{10,... | collective-permute-start | bytes 786440 | tf_op jit(solution)/shard_map/ppermute | solution.py:590
  54.5 11.6 %collective-permute-start.15 = (bf16[128,1024]{1,0:T(8,128)(2,1)S(1)}, bf16[128,1024]{1,0:T(8,128)(2,1)S(1)}, u32[]{:S(2)}, u32[]{:S(2)}) collective-permute-start(bf16[128,1024]{1,0:T(8,128)(2,1)S(1)} %collective-permute-done.13.refs_10_), channel_id=1, source_target_pairs={{0,4},{1,5},{2,6},{3,7},{4,0},{5,1},{6,2},{7,3},{8,12},{9,13},{10,... | collective-permute-start | bytes 786440 | tf_op jit(solution)/shard_map/ppermute | solution.py:590
  71.7 12.9 %collective-permute-start.20 = (bf16[128,1024]{1,0:T(8,128)(2,1)S(1)}, bf16[128,1024]{1,0:T(8,128)(2,1)S(1)}, u32[]{:S(2)}, u32[]{:S(2)}) collective-permute-start(bf16[128,1024]{1,0:T(8,128)(2,1)S(1)} %get-tuple-element.152), channel_id=1, source_target_pairs={{0,6},{1,7},{2,4},{3,5},{4,2},{5,3},{6,0},{7,1},{8,14},{9,15},{10,... | collective-permute-start | bytes 786440 | tf_op jit(solution)/shard_map/ppermute | solution.py:590
  72.6 15.0 %collective-permute-start.34 = (bf16[2,128,768]{2,1,0:T(8,128)(2,1)S(1)}, bf16[2,128,768]{2,1,0:T(8,128)(2,1)S(1)}, u32[]{:S(2)}, u32[]{:S(2)}) collective-permute-start(bf16[2,128,768]{2,1,0:T(8,128)(2,1)S(1)} %collective-permute-done.16.refs_18_), channel_id=1, source_target_pairs={{0,8},{1,9},{2,10},{3,11},{4,12},{5,13},{6,14},{7,15},{8,0},{9,1},... | collective-permute-start | bytes 1179656 | tf_op jit(solution)/shard_map/ppermute | solution.py:590
  73.1 11.8 %collective-permute-start.28 = (bf16[128,1024]{1,0:T(8,128)(2,1)S(1)}, bf16[128,1024]{1,0:T(8,128)(2,1)S(1)}, u32[]{:S(2)}, u32[]{:S(2)}) collective-permute-start(bf16[128,1024]{1,0:T(8,128)(2,1)S(1)} %collective-permute-done.2.refs_8_.cot), channel_id=1, source_target_pairs={{0,1},{1,0},{2,3},{3,2},{4,5},{5,4},{6,7},{7,6},{8,9},{9,8},{10,11... | collective-permute-start | bytes 786440 | tf_op jit(solution)/shard_map/ppermute | solution.py:590
  87.7 13.5 %collective-permute-start.26 = (bf16[128,1024]{1,0:T(8,128)(2,1)S(1)}, bf16[128,1024]{1,0:T(8,128)(2,1)S(1)}, u32[]{:S(2)}, u32[]{:S(2)}) collective-permute-start(bf16[128,1024]{1,0:T(8,128)(2,1)S(1)} %get-tuple-element.154.refs_0_), channel_id=1, source_target_pairs={{0,6},{1,7},{2,4},{3,5},{4,2},{5,3},{6,0},{7,1},{8,14},{9,15},{10,... | collective-permute-start | bytes 786440 | tf_op jit(solution)/shard_map/ppermute | solution.py:590
  89.3 11.9 %collective-permute-start.35 = (bf16[2,128,768]{2,1,0:T(8,128)(2,1)S(1)}, bf16[2,128,768]{2,1,0:T(8,128)(2,1)S(1)}, u32[]{:S(2)}, u32[]{:S(2)}) collective-permute-start(bf16[2,128,768]{2,1,0:T(8,128)(2,1)S(1)} %collective-permute-done.34.refs_20_), channel_id=1, source_target_pairs={{0,1},{1,0},{2,3},{3,2},{4,5},{5,4},{6,7},{7,6},{8,9},{9,8},{10,11... | collective-permute-start | bytes 1179656 | tf_op jit(solution)/shard_map/ppermute | solution.py:590
  89.3 11.9 %collective-permute-start.21 = (bf16[128,1024]{1,0:T(8,128)(2,1)S(1)}, bf16[128,1024]{1,0:T(8,128)(2,1)S(1)}, u32[]{:S(2)}, u32[]{:S(2)}) collective-permute-start(bf16[128,1024]{1,0:T(8,128)(2,1)S(1)} %get-tuple-element.154.refs_0_), channel_id=1, source_target_pairs={{0,1},{1,0},{2,3},{3,2},{4,5},{5,4},{6,7},{7,6},{8,9},{9,8},{10,11... | collective-permute-start | bytes 786440 | tf_op jit(solution)/shard_map/ppermute | solution.py:590
  114.4 17.3 %collective-permute-start.41 = (bf16[2,384,384]{2,1,0:T(8,128)(2,1)S(1)}, bf16[2,384,384]{2,1,0:T(8,128)(2,1)S(1)}, u32[]{:S(2)}, u32[]{:S(2)}) collective-permute-start(bf16[2,384,384]{2,1,0:T(8,128)(2,1)S(1)} %get-tuple-element.163), channel_id=1, source_target_pairs={{0,8},{1,9},{2,10},{3,11},{4,12},{5,13},{6,14},{7,15},{8,0},{9,1},... | collective-permute-start | bytes 1769480 | tf_op jit(solution)/shard_map/ppermute | solution.py:590
  115.9 9.2 %collective-permute-start.39 = (bf16[128,1024]{1,0:T(8,128)(2,1)S(1)}, bf16[128,1024]{1,0:T(8,128)(2,1)S(1)}, u32[]{:S(2)}, u32[]{:S(2)}) collective-permute-start(bf16[128,1024]{1,0:T(8,128)(2,1)S(1)} %get-tuple-element.173), channel_id=1, source_target_pairs={{0,4},{1,5},{2,6},{3,7},{4,0},{5,1},{6,2},{7,3},{8,12},{9,13},{10,... | collective-permute-start | bytes 786440 | tf_op jit(solution)/shard_map/ppermute | solution.py:590
  116.5 13.3 %collective-permute-start.40 = (bf16[128,1024]{1,0:T(8,128)(2,1)S(1)}, bf16[128,1024]{1,0:T(8,128)(2,1)S(1)}, u32[]{:S(2)}, u32[]{:S(2)}) collective-permute-start(bf16[128,1024]{1,0:T(8,128)(2,1)S(1)} %get-tuple-element.174), channel_id=1, source_target_pairs={{0,6},{1,7},{2,4},{3,5},{4,2},{5,3},{6,0},{7,1},{8,14},{9,15},{10,... | collective-permute-start | bytes 786440 | tf_op jit(solution)/shard_map/ppermute | solution.py:590
  118.4 30.4 %collective-permute-start.43 = (bf16[2,384,384]{2,1,0:T(8,128)(2,1)S(1)}, bf16[2,384,384]{2,1,0:T(8,128)(2,1)S(1)}, u32[]{:S(2)}, u32[]{:S(2)}) collective-permute-start(bf16[2,384,384]{2,1,0:T(8,128)(2,1)S(1)} %get-tuple-element.182), channel_id=1, source_target_pairs={{0,8},{1,9},{2,10},{3,11},{4,12},{5,13},{6,14},{7,15},{8,0},{9,1},... | collective-permute-start | bytes 1769480 | tf_op jit(solution)/shard_map/ppermute | solution.py:590
  130.1 18.7 %collective-permute-start.46 = (bf16[128,1024]{1,0:T(8,128)(2,1)S(1)}, bf16[128,1024]{1,0:T(8,128)(2,1)S(1)}, u32[]{:S(2)}, u32[]{:S(2)}) collective-permute-start(bf16[128,1024]{1,0:T(8,128)(2,1)S(1)} %get-tuple-element.179.refs_0_), channel_id=1, source_target_pairs={{0,2},{1,3},{2,0},{3,1},{4,6},{5,7},{6,4},{7,5},{8,10},{9,11},{10,... | collective-permute-start | bytes 786440 | tf_op jit(solution)/shard_map/ppermute | solution.py:590
  131.2 18.1 %collective-permute-start.48 = (bf16[128,1024]{1,0:T(8,128)(2,1)S(1)}, bf16[128,1024]{1,0:T(8,128)(2,1)S(1)}, u32[]{:S(2)}, u32[]{:S(2)}) collective-permute-start(bf16[128,1024]{1,0:T(8,128)(2,1)S(1)} %get-tuple-element.179.refs_0_), channel_id=1, source_target_pairs={{0,4},{1,5},{2,6},{3,7},{4,0},{5,1},{6,2},{7,3},{8,12},{9,13},{10,... | collective-permute-start | bytes 786440 | tf_op jit(solution)/shard_map/ppermute | solution.py:590
  131.9 17.5 %collective-permute-start.42 = (bf16[128,1024]{1,0:T(8,128)(2,1)S(1)}, bf16[128,1024]{1,0:T(8,128)(2,1)S(1)}, u32[]{:S(2)}, u32[]{:S(2)}) collective-permute-start(bf16[128,1024]{1,0:T(8,128)(2,1)S(1)} %get-tuple-element.179.refs_0_), channel_id=1, source_target_pairs={{0,6},{1,7},{2,4},{3,5},{4,2},{5,3},{6,0},{7,1},{8,14},{9,15},{10,... | collective-permute-start | bytes 786440 | tf_op jit(solution)/shard_map/ppermute | solution.py:590
  133.9 16.1 %collective-permute-start.44 = (bf16[384,384]{1,0:T(8,128)(2,1)S(1)}, bf16[384,384]{1,0:T(8,128)(2,1)S(1)}, u32[]{:S(2)}, u32[]{:S(2)}) collective-permute-start(bf16[384,384]{1,0:T(8,128)(2,1)S(1)} %get-tuple-element.178), channel_id=1, source_target_pairs={{0,16},{1,17},{2,18},{3,19},{4,20},{5,21},{6,22},{7,23},{8,24},{9,... | collective-permute-start | bytes 884744 | tf_op jit(solution)/shard_map/ppermute | solution.py:590
  150.0 16.1 %collective-permute-start.51 = (bf16[384,384]{1,0:T(8,128)(2,1)S(1)}, bf16[384,384]{1,0:T(8,128)(2,1)S(1)}, u32[]{:S(2)}, u32[]{:S(2)}) collective-permute-start(bf16[384,384]{1,0:T(8,128)(2,1)S(1)} %get-tuple-element.183), channel_id=1, source_target_pairs={{0,16},{1,17},{2,18},{3,19},{4,20},{5,21},{6,22},{7,23},{8,24},{9,... | collective-permute-start | bytes 884744 | tf_op jit(solution)/shard_map/ppermute | solution.py:590
  150.5 15.5 %collective-permute-start.52 = (bf16[2,128,1024]{2,1,0:T(8,128)(2,1)S(1)}, bf16[2,128,1024]{2,1,0:T(8,128)(2,1)S(1)}, u32[]{:S(2)}, u32[]{:S(2)}) collective-permute-start(bf16[2,128,1024]{2,1,0:T(8,128)(2,1)S(1)} %get-tuple-element.198), channel_id=1, source_target_pairs={{0,4},{1,5},{2,6},{3,7},{4,0},{5,1},{6,2},{7,3},{8,12},{9,13},{10,... | collective-permute-start | bytes 1572872 | tf_op jit(solution)/shard_map/ppermute | solution.py:590
  168.4 30.2 %collective-permute-start.58 = (bf16[2,320,512]{2,1,0:T(8,128)(2,1)S(1)}, bf16[2,320,512]{2,1,0:T(8,128)(2,1)S(1)}, u32[]{:S(2)}, u32[]{:S(2)}) collective-permute-start(bf16[2,320,512]{2,1,0:T(8,128)(2,1)S(1)} %get-tuple-element.208), channel_id=1, source_target_pairs={{0,8},{1,9},{2,10},{3,11},{4,12},{5,13},{6,14},{7,15},{8,0},{9,1},... | collective-permute-start | bytes 1966088 | tf_op jit(solution)/shard_map/ppermute | solution.py:590
  175.7 35.2 %collective-permute-start.65 = (bf16[384,768]{1,0:T(8,128)(2,1)S(1)}, bf16[384,768]{1,0:T(8,128)(2,1)S(1)}, u32[]{:S(2)}, u32[]{:S(2)}) collective-permute-start(bf16[384,768]{1,0:T(8,128)(2,1)S(1)} %feed_join.1.refs_0_), channel_id=1, source_target_pairs={{0,8},{1,9},{2,10},{3,11},{4,12},{5,13},{6,14},{7,15},{8,0},{9,1},... | collective-permute-start | bytes 1769480 | tf_op jit(solution)/shard_map/ppermute | solution.py:590
  178.4 33.3 %collective-permute-start.59 = (bf16[384,768]{1,0:T(8,128)(2,1)S(1)}, bf16[384,768]{1,0:T(8,128)(2,1)S(1)}, u32[]{:S(2)}, u32[]{:S(2)}) collective-permute-start(bf16[384,768]{1,0:T(8,128)(2,1)S(1)} %feed_join.1.refs_0_), channel_id=1, source_target_pairs={{0,4},{1,5},{2,6},{3,7},{4,0},{5,1},{6,2},{7,3},{8,12},{9,13},{10,... | collective-permute-start | bytes 1769480 | tf_op jit(solution)/shard_map/ppermute | solution.py:590
  179.2 32.5 %collective-permute-start.71 = (bf16[384,768]{1,0:T(8,128)(2,1)S(1)}, bf16[384,768]{1,0:T(8,128)(2,1)S(1)}, u32[]{:S(2)}, u32[]{:S(2)}) collective-permute-start(bf16[384,768]{1,0:T(8,128)(2,1)S(1)} %feed_join.1.refs_0_), channel_id=1, source_target_pairs={{0,16},{1,17},{2,18},{3,19},{4,20},{5,21},{6,22},{7,23},{8,24},{9,... | collective-permute-start | bytes 1769480 | tf_op jit(solution)/shard_map/ppermute | solution.py:590
  198.7 26.2 %collective-permute-start.60 = (bf16[320,512]{1,0:T(8,128)(2,1)S(1)}, bf16[320,512]{1,0:T(8,128)(2,1)S(1)}, u32[]{:S(2)}, u32[]{:S(2)}) collective-permute-start(bf16[320,512]{1,0:T(8,128)(2,1)S(1)} %get-tuple-element.225), channel_id=1, source_target_pairs={{0,16},{1,17},{2,18},{3,19},{4,20},{5,21},{6,22},{7,23},{8,24},{9,... | collective-permute-start | bytes 983048 | tf_op jit(solution)/shard_map/ppermute | solution.py:590
  198.8 27.2 %collective-permute-start.64 = (bf16[2,144,1024]{2,1,0:T(8,128)(2,1)S(1)}, bf16[2,144,1024]{2,1,0:T(8,128)(2,1)S(1)}, u32[]{:S(2)}, u32[]{:S(2)}) collective-permute-start(bf16[2,144,1024]{2,1,0:T(8,128)(2,1)S(1)} %get-tuple-element.232), channel_id=1, source_target_pairs={{0,4},{1,5},{2,6},{3,7},{4,0},{5,1},{6,2},{7,3},{8,12},{9,13},{10,... | collective-permute-start | bytes 1769480 | tf_op jit(solution)/shard_map/ppermute | solution.py:590
  210.9 16.1 %collective-permute-start.66 = (bf16[384,768]{1,0:T(8,128)(2,1)S(1)}, bf16[384,768]{1,0:T(8,128)(2,1)S(1)}, u32[]{:S(2)}, u32[]{:S(2)}) collective-permute-start(bf16[384,768]{1,0:T(8,128)(2,1)S(1)} %collective-permute-done.65.refs_2_), channel_id=1, source_target_pairs={{0,4},{1,5},{2,6},{3,7},{4,0},{5,1},{6,2},{7,3},{8,12},{9,13},{10,... | collective-permute-start | bytes 1769480 | tf_op jit(solution)/shard_map/ppermute | solution.py:590
  211.7 24.2 %collective-permute-start.78 = (bf16[384,768]{1,0:T(8,128)(2,1)S(1)}, bf16[384,768]{1,0:T(8,128)(2,1)S(1)}, u32[]{:S(2)}, u32[]{:S(2)}) collective-permute-start(bf16[384,768]{1,0:T(8,128)(2,1)S(1)} %collective-permute-done.71.refs_4_), channel_id=1, source_target_pairs={{0,8},{1,9},{2,10},{3,11},{4,12},{5,13},{6,14},{7,15},{8,0},{9,1},... | collective-permute-start | bytes 1769480 | tf_op jit(solution)/shard_map/ppermute | solution.py:590
  225.1 16.3 %collective-permute-start.72 = (bf16[384,768]{1,0:T(8,128)(2,1)S(1)}, bf16[384,768]{1,0:T(8,128)(2,1)S(1)}, u32[]{:S(2)}, u32[]{:S(2)}) collective-permute-start(bf16[384,768]{1,0:T(8,128)(2,1)S(1)} %collective-permute-done.71.refs_4_), channel_id=1, source_target_pairs={{0,4},{1,5},{2,6},{3,7},{4,0},{5,1},{6,2},{7,3},{8,12},{9,13},{10,... | collective-permute-start | bytes 1769480 | tf_op jit(solution)/shard_map/ppermute | solution.py:590
  231.6 17.0 %collective-permute-start.67 = (bf16[320,512]{1,0:T(8,128)(2,1)S(1)}, bf16[320,512]{1,0:T(8,128)(2,1)S(1)}, u32[]{:S(2)}, u32[]{:S(2)}) collective-permute-start(bf16[320,512]{1,0:T(8,128)(2,1)S(1)} %mixer_join.1.refs_0_), channel_id=1, source_target_pairs={{0,8},{1,9},{2,10},{3,11},{4,12},{5,13},{6,14},{7,15},{8,0},{9,1},... | collective-permute-start | bytes 983048 | tf_op jit(solution)/shard_map/ppermute | solution.py:590
  232.4 17.5 %collective-permute-start.69 = (bf16[320,512]{1,0:T(8,128)(2,1)S(1)}, bf16[320,512]{1,0:T(8,128)(2,1)S(1)}, u32[]{:S(2)}, u32[]{:S(2)}) collective-permute-start(bf16[320,512]{1,0:T(8,128)(2,1)S(1)} %mixer_join.1.refs_0_), channel_id=1, source_target_pairs={{0,16},{1,17},{2,18},{3,19},{4,20},{5,21},{6,22},{7,23},{8,24},{9,... | collective-permute-start | bytes 983048 | tf_op jit(solution)/shard_map/ppermute | solution.py:590
  234.8 15.2 %collective-permute-start.70 = (bf16[320,512]{1,0:T(8,128)(2,1)S(1)}, bf16[320,512]{1,0:T(8,128)(2,1)S(1)}, u32[]{:S(2)}, u32[]{:S(2)}) collective-permute-start(bf16[320,512]{1,0:T(8,128)(2,1)S(1)} %mixer_join.1.refs_0_), channel_id=1, source_target_pairs={{0,4},{1,5},{2,6},{3,7},{4,0},{5,1},{6,2},{7,3},{8,12},{9,13},{10,... | collective-permute-start | bytes 983048 | tf_op jit(solution)/shard_map/ppermute | solution.py:590
  241.3 19.7 %collective-permute-start.79 = (bf16[384,768]{1,0:T(8,128)(2,1)S(1)}, bf16[384,768]{1,0:T(8,128)(2,1)S(1)}, u32[]{:S(2)}, u32[]{:S(2)}) collective-permute-start(bf16[384,768]{1,0:T(8,128)(2,1)S(1)} %collective-permute-done.78.refs_6_), channel_id=1, source_target_pairs={{0,4},{1,5},{2,6},{3,7},{4,0},{5,1},{6,2},{7,3},{8,12},{9,13},{10,... | collective-permute-start | bytes 1769480 | tf_op jit(solution)/shard_map/ppermute | solution.py:590
  249.9 18.1 %collective-permute-start.75 = (bf16[320,512]{1,0:T(8,128)(2,1)S(1)}, bf16[320,512]{1,0:T(8,128)(2,1)S(1)}, u32[]{:S(2)}, u32[]{:S(2)}) collective-permute-start(bf16[320,512]{1,0:T(8,128)(2,1)S(1)} %collective-permute-done.67.refs_2_), channel_id=1, source_target_pairs={{0,4},{1,5},{2,6},{3,7},{4,0},{5,1},{6,2},{7,3},{8,12},{9,13},{10,... | collective-permute-start | bytes 983048 | tf_op jit(solution)/shard_map/ppermute | solution.py:590
  251.0 23.0 %collective-permute-start.76 = (bf16[320,512]{1,0:T(8,128)(2,1)S(1)}, bf16[320,512]{1,0:T(8,128)(2,1)S(1)}, u32[]{:S(2)}, u32[]{:S(2)}) collective-permute-start(bf16[320,512]{1,0:T(8,128)(2,1)S(1)} %collective-permute-done.69.refs_4_), channel_id=1, source_target_pairs={{0,4},{1,5},{2,6},{3,7},{4,0},{5,1},{6,2},{7,3},{8,12},{9,13},{10,... | collective-permute-start | bytes 983048 | tf_op jit(solution)/shard_map/ppermute | solution.py:590
  252.0 22.0 %collective-permute-start.77 = (bf16[320,512]{1,0:T(8,128)(2,1)S(1)}, bf16[320,512]{1,0:T(8,128)(2,1)S(1)}, u32[]{:S(2)}, u32[]{:S(2)}) collective-permute-start(bf16[320,512]{1,0:T(8,128)(2,1)S(1)} %collective-permute-done.69.refs_4_), channel_id=1, source_target_pairs={{0,8},{1,9},{2,10},{3,11},{4,12},{5,13},{6,14},{7,15},{8,0},{9,1},... | collective-permute-start | bytes 983048 | tf_op jit(solution)/shard_map/ppermute | solution.py:590
  252.4 26.0 %collective-permute-start.68 = (bf16[128,1024]{1,0:T(8,128)(2,1)S(1)}, bf16[128,1024]{1,0:T(8,128)(2,1)S(1)}, u32[]{:S(2)}, u32[]{:S(2)}) collective-permute-start(bf16[128,1024]{1,0:T(8,128)(2,1)S(1)} %output.1), channel_id=1, source_target_pairs={{0,0},{1,8},{2,16},{3,24},{4,4},{5,12},{6,20},{7,28},{8,1},{9,9},{... | collective-permute-start | bytes 786440 | tf_op jit(solution)/shard_map/ppermute | solution.py:590
  261.0 16.6 %collective-permute-start.74 = (bf16[128,1024]{1,0:T(8,128)(2,1)S(1)}, bf16[128,1024]{1,0:T(8,128)(2,1)S(1)}, u32[]{:S(2)}, u32[]{:S(2)}) collective-permute-start(bf16[128,1024]{1,0:T(8,128)(2,1)S(1)} %get-tuple-element.245), channel_id=1, source_target_pairs={{0,0},{1,8},{2,16},{3,24},{4,4},{5,12},{6,20},{7,28},{8,1},{9,9},{... | collective-permute-start | bytes 786440 | tf_op jit(solution)/shard_map/ppermute | solution.py:590
  (49 other events, 507.9 us)
